TPU v7x, 32 devices: a whole 2x2x4 slice. The times are simulated.
32 devices in a mesh: depth: 4 (over y, core), freq: 8 (over z, x).
Axes of the slice: x: 2, y: 2, z: 4, core: 2. Of those that a mesh axis runs over, the one named last changes fastest.
Arguments:
- source_top: bfloat16 [2, 8, 2, 512, 512], P(None, 'freq'), may hold values from -6 to 6
- receiver_top: bfloat16 [2, 8, 2, 512, 512], P(None, 'freq'), may hold values from -6 to 6
- slowness_codes: int32 [4, 1024, 1024], P('depth'), may hold values from 0 to 31
- slowness_table: float32 [32], replicated, may hold values from 0.8 to 1.25
- anchors: int32 [2, 2], replicated, may hold values from 0 to 512, as said below
Outputs:
- image: float32 [4, 15, 512, 512], P('depth', None, 'freq')
Inputs may be any that keep to these rules, and one draw needn't show every extreme that they name: `anchors`: each of the two coordinates is 0 for some shot and 512 for another.
All inputs are finite; a program needn't handle non-finite values.
Results may differ from a plain program's by a relative error of at most 0.03.
Values may be sent and summed in bfloat16 or wider, within the bound.
No kernel may reach another device: no remote copies, remote signals or barrier semaphores. Data moves between devices by JAX's collectives and lax.ppermute only.
A program may use at most 192 MiB of HBM per device.

v0:
```python
import math

import jax
import jax.numpy as jnp
from jax import lax
from jax.sharding import PartitionSpec as P

LAG = 7


def transform_tables(length):
    position = jnp.arange(length, dtype=jnp.int32)
    product = position[:, None] * position[None, :] % length
    angles = product.astype(jnp.float32) * (2.0 * math.pi / length)
    factor = 1.0 / math.sqrt(length)
    return (jnp.cos(angles) * factor, jnp.sin(angles) * factor)


def build_tables(len_x, len_y):
    cos_x, sin_x = transform_tables(len_x)
    cos_y, sin_y = transform_tables(len_y)
    fwd_x = jnp.stack([jnp.stack([cos_x, sin_x]), jnp.stack([-sin_x, cos_x])]).astype(jnp.bfloat16)
    inv_x = jnp.stack([jnp.stack([cos_x, -sin_x]), jnp.stack([sin_x, cos_x])]).astype(jnp.bfloat16)
    fwd_y = jnp.stack(
        [jnp.stack([cos_y, -sin_y], axis=1), jnp.stack([sin_y, cos_y], axis=1)]
    ).astype(jnp.bfloat16)
    inv_y = jnp.stack(
        [jnp.stack([cos_y, sin_y], axis=1), jnp.stack([-sin_y, cos_y], axis=1)]
    ).astype(jnp.bfloat16)
    return (fwd_x, inv_x, fwd_y, inv_y)


def wavenumbers(length):
    position = jnp.arange(length, dtype=jnp.int32)
    signed = jnp.where(position < length // 2, position, position - length)
    return signed.astype(jnp.float32) * (2.0 * math.pi / length)


def aperture_slowness(code_plane, slowness_table, corner, rows_x, rows_y):
    window = lax.dynamic_slice(code_plane, (corner[0], corner[1]), (rows_x, rows_y))
    levels = jnp.arange(slowness_table.shape[0], dtype=jnp.int32)
    return jnp.sum(
        jnp.where(window[None] == levels[:, None, None], slowness_table[:, None, None], 0.0), axis=0
    )


def propagators(slowness, angular, wave_x, wave_y):
    mean_slowness = jnp.mean(slowness)
    vertical = (angular * mean_slowness) ** 2 - wave_x[:, None] ** 2 - wave_y[None, :] ** 2
    travel = jnp.sqrt(jnp.maximum(vertical, 0.0))
    damping = jnp.exp(-jnp.sqrt(jnp.maximum(-vertical, 0.0)))
    screen_angle = angular * (slowness - mean_slowness)
    return (
        damping * jnp.cos(travel),
        damping * jnp.sin(travel),
        jnp.cos(screen_angle),
        jnp.sin(screen_angle),
    )


def advance(fields, tables, operators, kind_signs):
    fwd_x, inv_x, fwd_y, inv_y = tables
    conjugate = kind_signs[None, :, None, None]
    across_x = jnp.einsum(
        "pqxu,gfquy->gfpxy", fwd_x, fields, preferred_element_type=jnp.float32
    ).astype(jnp.bfloat16)
    second = jnp.einsum("gfqxu,qupb->gfxpb", across_x, fwd_y, preferred_element_type=jnp.float32)
    real_part = second[:, :, :, 0]
    imag_part = second[:, :, :, 1]
    phase_re = operators[0][:, None]
    phase_im = operators[1][:, None] * conjugate
    shifted = jnp.stack(
        [real_part * phase_re - imag_part * phase_im, real_part * phase_im + imag_part * phase_re],
        axis=3,
    ).astype(jnp.bfloat16)
    back_y = jnp.einsum(
        "gfxqu,qupb->gfxpb", shifted, inv_y, preferred_element_type=jnp.float32
    ).astype(jnp.bfloat16)
    fourth = jnp.einsum("pqxu,gfuqy->gfpxy", inv_x, back_y, preferred_element_type=jnp.float32)
    real_part = fourth[:, :, 0]
    imag_part = fourth[:, :, 1]
    turn_re = operators[2][:, None]
    turn_im = operators[3][:, None] * conjugate
    return jnp.stack(
        [real_part * turn_re - imag_part * turn_im, real_part * turn_im + imag_part * turn_re],
        axis=2,
    ).astype(jnp.bfloat16)


def correlate(source, receiver, row_count):
    lag_terms = []
    for offset in range(-LAG, LAG + 1):
        shifted_source = source[:, :, :, LAG - offset : LAG - offset + row_count].astype(
            jnp.float32
        )
        shifted_receiver = receiver[:, :, :, LAG + offset : LAG + offset + row_count].astype(
            jnp.float32
        )
        lag_terms.append(jnp.sum(shifted_source * shifted_receiver, axis=(1, 2)))
    return jnp.stack(lag_terms, axis=1)


def shards(source_top, receiver_top, slowness_codes, slowness_table, anchors):
    shot_count, freq_dev, unused_parts, rows_x, rows_y = source_top.shape
    planes = slowness_codes.shape[0]
    freq_count = lax.axis_size("freq")
    depth_count = lax.axis_size("depth")
    freq_total = freq_count * freq_dev
    depth_index = lax.axis_index("depth")
    factor = 1.0 / math.sqrt(2.0 * shot_count * freq_total)
    tables = build_tables(rows_x, rows_y)
    wave_x = wavenumbers(rows_x)
    wave_y = wavenumbers(rows_y)
    freq_first = lax.axis_index("freq") * freq_dev
    positions = (freq_first + jnp.arange(freq_dev, dtype=jnp.int32)).astype(jnp.float32)
    angular = jnp.reshape(math.pi * (0.45 + 0.5 * (positions + 0.5) / freq_total), (freq_dev, 1, 1))
    top_fields = jnp.stack([source_top, receiver_top], axis=2)

    def record_shot(record, plane_stack):
        padded = jnp.pad(plane_stack, ((0, 0), (0, 0), (0, 0), (0, 0), (LAG, LAG), (0, 0)))
        return record + correlate(padded[:, :, 0], padded[:, :, 1], rows_x)

    record = jnp.zeros((planes, 2 * LAG + 1, rows_x, rows_y), jnp.float32)
    items = 2 * shot_count // depth_count
    all_codes = lax.all_gather(slowness_codes, "depth", axis=0, tiled=True)
    which = depth_index * items + 0
    shot_pick = which // 2
    kind_pick = which % 2
    start = lax.dynamic_index_in_dim(top_fields, shot_pick, 0, keepdims=False)
    start = lax.dynamic_slice_in_dim(start, kind_pick, 1, 1)
    sign_one = jnp.reshape(jnp.where(kind_pick == 0, 1.0, -1.0).astype(jnp.float32), (1,))
    corner_pick = anchors[shot_pick]

    def chain_plane(current, code_plane, corner_pick=corner_pick, sign_one=sign_one):
        slowness = aperture_slowness(code_plane, slowness_table, corner_pick, rows_x, rows_y)
        operators = propagators(slowness, angular, wave_x, wave_y)
        current = advance(current, tables, operators, sign_one)
        return (current, current)

    unused_last, stack = lax.scan(chain_plane, start, all_codes)
    chain_stacks = [stack[:, :, 0]]
    chains = jnp.stack(chain_stacks)
    arrived = lax.all_to_all(chains, "depth", split_axis=1, concat_axis=0, tiled=True)
    arranged = arrived.reshape(shot_count, 2, planes, freq_dev, 2, rows_x, rows_y)
    arranged = jnp.transpose(arranged, (0, 2, 3, 1, 4, 5, 6))

    def chain_shot(shot_index, record_now):
        plane_stack = lax.dynamic_index_in_dim(arranged, shot_index, 0, keepdims=False)
        return record_shot(record_now, plane_stack)

    record = lax.fori_loop(0, shot_count, chain_shot, record)
    return lax.psum_scatter(
        (record * factor).astype(jnp.bfloat16), "freq", scatter_dimension=2, tiled=True
    ).astype(jnp.float32)


def solution(mesh):
    return jax.shard_map(
        shards,
        mesh=mesh,
        in_specs=(
            P(None, "freq", None, None, None),
            P(None, "freq", None, None, None),
            P("depth", None, None),
            P(),
            P(),
        ),
        out_specs=P("depth", None, "freq", None),
        check_vma=False,
    )
```

profile of v0, /device:TPU:4, one launch (start us, length us, event | category | flops | bytes accessed | tf_op | source)
XLA Modules:
  0.0 594.9 jit_solution(15359389341753195258)
XLA Ops:
  13.4 4.0 fusion.61
  17.4 4.4 negate_convert_fusion
  23.8 4.0 fusion.60
  27.8 4.0 multiply_convert_fusion.2
  31.8 4.0 negate_convert_fusion.1
  37.6 2.3 pad_maximum_fusion.1
  39.9 75.0 %all-gather.2.cloned.1.call-done = s32[4,1024,1024]{2,1,0:T(8,128)} async-done(((s32[1,1024,1024]{2,1,0:T(8,128)}), s32[4,1024,1024]{2,1,0:T(8,128)}) %all-gather.2.cloned.1.call-update) | async-done | bytes 16777232 | tf_op jit(solution)/shard_map/all_gather | solution.py:125
  114.9 175.3 %while.33 = (s32[]{:T(128)}, bf16[1,1,2,512,512]{3,4,2,1,0:T(8,128)(2,1)}, bf16[4,1,1,2,512,512]{4,5,3,2,1,0:T(8,128)(2,1)}, bf16[2,2,512,512]{3,2,1,0:T(8,128)(...) while((s32[]{:T(128)}, ...), condition=%wide.region_3.4_spmd.clone, body=%wide.region_0.3_spmd.clone.sunk | while | flops 4341111296 | bytes 32514932 | solution.py:140
  115.2 1.7 dynamic-slice_bitcast_fusion.2
  116.9 14.6 %select_reduce_fusion.3 = (f32[512,512]{1,0:T(8,128)S(1)}, f32[]{:T(128)}) fusion(f32[32]{0:T(128)S(1)} %get-tuple-element.725, s32[512,512]{1,0:T(8,128)S(1)} %dynamic-slice_bitcast_fusion.2), kind=kLoop, calls=%fused_computation.2.clone.1 | loop fusion | flops 33292288 | bytes 2097284 | tf_op jit(solution)/shard_map/while/body/eval_jaxpr/reduce_sum | solution.py:42
  132.2 4.9 convolution_bitcast_fusion.4
  137.1 6.1 %fusion.84 = (bf16[512,1,512]{2,0,1:T(8,128)(2,1)}, bf16[512,1,512]{2,0,1:T(8,128)(2,1)}) fusion(f32[]{:T(128)} %get-tuple-element.727, f32[1,1,512,2,512]{4,2,3,1,0:T(8,128)S(1)} %convolution_bitcast_fusion.4, f32[512]{0:T(512)S(1)} %bitcast.235, f32[512]{0:T(512)S(1)} %bitcast.234), kind=kLoop, calls=%fused_computation.43.clone.1 | loop fusion | flops 4194304 | bytes 3149828 | tf_op jit(solution)/shard_map/while/body/eval_jaxpr/stack | solution.py:72
  143.2 6.2 %convolution_bitcast_fusion.5 = f32[1,1,2,512,512]{3,4,2,1,0:T(8,128)} fusion(bf16[2,2,512,512]{3,2,1,0:T(8,128)(2,1)} %get-tuple-element.729, bf16[2,512,2,512]{3,1,0,2:T(8,128)(2,1)} %get-tuple-element.728, bf16[512,1,512]{2,0,1:T(8,128)(2,1)} %get-tuple-element.658, bf16[512,1,512]{2,0,1:T(8,128)(2,1)} %get-tuple-element.659), kind=kOutput, calls=%fused_computation.7.clone.1 | convolution fusion | flops 2150105088 | bytes 7340032 | tf_op jit(solution)/shard_map/while/body/eval_jaxpr/pqxu,gfuqy->gfpxy/dot_general | solution.py:79
  149.8 5.1 fusion.85
  157.0 1.7 dynamic-slice_bitcast_fusion.2
  158.7 14.6 %select_reduce_fusion.3 = (f32[512,512]{1,0:T(8,128)S(1)}, f32[]{:T(128)}) fusion(f32[32]{0:T(128)S(1)} %get-tuple-element.725, s32[512,512]{1,0:T(8,128)S(1)} %dynamic-slice_bitcast_fusion.2), kind=kLoop, calls=%fused_computation.2.clone.1 | loop fusion | flops 33292288 | bytes 2097284 | tf_op jit(solution)/shard_map/while/body/eval_jaxpr/reduce_sum | solution.py:42
  174.0 4.9 convolution_bitcast_fusion.4
  178.9 6.1 %fusion.84 = (bf16[512,1,512]{2,0,1:T(8,128)(2,1)}, bf16[512,1,512]{2,0,1:T(8,128)(2,1)}) fusion(f32[]{:T(128)} %get-tuple-element.727, f32[1,1,512,2,512]{4,2,3,1,0:T(8,128)S(1)} %convolution_bitcast_fusion.4, f32[512]{0:T(512)S(1)} %bitcast.235, f32[512]{0:T(512)S(1)} %bitcast.234), kind=kLoop, calls=%fused_computation.43.clone.1 | loop fusion | flops 4194304 | bytes 3149828 | tf_op jit(solution)/shard_map/while/body/eval_jaxpr/stack | solution.py:72
  185.0 6.2 %convolution_bitcast_fusion.5 = f32[1,1,2,512,512]{3,4,2,1,0:T(8,128)} fusion(bf16[2,2,512,512]{3,2,1,0:T(8,128)(2,1)} %get-tuple-element.729, bf16[2,512,2,512]{3,1,0,2:T(8,128)(2,1)} %get-tuple-element.728, bf16[512,1,512]{2,0,1:T(8,128)(2,1)} %get-tuple-element.658, bf16[512,1,512]{2,0,1:T(8,128)(2,1)} %get-tuple-element.659), kind=kOutput, calls=%fused_computation.7.clone.1 | convolution fusion | flops 2150105088 | bytes 7340032 | tf_op jit(solution)/shard_map/while/body/eval_jaxpr/pqxu,gfuqy->gfpxy/dot_general | solution.py:79
  191.6 5.1 fusion.85
  198.9 1.7 dynamic-slice_bitcast_fusion.2
  200.5 14.6 %select_reduce_fusion.3 = (f32[512,512]{1,0:T(8,128)S(1)}, f32[]{:T(128)}) fusion(f32[32]{0:T(128)S(1)} %get-tuple-element.725, s32[512,512]{1,0:T(8,128)S(1)} %dynamic-slice_bitcast_fusion.2), kind=kLoop, calls=%fused_computation.2.clone.1 | loop fusion | flops 33292288 | bytes 2097284 | tf_op jit(solution)/shard_map/while/body/eval_jaxpr/reduce_sum | solution.py:42
  215.9 4.9 convolution_bitcast_fusion.4
  220.8 6.1 %fusion.84 = (bf16[512,1,512]{2,0,1:T(8,128)(2,1)}, bf16[512,1,512]{2,0,1:T(8,128)(2,1)}) fusion(f32[]{:T(128)} %get-tuple-element.727, f32[1,1,512,2,512]{4,2,3,1,0:T(8,128)S(1)} %convolution_bitcast_fusion.4, f32[512]{0:T(512)S(1)} %bitcast.235, f32[512]{0:T(512)S(1)} %bitcast.234), kind=kLoop, calls=%fused_computation.43.clone.1 | loop fusion | flops 4194304 | bytes 3149828 | tf_op jit(solution)/shard_map/while/body/eval_jaxpr/stack | solution.py:72
  226.9 6.2 %convolution_bitcast_fusion.5 = f32[1,1,2,512,512]{3,4,2,1,0:T(8,128)} fusion(bf16[2,2,512,512]{3,2,1,0:T(8,128)(2,1)} %get-tuple-element.729, bf16[2,512,2,512]{3,1,0,2:T(8,128)(2,1)} %get-tuple-element.728, bf16[512,1,512]{2,0,1:T(8,128)(2,1)} %get-tuple-element.658, bf16[512,1,512]{2,0,1:T(8,128)(2,1)} %get-tuple-element.659), kind=kOutput, calls=%fused_computation.7.clone.1 | convolution fusion | flops 2150105088 | bytes 7340032 | tf_op jit(solution)/shard_map/while/body/eval_jaxpr/pqxu,gfuqy->gfpxy/dot_general | solution.py:79
  233.5 5.1 fusion.85
  240.7 1.7 dynamic-slice_bitcast_fusion.2
  242.3 14.6 %select_reduce_fusion.3 = (f32[512,512]{1,0:T(8,128)S(1)}, f32[]{:T(128)}) fusion(f32[32]{0:T(128)S(1)} %get-tuple-element.725, s32[512,512]{1,0:T(8,128)S(1)} %dynamic-slice_bitcast_fusion.2), kind=kLoop, calls=%fused_computation.2.clone.1 | loop fusion | flops 33292288 | bytes 2097284 | tf_op jit(solution)/shard_map/while/body/eval_jaxpr/reduce_sum | solution.py:42
  257.7 4.9 convolution_bitcast_fusion.4
  262.6 6.1 %fusion.84 = (bf16[512,1,512]{2,0,1:T(8,128)(2,1)}, bf16[512,1,512]{2,0,1:T(8,128)(2,1)}) fusion(f32[]{:T(128)} %get-tuple-element.727, f32[1,1,512,2,512]{4,2,3,1,0:T(8,128)S(1)} %convolution_bitcast_fusion.4, f32[512]{0:T(512)S(1)} %bitcast.235, f32[512]{0:T(512)S(1)} %bitcast.234), kind=kLoop, calls=%fused_computation.43.clone.1 | loop fusion | flops 4194304 | bytes 3149828 | tf_op jit(solution)/shard_map/while/body/eval_jaxpr/stack | solution.py:72
  268.7 6.2 %convolution_bitcast_fusion.5 = f32[1,1,2,512,512]{3,4,2,1,0:T(8,128)} fusion(bf16[2,2,512,512]{3,2,1,0:T(8,128)(2,1)} %get-tuple-element.729, bf16[2,512,2,512]{3,1,0,2:T(8,128)(2,1)} %get-tuple-element.728, bf16[512,1,512]{2,0,1:T(8,128)(2,1)} %get-tuple-element.658, bf16[512,1,512]{2,0,1:T(8,128)(2,1)} %get-tuple-element.659), kind=kOutput, calls=%fused_computation.7.clone.1 | convolution fusion | flops 2150105088 | bytes 7340032 | tf_op jit(solution)/shard_map/while/body/eval_jaxpr/pqxu,gfuqy->gfpxy/dot_general | solution.py:79
  275.3 5.1 fusion.85
  290.2 6.2 %all-to-all-start = ((bf16[1,4,1,2,512,512]{4,5,3,2,0,1:T(8,128)(2,1)}), bf16[1,4,1,2,512,512]{4,5,3,2,0,1:T(8,128)(2,1)}, u32[]{:S(2)}, u32[]{:S(2)}) async-start(bf16[1,4,1,2,512,512]{4,5,3,2,0,1:T(8,128)(2,1)} %bitcast.15), calls=%async_computation | async-start | bytes 8388608 | tf_op jit(solution)/shard_map/all_to_all | solution.py:143
  296.4 46.6 %all-to-all-done = bf16[1,4,1,2,512,512]{4,5,3,2,0,1:T(8,128)(2,1)} async-done(((bf16[1,4,1,2,512,512]{4,5,3,2,0,1:T(8,128)(2,1)}), bf16[1,4,1,2,512,512]{4,5,3,2,0,1:T(8,128)(2,1)}, u32[]{:S(2)}, u32[]{:S(2)}) %all-to-all-start) | async-done | bytes 4194336 | tf_op jit(solution)/shard_map/all_to_all | solution.py:143
  343.0 89.6 %while.34 = (s32[]{:T(128)}, f32[1,15,512,512]{3,2,1,0:T(8,128)}, bf16[2,1,1,2,2,512,512]{5,6,4,3,0,2,1:T(8,128)(2,1)}, s32[]{:T(128)}, s32[]{:T(128)}) while((s32[]{:T(128)}, f32[1,15,512,512]{3,2,1,0:T(8,128)}, bf16[2,1,1,2,2,512,512]{5,6,4,3,0,2,1:T(8,128)(2,1)}, s32[]{:T(128)}, s32[]{:T(128)}) %tuple.119), condition=%wide.region_20.21_spmd.clone, body=%wide.region_4.20_spmd.clone.sunk | while | flops 35389440 | bytes 138469456 | solution.py:151
  343.0 3.0 constant_dynamic-slice_fusion.3
  346.1 2.8 copy.39
  349.4 3.4 multiply_reduce_fusion.17
  359.2 5.0 multiply_reduce_fusion.18
  373.8 12.3 %select_add_fusion.2 = f32[1,15,512,512]{3,2,1,0:T(8,128)} fusion(f32[1,15,512,512]{3,2,1,0:T(8,128)} %bitcast_dynamic-update-slice_fusion.44, f32[1,15,512,512]{3,2,1,0:T(8,128)} %get-tuple-element.740, pred[]{:T(512)S(6)} %compare.33), kind=kLoop, calls=%fused_computation.55.clone.1 | loop fusion | flops 7864320 | bytes 47185920 | tf_op jit(solution)/shard_map/while/body/eval_jaxpr/add | solution.py:121
  386.0 3.0 constant_dynamic-slice_fusion.3
  389.0 2.8 copy.39
  392.4 3.4 multiply_reduce_fusion.17
  402.1 5.0 multiply_reduce_fusion.18
  416.7 15.9 %select_add_fusion.2 = f32[1,15,512,512]{3,2,1,0:T(8,128)} fusion(f32[1,15,512,512]{3,2,1,0:T(8,128)} %bitcast_dynamic-update-slice_fusion.44, f32[1,15,512,512]{3,2,1,0:T(8,128)} %get-tuple-element.740, pred[]{:T(512)S(6)} %compare.33), kind=kLoop, calls=%fused_computation.55.clone.1 | loop fusion | flops 7864320 | bytes 47185920 | tf_op jit(solution)/shard_map/while/body/eval_jaxpr/add | solution.py:121
  432.7 10.9 %multiply_convert_fusion = bf16[1,15,512,512]{3,2,1,0:T(8,128)(2,1)} fusion(f32[1,15,512,512]{3,2,1,0:T(8,128)} %get-tuple-element.366), kind=kLoop, calls=%fused_computation.91 | loop fusion | flops 7864320 | bytes 23592960 | tf_op jit(solution)/shard_map/convert_element_type | solution.py:153
  443.6 141.5 %reduce-scatter.2.cloned.1.call-done = bf16[1,15,64,512]{3,2,1,0:T(8,128)(2,1)} async-done(((bf16[1,15,512,512]{3,2,1,0:T(8,128)(2,1)}), bf16[1,15,64,512]{3,2,1,0:T(8,128)(2,1)}) %reduce-scatter.2.cloned.1.call-update) | async-done | bytes 983056 | tf_op jit(solution)/shard_map/reduce_scatter | solution.py:152
  585.1 2.7 convert_element_type.465
  (75 shorter events, 49.9 us)
Async XLA Ops:
  6.5 0.8 copy-start
  6.5 3.9 copy-start.2
  6.5 108.4 %all-gather.2.cloned.1.call-start = ((), (), s32[]{:S(2)}) async-start(), calls=%async_computation.2 | async-start | bytes 20971520 | tf_op jit(solution)/shard_map/all_gather | solution.py:125
  37.6 77.3 %copy-start.3 = (f32[32]{0:T(128)S(1)}, f32[32]{0:T(128)}, u32[]{:S(2)}) copy-start(f32[32]{0:T(128)} %param.12) | copy-start | bytes 388
  290.2 52.8 %all-to-all-start = ((bf16[1,4,1,2,512,512]{4,5,3,2,0,1:T(8,128)(2,1)}), bf16[1,4,1,2,512,512]{4,5,3,2,0,1:T(8,128)(2,1)}, u32[]{:S(2)}, u32[]{:S(2)}) async-start(bf16[1,4,1,2,512,512]{4,5,3,2,0,1:T(8,128)(2,1)} %bitcast.15), calls=%async_computation | async-start | bytes 8388608 | tf_op jit(solution)/shard_map/all_to_all | solution.py:143
  296.4 288.7 %reduce-scatter.2.cloned.1.call-start = ((), (), s32[]{:S(2)}) async-start(), calls=%async_computation.3 | async-start | bytes 8847360 | tf_op jit(solution)/shard_map/reduce_scatter | solution.py:152
  443.6 144.2 %copy-start.1 = (s32[2,2]{1,0:T(2,128)S(1)}, s32[2,2]{1,0:T(2,128)}, u32[]{:S(2)}) copy-start(s32[2,2]{1,0:T(2,128)} %param.13) | copy-start | bytes 52
Sparse Core Ops, SparseCore 0:
  8.9 105.9 all-gather.1
  443.7 141.3 reduce-scatter.1
where the time goes:
time: 605 us; the launch traced here: 595 us
  waiting for transfers between devices  264 us (44%)
  other arithmetic  196 us (32%)
  local copies, waits for them, and re-layouts  56.2 us (9%)
  matrix products  44.6 us (7%)
  between operations  17.4 us (3%)
  loops' own time  10.9 us (2%)
  starting transfers between devices  6.23 us (1%)
    reduce_scatter x1, waiting for transfers between devices, shards(): lax.psum_scatter((record * factor).astype(jnp.bfloat16), 'freq', scatter_...  141 us
    all_gather x1, waiting for transfers between devices, shards(): all_codes = lax.all_gather(slowness_codes, 'depth', axis=0, tiled=True)  75 us
    reduce_sum x4, other arithmetic, aperture_slowness(): jnp.sum(jnp.where(window[None] == levels[:, None, None], slowness_table[:...  58.6 us
    all_to_all x1, waiting for transfers between devices, shards(): lax.all_to_all(chains, 'depth', split_axis=1, concat_axis=0, tiled=True)  46.6 us
    another operation x9, other arithmetic  40.7 us
    while x28, local copies, waits for them, and re-layouts  29.9 us
    add x2, other arithmetic, record_shot(): return record + correlate(padded[:, :, 0], padded[:, :, 1], rows_x)  28.2 us
    dot_general x4, matrix products, advance(): jnp.einsum('pqxu,gfuqy->gfpxy', inv_x, back_y, preferred_element_type=jnp...  25 us
  transfers between devices with their start and end apart: 3, of which 3 were waited for; matrix products, arithmetic and copies ran while one was open for 5% of the time, Pallas kernels for 0%

commit v1 on v0

v1 whole, which is shorter than its diff:
```python
import functools
import math

import jax
import jax.numpy as jnp
import ml_dtypes
import numpy as np
from jax import lax
from jax.experimental import pallas as pl
from jax.experimental.pallas import tpu as pltpu
from jax.sharding import PartitionSpec as P

LAG = 7
HALO = 8
LANES = 128
AXES = ("depth", "freq")
VMEM_BYTES = 56 * 2**20


def parity_tables(length):
    position = np.arange(length, dtype=np.int64)
    product = position[:, None] * position[None, :] % length
    angles = product.astype(np.float32) * np.float32(2.0 * math.pi / length)
    factor = np.float32(1.0 / math.sqrt(length))
    cos, sin = np.cos(angles) * factor, np.sin(angles) * factor
    half = length // 2
    tables = []
    for parity in (0, 1):
        c, s = cos[parity::2, :half], sin[parity::2, :half]
        tables.append(np.block([[c, s], [-s, c]]).astype(ml_dtypes.bfloat16))
    return np.stack(tables)


def wavenumbers_squared(length):
    position = np.arange(length)
    signed = np.where(position < length // 2, position, position - length)
    wave = signed.astype(np.float32) * np.float32(2.0 * math.pi / length)
    squared = wave * wave
    return np.concatenate([squared[0::2], squared[1::2]])


Q_MAX = 14.0


def fit(function, degree):
    cheb = np.polynomial.chebyshev.Chebyshev.interpolate(
        lambda t: function((t + 1.0) * Q_MAX / 2), degree
    )
    return [float(v) for v in np.polynomial.chebyshev.cheb2poly(cheb.coef)]


COS_FIT = fit(lambda q: np.cos(np.sqrt(q)), 9)
SINC_FIT = fit(lambda q: np.sinc(np.sqrt(q) / np.pi), 9)


def horner(coefficients, t):
    total = jnp.full_like(t, coefficients[-1])
    for value in coefficients[-2::-1]:
        total = total * t + value
    return total


def cos_sin(square, root):
    t = square * (2.0 / Q_MAX) - 1.0
    return horner(COS_FIT, t), horner(SINC_FIT, t) * root


def lookup(table_row, codes):
    rows = codes.shape[0]
    parts = []
    for tile in range(codes.shape[1] // LANES):
        index = codes[:, tile * LANES : (tile + 1) * LANES]
        source = jnp.broadcast_to(table_row, (rows, LANES))
        parts.append(jnp.take_along_axis(source, index, axis=1, mode="promise_in_bounds"))
    return parts


def chain_kernel(
    place, angular_ref, source, receiver, code_own, code_core, code_y_same, code_y_cross,
    levels, left_x, right_x, left_y, right_y, wave_x, wave_y, *rest, strips, width, planes, shots,
):
    outs, (field, mid, padded) = rest[:-3], rest[-3:]
    tiles = len(outs) // 4
    own, same, core, cross = (outs[i * tiles : (i + 1) * tiles] for i in range(4))
    rows_x, rows_y = field.shape[1], field.shape[2]
    half_x, half_y = rows_x // 2, rows_y // 2
    first, my_core, my_parity = place[0], place[1], place[2]
    angular = angular_ref[0]
    f32, bf16 = jnp.float32, jnp.bfloat16

    field[0:2] = source[0, 0]
    field[2:4] = receiver[0, 0]
    padded[:, :, 0:HALO] = jnp.zeros((4, tiles, HALO, LANES), f32)
    padded[:, :, HALO + rows_x :] = jnp.zeros((4, tiles, HALO, LANES), f32)

    def step(t, carry):
        late = t >= planes - shots
        matched = lax.rem(t, shots) == my_core

        def codes_at(rows, cols):
            a = jnp.where(matched, code_own[rows, cols], code_core[rows, cols])
            b = jnp.where(matched, code_y_same[rows, cols], code_y_cross[rows, cols])
            return jnp.where(late, a, b).astype(f32).astype(jnp.int32)

        block = 64

        def add_block(i, total):
            rows = pl.ds(pl.multiple_of(i * block, block), block)
            parts = lookup(levels[0:1, :], codes_at(rows, slice(None)))
            value = functools.reduce(jnp.add, parts)
            return total + jnp.sum(value.reshape(block // 8, 8, LANES), axis=0)

        total = lax.fori_loop(0, rows_x // block, add_block, jnp.zeros((8, LANES), f32))
        base = jnp.sum(total) / (rows_x * rows_y)
        angle = angular * (levels[0:1, :] - base)
        screen_cos, screen_sin = cos_sin(angle * angle, angle)
        reach = angular * base
        reach = reach * reach

        def forward_x(i, carry):
            cols = pl.ds(pl.multiple_of(i * half_y, half_y), half_y)
            for kind in range(2):
                low = field[2 * kind : 2 * kind + 2, 0:half_x, cols].reshape(rows_x, half_y)
                high = field[2 * kind : 2 * kind + 2, half_x:, cols].reshape(rows_x, half_y)
                for parity, mixed in enumerate((low + high, low - high)):
                    out = jnp.dot(left_x[parity], mixed, preferred_element_type=f32).astype(bf16)
                    mid[2 * kind : 2 * kind + 2, parity * half_x : (parity + 1) * half_x, cols] = (
                        out.reshape(2, half_x, half_y)
                    )
            return carry

        lax.fori_loop(0, 2, forward_x, 0)

        rows_block = half_x // 2

        def along_y(i, carry):
            rows = pl.ds(pl.multiple_of(i * rows_block, rows_block), rows_block)
            blocks = mid[:, rows, :]
            low = jnp.concatenate(
                [jnp.concatenate([blocks[2 * k], blocks[2 * k + 1]], axis=1) for k in range(2)], axis=0
            )
            re = jnp.concatenate([blocks[0], blocks[2]], axis=0)
            im = jnp.concatenate([blocks[1], blocks[3]], axis=0)
            del low
            low = jnp.concatenate([re[:, :half_y], im[:, :half_y]], axis=1)
            high = jnp.concatenate([re[:, half_y:], im[:, half_y:]], axis=1)
            back = []
            for parity, mixed in enumerate((low + high, low - high)):
                spectrum = jnp.dot(mixed, right_y[parity], preferred_element_type=f32)
                q = reach - wave_x[rows, :] - wave_y[0:1, parity * half_y : (parity + 1) * half_y]
                root = jnp.sqrt(jnp.abs(q))
                cos, sin = cos_sin(q, root)
                phase_re = jnp.where(q > 0.0, cos, jnp.exp(-root))
                phase_im = jnp.where(q > 0.0, sin, 0.0)
                pieces = []
                for kind, sign in ((0, 1.0), (1, -1.0)):
                    part = spectrum[kind * rows_block : (kind + 1) * rows_block]
                    a, b = part[:, :half_y], part[:, half_y:]
                    if kind == 0:
                        pieces.append(
                            jnp.concatenate(
                                [a * phase_re - b * phase_im, a * phase_im + b * phase_re], axis=1
                            ).astype(bf16)
                        )
                    else:
                        pieces.append(
                            jnp.concatenate(
                                [a * phase_re + b * phase_im, b * phase_re - a * phase_im], axis=1
                            ).astype(bf16)
                        )
                shifted = jnp.concatenate(pieces, axis=0)
                back.append(jnp.dot(shifted, left_y[parity], preferred_element_type=f32))
            low = (back[0] + back[1]).astype(bf16)
            high = (back[0] - back[1]).astype(bf16)
            for kind in range(2):
                part = slice(kind * rows_block, (kind + 1) * rows_block)
                mid[2 * kind, rows, 0:half_y] = low[part, :half_y]
                mid[2 * kind, rows, half_y:] = high[part, :half_y]
                mid[2 * kind + 1, rows, 0:half_y] = low[part, half_y:]
                mid[2 * kind + 1, rows, half_y:] = high[part, half_y:]
            return carry

        lax.fori_loop(0, rows_x // rows_block, along_y, 0)

        def inverse_x(i, carry):
            cols = pl.ds(pl.multiple_of(i * LANES, LANES), LANES)
            turn = []
            for part in range(2):
                codes = codes_at(slice(part * half_x, (part + 1) * half_x), cols)
                turn.append((lookup(screen_cos, codes)[0], lookup(screen_sin, codes)[0]))
            for kind in range(2):
                even, odd = (
                    jnp.dot(
                        right_x[parity],
                        mid[
                            2 * kind : 2 * kind + 2, parity * half_x : (parity + 1) * half_x, cols
                        ].reshape(rows_x, LANES),
                        preferred_element_type=f32,
                    )
                    for parity in range(2)
                )
                for part, value in enumerate((even + odd, even - odd)):
                    a, b = value[:half_x], value[half_x:]
                    cos, sin = turn[part]
                    if kind == 0:
                        new_re, new_im = a * cos - b * sin, a * sin + b * cos
                    else:
                        new_re, new_im = a * cos + b * sin, b * cos - a * sin
                    rows = slice(part * half_x, (part + 1) * half_x)
                    field[2 * kind, rows, cols] = new_re.astype(bf16)
                    field[2 * kind + 1, rows, cols] = new_im.astype(bf16)
                    spot = slice(HALO + part * half_x, HALO + (part + 1) * half_x)
                    padded[2 * kind, i, spot] = new_re
                    padded[2 * kind + 1, i, spot] = new_im
            return carry

        lax.fori_loop(0, tiles, inverse_x, 0)

        def emit(targets, parity):
            def one(s, carry):
                start = pl.multiple_of((2 * s + parity) * width, 8)
                for tile in range(tiles):
                    for part in range(4):
                        targets[tile][part, s] = padded[
                            part, tile, pl.ds(start, width + 2 * HALO)
                        ].astype(bf16)
                return carry

            lax.fori_loop(0, strips, one, 0)

        @pl.when(late & matched)
        def _():
            emit(own, my_parity)
            emit(same, 1 - my_parity)

        @pl.when(late & jnp.logical_not(matched))
        def _():
            emit(core, my_parity)
            emit(cross, 1 - my_parity)

        return carry

    lax.fori_loop(first, planes, step, 0)


def correlate_kernel(order, *refs, width, partial, scale):
    del order
    fields, refs = refs[:4], refs[4:]
    received = None
    if partial:
        received, refs = refs[0], refs[1:]
    out, wide = refs[-2], refs[-1]
    for m in range(4):
        for part in range(4):
            wide[m * 4 + part] = fields[m][part, 0].astype(jnp.float32)
    for lag in range(2 * LAG + 1):
        shift = lag - LAG
        total = None
        for m in range(4):
            for part in range(2):
                term = (
                    wide[m * 4 + part, HALO - shift : HALO - shift + width]
                    * wide[m * 4 + 2 + part, HALO + shift : HALO + shift + width]
                )
                total = term if total is None else total + term
        if received is not None:
            total = total + received[lag].astype(jnp.float32)
        if scale is not None:
            out[0, lag] = total * scale
        else:
            out[lag] = total.astype(out.dtype)


def shards(source_top, receiver_top, slowness_codes, slowness_table, anchors):
    shots, _, _, rows_x, rows_y = source_top.shape
    freq_count = lax.axis_size("freq")
    depth_count = lax.axis_size("depth")
    planes = depth_count
    strips = freq_count // 2
    width = rows_x // freq_count
    lags = 2 * LAG + 1
    tiles = rows_y // LANES
    factor = 1.0 / math.sqrt(2.0 * shots * freq_count)
    depth_index = lax.axis_index("depth")
    freq_index = lax.axis_index("freq")
    my_core = depth_index % shots
    group = depth_index // shots
    my_parity = freq_index % 2
    bf16, f32 = jnp.bfloat16, jnp.float32

    def number(group_at, core_at, strip_at, parity_at):
        return (group_at * shots + core_at) * freq_count + strip_at * 2 + parity_at

    def pairs(move):
        found = []
        for g in range(depth_count // shots):
            for c in range(shots):
                for z in range(strips):
                    for x in range(2):
                        to = move(g, c, z, x)
                        if to is not None:
                            found.append((number(g, c, z, x), number(*to)))
        return found

    to_core = pairs(lambda g, c, z, x: (g, 1 - c, z, x))
    to_same = pairs(lambda g, c, z, x: (g, c, z, 1 - x))
    to_cross = pairs(lambda g, c, z, x: (g, 1 - c, z, 1 - x))
    up_same = pairs(lambda g, c, z, x: (1, c, z, x) if g == 0 else None)
    up_cross = pairs(lambda g, c, z, x: (1, 1 - c, z, x) if g == 0 else None)
    ring = [0] + list(range(1, strips, 2)) + list(range(2, strips, 2))[::-1]
    where = {z: p for p, z in enumerate(ring)}
    onward = pairs(lambda g, c, z, x: (g, c, ring[(where[z] + 1) % strips], x))
    plan = np.array(
        [[ring[(where[z] - 1 - s) % strips] for s in range(strips)] for z in range(strips)], np.int32
    )
    order = lax.dynamic_index_in_dim(jnp.asarray(plan), freq_index // 2, 0, keepdims=False)

    windows = [
        lax.dynamic_slice(
            slowness_codes[0], (anchors[s, 0], anchors[s, 1]), (rows_x, rows_y)
        ).astype(bf16)
        for s in range(shots)
    ]
    mine = jnp.where(my_core == 0, windows[0], windows[1])
    other = jnp.where(my_core == 0, windows[1], windows[0])
    code_y_same = lax.ppermute(mine, AXES, up_same)
    code_y_cross = lax.ppermute(other, AXES, up_cross)
    code_core = lax.ppermute(other, AXES, to_core)

    angular = math.pi * (0.45 + 0.5 * (freq_index.astype(f32) + 0.5) / freq_count)
    place = jnp.stack([(1 - group) * shots, my_core, my_parity]).astype(jnp.int32)
    levels = jnp.pad(slowness_table, (0, LANES - slowness_table.shape[0]))[None]
    tables_x, tables_y = parity_tables(rows_x), parity_tables(rows_y)
    wave_x = np.broadcast_to(wavenumbers_squared(rows_x)[:, None], (rows_x, 1))
    wave_y = wavenumbers_squared(rows_y)[None]
    height = width + 2 * HALO
    vmem = pl.BlockSpec(memory_space=pltpu.VMEM)
    top_spec = pl.BlockSpec(
        (1, 1, 2, rows_x, rows_y), lambda i, place, angular: (place[1], 0, 0, 0, 0)
    )
    outs = pl.pallas_call(
        functools.partial(
            chain_kernel, strips=strips, width=width, planes=planes, shots=shots
        ),
        out_shape=[jax.ShapeDtypeStruct((4, strips, height, LANES), bf16)] * (4 * tiles),
        grid_spec=pltpu.PrefetchScalarGridSpec(
            num_scalar_prefetch=2,
            grid=(1,),
            in_specs=[top_spec, top_spec] + [vmem] * 11,
            out_specs=[vmem] * (4 * tiles),
            scratch_shapes=[
                pltpu.VMEM((4, rows_x, rows_y), bf16),
                pltpu.VMEM((4, rows_x, rows_y), bf16),
                pltpu.VMEM((4, tiles, rows_x + 2 * HALO, LANES), f32),
            ],
        ),
        compiler_params=pltpu.CompilerParams(vmem_limit_bytes=VMEM_BYTES),
        name="chain",
    )(
        place,
        angular[None],
        source_top,
        receiver_top,
        mine,
        code_core,
        code_y_same,
        code_y_cross,
        levels,
        jnp.asarray(tables_x),
        jnp.asarray(np.swapaxes(tables_x, 1, 2)),
        jnp.asarray(tables_y),
        jnp.asarray(np.swapaxes(tables_y, 1, 2)),
        jnp.asarray(wave_x),
        jnp.asarray(wave_y),
    )

    def correlate(fields, received, step, buffer, tile):
        last = step == strips - 1
        field_spec = pl.BlockSpec((4, 1, height, LANES), lambda i, order: (0, order[step], 0, 0))
        in_specs = [field_spec] * 4
        operands = list(fields)
        image_spec = pl.BlockSpec((lags, width, LANES), lambda i, order: (0, 0, 0))
        if received is not None:
            in_specs.append(image_spec)
            operands.append(received)
        aliases = {}
        if last:
            out_shape = jax.ShapeDtypeStruct((1, lags, width, rows_y), f32)
            out_spec = pl.BlockSpec((1, lags, width, LANES), lambda i, order: (0, 0, 0, tile))
            if buffer is not None:
                in_specs.append(pl.BlockSpec(memory_space=pl.ANY))
                operands.append(buffer)
                aliases = {len(operands): 0}
        else:
            out_shape = jax.ShapeDtypeStruct((lags, width, LANES), bf16)
            out_spec = image_spec
        return pl.pallas_call(
            functools.partial(
                correlate_kernel,
                width=width,
                partial=received is not None,
                scale=factor if last else None,
            ),
            out_shape=out_shape,
            grid_spec=pltpu.PrefetchScalarGridSpec(
                num_scalar_prefetch=1,
                grid=(1,),
                in_specs=in_specs,
                out_specs=out_spec,
                scratch_shapes=[pltpu.VMEM((16, height, LANES), f32)],
            ),
            input_output_aliases=aliases,
            compiler_params=pltpu.CompilerParams(vmem_limit_bytes=16 * 2**20),
            cost_estimate=pl.CostEstimate(flops=10**8, bytes_accessed=2 * 10**6, transcendentals=0),
            name="correlate",
        )(order, *operands)

    image = None
    for tile in range(tiles):
        own, same, core, cross = (outs[i * tiles + tile] for i in range(4))
        fields = (
            own,
            lax.ppermute(same, AXES, to_same),
            lax.ppermute(core, AXES, to_core),
            lax.ppermute(cross, AXES, to_cross),
        )
        received = None
        for step in range(strips):
            result = correlate(fields, received, step, image, tile)
            if step < strips - 1:
                received = lax.ppermute(result, AXES, onward)
            else:
                image = result
    return image


def solution(mesh):
    return jax.shard_map(
        shards,
        mesh=mesh,
        in_specs=(
            P(None, "freq", None, None, None),
            P(None, "freq", None, None, None),
            P("depth", None, None),
            P(),
            P(),
        ),
        out_specs=P("depth", None, "freq", None),
        check_vma=False,
    )
```

time: 605 us -> 202 us (0.33); the launches traced: 595 us -> 201 us
  other arithmetic: 196 us -> 2.81 us
  waiting for transfers between devices: 264 us -> 84.5 us
  Pallas kernels: 0 us -> 67.8 us
  local copies, waits for them, and re-layouts: 56.2 us -> 10.6 us
  matrix products: 44.6 us -> 0 us
  starting transfers between devices: 6.23 us -> 28.1 us
  loops' own time: 10.9 us -> 0 us
  between operations: 17.4 us -> 7.61 us
    reduce_scatter x1 -> x0, waiting for transfers between devices: 141 us -> none  [shards(): lax.psum_scatter((record * factor).astype(jnp.bfloat16), 'freq', scatter_...]
    ppermute x0 -> x27, waiting for transfers between devices: none -> 84.5 us  [the longest x12 29.3 us: shards(): received = lax.ppermute(result, AXES, onward)]
    reduce_sum x8 -> x0, other arithmetic: 75.2 us -> none  [the longest x4 58.6 us: aperture_slowness(): jnp.sum(jnp.where(window[None] == levels[:, None, None], slowness_table[:...]
    all_gather x1 -> x0, waiting for transfers between devices: 75 us -> none  [shards(): all_codes = lax.all_gather(slowness_codes, 'depth', axis=0, tiled=True)]
    another operation x23 -> x1, other arithmetic: 74.4 us -> 0.56 us  [shards(): jnp.stack([(1 - group) * shots, my_core, my_parity]).astype(jnp.int32)]
    pallas_call x0 -> x17, Pallas kernels: none -> 67.8 us  [the longest x1 49.2 us: shards(): pl.pallas_call(functools.partial(chain_kernel, strips=strips, width=width...]
    all_to_all x1 -> x0, waiting for transfers between devices: 46.6 us -> none  [shards(): lax.all_to_all(chains, 'depth', split_axis=1, concat_axis=0, tiled=True)]
    dot_general x8 -> x0, matrix products: 44.6 us -> none  [the longest x4 25 us: advance(): jnp.einsum('pqxu,gfuqy->gfpxy', inv_x, back_y, preferred_element_type=jnp...]
  transfers between devices with their start and end apart: 3 -> 27, of which waited for: 3 -> 18; matrix products, arithmetic and copies ran while one was open for 5% -> 1% of each run, Pallas kernels for 0% -> 8%
where the time goes in v1:
time: 202 us; the launch traced here: 201 us
  waiting for transfers between devices  84.5 us (42%)
  Pallas kernels  67.8 us (34%)
  starting transfers between devices  28.1 us (14%)
  local copies, waits for them, and re-layouts  10.6 us (5%)
  between operations  7.61 us (4%)
  other arithmetic  2.81 us (1%)
    pallas_call x1, Pallas kernels, shards(): pl.pallas_call(functools.partial(chain_kernel, strips=strips, width=width...  49.2 us
    ppermute x12, waiting for transfers between devices, shards(): received = lax.ppermute(result, AXES, onward)  29.3 us
    ppermute x4, waiting for transfers between devices, shards(): lax.ppermute(same, AXES, to_same)  20.8 us
    pallas_call x16, Pallas kernels, correlate(): pl.pallas_call(functools.partial(correlate_kernel, width=width, partial=r...  18.5 us
    ppermute x12, starting transfers between devices, shards(): received = lax.ppermute(result, AXES, onward)  14.2 us
    ppermute x1, waiting for transfers between devices, shards(): code_y_same = lax.ppermute(mine, AXES, up_same)  12.8 us
    ppermute x4, waiting for transfers between devices, shards(): lax.ppermute(cross, AXES, to_cross)  11.2 us
    ppermute x1, waiting for transfers between devices, shards(): code_y_cross = lax.ppermute(other, AXES, up_cross)  10.4 us
  transfers between devices with their start and end apart: 27, of which 18 were waited for; matrix products, arithmetic and copies ran while one was open for 1% of the time, Pallas kernels for 8%

profile of v1, /device:TPU:4, one launch (start us, length us, event | category | flops | bytes accessed | tf_op | source)
XLA Modules:
  0.0 201.3 jit_solution(2704047868123405648)
XLA Ops:
  0.0 1.5 fusion.1
  8.9 2.2 %select_bitcast_fusion = (bf16[512,512]{1,0:T(8,128)(2,1)S(1)}, bf16[512,512]{1,0:T(8,128)(2,1)S(1)}) fusion(pred[]{:T(512)S(6)} %eq.7, s32[1,1024,1024]{2,1,0:T(8,128)} %param.14, s32[]{:T(128)S(6)} %select_n.57, s32[]{:T(128)S(6)} %select_n.58, s32[]{:T(128)S(6)} %select_n.59, s32[]{:T(128)S(6)} %select_n.60), kind=kLoop, calls=%fused_computation.2 | loop fusion | flops 1048576 | bytes 3145745 | tf_op jit(solution)/shard_map/jit(_where)/select_n | solution.py:325
  11.2 1.3 collective-permute-start.1
  12.5 1.3 collective-permute-start.2
  15.0 12.8 %collective-permute-done.1.code_y_same = bf16[512,512]{1,0:T(8,128)(2,1)S(1)} collective-permute-done((bf16[512,512]{1,0:T(8,128)(2,1)S(1)}, bf16[512,512]{1,0:T(8,128)(2,1)S(1)}, u32[]{:S(2)}, u32[]{:S(2)}) %collective-permute-start.1) | collective-permute-done | bytes 524320 | tf_op jit(solution)/shard_map/ppermute | solution.py:326
  27.8 10.4 %collective-permute-done.2.code_y_cross = bf16[512,512]{1,0:T(8,128)(2,1)S(1)} collective-permute-done((bf16[512,512]{1,0:T(8,128)(2,1)S(1)}, bf16[512,512]{1,0:T(8,128)(2,1)S(1)}, u32[]{:S(2)}, u32[]{:S(2)}) %collective-permute-start.2) | collective-permute-done | bytes 524320 | tf_op jit(solution)/shard_map/ppermute | solution.py:327
  39.1 49.2 %chain.1 = (bf16[4,4,80,128]{3,2,1,0:T(8,128)(2,1)}, bf16[4,4,80,128]{3,2,1,0:T(8,128)(2,1)}, bf16[4,4,80,128]{3,2,1,0:T(8,128)(2,1)}, bf16[4,4,80,128]{3,2,1,0:...) custom-call(s32[3]{0:T(128)} %pad_add_fusion.place, ...), custom_call_target="tpu_custom_call" | custom-call | tf_op jit(solution)/shard_map/chain/pallas_call | solution.py:341
  88.3 1.5 collective-permute-start.21
  90.5 1.5 collective-permute-start.15
  92.0 7.1 %collective-permute-done.21.refs_1_ = bf16[4,4,80,128]{3,2,1,0:T(8,128)(2,1)S(1)} collective-permute-done((bf16[4,4,80,128]{3,2,1,0:T(8,128)(2,1)}, bf16[4,4,80,128]{3,2,1,0:T(8,128)(2,1)S(1)}, u32[]{:S(2)}, u32[]{:S(2)}) %collective-permute-start.21) | collective-permute-done | bytes 327712 | tf_op jit(solution)/shard_map/ppermute | solution.py:423
  100.5 1.6 collective-permute-start.10
  102.1 3.1 %collective-permute-done.23.refs_3_ = bf16[4,4,80,128]{3,2,1,0:T(8,128)(2,1)S(1)} collective-permute-done((bf16[4,4,80,128]{3,2,1,0:T(8,128)(2,1)}, bf16[4,4,80,128]{3,2,1,0:T(8,128)(2,1)S(1)}, u32[]{:S(2)}, u32[]{:S(2)}) %collective-permute-start.23) | collective-permute-done | bytes 327712 | tf_op jit(solution)/shard_map/ppermute | solution.py:425
  105.9 1.8 collective-permute-start.11
  107.7 5.4 %collective-permute-done.15.refs_1_ = bf16[4,4,80,128]{3,2,1,0:T(8,128)(2,1)S(1)} collective-permute-done((bf16[4,4,80,128]{3,2,1,0:T(8,128)(2,1)}, bf16[4,4,80,128]{3,2,1,0:T(8,128)(2,1)S(1)}, u32[]{:S(2)}, u32[]{:S(2)}) %collective-permute-start.15) | collective-permute-done | bytes 327712 | tf_op jit(solution)/shard_map/ppermute | solution.py:423
  113.1 1.5 collective-permute-start.9
  115.2 4.1 %collective-permute-done.17.refs_3_ = bf16[4,4,80,128]{3,2,1,0:T(8,128)(2,1)S(1)} collective-permute-done((bf16[4,4,80,128]{3,2,1,0:T(8,128)(2,1)}, bf16[4,4,80,128]{3,2,1,0:T(8,128)(2,1)S(1)}, u32[]{:S(2)}, u32[]{:S(2)}) %collective-permute-start.17) | collective-permute-done | bytes 327712 | tf_op jit(solution)/shard_map/ppermute | solution.py:425
  119.3 1.0 collective-permute-start.4
  120.3 1.1 collective-permute-start.5
  122.1 1.0 copy-done.4
  123.0 1.0 copy-done.7
  124.0 1.0 copy-done.9
  125.0 1.0 copy-done.11
  126.9 1.6 collective-permute-start.24
  128.5 1.0 copy-done.2
  130.5 3.7 %collective-permute-done.9.refs_1_ = bf16[4,4,80,128]{3,2,1,0:T(8,128)(2,1)S(1)} collective-permute-done((bf16[4,4,80,128]{3,2,1,0:T(8,128)(2,1)}, bf16[4,4,80,128]{3,2,1,0:T(8,128)(2,1)S(1)}, u32[]{:S(2)}, u32[]{:S(2)}) %collective-permute-start.9) | collective-permute-done | bytes 327712 | tf_op jit(solution)/shard_map/ppermute | solution.py:423
  134.2 1.6 collective-permute-start.18
  136.7 4.5 %collective-permute-done.3.refs_1_ = bf16[4,4,80,128]{3,2,1,0:T(8,128)(2,1)S(1)} collective-permute-done((bf16[4,4,80,128]{3,2,1,0:T(8,128)(2,1)}, bf16[4,4,80,128]{3,2,1,0:T(8,128)(2,1)S(1)}, u32[]{:S(2)}, u32[]{:S(2)}) %collective-permute-start.3) | collective-permute-done | bytes 327712 | tf_op jit(solution)/shard_map/ppermute | solution.py:423
  141.2 1.6 collective-permute-start.12
  142.8 4.0 %collective-permute-done.5.refs_3_ = bf16[4,4,80,128]{3,2,1,0:T(8,128)(2,1)S(1)} collective-permute-done((bf16[4,4,80,128]{3,2,1,0:T(8,128)(2,1)}, bf16[4,4,80,128]{3,2,1,0:T(8,128)(2,1)S(1)}, u32[]{:S(2)}, u32[]{:S(2)}) %collective-permute-start.5) | collective-permute-done | bytes 327712 | tf_op jit(solution)/shard_map/ppermute | solution.py:425
  147.7 1.7 collective-permute-start.6
  149.4 1.0 correlate.26
  150.4 2.6 %collective-permute-start.25 = (bf16[15,64,128]{2,1,0:T(8,128)(2,1)S(1)}, bf16[15,64,128]{2,1,0:T(8,128)(2,1)S(1)}, u32[]{:S(2)}, u32[]{:S(2)}) collective-permute-start(bf16[15,64,128]{2,1,0:T(8,128)(2,1)S(1)} %correlate.26), channel_id=1, source_target_pairs={{0,2},{1,3},{2,6},{3,7},{4,0},{5,1},{6,4},{7,5},{8,10},{9,11},{10,... | collective-permute-start | bytes 737288 | tf_op jit(solution)/shard_map/ppermute | solution.py:431
  153.0 1.0 correlate.23
  154.4 1.0 correlate.20
  155.8 1.7 collective-permute-done.6.refs_4_
  157.5 1.0 correlate.17
  159.3 3.4 %collective-permute-done.25.refs_4_ = bf16[15,64,128]{2,1,0:T(8,128)(2,1)S(1)} collective-permute-done((bf16[15,64,128]{2,1,0:T(8,128)(2,1)S(1)}, bf16[15,64,128]{2,1,0:T(8,128)(2,1)S(1)}, u32[]{:S(2)}, u32[]{:S(2)}) %collective-permute-start.25) | collective-permute-done | bytes 245792 | tf_op jit(solution)/shard_map/ppermute | solution.py:431
  164.6 3.4 %collective-permute-done.19.refs_4_ = bf16[15,64,128]{2,1,0:T(8,128)(2,1)S(1)} collective-permute-done((bf16[15,64,128]{2,1,0:T(8,128)(2,1)S(1)}, bf16[15,64,128]{2,1,0:T(8,128)(2,1)S(1)}, u32[]{:S(2)}, u32[]{:S(2)}) %collective-permute-start.19) | collective-permute-done | bytes 245792 | tf_op jit(solution)/shard_map/ppermute | solution.py:431
  169.9 3.4 %collective-permute-done.13.refs_4_ = bf16[15,64,128]{2,1,0:T(8,128)(2,1)S(1)} collective-permute-done((bf16[15,64,128]{2,1,0:T(8,128)(2,1)S(1)}, bf16[15,64,128]{2,1,0:T(8,128)(2,1)S(1)}, u32[]{:S(2)}, u32[]{:S(2)}) %collective-permute-start.13) | collective-permute-done | bytes 245792 | tf_op jit(solution)/shard_map/ppermute | solution.py:431
  175.1 3.4 %collective-permute-done.7.refs_4_ = bf16[15,64,128]{2,1,0:T(8,128)(2,1)S(1)} collective-permute-done((bf16[15,64,128]{2,1,0:T(8,128)(2,1)S(1)}, bf16[15,64,128]{2,1,0:T(8,128)(2,1)S(1)}, u32[]{:S(2)}, u32[]{:S(2)}) %collective-permute-start.7) | collective-permute-done | bytes 245792 | tf_op jit(solution)/shard_map/ppermute | solution.py:431
  180.4 3.4 %collective-permute-done.26.refs_4_ = bf16[15,64,128]{2,1,0:T(8,128)(2,1)S(1)} collective-permute-done((bf16[15,64,128]{2,1,0:T(8,128)(2,1)S(1)}, bf16[15,64,128]{2,1,0:T(8,128)(2,1)S(1)}, u32[]{:S(2)}, u32[]{:S(2)}) %collective-permute-start.26) | collective-permute-done | bytes 245792 | tf_op jit(solution)/shard_map/ppermute | solution.py:431
  183.8 1.8 correlate.28.refs_5_
  185.6 3.5 %collective-permute-done.20.refs_4_ = bf16[15,64,128]{2,1,0:T(8,128)(2,1)S(1)} collective-permute-done((bf16[15,64,128]{2,1,0:T(8,128)(2,1)S(1)}, bf16[15,64,128]{2,1,0:T(8,128)(2,1)S(1)}, u32[]{:S(2)}, u32[]{:S(2)}) %collective-permute-start.20) | collective-permute-done | bytes 245792 | tf_op jit(solution)/shard_map/ppermute | solution.py:431
  189.1 1.8 correlate.29.refs_5_
  190.9 3.5 %collective-permute-done.14.refs_4_ = bf16[15,64,128]{2,1,0:T(8,128)(2,1)S(1)} collective-permute-done((bf16[15,64,128]{2,1,0:T(8,128)(2,1)S(1)}, bf16[15,64,128]{2,1,0:T(8,128)(2,1)S(1)}, u32[]{:S(2)}, u32[]{:S(2)}) %collective-permute-start.14) | collective-permute-done | bytes 245792 | tf_op jit(solution)/shard_map/ppermute | solution.py:431
  194.4 1.8 correlate.30.refs_5_
  196.1 3.4 %collective-permute-done.8.refs_4_ = bf16[15,64,128]{2,1,0:T(8,128)(2,1)S(1)} collective-permute-done((bf16[15,64,128]{2,1,0:T(8,128)(2,1)S(1)}, bf16[15,64,128]{2,1,0:T(8,128)(2,1)S(1)}, u32[]{:S(2)}, u32[]{:S(2)}) %collective-permute-start.8) | collective-permute-done | bytes 245792 | tf_op jit(solution)/shard_map/ppermute | solution.py:431
  199.5 1.8 correlate.31
  (62 shorter events, 18.9 us)
Async XLA Ops:
  0.0 13.9 %copy-start.16 = (f32[32]{0:T(128)S(1)}, f32[32]{0:T(128)}, u32[]{:S(2)}) copy-start(f32[32]{0:T(128)} %param.15) | copy-start | bytes 388
  11.1 27.1 %copy-start.12 = (bf16[512,512]{1,0:T(8,128)(2,1)}, bf16[512,512]{1,0:T(8,128)(2,1)S(1)}, u32[]{:S(2)}) copy-start(bf16[512,512]{1,0:T(8,128)(2,1)S(1)} %get-tuple-element.38.code_own) | copy-start | bytes 1572868
  11.1 3.9 %collective-permute-start = (bf16[512,512]{1,0:T(8,128)(2,1)S(1)}, bf16[512,512]{1,0:T(8,128)(2,1)S(1)}, u32[]{:S(2)}, u32[]{:S(2)}) collective-permute-start(bf16[512,512]{1,0:T(8,128)(2,1)S(1)} %get-tuple-element.37), channel_id=1, source_target_pairs={{0,8},{1,9},{2,10},{3,11},{4,12},{5,13},{6,14},{7,15},{8,0},{9,1},... | collective-permute-start | bytes 1572872 | tf_op jit(solution)/shard_map/ppermute | solution.py:328
  11.2 16.6 %collective-permute-start.1 = (bf16[512,512]{1,0:T(8,128)(2,1)S(1)}, bf16[512,512]{1,0:T(8,128)(2,1)S(1)}, u32[]{:S(2)}, u32[]{:S(2)}) collective-permute-start(bf16[512,512]{1,0:T(8,128)(2,1)S(1)} %get-tuple-element.38.code_own), channel_id=1, source_target_pairs={{0,16},{1,17},{2,18},{3,19},{4,20},{5,21},{6,22},{7,23},{8,24},{9,... | collective-permute-start | bytes 1572872 | tf_op jit(solution)/shard_map/ppermute | solution.py:326
  12.5 25.7 %collective-permute-start.2 = (bf16[512,512]{1,0:T(8,128)(2,1)S(1)}, bf16[512,512]{1,0:T(8,128)(2,1)S(1)}, u32[]{:S(2)}, u32[]{:S(2)}) collective-permute-start(bf16[512,512]{1,0:T(8,128)(2,1)S(1)} %get-tuple-element.37), channel_id=1, source_target_pairs={{0,24},{1,25},{2,26},{3,27},{4,28},{5,29},{6,30},{7,31},{8,16},{9,... | collective-permute-start | bytes 1572872 | tf_op jit(solution)/shard_map/ppermute | solution.py:327
  15.0 23.3 %copy-start.13 = (bf16[512,512]{1,0:T(8,128)(2,1)}, bf16[512,512]{1,0:T(8,128)(2,1)S(1)}, u32[]{:S(2)}) copy-start(bf16[512,512]{1,0:T(8,128)(2,1)S(1)} %collective-permute-done.code_core) | copy-start | bytes 1572868
  27.8 10.4 %copy-start.14 = (bf16[512,512]{1,0:T(8,128)(2,1)}, bf16[512,512]{1,0:T(8,128)(2,1)S(1)}, u32[]{:S(2)}) copy-start(bf16[512,512]{1,0:T(8,128)(2,1)S(1)} %collective-permute-done.1.code_y_same) | copy-start | bytes 1572868
  38.3 0.8 copy-start.15
  88.3 47.5 %copy-start.1 = (bf16[4,4,80,128]{3,2,1,0:T(8,128)(2,1)S(1)}, bf16[4,4,80,128]{3,2,1,0:T(8,128)(2,1)}, u32[]{:S(2)}) copy-start(bf16[4,4,80,128]{3,2,1,0:T(8,128)(2,1)} %get-tuple-element.25.refs_0_) | copy-start | bytes 983044
  88.3 10.8 %collective-permute-start.21 = (bf16[4,4,80,128]{3,2,1,0:T(8,128)(2,1)}, bf16[4,4,80,128]{3,2,1,0:T(8,128)(2,1)S(1)}, u32[]{:S(2)}, u32[]{:S(2)}) collective-permute-start(bf16[4,4,80,128]{3,2,1,0:T(8,128)(2,1)} %get-tuple-element.34), channel_id=1, source_target_pairs={{0,1},{1,0},{2,3},{3,2},{4,5},{5,4},{6,7},{7,6},{8,9},{9,8},{10,11... | collective-permute-start | bytes 983048 | tf_op jit(solution)/shard_map/ppermute | solution.py:423
  89.8 10.0 %collective-permute-start.22 = (bf16[4,4,80,128]{3,2,1,0:T(8,128)(2,1)}, bf16[4,4,80,128]{3,2,1,0:T(8,128)(2,1)S(1)}, u32[]{:S(2)}, u32[]{:S(2)}) collective-permute-start(bf16[4,4,80,128]{3,2,1,0:T(8,128)(2,1)} %get-tuple-element.35), channel_id=1, source_target_pairs={{0,8},{1,9},{2,10},{3,11},{4,12},{5,13},{6,14},{7,15},{8,0},{9,1},... | collective-permute-start | bytes 983048 | tf_op jit(solution)/shard_map/ppermute | solution.py:424
  89.8 15.4 %collective-permute-start.23 = (bf16[4,4,80,128]{3,2,1,0:T(8,128)(2,1)}, bf16[4,4,80,128]{3,2,1,0:T(8,128)(2,1)S(1)}, u32[]{:S(2)}, u32[]{:S(2)}) collective-permute-start(bf16[4,4,80,128]{3,2,1,0:T(8,128)(2,1)} %get-tuple-element.36), channel_id=1, source_target_pairs={{0,9},{1,8},{2,11},{3,10},{4,13},{5,12},{6,15},{7,14},{8,1},{9,0},... | collective-permute-start | bytes 983048 | tf_op jit(solution)/shard_map/ppermute | solution.py:425
  90.5 22.7 %collective-permute-start.15 = (bf16[4,4,80,128]{3,2,1,0:T(8,128)(2,1)}, bf16[4,4,80,128]{3,2,1,0:T(8,128)(2,1)S(1)}, u32[]{:S(2)}, u32[]{:S(2)}) collective-permute-start(bf16[4,4,80,128]{3,2,1,0:T(8,128)(2,1)} %get-tuple-element.30), channel_id=1, source_target_pairs={{0,1},{1,0},{2,3},{3,2},{4,5},{5,4},{6,7},{7,6},{8,9},{9,8},{10,11... | collective-permute-start | bytes 983048 | tf_op jit(solution)/shard_map/ppermute | solution.py:423
  92.0 22.7 %collective-permute-start.16 = (bf16[4,4,80,128]{3,2,1,0:T(8,128)(2,1)}, bf16[4,4,80,128]{3,2,1,0:T(8,128)(2,1)S(1)}, u32[]{:S(2)}, u32[]{:S(2)}) collective-permute-start(bf16[4,4,80,128]{3,2,1,0:T(8,128)(2,1)} %get-tuple-element.31), channel_id=1, source_target_pairs={{0,8},{1,9},{2,10},{3,11},{4,12},{5,13},{6,14},{7,15},{8,0},{9,1},... | collective-permute-start | bytes 983048 | tf_op jit(solution)/shard_map/ppermute | solution.py:424
  99.1 0.7 copy-start.6
  99.8 19.4 %collective-permute-start.17 = (bf16[4,4,80,128]{3,2,1,0:T(8,128)(2,1)}, bf16[4,4,80,128]{3,2,1,0:T(8,128)(2,1)S(1)}, u32[]{:S(2)}, u32[]{:S(2)}) collective-permute-start(bf16[4,4,80,128]{3,2,1,0:T(8,128)(2,1)} %get-tuple-element.32), channel_id=1, source_target_pairs={{0,9},{1,8},{2,11},{3,10},{4,13},{5,12},{6,15},{7,14},{8,1},{9,0},... | collective-permute-start | bytes 983048 | tf_op jit(solution)/shard_map/ppermute | solution.py:425
  99.8 0.7 copy-start.8
  100.5 19.7 %collective-permute-start.10 = (bf16[4,4,80,128]{3,2,1,0:T(8,128)(2,1)}, bf16[4,4,80,128]{3,2,1,0:T(8,128)(2,1)S(1)}, u32[]{:S(2)}, u32[]{:S(2)}) collective-permute-start(bf16[4,4,80,128]{3,2,1,0:T(8,128)(2,1)} %get-tuple-element.27), channel_id=1, source_target_pairs={{0,8},{1,9},{2,10},{3,11},{4,12},{5,13},{6,14},{7,15},{8,0},{9,1},... | collective-permute-start | bytes 983048 | tf_op jit(solution)/shard_map/ppermute | solution.py:424
  105.2 0.7 copy-start.10
  105.9 21.0 %collective-permute-start.11 = (bf16[4,4,80,128]{3,2,1,0:T(8,128)(2,1)}, bf16[4,4,80,128]{3,2,1,0:T(8,128)(2,1)S(1)}, u32[]{:S(2)}, u32[]{:S(2)}) collective-permute-start(bf16[4,4,80,128]{3,2,1,0:T(8,128)(2,1)} %get-tuple-element.28), channel_id=1, source_target_pairs={{0,9},{1,8},{2,11},{3,10},{4,13},{5,12},{6,15},{7,14},{8,1},{9,0},... | collective-permute-start | bytes 983048 | tf_op jit(solution)/shard_map/ppermute | solution.py:425
  113.1 21.1 %collective-permute-start.9 = (bf16[4,4,80,128]{3,2,1,0:T(8,128)(2,1)}, bf16[4,4,80,128]{3,2,1,0:T(8,128)(2,1)S(1)}, u32[]{:S(2)}, u32[]{:S(2)}) collective-permute-start(bf16[4,4,80,128]{3,2,1,0:T(8,128)(2,1)} %get-tuple-element.26), channel_id=1, source_target_pairs={{0,1},{1,0},{2,3},{3,2},{4,5},{5,4},{6,7},{7,6},{8,9},{9,8},{10,11... | collective-permute-start | bytes 983048 | tf_op jit(solution)/shard_map/ppermute | solution.py:423
  114.6 26.6 %collective-permute-start.3 = (bf16[4,4,80,128]{3,2,1,0:T(8,128)(2,1)}, bf16[4,4,80,128]{3,2,1,0:T(8,128)(2,1)S(1)}, u32[]{:S(2)}, u32[]{:S(2)}) collective-permute-start(bf16[4,4,80,128]{3,2,1,0:T(8,128)(2,1)} %get-tuple-element.22), channel_id=1, source_target_pairs={{0,1},{1,0},{2,3},{3,2},{4,5},{5,4},{6,7},{7,6},{8,9},{9,8},{10,11... | collective-permute-start | bytes 983048 | tf_op jit(solution)/shard_map/ppermute | solution.py:423
  119.3 23.5 %collective-permute-start.4 = (bf16[4,4,80,128]{3,2,1,0:T(8,128)(2,1)}, bf16[4,4,80,128]{3,2,1,0:T(8,128)(2,1)S(1)}, u32[]{:S(2)}, u32[]{:S(2)}) collective-permute-start(bf16[4,4,80,128]{3,2,1,0:T(8,128)(2,1)} %get-tuple-element.23), channel_id=1, source_target_pairs={{0,8},{1,9},{2,10},{3,11},{4,12},{5,13},{6,14},{7,15},{8,0},{9,1},... | collective-permute-start | bytes 983048 | tf_op jit(solution)/shard_map/ppermute | solution.py:424
  120.3 26.5 %collective-permute-start.5 = (bf16[4,4,80,128]{3,2,1,0:T(8,128)(2,1)}, bf16[4,4,80,128]{3,2,1,0:T(8,128)(2,1)S(1)}, u32[]{:S(2)}, u32[]{:S(2)}) collective-permute-start(bf16[4,4,80,128]{3,2,1,0:T(8,128)(2,1)} %get-tuple-element.24), channel_id=1, source_target_pairs={{0,9},{1,8},{2,11},{3,10},{4,13},{5,12},{6,15},{7,14},{8,1},{9,0},... | collective-permute-start | bytes 983048 | tf_op jit(solution)/shard_map/ppermute | solution.py:425
  122.0 1.0 copy-start.4
  123.0 1.0 copy-start.7
  124.0 1.0 copy-start.9
  125.0 1.0 copy-start.11
  125.9 20.8 %copy-start = (bf16[4,4,80,128]{3,2,1,0:T(8,128)(2,1)S(1)}, bf16[4,4,80,128]{3,2,1,0:T(8,128)(2,1)}, u32[]{:S(2)}) copy-start(bf16[4,4,80,128]{3,2,1,0:T(8,128)(2,1)} %get-tuple-element.21.refs_0_) | copy-start | bytes 983044
  126.9 22.5 %collective-permute-start.24 = (bf16[15,64,128]{2,1,0:T(8,128)(2,1)S(1)}, bf16[15,64,128]{2,1,0:T(8,128)(2,1)S(1)}, u32[]{:S(2)}, u32[]{:S(2)}) collective-permute-start(bf16[15,64,128]{2,1,0:T(8,128)(2,1)S(1)} %correlate.25), channel_id=1, source_target_pairs={{0,2},{1,3},{2,6},{3,7},{4,0},{5,1},{6,4},{7,5},{8,10},{9,11},{10,... | collective-permute-start | bytes 737288 | tf_op jit(solution)/shard_map/ppermute | solution.py:431
  128.5 1.0 copy-start.2
  129.5 19.9 %copy-start.5 = (bf16[4,4,80,128]{3,2,1,0:T(8,128)(2,1)S(1)}, bf16[4,4,80,128]{3,2,1,0:T(8,128)(2,1)}, u32[]{:S(2)}) copy-start(bf16[4,4,80,128]{3,2,1,0:T(8,128)(2,1)} %get-tuple-element.33.refs_0_) | copy-start | bytes 983044
  134.2 18.8 %collective-permute-start.18 = (bf16[15,64,128]{2,1,0:T(8,128)(2,1)S(1)}, bf16[15,64,128]{2,1,0:T(8,128)(2,1)S(1)}, u32[]{:S(2)}, u32[]{:S(2)}) collective-permute-start(bf16[15,64,128]{2,1,0:T(8,128)(2,1)S(1)} %correlate.22), channel_id=1, source_target_pairs={{0,2},{1,3},{2,6},{3,7},{4,0},{5,1},{6,4},{7,5},{8,10},{9,11},{10,... | collective-permute-start | bytes 737288 | tf_op jit(solution)/shard_map/ppermute | solution.py:431
  135.8 17.2 %copy-start.3 = (bf16[4,4,80,128]{3,2,1,0:T(8,128)(2,1)S(1)}, bf16[4,4,80,128]{3,2,1,0:T(8,128)(2,1)}, u32[]{:S(2)}) copy-start(bf16[4,4,80,128]{3,2,1,0:T(8,128)(2,1)} %get-tuple-element.29.refs_0_) | copy-start | bytes 983044
  141.2 13.2 %collective-permute-start.12 = (bf16[15,64,128]{2,1,0:T(8,128)(2,1)S(1)}, bf16[15,64,128]{2,1,0:T(8,128)(2,1)S(1)}, u32[]{:S(2)}, u32[]{:S(2)}) collective-permute-start(bf16[15,64,128]{2,1,0:T(8,128)(2,1)S(1)} %correlate.19), channel_id=1, source_target_pairs={{0,2},{1,3},{2,6},{3,7},{4,0},{5,1},{6,4},{7,5},{8,10},{9,11},{10,... | collective-permute-start | bytes 737288 | tf_op jit(solution)/shard_map/ppermute | solution.py:431
  147.7 9.8 %collective-permute-start.6 = (bf16[15,64,128]{2,1,0:T(8,128)(2,1)S(1)}, bf16[15,64,128]{2,1,0:T(8,128)(2,1)S(1)}, u32[]{:S(2)}, u32[]{:S(2)}) collective-permute-start(bf16[15,64,128]{2,1,0:T(8,128)(2,1)S(1)} %correlate.16), channel_id=1, source_target_pairs={{0,2},{1,3},{2,6},{3,7},{4,0},{5,1},{6,4},{7,5},{8,10},{9,11},{10,... | collective-permute-start | bytes 737288 | tf_op jit(solution)/shard_map/ppermute | solution.py:431
  150.4 12.4 %collective-permute-start.25 = (bf16[15,64,128]{2,1,0:T(8,128)(2,1)S(1)}, bf16[15,64,128]{2,1,0:T(8,128)(2,1)S(1)}, u32[]{:S(2)}, u32[]{:S(2)}) collective-permute-start(bf16[15,64,128]{2,1,0:T(8,128)(2,1)S(1)} %correlate.26), channel_id=1, source_target_pairs={{0,2},{1,3},{2,6},{3,7},{4,0},{5,1},{6,4},{7,5},{8,10},{9,11},{10,... | collective-permute-start | bytes 737288 | tf_op jit(solution)/shard_map/ppermute | solution.py:431
  154.0 14.1 %collective-permute-start.19 = (bf16[15,64,128]{2,1,0:T(8,128)(2,1)S(1)}, bf16[15,64,128]{2,1,0:T(8,128)(2,1)S(1)}, u32[]{:S(2)}, u32[]{:S(2)}) collective-permute-start(bf16[15,64,128]{2,1,0:T(8,128)(2,1)S(1)} %correlate.23), channel_id=1, source_target_pairs={{0,2},{1,3},{2,6},{3,7},{4,0},{5,1},{6,4},{7,5},{8,10},{9,11},{10,... | collective-permute-start | bytes 737288 | tf_op jit(solution)/shard_map/ppermute | solution.py:431
  155.4 17.9 %collective-permute-start.13 = (bf16[15,64,128]{2,1,0:T(8,128)(2,1)S(1)}, bf16[15,64,128]{2,1,0:T(8,128)(2,1)S(1)}, u32[]{:S(2)}, u32[]{:S(2)}) collective-permute-start(bf16[15,64,128]{2,1,0:T(8,128)(2,1)S(1)} %correlate.20), channel_id=1, source_target_pairs={{0,2},{1,3},{2,6},{3,7},{4,0},{5,1},{6,4},{7,5},{8,10},{9,11},{10,... | collective-permute-start | bytes 737288 | tf_op jit(solution)/shard_map/ppermute | solution.py:431
  158.5 20.1 %collective-permute-start.7 = (bf16[15,64,128]{2,1,0:T(8,128)(2,1)S(1)}, bf16[15,64,128]{2,1,0:T(8,128)(2,1)S(1)}, u32[]{:S(2)}, u32[]{:S(2)}) collective-permute-start(bf16[15,64,128]{2,1,0:T(8,128)(2,1)S(1)} %correlate.17), channel_id=1, source_target_pairs={{0,2},{1,3},{2,6},{3,7},{4,0},{5,1},{6,4},{7,5},{8,10},{9,11},{10,... | collective-permute-start | bytes 737288 | tf_op jit(solution)/shard_map/ppermute | solution.py:431
  163.7 20.1 %collective-permute-start.26 = (bf16[15,64,128]{2,1,0:T(8,128)(2,1)S(1)}, bf16[15,64,128]{2,1,0:T(8,128)(2,1)S(1)}, u32[]{:S(2)}, u32[]{:S(2)}) collective-permute-start(bf16[15,64,128]{2,1,0:T(8,128)(2,1)S(1)} %correlate.27), channel_id=1, source_target_pairs={{0,2},{1,3},{2,6},{3,7},{4,0},{5,1},{6,4},{7,5},{8,10},{9,11},{10,... | collective-permute-start | bytes 737288 | tf_op jit(solution)/shard_map/ppermute | solution.py:431
  169.0 20.1 %collective-permute-start.20 = (bf16[15,64,128]{2,1,0:T(8,128)(2,1)S(1)}, bf16[15,64,128]{2,1,0:T(8,128)(2,1)S(1)}, u32[]{:S(2)}, u32[]{:S(2)}) collective-permute-start(bf16[15,64,128]{2,1,0:T(8,128)(2,1)S(1)} %correlate.24), channel_id=1, source_target_pairs={{0,2},{1,3},{2,6},{3,7},{4,0},{5,1},{6,4},{7,5},{8,10},{9,11},{10,... | collective-permute-start | bytes 737288 | tf_op jit(solution)/shard_map/ppermute | solution.py:431
  174.3 20.1 %collective-permute-start.14 = (bf16[15,64,128]{2,1,0:T(8,128)(2,1)S(1)}, bf16[15,64,128]{2,1,0:T(8,128)(2,1)S(1)}, u32[]{:S(2)}, u32[]{:S(2)}) collective-permute-start(bf16[15,64,128]{2,1,0:T(8,128)(2,1)S(1)} %correlate.21), channel_id=1, source_target_pairs={{0,2},{1,3},{2,6},{3,7},{4,0},{5,1},{6,4},{7,5},{8,10},{9,11},{10,... | collective-permute-start | bytes 737288 | tf_op jit(solution)/shard_map/ppermute | solution.py:431
  179.5 20.0 %collective-permute-start.8 = (bf16[15,64,128]{2,1,0:T(8,128)(2,1)S(1)}, bf16[15,64,128]{2,1,0:T(8,128)(2,1)S(1)}, u32[]{:S(2)}, u32[]{:S(2)}) collective-permute-start(bf16[15,64,128]{2,1,0:T(8,128)(2,1)S(1)} %correlate.18), channel_id=1, source_target_pairs={{0,2},{1,3},{2,6},{3,7},{4,0},{5,1},{6,4},{7,5},{8,10},{9,11},{10,... | collective-permute-start | bytes 737288 | tf_op jit(solution)/shard_map/ppermute | solution.py:431

commit v2 on v1

v2 whole, which is shorter than its diff:
```python
import functools
import math

import jax
import jax.numpy as jnp
import ml_dtypes
import numpy as np
from jax import lax
from jax.experimental import pallas as pl
from jax.experimental.pallas import tpu as pltpu
from jax.sharding import PartitionSpec as P

LAG = 7
HALO = 8
LANES = 128
AXES = ("depth", "freq")
VMEM_BYTES = 56 * 2**20


def parity_tables(length):
    position = np.arange(length, dtype=np.int64)
    product = position[:, None] * position[None, :] % length
    angles = product.astype(np.float32) * np.float32(2.0 * math.pi / length)
    factor = np.float32(1.0 / math.sqrt(length))
    cos, sin = np.cos(angles) * factor, np.sin(angles) * factor
    half = length // 2
    tables = []
    for parity in (0, 1):
        c, s = cos[parity::2, :half], sin[parity::2, :half]
        tables.append(np.block([[c, s], [-s, c]]).astype(ml_dtypes.bfloat16))
    return np.stack(tables)


def wavenumbers_squared(length):
    position = np.arange(length)
    signed = np.where(position < length // 2, position, position - length)
    wave = signed.astype(np.float32) * np.float32(2.0 * math.pi / length)
    squared = wave * wave
    return np.concatenate([squared[0::2], squared[1::2]])


Q_MAX = 14.0


def fit(function, degree):
    cheb = np.polynomial.chebyshev.Chebyshev.interpolate(
        lambda t: function((t + 1.0) * Q_MAX / 2), degree
    )
    return [float(v) for v in np.polynomial.chebyshev.cheb2poly(cheb.coef)]


COS_FIT = fit(lambda q: np.cos(np.sqrt(q)), 7)
SINC_FIT = fit(lambda q: np.sinc(np.sqrt(q) / np.pi), 7)


def horner(coefficients, t):
    total = jnp.full_like(t, coefficients[-1])
    for value in coefficients[-2::-1]:
        total = total * t + value
    return total


def cos_sin(square, root):
    t = square * (2.0 / Q_MAX) - 1.0
    return horner(COS_FIT, t), horner(SINC_FIT, t) * root


def lookup(table_row, codes):
    rows = codes.shape[0]
    parts = []
    for tile in range(codes.shape[1] // LANES):
        index = codes[:, tile * LANES : (tile + 1) * LANES]
        source = jnp.broadcast_to(table_row, (rows, LANES))
        parts.append(jnp.take_along_axis(source, index, axis=1, mode="promise_in_bounds"))
    return parts


def chain_kernel(
    place, order, angular_ref, *refs, begin, end, strips, width, tiles, shots, opening, closing,
):
    refs = list(refs)
    state = [refs.pop(0) for _ in range(2 if opening else 1)]
    codes = [refs.pop(0) for _ in range(end - begin)]
    levels, left_x, right_x, left_y, right_y, wave_x, wave_y = (refs.pop(0) for _ in range(7))
    padded = refs.pop() if closing else None
    mid = refs.pop()
    field = refs.pop() if closing else refs.pop(0)
    outs = refs
    rows_x, rows_y = field.shape[1], field.shape[2]
    half_x, half_y = rows_x // 2, rows_y // 2
    first, my_core, my_parity = place[0], place[1], place[2]
    angular = angular_ref[0]
    f32, bf16 = jnp.float32, jnp.bfloat16

    if opening:
        field[0:2] = state[0][0, 0]
        field[2:4] = state[1][0, 0]
    else:
        field[...] = state[0][...]
    if closing:
        padded[:, :, 0:HALO] = jnp.zeros((4, tiles, HALO, LANES), f32)
        padded[:, :, HALO + rows_x :] = jnp.zeros((4, tiles, HALO, LANES), f32)

    def step(t, carry):
        def codes_at(rows, cols):
            value = codes[end - begin - 1][rows, cols]
            for j in range(end - begin - 2, -1, -1):
                value = jnp.where(t == begin + j, codes[j][rows, cols], value)
            return value.astype(f32).astype(jnp.int32)

        def forward_x(i, carry):
            cols = pl.ds(pl.multiple_of(i * half_y, half_y), half_y)
            for part in range(2):
                index = codes_at(slice(part * half_x, (part + 1) * half_x), cols)
                value = functools.reduce(jnp.add, lookup(levels[0:1, :], index))
                carry = carry + jnp.sum(value.reshape(half_x // 8, 8, LANES), axis=0)
            for kind in range(2):
                low = field[2 * kind : 2 * kind + 2, 0:half_x, cols].reshape(rows_x, half_y)
                high = field[2 * kind : 2 * kind + 2, half_x:, cols].reshape(rows_x, half_y)
                for parity, mixed in enumerate((low + high, low - high)):
                    out = jnp.dot(left_x[parity], mixed, preferred_element_type=f32).astype(bf16)
                    mid[2 * kind : 2 * kind + 2, parity * half_x : (parity + 1) * half_x, cols] = (
                        out.reshape(2, half_x, half_y)
                    )
            return carry

        total = lax.fori_loop(0, 2, forward_x, jnp.zeros((8, LANES), f32))
        base = jnp.sum(total) / (rows_x * rows_y)
        angle = angular * (levels[0:1, :] - base)
        screen_cos, screen_sin = cos_sin(angle * angle, angle)
        reach = angular * base
        reach = reach * reach

        rows_block = half_x

        def along_y(i, carry):
            rows = pl.ds(pl.multiple_of(i * rows_block, rows_block), rows_block)
            blocks = mid[:, rows, :]
            re = jnp.concatenate([blocks[0], blocks[2]], axis=0)
            im = jnp.concatenate([blocks[1], blocks[3]], axis=0)
            low = jnp.concatenate([re[:, :half_y], im[:, :half_y]], axis=1)
            high = jnp.concatenate([re[:, half_y:], im[:, half_y:]], axis=1)
            back = []
            for parity, mixed in enumerate((low + high, low - high)):
                spectrum = jnp.dot(mixed, right_y[parity], preferred_element_type=f32)
                q = reach - wave_x[rows, :] - wave_y[0:1, parity * half_y : (parity + 1) * half_y]
                root = jnp.sqrt(jnp.abs(q))
                cos, sin = cos_sin(q, root)
                phase_re = jnp.where(q > 0.0, cos, jnp.exp(-root))
                phase_im = jnp.where(q > 0.0, sin, 0.0)
                pieces = []
                for kind, sign in ((0, 1.0), (1, -1.0)):
                    part = spectrum[kind * rows_block : (kind + 1) * rows_block]
                    a, b = part[:, :half_y], part[:, half_y:]
                    if kind == 0:
                        pieces.append(
                            jnp.concatenate(
                                [a * phase_re - b * phase_im, a * phase_im + b * phase_re], axis=1
                            ).astype(bf16)
                        )
                    else:
                        pieces.append(
                            jnp.concatenate(
                                [a * phase_re + b * phase_im, b * phase_re - a * phase_im], axis=1
                            ).astype(bf16)
                        )
                shifted = jnp.concatenate(pieces, axis=0)
                back.append(jnp.dot(shifted, left_y[parity], preferred_element_type=f32))
            low = (back[0] + back[1]).astype(bf16)
            high = (back[0] - back[1]).astype(bf16)
            for kind in range(2):
                part = slice(kind * rows_block, (kind + 1) * rows_block)
                mid[2 * kind, rows, 0:half_y] = low[part, :half_y]
                mid[2 * kind, rows, half_y:] = high[part, :half_y]
                mid[2 * kind + 1, rows, 0:half_y] = low[part, half_y:]
                mid[2 * kind + 1, rows, half_y:] = high[part, half_y:]
            return carry

        lax.fori_loop(0, rows_x // rows_block, along_y, 0)

        def inverse_x(i, carry):
            cols = pl.ds(pl.multiple_of(i * half_y, half_y), half_y)
            turn = []
            for part in range(2):
                codes = codes_at(slice(part * half_x, (part + 1) * half_x), cols)
                turn.append(tuple(jnp.concatenate(lookup(v, codes), axis=1) for v in (screen_cos, screen_sin)))
            for kind in range(2):
                even, odd = (
                    jnp.dot(
                        right_x[parity],
                        mid[
                            2 * kind : 2 * kind + 2, parity * half_x : (parity + 1) * half_x, cols
                        ].reshape(rows_x, half_y),
                        preferred_element_type=f32,
                    )
                    for parity in range(2)
                )
                for part, value in enumerate((even + odd, even - odd)):
                    a, b = value[:half_x], value[half_x:]
                    cos, sin = turn[part]
                    if kind == 0:
                        new_re, new_im = a * cos - b * sin, a * sin + b * cos
                    else:
                        new_re, new_im = a * cos + b * sin, b * cos - a * sin
                    rows = slice(part * half_x, (part + 1) * half_x)
                    field[2 * kind, rows, cols] = new_re.astype(bf16)
                    field[2 * kind + 1, rows, cols] = new_im.astype(bf16)
                    spot = slice(HALO + part * half_x, HALO + (part + 1) * half_x)
                    for j in range(half_y // LANES if closing else 0):
                        lanes = slice(j * LANES, (j + 1) * LANES)
                        padded[2 * kind, i * (half_y // LANES) + j, spot] = new_re[:, lanes]
                        padded[2 * kind + 1, i * (half_y // LANES) + j, spot] = new_im[:, lanes]
            return carry

        lax.fori_loop(0, 2, inverse_x, 0)

        if not closing:
            return carry

        def emit(target, parity):
            for s in range(strips):
                start = pl.multiple_of((2 * order[s] + parity) * width, 8)
                for tile in range(tiles):
                    half, at = divmod(tile, tiles // 2)
                    for part in range(4):
                        piece = padded[part, tile, pl.ds(start, width + 2 * HALO)]
                        outs[(target * strips + s) * 2 + half][part, at] = piece.astype(bf16)

        matched = t == end - shots + my_core

        @pl.when(matched)
        def _():
            emit(0, my_parity)
            emit(1, 1 - my_parity)

        @pl.when(jnp.logical_not(matched) & (t >= end - shots))
        def _():
            emit(2, my_parity)
            emit(3, 1 - my_parity)

        return carry

    lax.fori_loop(jnp.maximum(first, begin), end, step, 0)


def correlate_kernel(*refs, width, tiles, partial, scale):
    fields, refs = refs[:4], refs[4:]
    received = None
    if partial:
        received, refs = refs[0], refs[1:]
    out, wide = refs[-2], refs[-1]
    for tile in range(tiles):
        lanes = slice(tile * LANES, (tile + 1) * LANES)
        for m in range(4):
            for part in range(4):
                wide[m * 4 + part] = fields[m][part, tile].astype(jnp.float32)
        for lag in range(2 * LAG + 1):
            shift = lag - LAG
            total = None
            for m in range(4):
                for part in range(2):
                    term = (
                        wide[m * 4 + part, HALO - shift : HALO - shift + width]
                        * wide[m * 4 + 2 + part, HALO + shift : HALO + shift + width]
                    )
                    total = term if total is None else total + term
            if received is not None:
                total = total + received[lag, tile].astype(jnp.float32)
            if scale is not None:
                out[0, lag, :, lanes] = total * scale
            else:
                out[lag, tile] = total.astype(out.dtype)


def window_kernel(place, anchors, codes, out):
    del place, anchors
    out[...] = codes[0].astype(jnp.float32).astype(out.dtype)


def chain(
    place, order, angular, state, codes, table, begin, end, strips, width, shots, opening, closing
):
    rows_x, rows_y = state[0].shape[-2:]
    tiles = rows_y // LANES
    bf16, f32 = jnp.bfloat16, jnp.float32
    levels = jnp.pad(table, (0, LANES - table.shape[0]))[None]
    tables_x, tables_y = parity_tables(rows_x), parity_tables(rows_y)
    wave_x = np.broadcast_to(wavenumbers_squared(rows_x)[:, None], (rows_x, 1))
    wave_y = wavenumbers_squared(rows_y)[None]
    height = width + 2 * HALO
    vmem = pl.BlockSpec(memory_space=pltpu.VMEM)
    top_spec = pl.BlockSpec(
        (1, 1, 2, rows_x, rows_y), lambda i, place, order, angular: (place[1], 0, 0, 0, 0)
    )
    whole = (4, rows_x, rows_y)
    scratch = [pltpu.VMEM(whole, bf16)]
    if closing:
        out_shape = [jax.ShapeDtypeStruct((4, tiles // 2, height, LANES), bf16)] * (8 * strips)
        scratch = scratch + [
            pltpu.VMEM(whole, bf16),
            pltpu.VMEM((4, tiles, rows_x + 2 * HALO, LANES), f32),
        ]
    else:
        out_shape = [jax.ShapeDtypeStruct(whole, bf16)]
    return pl.pallas_call(
        functools.partial(
            chain_kernel, begin=begin, end=end, strips=strips, width=width, tiles=tiles,
            shots=shots, opening=opening, closing=closing,
        ),
        out_shape=out_shape,
        grid_spec=pltpu.PrefetchScalarGridSpec(
            num_scalar_prefetch=3,
            grid=(1,),
            in_specs=([top_spec] * 2 if opening else [vmem]) + [vmem] * (7 + len(codes)),
            out_specs=[vmem] * len(out_shape),
            scratch_shapes=scratch,
        ),
        compiler_params=pltpu.CompilerParams(vmem_limit_bytes=VMEM_BYTES),
        name="chain",
    )(
        place, order, angular, *state, *codes, levels,
        jnp.asarray(tables_x),
        jnp.asarray(np.swapaxes(tables_x, 1, 2)),
        jnp.asarray(tables_y),
        jnp.asarray(np.swapaxes(tables_y, 1, 2)),
        jnp.asarray(wave_x),
        jnp.asarray(wave_y),
    )


def shards(source_top, receiver_top, slowness_codes, slowness_table, anchors):
    shots, _, _, rows_x, rows_y = source_top.shape
    freq_count = lax.axis_size("freq")
    depth_count = lax.axis_size("depth")
    strips = freq_count // 2
    width = rows_x // freq_count
    lags = 2 * LAG + 1
    tiles = rows_y // LANES
    factor = 1.0 / math.sqrt(2.0 * shots * freq_count)
    depth_index = lax.axis_index("depth")
    freq_index = lax.axis_index("freq")
    my_core = depth_index % shots
    group = depth_index // shots
    my_parity = freq_index % 2
    bf16, f32 = jnp.bfloat16, jnp.float32

    def number(group_at, core_at, strip_at, parity_at):
        return (group_at * shots + core_at) * freq_count + strip_at * 2 + parity_at

    def pairs(move):
        found = []
        for g in range(depth_count // shots):
            for c in range(shots):
                for z in range(strips):
                    for x in range(2):
                        to = move(g, c, z, x)
                        if to is not None:
                            found.append((number(g, c, z, x), number(*to)))
        return found

    to_core = pairs(lambda g, c, z, x: (g, 1 - c, z, x))
    to_same = pairs(lambda g, c, z, x: (g, c, z, 1 - x))
    to_cross = pairs(lambda g, c, z, x: (g, 1 - c, z, 1 - x))
    up = pairs(lambda g, c, z, x: (1, c, z, x) if g == 0 else None)
    ring = [0] + list(range(1, strips, 2)) + list(range(2, strips, 2))[::-1]
    where = {z: p for p, z in enumerate(ring)}
    onward = pairs(lambda g, c, z, x: (g, c, ring[(where[z] + 1) % strips], x))
    plan = np.array(
        [[ring[(where[z] - 1 - s) % strips] for s in range(strips)] for z in range(strips)], np.int32
    )
    order = lax.dynamic_index_in_dim(jnp.asarray(plan), freq_index // 2, 0, keepdims=False)
    place = jnp.stack([(1 - group) * shots, my_core, my_parity]).astype(jnp.int32)

    def window(flip):
        def block(i, place, anchors):
            shot = jnp.abs(place[1] - flip)
            return (0, anchors[shot, 0] // rows_x, anchors[shot, 1] // rows_y)

        return pl.pallas_call(
            window_kernel,
            out_shape=jax.ShapeDtypeStruct((rows_x, rows_y), bf16),
            grid_spec=pltpu.PrefetchScalarGridSpec(
                num_scalar_prefetch=2,
                grid=(1,),
                in_specs=[pl.BlockSpec((1, rows_x, rows_y), block)],
                out_specs=pl.BlockSpec((rows_x, rows_y), lambda i, place, anchors: (0, 0)),
            ),
            name="window",
        )(place, anchors, slowness_codes)

    other = window(1)
    mine = window(0)
    from_core = lax.ppermute(other, AXES, to_core)
    near = [jnp.where(my_core == p, mine, from_core) for p in range(shots)]
    far = [lax.ppermute(near[p], AXES, up) for p in range(shots)]

    angular = math.pi * (0.45 + 0.5 * (freq_index.astype(f32) + 0.5) / freq_count)
    common = dict(strips=strips, width=width, shots=shots)
    start = (place, order, angular[None])
    state = chain(
        *start, (source_top, receiver_top), far[:1], slowness_table, 0, 1,
        opening=True, closing=False, **common,
    )
    outs = chain(
        *start, state, far[1:] + near, slowness_table, 1, 2 * shots,
        opening=False, closing=True, **common,
    )
    height = width + 2 * HALO

    def correlate(fields, received, last, buffer, half):
        operands = list(fields)
        field_spec = pl.BlockSpec((4, tiles // 2, height, LANES), lambda i: (0, 0, 0, 0))
        image_spec = pl.BlockSpec((lags, tiles // 2, width, LANES), lambda i: (0, 0, 0, 0))
        in_specs = [field_spec] * 4
        if received is not None:
            in_specs.append(image_spec)
            operands.append(received)
        aliases = {}
        if last:
            out_shape = jax.ShapeDtypeStruct((1, lags, width, rows_y), f32)
            out_spec = pl.BlockSpec((1, lags, width, rows_y // 2), lambda i: (0, 0, 0, half))
            if buffer is not None:
                in_specs.append(pl.BlockSpec(memory_space=pl.ANY))
                aliases = {len(operands): 0}
                operands.append(buffer)
        else:
            out_shape = jax.ShapeDtypeStruct((lags, tiles // 2, width, LANES), bf16)
            out_spec = image_spec
        return pl.pallas_call(
            functools.partial(
                correlate_kernel,
                width=width,
                tiles=tiles // 2,
                partial=received is not None,
                scale=factor if last else None,
            ),
            out_shape=out_shape,
            grid=(1,),
            in_specs=in_specs,
            out_specs=out_spec,
            scratch_shapes=[pltpu.VMEM((16, height, LANES), f32)],
            input_output_aliases=aliases,
            compiler_params=pltpu.CompilerParams(vmem_limit_bytes=16 * 2**20),
            cost_estimate=pl.CostEstimate(flops=10**9, bytes_accessed=6 * 10**6, transcendentals=0),
            name="correlate",
        )(*operands)

    def fetch(step, half):
        own, same, core, cross = (outs[(i * strips + step) * 2 + half] for i in range(4))
        return (
            own,
            lax.ppermute(same, AXES, to_same),
            lax.ppermute(core, AXES, to_core),
            lax.ppermute(cross, AXES, to_cross),
        )

    image = None
    received = [None, None]
    for step in range(strips):
        for half in range(2):
            last = step == strips - 1
            result = correlate(fetch(step, half), received[half], last, image, half)
            if last:
                image = result
            else:
                received[half] = lax.ppermute(result, AXES, onward)
    return image


def solution(mesh):
    return jax.shard_map(
        shards,
        mesh=mesh,
        in_specs=(
            P(None, "freq", None, None, None),
            P(None, "freq", None, None, None),
            P("depth", None, None),
            P(),
            P(),
        ),
        out_specs=P("depth", None, "freq", None),
        check_vma=False,
    )
```

time: 202 us -> 146 us (0.72)
  waiting for transfers between devices: 84.5 us -> 55.7 us
  Pallas kernels: 67.8 us -> 53.3 us
  between operations: 7.61 us -> 0.37 us
  local copies, waits for them, and re-layouts: 10.6 us -> 4.4 us
    ppermute x27 -> x33, waiting for transfers between devices: 84.5 us -> 55.7 us  [the longest x8 18.6 us: fetch(): lax.ppermute(same, AXES, to_same)]
    pallas_call x17 -> x12, Pallas kernels: 67.8 us -> 53.3 us  [the longest x2 39.6 us: chain(): pl.pallas_call(functools.partial(chain_kernel, begin=begin, end=end, stri...]
    unnamed x34 -> x62, local copies, waits for them, and re-layouts: 7.84 us -> 2.61 us
    ppermute x27 -> x33, starting transfers between devices: 28.1 us -> 29.9 us  [the longest x6 10.5 us: shards(): received[half] = lax.ppermute(result, AXES, onward)]
  transfers between devices with their start and end apart: 27 -> 33, of which waited for: 18 -> 19; matrix products, arithmetic and copies ran while one was open for 1% -> 1% of each run, Pallas kernels for 8% -> 14%
where the time goes in v2:
time: 146 us
  waiting for transfers between devices  55.7 us (38%)
  Pallas kernels  53.3 us (37%)
  starting transfers between devices  29.9 us (20%)
  local copies, waits for them, and re-layouts  4.4 us (3%)
  other arithmetic  1.78 us (1%)
    pallas_call x2, Pallas kernels, chain(): pl.pallas_call(functools.partial(chain_kernel, begin=begin, end=end, stri...  39.6 us
    ppermute x8, waiting for transfers between devices, fetch(): lax.ppermute(same, AXES, to_same)  18.6 us
    ppermute x8, waiting for transfers between devices, fetch(): lax.ppermute(cross, AXES, to_cross)  14.8 us
    ppermute x2, waiting for transfers between devices, shards(): far = [lax.ppermute(near[p], AXES, up) for p in range(shots)]  12.2 us
    ppermute x6, starting transfers between devices, shards(): received[half] = lax.ppermute(result, AXES, onward)  10.5 us
    ppermute x6, waiting for transfers between devices, shards(): received[half] = lax.ppermute(result, AXES, onward)  10.1 us
    ppermute x8, starting transfers between devices, fetch(): lax.ppermute(cross, AXES, to_cross)  8.31 us
    pallas_call x8, Pallas kernels, correlate(): pl.pallas_call(functools.partial(correlate_kernel, width=width, tiles=til...  8.15 us
  transfers between devices with their start and end apart: 33, of which 19 were waited for; matrix products, arithmetic and copies ran while one was open for 1% of the time, Pallas kernels for 14%

profile of v2, /device:TPU:4, one launch (start us, length us, event | category | flops | bytes accessed | tf_op | source)
XLA Modules:
  0.0 145.5 jit_solution(16993629321805114872)
XLA Ops:
  0.7 2.8 %window.3 = bf16[512,512]{1,0:T(8,128)(2,1)} custom-call(s32[3]{0:T(128)} %pad_add_fusion.place, s32[2,2]{1,0:T(2,128)} %anchors.3, s32[1,1024,1024]{2,1,0:T(8,128)} %codes.3), custom_call_target="tpu_custom_call" | custom-call | tf_op jit(solution)/shard_map/window/pallas_call | solution.py:379
  3.5 2.8 %window.2 = bf16[512,512]{1,0:T(8,128)(2,1)} custom-call(s32[3]{0:T(128)} %pad_add_fusion.place, s32[2,2]{1,0:T(2,128)} %anchors.3, s32[1,1024,1024]{2,1,0:T(8,128)} %codes.3), custom_call_target="tpu_custom_call" | custom-call | tf_op jit(solution)/shard_map/window/pallas_call | solution.py:379
  6.2 1.1 broadcast_select_fusion
  7.4 1.3 collective-permute-start.1
  8.7 1.3 collective-permute-start.2
  10.5 1.3 dynamic-slice_bitcast_fusion.order
  11.8 12.2 %collective-permute-done.1.refs_2_ = bf16[512,512]{1,0:T(8,128)(2,1)S(1)} collective-permute-done((bf16[512,512]{1,0:T(8,128)(2,1)S(1)}, bf16[512,512]{1,0:T(8,128)(2,1)S(1)}, u32[]{:S(2)}, u32[]{:S(2)}) %collective-permute-start.1) | collective-permute-done | bytes 524320 | tf_op jit(solution)/shard_map/ppermute | solution.py:395
  24.0 0.8 copy-done.11
  24.8 11.9 %chain.2.refs_0_ = bf16[4,512,512]{2,1,0:T(8,128)(2,1)} custom-call(s32[3]{0:T(128)} %pad_add_fusion.place, s32[4]{0:T(128)} %dynamic-slice_bitcast_fusion.order, f32[1]{0:T(128)} %bitcast.4.angular_ref, bf16[2,1,2,512,512]{4,3,2,1,0:T(8,128)(2,1)} %refs_0_.1, bf16[2,1,2,512,512]{4,3,2,1,0:T(8,128)(2,1)} %refs_1_.1, bf16[512,512]{1,0:T(8,128)(2,1)} %copy-done.11, ...), custom_call_target="tpu_custom_call" | custom-call | tf_op jit(solution)/shard_map/chain/pallas_call | solution.py:305
  36.7 0.8 copy-done.10
  37.5 27.7 %chain.3 = (bf16[4,2,80,128]{3,2,1,0:T(8,128)(2,1)}, bf16[4,2,80,128]{3,2,1,0:T(8,128)(2,1)}, bf16[4,2,80,128]{3,2,1,0:T(8,128)(2,1)}, bf16[4,2,80,128]{3,2,1,0:...) custom-call(s32[3]{0:T(128)} %pad_add_fusion.place, ...), custom_call_target="tpu_custom_call" | custom-call | tf_op jit(solution)/shard_map/chain/pallas_call | solution.py:305
  65.2 1.6 %collective-permute-start.27 = (bf16[4,2,80,128]{3,2,1,0:T(8,128)(2,1)}, bf16[4,2,80,128]{3,2,1,0:T(8,128)(2,1)S(1)}, u32[]{:S(2)}, u32[]{:S(2)}) collective-permute-start(bf16[4,2,80,128]{3,2,1,0:T(8,128)(2,1)} %get-tuple-element.66), channel_id=1, source_target_pairs={{0,1},{1,0},{2,3},{3,2},{4,5},{5,4},{6,7},{7,6},{8,9},{9,8},{10,11... | collective-permute-start | bytes 491528 | tf_op jit(solution)/shard_map/ppermute | solution.py:452
  67.4 1.5 %collective-permute-start.12 = (bf16[4,2,80,128]{3,2,1,0:T(8,128)(2,1)}, bf16[4,2,80,128]{3,2,1,0:T(8,128)(2,1)S(1)}, u32[]{:S(2)}, u32[]{:S(2)}) collective-permute-start(bf16[4,2,80,128]{3,2,1,0:T(8,128)(2,1)} %get-tuple-element.50), channel_id=1, source_target_pairs={{0,1},{1,0},{2,3},{3,2},{4,5},{5,4},{6,7},{7,6},{8,9},{9,8},{10,11... | collective-permute-start | bytes 491528 | tf_op jit(solution)/shard_map/ppermute | solution.py:452
  68.9 3.0 %collective-permute-done.27.refs_1_ = bf16[4,2,80,128]{3,2,1,0:T(8,128)(2,1)S(1)} collective-permute-done((bf16[4,2,80,128]{3,2,1,0:T(8,128)(2,1)}, bf16[4,2,80,128]{3,2,1,0:T(8,128)(2,1)S(1)}, u32[]{:S(2)}, u32[]{:S(2)}) %collective-permute-start.27) | collective-permute-done | bytes 163872 | tf_op jit(solution)/shard_map/ppermute | solution.py:452
  71.9 3.3 %collective-permute-done.29.refs_3_ = bf16[4,2,80,128]{3,2,1,0:T(8,128)(2,1)S(1)} collective-permute-done((bf16[4,2,80,128]{3,2,1,0:T(8,128)(2,1)}, bf16[4,2,80,128]{3,2,1,0:T(8,128)(2,1)S(1)}, u32[]{:S(2)}, u32[]{:S(2)}) %collective-permute-start.29) | collective-permute-done | bytes 163872 | tf_op jit(solution)/shard_map/ppermute | solution.py:454
  75.3 0.9 copy-done.7
  77.0 1.6 %collective-permute-start.30 = (bf16[15,2,64,128]{3,2,1,0:T(8,128)(2,1)S(1)}, bf16[15,2,64,128]{3,2,1,0:T(8,128)(2,1)S(1)}, u32[]{:S(2)}, u32[]{:S(2)}) collective-permute-start(bf16[15,2,64,128]{3,2,1,0:T(8,128)(2,1)S(1)} %correlate.11), channel_id=1, source_target_pairs={{0,2},{1,3},{2,6},{3,7},{4,0},{5,1},{6,4},{7,5},{8,10},{9,11},{10,... | collective-permute-start | bytes 1474568 | tf_op jit(solution)/shard_map/ppermute | solution.py:466
  78.9 1.6 %collective-permute-done.14.refs_3_ = bf16[4,2,80,128]{3,2,1,0:T(8,128)(2,1)S(1)} collective-permute-done((bf16[4,2,80,128]{3,2,1,0:T(8,128)(2,1)}, bf16[4,2,80,128]{3,2,1,0:T(8,128)(2,1)S(1)}, u32[]{:S(2)}, u32[]{:S(2)}) %collective-permute-start.14) | collective-permute-done | bytes 163872 | tf_op jit(solution)/shard_map/ppermute | solution.py:454
  80.6 0.8 correlate.8
  81.3 1.6 %collective-permute-start.15 = (bf16[15,2,64,128]{3,2,1,0:T(8,128)(2,1)S(1)}, bf16[15,2,64,128]{3,2,1,0:T(8,128)(2,1)S(1)}, u32[]{:S(2)}, u32[]{:S(2)}) collective-permute-start(bf16[15,2,64,128]{3,2,1,0:T(8,128)(2,1)S(1)} %correlate.8), channel_id=1, source_target_pairs={{0,2},{1,3},{2,6},{3,7},{4,0},{5,1},{6,4},{7,5},{8,10},{9,11},{10,... | collective-permute-start | bytes 1474568 | tf_op jit(solution)/shard_map/ppermute | solution.py:466
  83.7 1.3 collective-permute-start.25
  85.1 4.9 %collective-permute-done.24.refs_1_ = bf16[4,2,80,128]{3,2,1,0:T(8,128)(2,1)S(1)} collective-permute-done((bf16[4,2,80,128]{3,2,1,0:T(8,128)(2,1)S(1)}, bf16[4,2,80,128]{3,2,1,0:T(8,128)(2,1)S(1)}, u32[]{:S(2)}, u32[]{:S(2)}) %collective-permute-start.24) | collective-permute-done | bytes 163872 | tf_op jit(solution)/shard_map/ppermute | solution.py:452
  90.2 0.9 collective-permute-start.10
  91.1 1.9 %collective-permute-done.26.refs_3_ = bf16[4,2,80,128]{3,2,1,0:T(8,128)(2,1)S(1)} collective-permute-done((bf16[4,2,80,128]{3,2,1,0:T(8,128)(2,1)S(1)}, bf16[4,2,80,128]{3,2,1,0:T(8,128)(2,1)S(1)}, u32[]{:S(2)}, u32[]{:S(2)}) %collective-permute-start.26) | collective-permute-done | bytes 163872 | tf_op jit(solution)/shard_map/ppermute | solution.py:454
  93.5 0.8 correlate.12
  94.3 2.8 %collective-permute-start.31 = (bf16[15,2,64,128]{3,2,1,0:T(8,128)(2,1)S(1)}, bf16[15,2,64,128]{3,2,1,0:T(8,128)(2,1)S(1)}, u32[]{:S(2)}, u32[]{:S(2)}) collective-permute-start(bf16[15,2,64,128]{3,2,1,0:T(8,128)(2,1)S(1)} %correlate.12), channel_id=1, source_target_pairs={{0,2},{1,3},{2,6},{3,7},{4,0},{5,1},{6,4},{7,5},{8,10},{9,11},{10,... | collective-permute-start | bytes 1474568 | tf_op jit(solution)/shard_map/ppermute | solution.py:466
  97.2 2.7 %collective-permute-done.11.refs_3_ = bf16[4,2,80,128]{3,2,1,0:T(8,128)(2,1)S(1)} collective-permute-done((bf16[4,2,80,128]{3,2,1,0:T(8,128)(2,1)S(1)}, bf16[4,2,80,128]{3,2,1,0:T(8,128)(2,1)S(1)}, u32[]{:S(2)}, u32[]{:S(2)}) %collective-permute-start.11) | collective-permute-done | bytes 163872 | tf_op jit(solution)/shard_map/ppermute | solution.py:454
  99.9 2.7 %collective-permute-done.15.refs_4_ = bf16[15,2,64,128]{3,2,1,0:T(8,128)(2,1)S(1)} collective-permute-done((bf16[15,2,64,128]{3,2,1,0:T(8,128)(2,1)S(1)}, bf16[15,2,64,128]{3,2,1,0:T(8,128)(2,1)S(1)}, u32[]{:S(2)}, u32[]{:S(2)}) %collective-permute-start.15) | collective-permute-done | bytes 491552 | tf_op jit(solution)/shard_map/ppermute | solution.py:466
  102.6 0.8 correlate.9
  103.4 0.8 collective-permute-start.16
  105.0 1.3 collective-permute-start.23
  106.3 5.0 %collective-permute-done.21.refs_1_ = bf16[4,2,80,128]{3,2,1,0:T(8,128)(2,1)S(1)} collective-permute-done((bf16[4,2,80,128]{3,2,1,0:T(8,128)(2,1)S(1)}, bf16[4,2,80,128]{3,2,1,0:T(8,128)(2,1)S(1)}, u32[]{:S(2)}, u32[]{:S(2)}) %collective-permute-start.21) | collective-permute-done | bytes 163872 | tf_op jit(solution)/shard_map/ppermute | solution.py:452
  111.7 1.0 collective-permute-done.23.refs_3_
  112.7 2.2 %collective-permute-start.8 = (bf16[4,2,80,128]{3,2,1,0:T(8,128)(2,1)S(1)}, bf16[4,2,80,128]{3,2,1,0:T(8,128)(2,1)S(1)}, u32[]{:S(2)}, u32[]{:S(2)}) collective-permute-start(bf16[4,2,80,128]{3,2,1,0:T(8,128)(2,1)S(1)} %copy-done.18), channel_id=1, source_target_pairs={{0,9},{1,8},{2,11},{3,10},{4,13},{5,12},{6,15},{7,14},{8,1},{9,0},... | collective-permute-start | bytes 491528 | tf_op jit(solution)/shard_map/ppermute | solution.py:454
  114.9 0.8 correlate.13
  115.8 2.9 %collective-permute-start.32 = (bf16[15,2,64,128]{3,2,1,0:T(8,128)(2,1)S(1)}, bf16[15,2,64,128]{3,2,1,0:T(8,128)(2,1)S(1)}, u32[]{:S(2)}, u32[]{:S(2)}) collective-permute-start(bf16[15,2,64,128]{3,2,1,0:T(8,128)(2,1)S(1)} %correlate.13), channel_id=1, source_target_pairs={{0,2},{1,3},{2,6},{3,7},{4,0},{5,1},{6,4},{7,5},{8,10},{9,11},{10,... | collective-permute-start | bytes 1474568 | tf_op jit(solution)/shard_map/ppermute | solution.py:466
  118.6 0.8 collective-permute-done.8.refs_3_
  119.4 4.2 %collective-permute-done.16.refs_4_ = bf16[15,2,64,128]{3,2,1,0:T(8,128)(2,1)S(1)} collective-permute-done((bf16[15,2,64,128]{3,2,1,0:T(8,128)(2,1)S(1)}, bf16[15,2,64,128]{3,2,1,0:T(8,128)(2,1)S(1)}, u32[]{:S(2)}, u32[]{:S(2)}) %collective-permute-start.16) | collective-permute-done | bytes 491552 | tf_op jit(solution)/shard_map/ppermute | solution.py:466
  123.6 0.8 correlate.10
  124.4 0.8 collective-permute-start.17
  126.1 1.3 collective-permute-start.20
  127.4 5.0 %collective-permute-done.18.refs_1_ = bf16[4,2,80,128]{3,2,1,0:T(8,128)(2,1)S(1)} collective-permute-done((bf16[4,2,80,128]{3,2,1,0:T(8,128)(2,1)S(1)}, bf16[4,2,80,128]{3,2,1,0:T(8,128)(2,1)S(1)}, u32[]{:S(2)}, u32[]{:S(2)}) %collective-permute-start.18) | collective-permute-done | bytes 163872 | tf_op jit(solution)/shard_map/ppermute | solution.py:452
  132.8 1.0 collective-permute-done.20.refs_3_
  133.8 2.2 %collective-permute-start.5 = (bf16[4,2,80,128]{3,2,1,0:T(8,128)(2,1)S(1)}, bf16[4,2,80,128]{3,2,1,0:T(8,128)(2,1)S(1)}, u32[]{:S(2)}, u32[]{:S(2)}) collective-permute-start(bf16[4,2,80,128]{3,2,1,0:T(8,128)(2,1)S(1)} %copy-done.12), channel_id=1, source_target_pairs={{0,9},{1,8},{2,11},{3,10},{4,13},{5,12},{6,15},{7,14},{8,1},{9,0},... | collective-permute-start | bytes 491528 | tf_op jit(solution)/shard_map/ppermute | solution.py:454
  136.1 1.8 %correlate.14.refs_5_ = f32[1,15,64,512]{3,2,1,0:T(8,128)} custom-call(bf16[4,2,80,128]{3,2,1,0:T(8,128)(2,1)S(1)} %copy-done.1, bf16[4,2,80,128]{3,2,1,0:T(8,128)(2,1)S(1)} %collective-permute-done.18.refs_1_, bf16[4,2,80,128]{3,2,1,0:T(8,128)(2,1)S(1)} %collective-permute-done.19.refs_2_, bf16[4,2,80,128]{3,2,1,0:T(8,128)(2,1)S(1)} %collective-permute-done.20.refs_3_, ...), custom_call_target="tpu_custom_call" | custom-call | flops 1000000000 | bytes 6000000 | tf_op jit(solution)/shard_map/correlate/pallas_call | solution.py:429
  138.1 2.4 %collective-permute-done.5.refs_3_ = bf16[4,2,80,128]{3,2,1,0:T(8,128)(2,1)S(1)} collective-permute-done((bf16[4,2,80,128]{3,2,1,0:T(8,128)(2,1)S(1)}, bf16[4,2,80,128]{3,2,1,0:T(8,128)(2,1)S(1)}, u32[]{:S(2)}, u32[]{:S(2)}) %collective-permute-start.5) | collective-permute-done | bytes 163872 | tf_op jit(solution)/shard_map/ppermute | solution.py:454
  140.5 3.2 %collective-permute-done.17.refs_4_ = bf16[15,2,64,128]{3,2,1,0:T(8,128)(2,1)S(1)} collective-permute-done((bf16[15,2,64,128]{3,2,1,0:T(8,128)(2,1)S(1)}, bf16[15,2,64,128]{3,2,1,0:T(8,128)(2,1)S(1)}, u32[]{:S(2)}, u32[]{:S(2)}) %collective-permute-start.17) | collective-permute-done | bytes 491552 | tf_op jit(solution)/shard_map/ppermute | solution.py:466
  143.7 1.8 %correlate.15 = f32[1,15,64,512]{3,2,1,0:T(8,128)} custom-call(bf16[4,2,80,128]{3,2,1,0:T(8,128)(2,1)S(1)} %copy-done, bf16[4,2,80,128]{3,2,1,0:T(8,128)(2,1)S(1)} %collective-permute-done.3.refs_1_, bf16[4,2,80,128]{3,2,1,0:T(8,128)(2,1)S(1)} %collective-permute-done.4.refs_2_, ...), custom_call_target="tpu_custom_call", output_to_operand_aliasing={{}: (5, {})} | custom-call | flops 1000000000 | bytes 6000000 | tf_op jit(solution)/shard_map/correlate/pallas_call | solution.py:429
  (96 shorter events, 7.4 us)
Async XLA Ops:
  3.5 2.8 %collective-permute-start = (bf16[512,512]{1,0:T(8,128)(2,1)}, bf16[512,512]{1,0:T(8,128)(2,1)S(1)}, u32[]{:S(2)}, u32[]{:S(2)}) collective-permute-start(bf16[512,512]{1,0:T(8,128)(2,1)} %window.3), channel_id=1, source_target_pairs={{0,8},{1,9},{2,10},{3,11},{4,12},{5,13},{6,14},{7,15},{8,0},{9,1},... | collective-permute-start | bytes 1572872 | tf_op jit(solution)/shard_map/ppermute | solution.py:393
  7.4 29.3 %copy-start.8 = (bf16[512,512]{1,0:T(8,128)(2,1)}, bf16[512,512]{1,0:T(8,128)(2,1)S(1)}, u32[]{:S(2)}) copy-start(bf16[512,512]{1,0:T(8,128)(2,1)S(1)} %get-tuple-element.69.refs_3_) | copy-start | bytes 1572868
  7.4 29.3 %copy-start.9 = (bf16[512,512]{1,0:T(8,128)(2,1)}, bf16[512,512]{1,0:T(8,128)(2,1)S(1)}, u32[]{:S(2)}) copy-start(bf16[512,512]{1,0:T(8,128)(2,1)S(1)} %get-tuple-element.70.refs_2_) | copy-start | bytes 1572868
  7.4 16.6 %collective-permute-start.1 = (bf16[512,512]{1,0:T(8,128)(2,1)S(1)}, bf16[512,512]{1,0:T(8,128)(2,1)S(1)}, u32[]{:S(2)}, u32[]{:S(2)}) collective-permute-start(bf16[512,512]{1,0:T(8,128)(2,1)S(1)} %get-tuple-element.70.refs_2_), channel_id=1, source_target_pairs={{0,16},{1,17},{2,18},{3,19},{4,20},{5,21},{6,22},{7,23},{8,24},{9,... | collective-permute-start | bytes 1572872 | tf_op jit(solution)/shard_map/ppermute | solution.py:395
  8.7 28.0 %collective-permute-start.2 = (bf16[512,512]{1,0:T(8,128)(2,1)S(1)}, bf16[512,512]{1,0:T(8,128)(2,1)S(1)}, u32[]{:S(2)}, u32[]{:S(2)}) collective-permute-start(bf16[512,512]{1,0:T(8,128)(2,1)S(1)} %get-tuple-element.69.refs_3_), channel_id=1, source_target_pairs={{0,16},{1,17},{2,18},{3,19},{4,20},{5,21},{6,22},{7,23},{8,24},{9,... | collective-permute-start | bytes 1572872 | tf_op jit(solution)/shard_map/ppermute | solution.py:395
  65.2 6.7 %collective-permute-start.27 = (bf16[4,2,80,128]{3,2,1,0:T(8,128)(2,1)}, bf16[4,2,80,128]{3,2,1,0:T(8,128)(2,1)S(1)}, u32[]{:S(2)}, u32[]{:S(2)}) collective-permute-start(bf16[4,2,80,128]{3,2,1,0:T(8,128)(2,1)} %get-tuple-element.66), channel_id=1, source_target_pairs={{0,1},{1,0},{2,3},{3,2},{4,5},{5,4},{6,7},{7,6},{8,9},{9,8},{10,11... | collective-permute-start | bytes 491528 | tf_op jit(solution)/shard_map/ppermute | solution.py:452
  66.8 5.1 %collective-permute-start.28 = (bf16[4,2,80,128]{3,2,1,0:T(8,128)(2,1)}, bf16[4,2,80,128]{3,2,1,0:T(8,128)(2,1)S(1)}, u32[]{:S(2)}, u32[]{:S(2)}) collective-permute-start(bf16[4,2,80,128]{3,2,1,0:T(8,128)(2,1)} %get-tuple-element.67), channel_id=1, source_target_pairs={{0,8},{1,9},{2,10},{3,11},{4,12},{5,13},{6,14},{7,15},{8,0},{9,1},... | collective-permute-start | bytes 491528 | tf_op jit(solution)/shard_map/ppermute | solution.py:453
  66.8 8.5 %collective-permute-start.29 = (bf16[4,2,80,128]{3,2,1,0:T(8,128)(2,1)}, bf16[4,2,80,128]{3,2,1,0:T(8,128)(2,1)S(1)}, u32[]{:S(2)}, u32[]{:S(2)}) collective-permute-start(bf16[4,2,80,128]{3,2,1,0:T(8,128)(2,1)} %get-tuple-element.68), channel_id=1, source_target_pairs={{0,9},{1,8},{2,11},{3,10},{4,13},{5,12},{6,15},{7,14},{8,1},{9,0},... | collective-permute-start | bytes 491528 | tf_op jit(solution)/shard_map/ppermute | solution.py:454
  67.4 11.5 %collective-permute-start.12 = (bf16[4,2,80,128]{3,2,1,0:T(8,128)(2,1)}, bf16[4,2,80,128]{3,2,1,0:T(8,128)(2,1)S(1)}, u32[]{:S(2)}, u32[]{:S(2)}) collective-permute-start(bf16[4,2,80,128]{3,2,1,0:T(8,128)(2,1)} %get-tuple-element.50), channel_id=1, source_target_pairs={{0,1},{1,0},{2,3},{3,2},{4,5},{5,4},{6,7},{7,6},{8,9},{9,8},{10,11... | collective-permute-start | bytes 491528 | tf_op jit(solution)/shard_map/ppermute | solution.py:452
  68.9 10.0 %collective-permute-start.13 = (bf16[4,2,80,128]{3,2,1,0:T(8,128)(2,1)}, bf16[4,2,80,128]{3,2,1,0:T(8,128)(2,1)S(1)}, u32[]{:S(2)}, u32[]{:S(2)}) collective-permute-start(bf16[4,2,80,128]{3,2,1,0:T(8,128)(2,1)} %get-tuple-element.51), channel_id=1, source_target_pairs={{0,8},{1,9},{2,10},{3,11},{4,12},{5,13},{6,14},{7,15},{8,0},{9,1},... | collective-permute-start | bytes 491528 | tf_op jit(solution)/shard_map/ppermute | solution.py:453
  71.9 8.7 %collective-permute-start.14 = (bf16[4,2,80,128]{3,2,1,0:T(8,128)(2,1)}, bf16[4,2,80,128]{3,2,1,0:T(8,128)(2,1)S(1)}, u32[]{:S(2)}, u32[]{:S(2)}) collective-permute-start(bf16[4,2,80,128]{3,2,1,0:T(8,128)(2,1)} %get-tuple-element.52), channel_id=1, source_target_pairs={{0,9},{1,8},{2,11},{3,10},{4,13},{5,12},{6,15},{7,14},{8,1},{9,0},... | collective-permute-start | bytes 491528 | tf_op jit(solution)/shard_map/ppermute | solution.py:454
  77.0 16.0 %copy-start.24 = (bf16[4,2,80,128]{3,2,1,0:T(8,128)(2,1)S(1)}, bf16[4,2,80,128]{3,2,1,0:T(8,128)(2,1)}, u32[]{:S(2)}) copy-start(bf16[4,2,80,128]{3,2,1,0:T(8,128)(2,1)} %get-tuple-element.48) | copy-start | bytes 491524
  77.0 16.5 %copy-start.5 = (bf16[4,2,80,128]{3,2,1,0:T(8,128)(2,1)S(1)}, bf16[4,2,80,128]{3,2,1,0:T(8,128)(2,1)}, u32[]{:S(2)}) copy-start(bf16[4,2,80,128]{3,2,1,0:T(8,128)(2,1)} %get-tuple-element.61.refs_0_) | copy-start | bytes 491524
  77.0 16.5 %collective-permute-start.30 = (bf16[15,2,64,128]{3,2,1,0:T(8,128)(2,1)S(1)}, bf16[15,2,64,128]{3,2,1,0:T(8,128)(2,1)S(1)}, u32[]{:S(2)}, u32[]{:S(2)}) collective-permute-start(bf16[15,2,64,128]{3,2,1,0:T(8,128)(2,1)S(1)} %correlate.11), channel_id=1, source_target_pairs={{0,2},{1,3},{2,6},{3,7},{4,0},{5,1},{6,4},{7,5},{8,10},{9,11},{10,... | collective-permute-start | bytes 1474568 | tf_op jit(solution)/shard_map/ppermute | solution.py:466
  81.3 21.2 %copy-start.4 = (bf16[4,2,80,128]{3,2,1,0:T(8,128)(2,1)S(1)}, bf16[4,2,80,128]{3,2,1,0:T(8,128)(2,1)}, u32[]{:S(2)}) copy-start(bf16[4,2,80,128]{3,2,1,0:T(8,128)(2,1)} %get-tuple-element.45.refs_0_) | copy-start | bytes 491524
  81.3 21.2 %collective-permute-start.15 = (bf16[15,2,64,128]{3,2,1,0:T(8,128)(2,1)S(1)}, bf16[15,2,64,128]{3,2,1,0:T(8,128)(2,1)S(1)}, u32[]{:S(2)}, u32[]{:S(2)}) collective-permute-start(bf16[15,2,64,128]{3,2,1,0:T(8,128)(2,1)S(1)} %correlate.8), channel_id=1, source_target_pairs={{0,2},{1,3},{2,6},{3,7},{4,0},{5,1},{6,4},{7,5},{8,10},{9,11},{10,... | collective-permute-start | bytes 1474568 | tf_op jit(solution)/shard_map/ppermute | solution.py:466
  83.0 7.1 %collective-permute-start.24 = (bf16[4,2,80,128]{3,2,1,0:T(8,128)(2,1)S(1)}, bf16[4,2,80,128]{3,2,1,0:T(8,128)(2,1)S(1)}, u32[]{:S(2)}, u32[]{:S(2)}) collective-permute-start(bf16[4,2,80,128]{3,2,1,0:T(8,128)(2,1)S(1)} %copy-done.29), channel_id=1, source_target_pairs={{0,1},{1,0},{2,3},{3,2},{4,5},{5,4},{6,7},{7,6},{8,9},{9,8},{10,11... | collective-permute-start | bytes 491528 | tf_op jit(solution)/shard_map/ppermute | solution.py:452
  83.7 6.6 %collective-permute-start.25 = (bf16[4,2,80,128]{3,2,1,0:T(8,128)(2,1)S(1)}, bf16[4,2,80,128]{3,2,1,0:T(8,128)(2,1)S(1)}, u32[]{:S(2)}, u32[]{:S(2)}) collective-permute-start(bf16[4,2,80,128]{3,2,1,0:T(8,128)(2,1)S(1)} %copy-done.28), channel_id=1, source_target_pairs={{0,8},{1,9},{2,10},{3,11},{4,12},{5,13},{6,14},{7,15},{8,0},{9,1},... | collective-permute-start | bytes 491528 | tf_op jit(solution)/shard_map/ppermute | solution.py:453
  84.9 8.1 %collective-permute-start.26 = (bf16[4,2,80,128]{3,2,1,0:T(8,128)(2,1)S(1)}, bf16[4,2,80,128]{3,2,1,0:T(8,128)(2,1)S(1)}, u32[]{:S(2)}, u32[]{:S(2)}) collective-permute-start(bf16[4,2,80,128]{3,2,1,0:T(8,128)(2,1)S(1)} %copy-done.27), channel_id=1, source_target_pairs={{0,9},{1,8},{2,11},{3,10},{4,13},{5,12},{6,15},{7,14},{8,1},{9,0},... | collective-permute-start | bytes 491528 | tf_op jit(solution)/shard_map/ppermute | solution.py:454
  90.1 7.1 %collective-permute-start.9 = (bf16[4,2,80,128]{3,2,1,0:T(8,128)(2,1)S(1)}, bf16[4,2,80,128]{3,2,1,0:T(8,128)(2,1)S(1)}, u32[]{:S(2)}, u32[]{:S(2)}) collective-permute-start(bf16[4,2,80,128]{3,2,1,0:T(8,128)(2,1)S(1)} %copy-done.26), channel_id=1, source_target_pairs={{0,1},{1,0},{2,3},{3,2},{4,5},{5,4},{6,7},{7,6},{8,9},{9,8},{10,11... | collective-permute-start | bytes 491528 | tf_op jit(solution)/shard_map/ppermute | solution.py:452
  90.2 7.0 %collective-permute-start.10 = (bf16[4,2,80,128]{3,2,1,0:T(8,128)(2,1)S(1)}, bf16[4,2,80,128]{3,2,1,0:T(8,128)(2,1)S(1)}, u32[]{:S(2)}, u32[]{:S(2)}) collective-permute-start(bf16[4,2,80,128]{3,2,1,0:T(8,128)(2,1)S(1)} %copy-done.25), channel_id=1, source_target_pairs={{0,8},{1,9},{2,10},{3,11},{4,12},{5,13},{6,14},{7,15},{8,0},{9,1},... | collective-permute-start | bytes 491528 | tf_op jit(solution)/shard_map/ppermute | solution.py:453
  93.0 6.9 %collective-permute-start.11 = (bf16[4,2,80,128]{3,2,1,0:T(8,128)(2,1)S(1)}, bf16[4,2,80,128]{3,2,1,0:T(8,128)(2,1)S(1)}, u32[]{:S(2)}, u32[]{:S(2)}) collective-permute-start(bf16[4,2,80,128]{3,2,1,0:T(8,128)(2,1)S(1)} %copy-done.24), channel_id=1, source_target_pairs={{0,9},{1,8},{2,11},{3,10},{4,13},{5,12},{6,15},{7,14},{8,1},{9,0},... | collective-permute-start | bytes 491528 | tf_op jit(solution)/shard_map/ppermute | solution.py:454
  94.3 17.0 %copy-start.20 = (bf16[4,2,80,128]{3,2,1,0:T(8,128)(2,1)S(1)}, bf16[4,2,80,128]{3,2,1,0:T(8,128)(2,1)}, u32[]{:S(2)}) copy-start(bf16[4,2,80,128]{3,2,1,0:T(8,128)(2,1)} %get-tuple-element.42) | copy-start | bytes 491524
  94.3 17.4 %copy-start.19 = (bf16[4,2,80,128]{3,2,1,0:T(8,128)(2,1)S(1)}, bf16[4,2,80,128]{3,2,1,0:T(8,128)(2,1)}, u32[]{:S(2)}) copy-start(bf16[4,2,80,128]{3,2,1,0:T(8,128)(2,1)} %get-tuple-element.43) | copy-start | bytes 491524
  94.3 18.4 %copy-start.18 = (bf16[4,2,80,128]{3,2,1,0:T(8,128)(2,1)S(1)}, bf16[4,2,80,128]{3,2,1,0:T(8,128)(2,1)}, u32[]{:S(2)}) copy-start(bf16[4,2,80,128]{3,2,1,0:T(8,128)(2,1)} %get-tuple-element.44) | copy-start | bytes 491524
  94.3 20.6 %copy-start.3 = (bf16[4,2,80,128]{3,2,1,0:T(8,128)(2,1)S(1)}, bf16[4,2,80,128]{3,2,1,0:T(8,128)(2,1)}, u32[]{:S(2)}) copy-start(bf16[4,2,80,128]{3,2,1,0:T(8,128)(2,1)} %get-tuple-element.57.refs_0_) | copy-start | bytes 491524
  94.3 20.6 %collective-permute-start.31 = (bf16[15,2,64,128]{3,2,1,0:T(8,128)(2,1)S(1)}, bf16[15,2,64,128]{3,2,1,0:T(8,128)(2,1)S(1)}, u32[]{:S(2)}, u32[]{:S(2)}) collective-permute-start(bf16[15,2,64,128]{3,2,1,0:T(8,128)(2,1)S(1)} %correlate.12), channel_id=1, source_target_pairs={{0,2},{1,3},{2,6},{3,7},{4,0},{5,1},{6,4},{7,5},{8,10},{9,11},{10,... | collective-permute-start | bytes 1474568 | tf_op jit(solution)/shard_map/ppermute | solution.py:466
  103.3 20.3 %copy-start.2 = (bf16[4,2,80,128]{3,2,1,0:T(8,128)(2,1)S(1)}, bf16[4,2,80,128]{3,2,1,0:T(8,128)(2,1)}, u32[]{:S(2)}) copy-start(bf16[4,2,80,128]{3,2,1,0:T(8,128)(2,1)} %get-tuple-element.41.refs_0_) | copy-start | bytes 491524
  103.4 20.3 %collective-permute-start.16 = (bf16[15,2,64,128]{3,2,1,0:T(8,128)(2,1)S(1)}, bf16[15,2,64,128]{3,2,1,0:T(8,128)(2,1)S(1)}, u32[]{:S(2)}, u32[]{:S(2)}) collective-permute-start(bf16[15,2,64,128]{3,2,1,0:T(8,128)(2,1)S(1)} %correlate.9), channel_id=1, source_target_pairs={{0,2},{1,3},{2,6},{3,7},{4,0},{5,1},{6,4},{7,5},{8,10},{9,11},{10,... | collective-permute-start | bytes 1474568 | tf_op jit(solution)/shard_map/ppermute | solution.py:466
  104.2 7.1 %collective-permute-start.21 = (bf16[4,2,80,128]{3,2,1,0:T(8,128)(2,1)S(1)}, bf16[4,2,80,128]{3,2,1,0:T(8,128)(2,1)S(1)}, u32[]{:S(2)}, u32[]{:S(2)}) collective-permute-start(bf16[4,2,80,128]{3,2,1,0:T(8,128)(2,1)S(1)} %copy-done.23), channel_id=1, source_target_pairs={{0,1},{1,0},{2,3},{3,2},{4,5},{5,4},{6,7},{7,6},{8,9},{9,8},{10,11... | collective-permute-start | bytes 491528 | tf_op jit(solution)/shard_map/ppermute | solution.py:452
  104.7 7.0 %collective-permute-start.22 = (bf16[4,2,80,128]{3,2,1,0:T(8,128)(2,1)S(1)}, bf16[4,2,80,128]{3,2,1,0:T(8,128)(2,1)S(1)}, u32[]{:S(2)}, u32[]{:S(2)}) collective-permute-start(bf16[4,2,80,128]{3,2,1,0:T(8,128)(2,1)S(1)} %copy-done.22), channel_id=1, source_target_pairs={{0,8},{1,9},{2,10},{3,11},{4,12},{5,13},{6,14},{7,15},{8,0},{9,1},... | collective-permute-start | bytes 491528 | tf_op jit(solution)/shard_map/ppermute | solution.py:453
  105.0 7.7 %collective-permute-start.23 = (bf16[4,2,80,128]{3,2,1,0:T(8,128)(2,1)S(1)}, bf16[4,2,80,128]{3,2,1,0:T(8,128)(2,1)S(1)}, u32[]{:S(2)}, u32[]{:S(2)}) collective-permute-start(bf16[4,2,80,128]{3,2,1,0:T(8,128)(2,1)S(1)} %copy-done.21), channel_id=1, source_target_pairs={{0,9},{1,8},{2,11},{3,10},{4,13},{5,12},{6,15},{7,14},{8,1},{9,0},... | collective-permute-start | bytes 491528 | tf_op jit(solution)/shard_map/ppermute | solution.py:454
  111.3 7.3 %collective-permute-start.6 = (bf16[4,2,80,128]{3,2,1,0:T(8,128)(2,1)S(1)}, bf16[4,2,80,128]{3,2,1,0:T(8,128)(2,1)S(1)}, u32[]{:S(2)}, u32[]{:S(2)}) collective-permute-start(bf16[4,2,80,128]{3,2,1,0:T(8,128)(2,1)S(1)} %copy-done.20), channel_id=1, source_target_pairs={{0,1},{1,0},{2,3},{3,2},{4,5},{5,4},{6,7},{7,6},{8,9},{9,8},{10,11... | collective-permute-start | bytes 491528 | tf_op jit(solution)/shard_map/ppermute | solution.py:452
  111.7 6.9 %collective-permute-start.7 = (bf16[4,2,80,128]{3,2,1,0:T(8,128)(2,1)S(1)}, bf16[4,2,80,128]{3,2,1,0:T(8,128)(2,1)S(1)}, u32[]{:S(2)}, u32[]{:S(2)}) collective-permute-start(bf16[4,2,80,128]{3,2,1,0:T(8,128)(2,1)S(1)} %copy-done.19), channel_id=1, source_target_pairs={{0,8},{1,9},{2,10},{3,11},{4,12},{5,13},{6,14},{7,15},{8,0},{9,1},... | collective-permute-start | bytes 491528 | tf_op jit(solution)/shard_map/ppermute | solution.py:453
  112.7 6.7 %collective-permute-start.8 = (bf16[4,2,80,128]{3,2,1,0:T(8,128)(2,1)S(1)}, bf16[4,2,80,128]{3,2,1,0:T(8,128)(2,1)S(1)}, u32[]{:S(2)}, u32[]{:S(2)}) collective-permute-start(bf16[4,2,80,128]{3,2,1,0:T(8,128)(2,1)S(1)} %copy-done.18), channel_id=1, source_target_pairs={{0,9},{1,8},{2,11},{3,10},{4,13},{5,12},{6,15},{7,14},{8,1},{9,0},... | collective-permute-start | bytes 491528 | tf_op jit(solution)/shard_map/ppermute | solution.py:454
  115.7 16.6 %copy-start.14 = (bf16[4,2,80,128]{3,2,1,0:T(8,128)(2,1)S(1)}, bf16[4,2,80,128]{3,2,1,0:T(8,128)(2,1)}, u32[]{:S(2)}) copy-start(bf16[4,2,80,128]{3,2,1,0:T(8,128)(2,1)} %get-tuple-element.38) | copy-start | bytes 491524
  115.7 17.1 %copy-start.13 = (bf16[4,2,80,128]{3,2,1,0:T(8,128)(2,1)S(1)}, bf16[4,2,80,128]{3,2,1,0:T(8,128)(2,1)}, u32[]{:S(2)}) copy-start(bf16[4,2,80,128]{3,2,1,0:T(8,128)(2,1)} %get-tuple-element.39) | copy-start | bytes 491524
  115.7 18.1 %copy-start.12 = (bf16[4,2,80,128]{3,2,1,0:T(8,128)(2,1)S(1)}, bf16[4,2,80,128]{3,2,1,0:T(8,128)(2,1)}, u32[]{:S(2)}) copy-start(bf16[4,2,80,128]{3,2,1,0:T(8,128)(2,1)} %get-tuple-element.40) | copy-start | bytes 491524
  115.7 20.3 %copy-start.1 = (bf16[4,2,80,128]{3,2,1,0:T(8,128)(2,1)S(1)}, bf16[4,2,80,128]{3,2,1,0:T(8,128)(2,1)}, u32[]{:S(2)}) copy-start(bf16[4,2,80,128]{3,2,1,0:T(8,128)(2,1)} %get-tuple-element.53.refs_0_) | copy-start | bytes 491524
  115.8 20.3 %collective-permute-start.32 = (bf16[15,2,64,128]{3,2,1,0:T(8,128)(2,1)S(1)}, bf16[15,2,64,128]{3,2,1,0:T(8,128)(2,1)S(1)}, u32[]{:S(2)}, u32[]{:S(2)}) collective-permute-start(bf16[15,2,64,128]{3,2,1,0:T(8,128)(2,1)S(1)} %correlate.13), channel_id=1, source_target_pairs={{0,2},{1,3},{2,6},{3,7},{4,0},{5,1},{6,4},{7,5},{8,10},{9,11},{10,... | collective-permute-start | bytes 1474568 | tf_op jit(solution)/shard_map/ppermute | solution.py:466
  124.4 19.3 %copy-start = (bf16[4,2,80,128]{3,2,1,0:T(8,128)(2,1)S(1)}, bf16[4,2,80,128]{3,2,1,0:T(8,128)(2,1)}, u32[]{:S(2)}) copy-start(bf16[4,2,80,128]{3,2,1,0:T(8,128)(2,1)} %get-tuple-element.37.refs_0_) | copy-start | bytes 491524
  124.4 19.3 %collective-permute-start.17 = (bf16[15,2,64,128]{3,2,1,0:T(8,128)(2,1)S(1)}, bf16[15,2,64,128]{3,2,1,0:T(8,128)(2,1)S(1)}, u32[]{:S(2)}, u32[]{:S(2)}) collective-permute-start(bf16[15,2,64,128]{3,2,1,0:T(8,128)(2,1)S(1)} %correlate.10), channel_id=1, source_target_pairs={{0,2},{1,3},{2,6},{3,7},{4,0},{5,1},{6,4},{7,5},{8,10},{9,11},{10,... | collective-permute-start | bytes 1474568 | tf_op jit(solution)/shard_map/ppermute | solution.py:466
  125.2 7.1 %collective-permute-start.18 = (bf16[4,2,80,128]{3,2,1,0:T(8,128)(2,1)S(1)}, bf16[4,2,80,128]{3,2,1,0:T(8,128)(2,1)S(1)}, u32[]{:S(2)}, u32[]{:S(2)}) collective-permute-start(bf16[4,2,80,128]{3,2,1,0:T(8,128)(2,1)S(1)} %copy-done.17), channel_id=1, source_target_pairs={{0,1},{1,0},{2,3},{3,2},{4,5},{5,4},{6,7},{7,6},{8,9},{9,8},{10,11... | collective-permute-start | bytes 491528 | tf_op jit(solution)/shard_map/ppermute | solution.py:452
  125.8 7.0 %collective-permute-start.19 = (bf16[4,2,80,128]{3,2,1,0:T(8,128)(2,1)S(1)}, bf16[4,2,80,128]{3,2,1,0:T(8,128)(2,1)S(1)}, u32[]{:S(2)}, u32[]{:S(2)}) collective-permute-start(bf16[4,2,80,128]{3,2,1,0:T(8,128)(2,1)S(1)} %copy-done.16), channel_id=1, source_target_pairs={{0,8},{1,9},{2,10},{3,11},{4,12},{5,13},{6,14},{7,15},{8,0},{9,1},... | collective-permute-start | bytes 491528 | tf_op jit(solution)/shard_map/ppermute | solution.py:453
  126.1 7.8 %collective-permute-start.20 = (bf16[4,2,80,128]{3,2,1,0:T(8,128)(2,1)S(1)}, bf16[4,2,80,128]{3,2,1,0:T(8,128)(2,1)S(1)}, u32[]{:S(2)}, u32[]{:S(2)}) collective-permute-start(bf16[4,2,80,128]{3,2,1,0:T(8,128)(2,1)S(1)} %copy-done.15), channel_id=1, source_target_pairs={{0,9},{1,8},{2,11},{3,10},{4,13},{5,12},{6,15},{7,14},{8,1},{9,0},... | collective-permute-start | bytes 491528 | tf_op jit(solution)/shard_map/ppermute | solution.py:454
  132.4 5.8 %collective-permute-start.3 = (bf16[4,2,80,128]{3,2,1,0:T(8,128)(2,1)S(1)}, bf16[4,2,80,128]{3,2,1,0:T(8,128)(2,1)S(1)}, u32[]{:S(2)}, u32[]{:S(2)}) collective-permute-start(bf16[4,2,80,128]{3,2,1,0:T(8,128)(2,1)S(1)} %copy-done.14), channel_id=1, source_target_pairs={{0,1},{1,0},{2,3},{3,2},{4,5},{5,4},{6,7},{7,6},{8,9},{9,8},{10,11... | collective-permute-start | bytes 491528 | tf_op jit(solution)/shard_map/ppermute | solution.py:452
  132.8 5.3 %collective-permute-start.4 = (bf16[4,2,80,128]{3,2,1,0:T(8,128)(2,1)S(1)}, bf16[4,2,80,128]{3,2,1,0:T(8,128)(2,1)S(1)}, u32[]{:S(2)}, u32[]{:S(2)}) collective-permute-start(bf16[4,2,80,128]{3,2,1,0:T(8,128)(2,1)S(1)} %copy-done.13), channel_id=1, source_target_pairs={{0,8},{1,9},{2,10},{3,11},{4,12},{5,13},{6,14},{7,15},{8,0},{9,1},... | collective-permute-start | bytes 491528 | tf_op jit(solution)/shard_map/ppermute | solution.py:453
  133.8 6.7 %collective-permute-start.5 = (bf16[4,2,80,128]{3,2,1,0:T(8,128)(2,1)S(1)}, bf16[4,2,80,128]{3,2,1,0:T(8,128)(2,1)S(1)}, u32[]{:S(2)}, u32[]{:S(2)}) collective-permute-start(bf16[4,2,80,128]{3,2,1,0:T(8,128)(2,1)S(1)} %copy-done.12), channel_id=1, source_target_pairs={{0,9},{1,8},{2,11},{3,10},{4,13},{5,12},{6,15},{7,14},{8,1},{9,0},... | collective-permute-start | bytes 491528 | tf_op jit(solution)/shard_map/ppermute | solution.py:454
  (16 other events, 129.9 us)

commit v3 on v2

v3 whole, which is shorter than its diff:
```python
import functools
import math

import jax
import jax.numpy as jnp
import ml_dtypes
import numpy as np
from jax import lax
from jax.experimental import pallas as pl
from jax.experimental.pallas import tpu as pltpu
from jax.sharding import PartitionSpec as P

LAG = 7
HALO = 8
LANES = 128
AXES = ("depth", "freq")
VMEM_BYTES = 56 * 2**20


def parity_tables(length):
    position = np.arange(length, dtype=np.int64)
    product = position[:, None] * position[None, :] % length
    angles = product.astype(np.float32) * np.float32(2.0 * math.pi / length)
    factor = np.float32(1.0 / math.sqrt(length))
    cos, sin = np.cos(angles) * factor, np.sin(angles) * factor
    half = length // 2
    tables = []
    for parity in (0, 1):
        c, s = cos[parity::2, :half], sin[parity::2, :half]
        tables.append(np.block([[c, s], [-s, c]]).astype(ml_dtypes.bfloat16))
    return np.stack(tables)


def wavenumbers_squared(length):
    position = np.arange(length)
    signed = np.where(position < length // 2, position, position - length)
    wave = signed.astype(np.float32) * np.float32(2.0 * math.pi / length)
    squared = wave * wave
    return np.concatenate([squared[0::2], squared[1::2]])


Q_MAX = 14.0


def fit(function, degree):
    cheb = np.polynomial.chebyshev.Chebyshev.interpolate(
        lambda t: function((t + 1.0) * Q_MAX / 2), degree
    )
    return [float(v) for v in np.polynomial.chebyshev.cheb2poly(cheb.coef)]


COS_FIT = fit(lambda q: np.cos(np.sqrt(q)), 7)
SINC_FIT = fit(lambda q: np.sinc(np.sqrt(q) / np.pi), 7)


def horner(coefficients, t):
    total = jnp.full_like(t, coefficients[-1])
    for value in coefficients[-2::-1]:
        total = total * t + value
    return total


def cos_sin(square, root):
    t = square * (2.0 / Q_MAX) - 1.0
    return horner(COS_FIT, t), horner(SINC_FIT, t) * root


def lookup(table_row, codes):
    rows = codes.shape[0]
    parts = []
    for tile in range(codes.shape[1] // LANES):
        index = codes[:, tile * LANES : (tile + 1) * LANES]
        source = jnp.broadcast_to(table_row, (rows, LANES))
        parts.append(jnp.take_along_axis(source, index, axis=1, mode="promise_in_bounds"))
    return parts


def pick(flag, pair, *where):
    return jnp.where(flag, pair[0][where], pair[1][where])


def codes_of(flag, pair, rows, cols):
    return pick(flag, pair, rows, cols).astype(jnp.float32).astype(jnp.int32)


def chain_kernel(
    place, angular_ref, *refs, top, screened, planes, closing, strips, width, tiles, groups, shots
):
    refs = list(refs)

    def take(count):
        return [refs.pop(0) for _ in range(count)]

    tops = take(2) if top else None
    if screened:
        (before,) = take(1)
        before_codes, before_means = take(2), take(2)
    codes = [take(2) for _ in range(planes)] if closing else None
    means = [take(2) for _ in range(planes)]
    levels, left_x, right_x, left_y, right_y, wave_x, wave_y = take(7)
    if closing:
        field, mid, padded = refs[-3:]
        outs = refs[:-3]
    else:
        after, field, mid = refs
    rows_x, rows_y = field.shape[1], field.shape[2]
    half_x, half_y = rows_x // 2, rows_y // 2
    group, my_core, my_parity, spot = place[0], place[1], place[2], place[3]
    angular = angular_ref[0]
    f32, bf16 = jnp.float32, jnp.bfloat16
    lower_planes = group == 0

    def screen_table(mean):
        angle = angular * (levels[0:1, :] - mean)
        return cos_sin(angle * angle, angle)

    def turned(kind, a, b, cos, sin):
        if kind == 0:
            return a * cos - b * sin, a * sin + b * cos
        return a * cos + b * sin, b * cos - a * sin

    def load_top():
        field[0:2] = tops[0][0, 0]
        field[2:4] = tops[1][0, 0]

    def load_screened(index):
        flag = index == my_core
        tables = screen_table(pick(flag, before_means))

        def block(i, carry):
            rows = pl.ds(pl.multiple_of(i * 64, 64), 64)
            at = codes_of(flag, before_codes, rows, slice(None))
            cos, sin = (jnp.concatenate(lookup(table, at), axis=1) for table in tables)
            for kind in range(2):
                re, im = turned(kind, before[2 * kind, rows], before[2 * kind + 1, rows], cos, sin)
                field[2 * kind, rows] = re.astype(bf16)
                field[2 * kind + 1, rows] = im.astype(bf16)
            return carry

        lax.fori_loop(0, rows_x // 64, block, 0)

    def transforms(mean, sink):
        reach = angular * mean[0:1, 0:1]
        reach = reach * reach

        def forward_x(i, carry):
            cols = pl.ds(pl.multiple_of(i * half_y, half_y), half_y)
            for kind in range(2):
                low = field[2 * kind : 2 * kind + 2, 0:half_x, cols].reshape(rows_x, half_y)
                high = field[2 * kind : 2 * kind + 2, half_x:, cols].reshape(rows_x, half_y)
                for parity, mixed in enumerate((low + high, low - high)):
                    out = jnp.dot(left_x[parity], mixed, preferred_element_type=f32).astype(bf16)
                    mid[2 * kind : 2 * kind + 2, parity * half_x : (parity + 1) * half_x, cols] = (
                        out.reshape(2, half_x, half_y)
                    )
            return carry

        lax.fori_loop(0, 2, forward_x, 0)

        def along_y(i, carry):
            rows = pl.ds(pl.multiple_of(i * half_x, half_x), half_x)
            blocks = mid[:, rows, :]
            re = jnp.concatenate([blocks[0], blocks[2]], axis=0)
            im = jnp.concatenate([blocks[1], blocks[3]], axis=0)
            low = jnp.concatenate([re[:, :half_y], im[:, :half_y]], axis=1)
            high = jnp.concatenate([re[:, half_y:], im[:, half_y:]], axis=1)
            back = []
            for parity, mixed in enumerate((low + high, low - high)):
                spectrum = jnp.dot(mixed, right_y[parity], preferred_element_type=f32)
                q = reach - wave_x[rows, :] - wave_y[0:1, parity * half_y : (parity + 1) * half_y]
                root = jnp.sqrt(jnp.abs(q))
                cos, sin = cos_sin(q, root)
                phase_re = jnp.where(q > 0.0, cos, jnp.exp(-root))
                phase_im = jnp.where(q > 0.0, sin, 0.0)
                pieces = []
                for kind in range(2):
                    part = spectrum[kind * half_x : (kind + 1) * half_x]
                    new = turned(kind, part[:, :half_y], part[:, half_y:], phase_re, phase_im)
                    pieces.append(jnp.concatenate(new, axis=1).astype(bf16))
                shifted = jnp.concatenate(pieces, axis=0)
                back.append(jnp.dot(shifted, left_y[parity], preferred_element_type=f32))
            low = (back[0] + back[1]).astype(bf16)
            high = (back[0] - back[1]).astype(bf16)
            for kind in range(2):
                part = slice(kind * half_x, (kind + 1) * half_x)
                mid[2 * kind, rows, 0:half_y] = low[part, :half_y]
                mid[2 * kind, rows, half_y:] = high[part, :half_y]
                mid[2 * kind + 1, rows, 0:half_y] = low[part, half_y:]
                mid[2 * kind + 1, rows, half_y:] = high[part, half_y:]
            return carry

        lax.fori_loop(0, 2, along_y, 0)

        def inverse_x(i, carry):
            cols = pl.ds(pl.multiple_of(i * half_y, half_y), half_y)
            give = sink(i, cols)
            for kind in range(2):
                even, odd = (
                    jnp.dot(
                        right_x[parity],
                        mid[
                            2 * kind : 2 * kind + 2, parity * half_x : (parity + 1) * half_x, cols
                        ].reshape(rows_x, half_y),
                        preferred_element_type=f32,
                    )
                    for parity in range(2)
                )
                for part, value in enumerate((even + odd, even - odd)):
                    give(kind, part, value[:half_x], value[half_x:])
            return carry

        lax.fori_loop(0, 2, inverse_x, 0)

    def rows_of(part):
        return slice(part * half_x, (part + 1) * half_x)

    def sink_plain(i, cols):
        def give(kind, part, a, b):
            after[2 * kind, rows_of(part), cols] = a
            after[2 * kind + 1, rows_of(part), cols] = b

        return give

    def sink_screened(tables, flag, pair):
        def sink(i, cols):
            turn = []
            for part in range(2):
                at = codes_of(flag, pair, rows_of(part), cols)
                turn.append([jnp.concatenate(lookup(table, at), axis=1) for table in tables])

            def give(kind, part, a, b):
                for j, value in enumerate(turned(kind, a, b, *turn[part])):
                    field[2 * kind + j, rows_of(part), cols] = value.astype(bf16)
                    start = HALO + part * half_x
                    for k in range(half_y // LANES):
                        padded[2 * kind + j, i * (half_y // LANES) + k, start : start + half_x] = (
                            value[:, k * LANES : (k + 1) * LANES]
                        )

            return give

        return sink

    def emit(target, parity):
        for s in range(strips):
            p = lax.rem(spot + (strips - 1 - s), strips)
            strip = jnp.where(p == 0, 0, jnp.where(p <= strips // 2, 2 * p - 1, 2 * (strips - p)))
            start = pl.multiple_of((2 * strip + parity) * width, 8)
            for g, (first, last) in enumerate(groups):
                for tile in range(first, last):
                    for part in range(4):
                        piece = padded[part, tile, pl.ds(start, width + 2 * HALO)]
                        outs[(target * strips + s) * len(groups) + g][part, tile - first] = (
                            piece.astype(bf16)
                        )

    if not closing:

        @pl.when(jnp.logical_not(lower_planes))
        def _():
            index = 0
            if screened:
                load_screened(0)
                index = 1
            else:
                load_top()
            transforms(pick(index == my_core, means[0]), sink_plain)

        return

    @pl.when(lower_planes)
    def _():
        load_top()

    @pl.when(jnp.logical_not(lower_planes))
    def _():
        load_screened(shots - 1)

    padded[:, :, 0:HALO] = jnp.zeros((4, tiles, HALO, LANES), f32)
    padded[:, :, HALO + rows_x :] = jnp.zeros((4, tiles, HALO, LANES), f32)
    for t in range(planes):
        flag = my_core == t
        mean = pick(flag, means[t])
        transforms(mean, sink_screened(screen_table(mean), flag, codes[t]))

        @pl.when(flag)
        def _():
            emit(0, my_parity)
            emit(1, 1 - my_parity)

        @pl.when(jnp.logical_not(flag))
        def _():
            emit(2, my_parity)
            emit(3, 1 - my_parity)


def correlate_kernel(*refs, width, tiles, partial, scale):
    fields, refs = refs[:4], refs[4:]
    received = None
    if partial:
        received, refs = refs[0], refs[1:]
    out, wide = refs[-2], refs[-1]
    for tile in range(tiles):
        lanes = slice(tile * LANES, (tile + 1) * LANES)
        for m in range(4):
            for part in range(4):
                wide[m * 4 + part] = fields[m][part, tile].astype(jnp.float32)
        for lag in range(2 * LAG + 1):
            shift = lag - LAG
            total = None
            for m in range(4):
                for part in range(2):
                    term = (
                        wide[m * 4 + part, HALO - shift : HALO - shift + width]
                        * wide[m * 4 + 2 + part, HALO + shift : HALO + shift + width]
                    )
                    total = term if total is None else total + term
            if received is not None:
                total = total + received[lag, tile].astype(jnp.float32)
            if scale is not None:
                out[0, lag, :, lanes] = total * scale
            else:
                out[lag, tile] = total.astype(out.dtype)


def window_kernel(place, anchors, mine, other, table, *refs, cells):
    del place, anchors
    out_mine, out_other, mean_mine, mean_other, levels = refs
    levels[0:1, 0 : table.shape[1]] = table[...]
    i = pl.program_id(0)
    for codes, out, mean in ((mine, out_mine, mean_mine), (other, out_other, mean_other)):
        out[...] = codes[0].astype(jnp.float32).astype(out.dtype)
        value = functools.reduce(jnp.add, lookup(levels[0:1, :], codes[0]))
        value = jnp.sum(value, axis=0, keepdims=True)

        @pl.when(i == 0)
        def _(value=value, mean=mean):
            mean[...] = value

        @pl.when(i > 0)
        def _(value=value, mean=mean):
            mean[...] += value

        @pl.when(i == pl.num_programs(0) - 1)
        def _(mean=mean):
            mean[...] = jnp.broadcast_to(
                jnp.sum(mean[...], axis=1, keepdims=True) / cells, mean.shape
            )


def chain(
    place, angular, table, *, tops=None, before=None, codes=(), means=(), strips, width, groups, shots
):
    closing = bool(codes)
    rows_x, rows_y = (tops[0] if tops else before[0]).shape[-2:]
    tiles = rows_y // LANES
    bf16, f32 = jnp.bfloat16, jnp.float32
    tables_x, tables_y = parity_tables(rows_x), parity_tables(rows_y)
    wave_x = np.broadcast_to(wavenumbers_squared(rows_x)[:, None], (rows_x, 1))
    wave_y = wavenumbers_squared(rows_y)[None]
    height = width + 2 * HALO
    vmem = pl.BlockSpec(memory_space=pltpu.VMEM)
    top_spec = pl.BlockSpec(
        (1, 1, 2, rows_x, rows_y), lambda i, place, angular: (place[1], 0, 0, 0, 0)
    )
    operands = []
    in_specs = []
    if tops:
        operands += list(tops)
        in_specs += [top_spec] * 2
    if before:
        state, before_codes, before_means = before
        operands += [state, *before_codes, *before_means]
    for pair in (*codes, *means):
        operands += list(pair)
    operands += [
        jnp.pad(table, (0, LANES - table.shape[0]))[None],
        jnp.asarray(tables_x),
        jnp.asarray(np.swapaxes(tables_x, 1, 2)),
        jnp.asarray(tables_y),
        jnp.asarray(np.swapaxes(tables_y, 1, 2)),
        jnp.asarray(wave_x),
        jnp.asarray(wave_y),
    ]
    in_specs += [vmem] * (len(operands) - len(in_specs))
    whole = (4, rows_x, rows_y)
    scratch = [pltpu.VMEM(whole, bf16), pltpu.VMEM(whole, bf16)]
    if closing:
        out_shape = [
            jax.ShapeDtypeStruct((4, last - first, height, LANES), bf16)
            for _ in range(4 * strips)
            for first, last in groups
        ]
        scratch.append(pltpu.VMEM((4, tiles, rows_x + 2 * HALO, LANES), f32))
    else:
        out_shape = [jax.ShapeDtypeStruct(whole, f32)]
    return pl.pallas_call(
        functools.partial(
            chain_kernel, top=bool(tops), screened=bool(before), planes=len(means), closing=closing,
            strips=strips, width=width, tiles=tiles, groups=groups, shots=shots,
        ),
        out_shape=out_shape,
        grid_spec=pltpu.PrefetchScalarGridSpec(
            num_scalar_prefetch=2,
            grid=(1,),
            in_specs=in_specs,
            out_specs=[vmem] * len(out_shape),
            scratch_shapes=scratch,
        ),
        compiler_params=pltpu.CompilerParams(vmem_limit_bytes=VMEM_BYTES),
        cost_estimate=pl.CostEstimate(
            flops=9 * 10**9 * len(means), bytes_accessed=10**7, transcendentals=0
        ),
        name="chain",
    )(place, angular, *operands)


def windows(place, anchors, slowness_codes, table, rows_x, rows_y):
    steps = 8
    rows = rows_x // steps

    def block(flip):
        def index(i, place, anchors):
            shot = jnp.abs(place[1] - flip)
            return (0, anchors[shot, 0] // rows + i, anchors[shot, 1] // rows_y)

        return pl.BlockSpec((1, rows, rows_y), index)

    code_shape = jax.ShapeDtypeStruct((rows_x, rows_y), jnp.bfloat16)
    mean_shape = jax.ShapeDtypeStruct((1, LANES), jnp.float32)
    code_spec = pl.BlockSpec((rows, rows_y), lambda i, place, anchors: (i, 0))
    mean_spec = pl.BlockSpec((1, LANES), lambda i, place, anchors: (0, 0))
    return pl.pallas_call(
        functools.partial(window_kernel, cells=rows_x * rows_y),
        out_shape=[code_shape, code_shape, mean_shape, mean_shape],
        grid_spec=pltpu.PrefetchScalarGridSpec(
            num_scalar_prefetch=2,
            grid=(steps,),
            in_specs=[
                block(0),
                block(1),
                pl.BlockSpec((1, table.shape[0]), lambda i, place, anchors: (0, 0)),
            ],
            out_specs=[code_spec, code_spec, mean_spec, mean_spec],
            scratch_shapes=[pltpu.VMEM((8, LANES), jnp.float32)],
        ),
        name="windows",
    )(place, anchors, slowness_codes, slowness_codes, table[None])


def shards(source_top, receiver_top, slowness_codes, slowness_table, anchors):
    shots, _, _, rows_x, rows_y = source_top.shape
    freq_count = lax.axis_size("freq")
    depth_count = lax.axis_size("depth")
    strips = freq_count // 2
    width = rows_x // freq_count
    lags = 2 * LAG + 1
    tiles = rows_y // LANES
    groups = [(0, tiles // 2), (tiles // 2, tiles)]
    factor = 1.0 / math.sqrt(2.0 * shots * freq_count)
    depth_index = lax.axis_index("depth")
    freq_index = lax.axis_index("freq")
    my_core = depth_index % shots
    group = depth_index // shots
    bf16, f32 = jnp.bfloat16, jnp.float32

    def number(group_at, core_at, strip_at, parity_at):
        return (group_at * shots + core_at) * freq_count + strip_at * 2 + parity_at

    def pairs(move):
        found = []
        for g in range(depth_count // shots):
            for c in range(shots):
                for z in range(strips):
                    for x in range(2):
                        to = move(g, c, z, x)
                        if to is not None:
                            found.append((number(g, c, z, x), number(*to)))
        return found

    def send(value, move):
        return lax.ppermute(value, AXES, pairs(move))

    def to_core(g, c, z, x):
        return (g, 1 - c, z, x)

    def to_same(g, c, z, x):
        return (g, c, z, 1 - x)

    def to_cross(g, c, z, x):
        return (g, 1 - c, z, 1 - x)

    def up(core):
        return lambda g, c, z, x: (1, c, z, x) if g == 0 and c == core else None

    def up_same(g, c, z, x):
        return (1, c, z, x) if g == 0 else None

    def up_cross(g, c, z, x):
        return (1, 1 - c, z, x) if g == 0 else None

    ring = [0] + list(range(1, strips, 2)) + list(range(2, strips, 2))[::-1]
    spots = {z: p for p, z in enumerate(ring)}

    def onward(g, c, z, x):
        return (g, c, ring[(spots[z] + 1) % strips], x)

    my_strip = freq_index // 2
    spot = jnp.where(
        my_strip == 0,
        0,
        jnp.where(my_strip % 2 == 1, (my_strip + 1) // 2, strips - my_strip // 2),
    )
    place = jnp.stack([group, my_core, freq_index % 2, spot]).astype(jnp.int32)

    mine, other, mean_mine, mean_other = windows(
        place, anchors, slowness_codes, slowness_table, rows_x, rows_y
    )
    far_means = (send(mean_mine, up_same), send(mean_other, up_cross))
    from_core = send(other, to_core)
    near_means = (mean_mine, send(mean_other, to_core))
    far_first = (send(mine, up(0)), send(from_core, up(1)))
    mine_later, from_core_later, _ = lax.optimization_barrier((mine, from_core, mean_mine))
    far_second = (send(mine_later, up(1)), send(from_core_later, up(0)))
    near = (mine, from_core)

    angular = (math.pi * (0.45 + 0.5 * (freq_index.astype(f32) + 0.5) / freq_count))[None]
    common = dict(strips=strips, width=width, groups=groups, shots=shots)
    tops = (source_top, receiver_top)
    (state,) = chain(place, angular, slowness_table, tops=tops, means=[far_means], **common)
    (state,) = chain(
        place, angular, slowness_table, before=(state, far_first, far_means), means=[far_means],
        **common,
    )
    outs = chain(
        place, angular, slowness_table, tops=tops, before=(state, far_second, far_means),
        codes=[near] * shots, means=[near_means] * shots, **common,
    )
    height = width + 2 * HALO

    def correlate(fields, received, last, buffer, g):
        first, end = groups[g]
        count = end - first
        operands = list(fields)
        field_spec = pl.BlockSpec((4, count, height, LANES), lambda i: (0, 0, 0, 0))
        image_spec = pl.BlockSpec((lags, count, width, LANES), lambda i: (0, 0, 0, 0))
        in_specs = [field_spec] * 4
        if received is not None:
            in_specs.append(image_spec)
            operands.append(received)
        aliases = {}
        if last:
            out_shape = jax.ShapeDtypeStruct((1, lags, width, rows_y), f32)
            out_spec = pl.BlockSpec(
                (1, lags, width, count * LANES), lambda i: (0, 0, 0, first // count)
            )
            if buffer is not None:
                in_specs.append(pl.BlockSpec(memory_space=pl.ANY))
                aliases = {len(operands): 0}
                operands.append(buffer)
        else:
            out_shape = jax.ShapeDtypeStruct((lags, count, width, LANES), bf16)
            out_spec = image_spec
        return pl.pallas_call(
            functools.partial(
                correlate_kernel,
                width=width,
                tiles=count,
                partial=received is not None,
                scale=factor if last else None,
            ),
            out_shape=out_shape,
            grid=(1,),
            in_specs=in_specs,
            out_specs=out_spec,
            scratch_shapes=[pltpu.VMEM((16, height, LANES), f32)],
            input_output_aliases=aliases,
            compiler_params=pltpu.CompilerParams(vmem_limit_bytes=16 * 2**20),
            cost_estimate=pl.CostEstimate(flops=10**9, bytes_accessed=6 * 10**6, transcendentals=0),
            name="correlate",
        )(*operands)

    def fetch(step, g):
        own, same, core, cross = (outs[(i * strips + step) * len(groups) + g] for i in range(4))
        return own, send(same, to_same), send(core, to_core), send(cross, to_cross)

    image = None
    received = [None] * len(groups)
    for step in range(strips):
        for g in range(len(groups)):
            last = step == strips - 1
            result = correlate(fetch(step, g), received[g], last, image, g)
            if last:
                image = result
            else:
                received[g] = send(result, onward)
    return image


def solution(mesh):
    return jax.shard_map(
        shards,
        mesh=mesh,
        in_specs=(
            P(None, "freq", None, None, None),
            P(None, "freq", None, None, None),
            P("depth", None, None),
            P(),
            P(),
        ),
        out_specs=P("depth", None, "freq", None),
        check_vma=False,
    )
```

time: 146 us -> 154 us (1.055)
  Pallas kernels: 53.3 us -> 67.6 us
  waiting for transfers between devices: 55.7 us -> 45.5 us
  starting transfers between devices: 29.9 us -> 33.8 us
    pallas_call x12, Pallas kernels: 53.3 us -> 67.6 us  [the longest x3 51.6 us: chain(): pl.pallas_call(functools.partial(chain_kernel, top=bool(tops), screened=b...]
    ppermute x33 -> x38, waiting for transfers between devices: 55.7 us -> 45.5 us  [send(): return lax.ppermute(value, AXES, pairs(move))]
    ppermute x33 -> x38, starting transfers between devices: 29.9 us -> 33.8 us  [send(): return lax.ppermute(value, AXES, pairs(move))]
    unnamed x62 -> x72, local copies, waits for them, and re-layouts: 2.61 us -> 4.74 us
  transfers between devices with their start and end apart: 33 -> 38, of which waited for: 19 -> 19; matrix products, arithmetic and copies ran while one was open for 1% -> 0% of each run, Pallas kernels for 14% -> 22%
where the time goes in v3:
time: 154 us; the launch traced here: 153 us
  Pallas kernels  67.6 us (44%)
  waiting for transfers between devices  45.5 us (30%)
  starting transfers between devices  33.8 us (22%)
  local copies, waits for them, and re-layouts  5.34 us (3%)
    pallas_call x3, Pallas kernels, chain(): pl.pallas_call(functools.partial(chain_kernel, top=bool(tops), screened=b...  51.6 us
    ppermute x38, waiting for transfers between devices, send(): return lax.ppermute(value, AXES, pairs(move))  45.5 us
    ppermute x38, starting transfers between devices, send(): return lax.ppermute(value, AXES, pairs(move))  33.8 us
    pallas_call x8, Pallas kernels, correlate(): pl.pallas_call(functools.partial(correlate_kernel, width=width, tiles=cou...  8.15 us
    pallas_call x1, Pallas kernels, windows(): pl.pallas_call(functools.partial(window_kernel, cells=rows_x * rows_y), o...  7.85 us
    unnamed x72, local copies, waits for them, and re-layouts  4.74 us
  transfers between devices with their start and end apart: 38, of which 19 were waited for; matrix products, arithmetic and copies ran while one was open for 0% of the time, Pallas kernels for 22%

profile of v3, /device:TPU:4, one launch (start us, length us, event | category | flops | bytes accessed | tf_op | source)
XLA Modules:
  0.0 153.2 jit_solution(13576041916334479598)
XLA Ops:
  0.6 7.9 %windows.1 = (bf16[512,512]{1,0:T(8,128)(2,1)}, bf16[512,512]{1,0:T(8,128)(2,1)}, f32[1,128]{1,0:T(1,128)}, f32[1,128]{1,0:T(1,128)}) custom-call(s32[4]{0:T(128)} %pad_add_fusion.place, s32[2,2]{1,0:T(2,128)} %anchors.1, s32[1,1024,1024]{2,1,0:T(8,128)} %other.1, s32[1,1024,1024]{2,1,0:T(8,128)} %other.1, f32[1,32]{1,0:T(1,128)} %bitcast.8), custom_call_target="tpu_custom_call" | custom-call | tf_op jit(solution)/shard_map/windows/pallas_call | solution.py:433
  8.9 1.3 collective-permute-start.1
  10.2 1.3 collective-permute-start
  11.5 1.3 collective-permute-start.2
  14.2 1.7 %collective-permute-done.refs_2_.refs_3_.refs_5_ = f32[1,128]{1,0:T(1,128)S(1)} collective-permute-done((f32[1,128]{1,0:T(1,128)}, f32[1,128]{1,0:T(1,128)S(1)}, u32[]{:S(2)}, u32[]{:S(2)}) %collective-permute-start) | collective-permute-done | bytes 544 | tf_op jit(solution)/shard_map/ppermute | solution.py:482
  16.4 12.3 %chain.3.refs_0_ = f32[4,512,512]{2,1,0:T(8,128)} custom-call(s32[4]{0:T(128)} %pad_add_fusion.place, f32[1]{0:T(128)} %bitcast.4.angular_ref, bf16[2,1,2,512,512]{4,3,2,1,0:T(8,128)(2,1)} %refs_0_.3, bf16[2,1,2,512,512]{4,3,2,1,0:T(8,128)(2,1)} %refs_1_.3, f32[1,128]{1,0:T(1,128)} %copy-done.35, f32[1,128]{1,0:T(1,128)} %copy-done.34, ...), custom_call_target="tpu_custom_call" | custom-call | flops 8999999488 | bytes 10000000 | tf_op jit(solution)/shard_map/chain/pallas_call | solution.py:397
  29.4 1.3 collective-permute-start.6
  30.7 0.8 copy-done.13
  31.5 0.8 copy-done.14
  32.3 14.9 %chain.4.refs_2_ = f32[4,512,512]{2,1,0:T(8,128)} custom-call(s32[4]{0:T(128)} %pad_add_fusion.place, f32[1]{0:T(128)} %bitcast.4.angular_ref, f32[4,512,512]{2,1,0:T(8,128)} %chain.3.refs_0_, bf16[512,512]{1,0:T(8,128)(2,1)} %copy-done.13, bf16[512,512]{1,0:T(8,128)(2,1)} %copy-done.14, f32[1,128]{1,0:T(1,128)} %copy-done.35, f32[1,128]{1,0:T(1,128)} %copy-done.34, ...), custom_call_target="tpu_custom_call" | custom-call | flops 8999999488 | bytes 10000000 | tf_op jit(solution)/shard_map/chain/pallas_call | solution.py:397
  48.0 0.8 copy-done.12
  48.8 24.4 %chain.5 = (bf16[4,2,80,128]{3,2,1,0:T(8,128)(2,1)}, bf16[4,2,80,128]{3,2,1,0:T(8,128)(2,1)}, bf16[4,2,80,128]{3,2,1,0:T(8,128)(2,1)}, bf16[4,2,80,128]{3,2,1,0:...) custom-call(s32[4]{0:T(128)} %pad_add_fusion.place, ...), custom_call_target="tpu_custom_call" | custom-call | flops 17999998976 | bytes 10000000 | tf_op jit(solution)/shard_map/chain/pallas_call | solution.py:397
  73.3 1.6 %collective-permute-start.32 = (bf16[4,2,80,128]{3,2,1,0:T(8,128)(2,1)}, bf16[4,2,80,128]{3,2,1,0:T(8,128)(2,1)S(1)}, u32[]{:S(2)}, u32[]{:S(2)}) collective-permute-start(bf16[4,2,80,128]{3,2,1,0:T(8,128)(2,1)} %get-tuple-element.78), channel_id=1, source_target_pairs={{0,1},{1,0},{2,3},{3,2},{4,5},{5,4},{6,7},{7,6},{8,9},{9,8},{10,11... | collective-permute-start | bytes 491528 | tf_op jit(solution)/shard_map/ppermute | solution.py:482
  75.5 1.6 %collective-permute-start.17 = (bf16[4,2,80,128]{3,2,1,0:T(8,128)(2,1)}, bf16[4,2,80,128]{3,2,1,0:T(8,128)(2,1)S(1)}, u32[]{:S(2)}, u32[]{:S(2)}) collective-permute-start(bf16[4,2,80,128]{3,2,1,0:T(8,128)(2,1)} %get-tuple-element.62), channel_id=1, source_target_pairs={{0,1},{1,0},{2,3},{3,2},{4,5},{5,4},{6,7},{7,6},{8,9},{9,8},{10,11... | collective-permute-start | bytes 491528 | tf_op jit(solution)/shard_map/ppermute | solution.py:482
  77.0 2.8 %collective-permute-done.32.refs_1_ = bf16[4,2,80,128]{3,2,1,0:T(8,128)(2,1)S(1)} collective-permute-done((bf16[4,2,80,128]{3,2,1,0:T(8,128)(2,1)}, bf16[4,2,80,128]{3,2,1,0:T(8,128)(2,1)S(1)}, u32[]{:S(2)}, u32[]{:S(2)}) %collective-permute-start.32) | collective-permute-done | bytes 163872 | tf_op jit(solution)/shard_map/ppermute | solution.py:482
  79.9 3.5 %collective-permute-done.34.refs_3_ = bf16[4,2,80,128]{3,2,1,0:T(8,128)(2,1)S(1)} collective-permute-done((bf16[4,2,80,128]{3,2,1,0:T(8,128)(2,1)}, bf16[4,2,80,128]{3,2,1,0:T(8,128)(2,1)S(1)}, u32[]{:S(2)}, u32[]{:S(2)}) %collective-permute-start.34) | collective-permute-done | bytes 163872 | tf_op jit(solution)/shard_map/ppermute | solution.py:482
  83.4 0.9 copy-done.7
  84.3 0.8 correlate.11
  85.1 1.5 collective-permute-start.35
  86.8 1.8 %collective-permute-done.19.refs_3_ = bf16[4,2,80,128]{3,2,1,0:T(8,128)(2,1)S(1)} collective-permute-done((bf16[4,2,80,128]{3,2,1,0:T(8,128)(2,1)}, bf16[4,2,80,128]{3,2,1,0:T(8,128)(2,1)S(1)}, u32[]{:S(2)}, u32[]{:S(2)}) %collective-permute-start.19) | collective-permute-done | bytes 163872 | tf_op jit(solution)/shard_map/ppermute | solution.py:482
  89.4 1.5 %collective-permute-start.20 = (bf16[15,2,64,128]{3,2,1,0:T(8,128)(2,1)S(1)}, bf16[15,2,64,128]{3,2,1,0:T(8,128)(2,1)S(1)}, u32[]{:S(2)}, u32[]{:S(2)}) collective-permute-start(bf16[15,2,64,128]{3,2,1,0:T(8,128)(2,1)S(1)} %correlate.8), channel_id=1, source_target_pairs={{0,2},{1,3},{2,6},{3,7},{4,0},{5,1},{6,4},{7,5},{8,10},{9,11},{10,... | collective-permute-start | bytes 1474568 | tf_op jit(solution)/shard_map/ppermute | solution.py:482
  91.5 1.3 collective-permute-start.30
  93.1 4.9 %collective-permute-done.29.refs_1_ = bf16[4,2,80,128]{3,2,1,0:T(8,128)(2,1)S(1)} collective-permute-done((bf16[4,2,80,128]{3,2,1,0:T(8,128)(2,1)S(1)}, bf16[4,2,80,128]{3,2,1,0:T(8,128)(2,1)S(1)}, u32[]{:S(2)}, u32[]{:S(2)}) %collective-permute-start.29) | collective-permute-done | bytes 163872 | tf_op jit(solution)/shard_map/ppermute | solution.py:482
  98.0 0.9 collective-permute-start.15
  99.0 2.0 %collective-permute-done.31.refs_3_ = bf16[4,2,80,128]{3,2,1,0:T(8,128)(2,1)S(1)} collective-permute-done((bf16[4,2,80,128]{3,2,1,0:T(8,128)(2,1)S(1)}, bf16[4,2,80,128]{3,2,1,0:T(8,128)(2,1)S(1)}, u32[]{:S(2)}, u32[]{:S(2)}) %collective-permute-start.31) | collective-permute-done | bytes 163872 | tf_op jit(solution)/shard_map/ppermute | solution.py:482
  101.3 0.8 correlate.12
  102.1 2.7 %collective-permute-start.36 = (bf16[15,2,64,128]{3,2,1,0:T(8,128)(2,1)S(1)}, bf16[15,2,64,128]{3,2,1,0:T(8,128)(2,1)S(1)}, u32[]{:S(2)}, u32[]{:S(2)}) collective-permute-start(bf16[15,2,64,128]{3,2,1,0:T(8,128)(2,1)S(1)} %correlate.12), channel_id=1, source_target_pairs={{0,2},{1,3},{2,6},{3,7},{4,0},{5,1},{6,4},{7,5},{8,10},{9,11},{10,... | collective-permute-start | bytes 1474568 | tf_op jit(solution)/shard_map/ppermute | solution.py:482
  105.2 2.7 %collective-permute-done.16.refs_3_ = bf16[4,2,80,128]{3,2,1,0:T(8,128)(2,1)S(1)} collective-permute-done((bf16[4,2,80,128]{3,2,1,0:T(8,128)(2,1)S(1)}, bf16[4,2,80,128]{3,2,1,0:T(8,128)(2,1)S(1)}, u32[]{:S(2)}, u32[]{:S(2)}) %collective-permute-start.16) | collective-permute-done | bytes 163872 | tf_op jit(solution)/shard_map/ppermute | solution.py:482
  107.9 2.9 %collective-permute-done.20.refs_4_ = bf16[15,2,64,128]{3,2,1,0:T(8,128)(2,1)S(1)} collective-permute-done((bf16[15,2,64,128]{3,2,1,0:T(8,128)(2,1)S(1)}, bf16[15,2,64,128]{3,2,1,0:T(8,128)(2,1)S(1)}, u32[]{:S(2)}, u32[]{:S(2)}) %collective-permute-start.20) | collective-permute-done | bytes 491552 | tf_op jit(solution)/shard_map/ppermute | solution.py:482
  110.7 0.8 correlate.9
  112.6 0.8 collective-permute-start.27
  113.4 1.0 collective-permute-start.28
  114.4 5.0 %collective-permute-done.26.refs_1_ = bf16[4,2,80,128]{3,2,1,0:T(8,128)(2,1)S(1)} collective-permute-done((bf16[4,2,80,128]{3,2,1,0:T(8,128)(2,1)S(1)}, bf16[4,2,80,128]{3,2,1,0:T(8,128)(2,1)S(1)}, u32[]{:S(2)}, u32[]{:S(2)}) %collective-permute-start.26) | collective-permute-done | bytes 163872 | tf_op jit(solution)/shard_map/ppermute | solution.py:482
  119.6 0.9 collective-permute-done.28.refs_3_
  120.5 2.2 %collective-permute-start.13 = (bf16[4,2,80,128]{3,2,1,0:T(8,128)(2,1)S(1)}, bf16[4,2,80,128]{3,2,1,0:T(8,128)(2,1)S(1)}, u32[]{:S(2)}, u32[]{:S(2)}) collective-permute-start(bf16[4,2,80,128]{3,2,1,0:T(8,128)(2,1)S(1)} %copy-done.21), channel_id=1, source_target_pairs={{0,9},{1,8},{2,11},{3,10},{4,13},{5,12},{6,15},{7,14},{8,1},{9,0},... | collective-permute-start | bytes 491528 | tf_op jit(solution)/shard_map/ppermute | solution.py:482
  122.7 0.8 correlate.13
  123.6 2.9 %collective-permute-start.37 = (bf16[15,2,64,128]{3,2,1,0:T(8,128)(2,1)S(1)}, bf16[15,2,64,128]{3,2,1,0:T(8,128)(2,1)S(1)}, u32[]{:S(2)}, u32[]{:S(2)}) collective-permute-start(bf16[15,2,64,128]{3,2,1,0:T(8,128)(2,1)S(1)} %correlate.13), channel_id=1, source_target_pairs={{0,2},{1,3},{2,6},{3,7},{4,0},{5,1},{6,4},{7,5},{8,10},{9,11},{10,... | collective-permute-start | bytes 1474568 | tf_op jit(solution)/shard_map/ppermute | solution.py:482
  126.5 1.2 collective-permute-done.13.refs_3_
  127.7 4.1 %collective-permute-done.21.refs_4_ = bf16[15,2,64,128]{3,2,1,0:T(8,128)(2,1)S(1)} collective-permute-done((bf16[15,2,64,128]{3,2,1,0:T(8,128)(2,1)S(1)}, bf16[15,2,64,128]{3,2,1,0:T(8,128)(2,1)S(1)}, u32[]{:S(2)}, u32[]{:S(2)}) %collective-permute-start.21) | collective-permute-done | bytes 491552 | tf_op jit(solution)/shard_map/ppermute | solution.py:482
  131.8 0.8 correlate.10
  134.5 1.0 collective-permute-start.25
  135.5 5.0 %collective-permute-done.23.refs_1_ = bf16[4,2,80,128]{3,2,1,0:T(8,128)(2,1)S(1)} collective-permute-done((bf16[4,2,80,128]{3,2,1,0:T(8,128)(2,1)S(1)}, bf16[4,2,80,128]{3,2,1,0:T(8,128)(2,1)S(1)}, u32[]{:S(2)}, u32[]{:S(2)}) %collective-permute-start.23) | collective-permute-done | bytes 163872 | tf_op jit(solution)/shard_map/ppermute | solution.py:482
  141.1 1.0 collective-permute-done.25.refs_3_
  142.1 2.2 %collective-permute-start.10 = (bf16[4,2,80,128]{3,2,1,0:T(8,128)(2,1)S(1)}, bf16[4,2,80,128]{3,2,1,0:T(8,128)(2,1)S(1)}, u32[]{:S(2)}, u32[]{:S(2)}) collective-permute-start(bf16[4,2,80,128]{3,2,1,0:T(8,128)(2,1)S(1)} %copy-done.15), channel_id=1, source_target_pairs={{0,9},{1,8},{2,11},{3,10},{4,13},{5,12},{6,15},{7,14},{8,1},{9,0},... | collective-permute-start | bytes 491528 | tf_op jit(solution)/shard_map/ppermute | solution.py:482
  144.3 1.8 %correlate.14.refs_5_ = f32[1,15,64,512]{3,2,1,0:T(8,128)} custom-call(bf16[4,2,80,128]{3,2,1,0:T(8,128)(2,1)S(1)} %copy-done.1, bf16[4,2,80,128]{3,2,1,0:T(8,128)(2,1)S(1)} %collective-permute-done.23.refs_1_, bf16[4,2,80,128]{3,2,1,0:T(8,128)(2,1)S(1)} %collective-permute-done.24.refs_2_, bf16[4,2,80,128]{3,2,1,0:T(8,128)(2,1)S(1)} %collective-permute-done.25.refs_3_, ...), custom_call_target="tpu_custom_call" | custom-call | flops 1000000000 | bytes 6000000 | tf_op jit(solution)/shard_map/correlate/pallas_call | solution.py:564
  146.7 2.2 %collective-permute-done.10.refs_3_ = bf16[4,2,80,128]{3,2,1,0:T(8,128)(2,1)S(1)} collective-permute-done((bf16[4,2,80,128]{3,2,1,0:T(8,128)(2,1)S(1)}, bf16[4,2,80,128]{3,2,1,0:T(8,128)(2,1)S(1)}, u32[]{:S(2)}, u32[]{:S(2)}) %collective-permute-start.10) | collective-permute-done | bytes 163872 | tf_op jit(solution)/shard_map/ppermute | solution.py:482
  148.9 2.5 %collective-permute-done.22.refs_4_ = bf16[15,2,64,128]{3,2,1,0:T(8,128)(2,1)S(1)} collective-permute-done((bf16[15,2,64,128]{3,2,1,0:T(8,128)(2,1)S(1)}, bf16[15,2,64,128]{3,2,1,0:T(8,128)(2,1)S(1)}, u32[]{:S(2)}, u32[]{:S(2)}) %collective-permute-start.22) | collective-permute-done | bytes 491552 | tf_op jit(solution)/shard_map/ppermute | solution.py:482
  151.5 1.8 %correlate.15 = f32[1,15,64,512]{3,2,1,0:T(8,128)} custom-call(bf16[4,2,80,128]{3,2,1,0:T(8,128)(2,1)S(1)} %copy-done, bf16[4,2,80,128]{3,2,1,0:T(8,128)(2,1)S(1)} %collective-permute-done.8.refs_1_, bf16[4,2,80,128]{3,2,1,0:T(8,128)(2,1)S(1)} %collective-permute-done.9.refs_2_, ...), custom_call_target="tpu_custom_call", output_to_operand_aliasing={{}: (5, {})} | custom-call | flops 1000000000 | bytes 6000000 | tf_op jit(solution)/shard_map/correlate/pallas_call | solution.py:564
  (114 shorter events, 11.9 us)
Async XLA Ops:
  8.4 5.0 %collective-permute-start.3 = (bf16[512,512]{1,0:T(8,128)(2,1)}, bf16[512,512]{1,0:T(8,128)(2,1)S(1)}, u32[]{:S(2)}, u32[]{:S(2)}) collective-permute-start(bf16[512,512]{1,0:T(8,128)(2,1)} %get-tuple-element.46), channel_id=1, source_target_pairs={{0,8},{1,9},{2,10},{3,11},{4,12},{5,13},{6,14},{7,15},{8,0},{9,1},... | collective-permute-start | bytes 1572872 | tf_op jit(solution)/shard_map/ppermute | solution.py:482
  8.4 38.8 %collective-permute-start.7 = (f32[1,128]{1,0:T(1,128)}, f32[1,128]{1,0:T(1,128)S(1)}, u32[]{:S(2)}, u32[]{:S(2)}) collective-permute-start(f32[1,128]{1,0:T(1,128)} %get-tuple-element.44), channel_id=1, source_target_pairs={{0,8},{1,9},{2,10},{3,11},{4,12},{5,13},{6,14},{7,15},{8,0},{9,1},... | collective-permute-start | bytes 1544 | tf_op jit(solution)/shard_map/ppermute | solution.py:482
  8.9 5.2 %collective-permute-start.1 = (f32[1,128]{1,0:T(1,128)}, f32[1,128]{1,0:T(1,128)S(1)}, u32[]{:S(2)}, u32[]{:S(2)}) collective-permute-start(f32[1,128]{1,0:T(1,128)} %get-tuple-element.44), channel_id=1, source_target_pairs={{0,24},{1,25},{2,26},{3,27},{4,28},{5,29},{6,30},{7,31},{8,16},{9,... | collective-permute-start | bytes 1544 | tf_op jit(solution)/shard_map/ppermute | solution.py:482
  10.2 5.6 %collective-permute-start = (f32[1,128]{1,0:T(1,128)}, f32[1,128]{1,0:T(1,128)S(1)}, u32[]{:S(2)}, u32[]{:S(2)}) collective-permute-start(f32[1,128]{1,0:T(1,128)} %get-tuple-element.43.refs_11_.refs_13_), channel_id=1, source_target_pairs={{0,16},{1,17},{2,18},{3,19},{4,20},{5,21},{6,22},{7,23},{8,24},{9,... | collective-permute-start | bytes 1544 | tf_op jit(solution)/shard_map/ppermute | solution.py:482
  11.5 19.2 %collective-permute-start.2 = (bf16[512,512]{1,0:T(8,128)(2,1)}, bf16[512,512]{1,0:T(8,128)(2,1)S(1)}, u32[]{:S(2)}, u32[]{:S(2)}) collective-permute-start(bf16[512,512]{1,0:T(8,128)(2,1)} %get-tuple-element.47.refs_7_.refs_9_), channel_id=1, source_target_pairs={{0,16},{1,17},{2,18},{3,19},{4,20},{5,21},{6,22},{7,23}} | collective-permute-start | bytes 1572872 | tf_op jit(solution)/shard_map/ppermute | solution.py:482
  13.4 17.3 %collective-permute-start.4 = (bf16[512,512]{1,0:T(8,128)(2,1)S(1)}, bf16[512,512]{1,0:T(8,128)(2,1)S(1)}, u32[]{:S(2)}, u32[]{:S(2)}) collective-permute-start(bf16[512,512]{1,0:T(8,128)(2,1)S(1)} %collective-permute-done.3.refs_8_.refs_10_), channel_id=1, source_target_pairs={{8,24},{9,25},{10,26},{11,27},{12,28},{13,29},{14,30},{15,31}} | collective-permute-start | bytes 1572872 | tf_op jit(solution)/shard_map/ppermute | solution.py:482
  28.7 18.5 %collective-permute-start.5 = (bf16[512,512]{1,0:T(8,128)(2,1)S(1)}, bf16[512,512]{1,0:T(8,128)(2,1)S(1)}, u32[]{:S(2)}, u32[]{:S(2)}) collective-permute-start(bf16[512,512]{1,0:T(8,128)(2,1)S(1)} %copy-done.9), channel_id=1, source_target_pairs={{8,24},{9,25},{10,26},{11,27},{12,28},{13,29},{14,30},{15,31}} | collective-permute-start | bytes 1572872 | tf_op jit(solution)/shard_map/ppermute | solution.py:482
  29.4 17.8 %collective-permute-start.6 = (bf16[512,512]{1,0:T(8,128)(2,1)S(1)}, bf16[512,512]{1,0:T(8,128)(2,1)S(1)}, u32[]{:S(2)}, u32[]{:S(2)}) collective-permute-start(bf16[512,512]{1,0:T(8,128)(2,1)S(1)} %collective-permute-done.3.refs_8_.refs_10_), channel_id=1, source_target_pairs={{0,16},{1,17},{2,18},{3,19},{4,20},{5,21},{6,22},{7,23}} | collective-permute-start | bytes 1572872 | tf_op jit(solution)/shard_map/ppermute | solution.py:482
  73.3 6.6 %collective-permute-start.32 = (bf16[4,2,80,128]{3,2,1,0:T(8,128)(2,1)}, bf16[4,2,80,128]{3,2,1,0:T(8,128)(2,1)S(1)}, u32[]{:S(2)}, u32[]{:S(2)}) collective-permute-start(bf16[4,2,80,128]{3,2,1,0:T(8,128)(2,1)} %get-tuple-element.78), channel_id=1, source_target_pairs={{0,1},{1,0},{2,3},{3,2},{4,5},{5,4},{6,7},{7,6},{8,9},{9,8},{10,11... | collective-permute-start | bytes 491528 | tf_op jit(solution)/shard_map/ppermute | solution.py:482
  74.9 5.0 %collective-permute-start.33 = (bf16[4,2,80,128]{3,2,1,0:T(8,128)(2,1)}, bf16[4,2,80,128]{3,2,1,0:T(8,128)(2,1)S(1)}, u32[]{:S(2)}, u32[]{:S(2)}) collective-permute-start(bf16[4,2,80,128]{3,2,1,0:T(8,128)(2,1)} %get-tuple-element.79), channel_id=1, source_target_pairs={{0,8},{1,9},{2,10},{3,11},{4,12},{5,13},{6,14},{7,15},{8,0},{9,1},... | collective-permute-start | bytes 491528 | tf_op jit(solution)/shard_map/ppermute | solution.py:482
  74.9 8.5 %collective-permute-start.34 = (bf16[4,2,80,128]{3,2,1,0:T(8,128)(2,1)}, bf16[4,2,80,128]{3,2,1,0:T(8,128)(2,1)S(1)}, u32[]{:S(2)}, u32[]{:S(2)}) collective-permute-start(bf16[4,2,80,128]{3,2,1,0:T(8,128)(2,1)} %get-tuple-element.80), channel_id=1, source_target_pairs={{0,9},{1,8},{2,11},{3,10},{4,13},{5,12},{6,15},{7,14},{8,1},{9,0},... | collective-permute-start | bytes 491528 | tf_op jit(solution)/shard_map/ppermute | solution.py:482
  75.5 11.3 %collective-permute-start.17 = (bf16[4,2,80,128]{3,2,1,0:T(8,128)(2,1)}, bf16[4,2,80,128]{3,2,1,0:T(8,128)(2,1)S(1)}, u32[]{:S(2)}, u32[]{:S(2)}) collective-permute-start(bf16[4,2,80,128]{3,2,1,0:T(8,128)(2,1)} %get-tuple-element.62), channel_id=1, source_target_pairs={{0,1},{1,0},{2,3},{3,2},{4,5},{5,4},{6,7},{7,6},{8,9},{9,8},{10,11... | collective-permute-start | bytes 491528 | tf_op jit(solution)/shard_map/ppermute | solution.py:482
  77.0 9.8 %collective-permute-start.18 = (bf16[4,2,80,128]{3,2,1,0:T(8,128)(2,1)}, bf16[4,2,80,128]{3,2,1,0:T(8,128)(2,1)S(1)}, u32[]{:S(2)}, u32[]{:S(2)}) collective-permute-start(bf16[4,2,80,128]{3,2,1,0:T(8,128)(2,1)} %get-tuple-element.63), channel_id=1, source_target_pairs={{0,8},{1,9},{2,10},{3,11},{4,12},{5,13},{6,14},{7,15},{8,0},{9,1},... | collective-permute-start | bytes 491528 | tf_op jit(solution)/shard_map/ppermute | solution.py:482
  79.9 8.8 %collective-permute-start.19 = (bf16[4,2,80,128]{3,2,1,0:T(8,128)(2,1)}, bf16[4,2,80,128]{3,2,1,0:T(8,128)(2,1)S(1)}, u32[]{:S(2)}, u32[]{:S(2)}) collective-permute-start(bf16[4,2,80,128]{3,2,1,0:T(8,128)(2,1)} %get-tuple-element.64), channel_id=1, source_target_pairs={{0,9},{1,8},{2,11},{3,10},{4,13},{5,12},{6,15},{7,14},{8,1},{9,0},... | collective-permute-start | bytes 491528 | tf_op jit(solution)/shard_map/ppermute | solution.py:482
  85.1 16.1 %collective-permute-start.35 = (bf16[15,2,64,128]{3,2,1,0:T(8,128)(2,1)S(1)}, bf16[15,2,64,128]{3,2,1,0:T(8,128)(2,1)S(1)}, u32[]{:S(2)}, u32[]{:S(2)}) collective-permute-start(bf16[15,2,64,128]{3,2,1,0:T(8,128)(2,1)S(1)} %correlate.11), channel_id=1, source_target_pairs={{0,2},{1,3},{2,6},{3,7},{4,0},{5,1},{6,4},{7,5},{8,10},{9,11},{10,... | collective-permute-start | bytes 1474568 | tf_op jit(solution)/shard_map/ppermute | solution.py:482
  89.4 21.4 %copy-start.4 = (bf16[4,2,80,128]{3,2,1,0:T(8,128)(2,1)S(1)}, bf16[4,2,80,128]{3,2,1,0:T(8,128)(2,1)}, u32[]{:S(2)}) copy-start(bf16[4,2,80,128]{3,2,1,0:T(8,128)(2,1)} %get-tuple-element.57.refs_0_) | copy-start | bytes 491524
  89.4 21.4 %collective-permute-start.20 = (bf16[15,2,64,128]{3,2,1,0:T(8,128)(2,1)S(1)}, bf16[15,2,64,128]{3,2,1,0:T(8,128)(2,1)S(1)}, u32[]{:S(2)}, u32[]{:S(2)}) collective-permute-start(bf16[15,2,64,128]{3,2,1,0:T(8,128)(2,1)S(1)} %correlate.8), channel_id=1, source_target_pairs={{0,2},{1,3},{2,6},{3,7},{4,0},{5,1},{6,4},{7,5},{8,10},{9,11},{10,... | collective-permute-start | bytes 1474568 | tf_op jit(solution)/shard_map/ppermute | solution.py:482
  90.9 7.1 %collective-permute-start.29 = (bf16[4,2,80,128]{3,2,1,0:T(8,128)(2,1)S(1)}, bf16[4,2,80,128]{3,2,1,0:T(8,128)(2,1)S(1)}, u32[]{:S(2)}, u32[]{:S(2)}) collective-permute-start(bf16[4,2,80,128]{3,2,1,0:T(8,128)(2,1)S(1)} %copy-done.32), channel_id=1, source_target_pairs={{0,1},{1,0},{2,3},{3,2},{4,5},{5,4},{6,7},{7,6},{8,9},{9,8},{10,11... | collective-permute-start | bytes 491528 | tf_op jit(solution)/shard_map/ppermute | solution.py:482
  91.5 6.5 %collective-permute-start.30 = (bf16[4,2,80,128]{3,2,1,0:T(8,128)(2,1)S(1)}, bf16[4,2,80,128]{3,2,1,0:T(8,128)(2,1)S(1)}, u32[]{:S(2)}, u32[]{:S(2)}) collective-permute-start(bf16[4,2,80,128]{3,2,1,0:T(8,128)(2,1)S(1)} %copy-done.31), channel_id=1, source_target_pairs={{0,8},{1,9},{2,10},{3,11},{4,12},{5,13},{6,14},{7,15},{8,0},{9,1},... | collective-permute-start | bytes 491528 | tf_op jit(solution)/shard_map/ppermute | solution.py:482
  92.8 8.2 %collective-permute-start.31 = (bf16[4,2,80,128]{3,2,1,0:T(8,128)(2,1)S(1)}, bf16[4,2,80,128]{3,2,1,0:T(8,128)(2,1)S(1)}, u32[]{:S(2)}, u32[]{:S(2)}) collective-permute-start(bf16[4,2,80,128]{3,2,1,0:T(8,128)(2,1)S(1)} %copy-done.30), channel_id=1, source_target_pairs={{0,9},{1,8},{2,11},{3,10},{4,13},{5,12},{6,15},{7,14},{8,1},{9,0},... | collective-permute-start | bytes 491528 | tf_op jit(solution)/shard_map/ppermute | solution.py:482
  98.0 7.1 %collective-permute-start.14 = (bf16[4,2,80,128]{3,2,1,0:T(8,128)(2,1)S(1)}, bf16[4,2,80,128]{3,2,1,0:T(8,128)(2,1)S(1)}, u32[]{:S(2)}, u32[]{:S(2)}) collective-permute-start(bf16[4,2,80,128]{3,2,1,0:T(8,128)(2,1)S(1)} %copy-done.29), channel_id=1, source_target_pairs={{0,1},{1,0},{2,3},{3,2},{4,5},{5,4},{6,7},{7,6},{8,9},{9,8},{10,11... | collective-permute-start | bytes 491528 | tf_op jit(solution)/shard_map/ppermute | solution.py:482
  98.0 7.1 %collective-permute-start.15 = (bf16[4,2,80,128]{3,2,1,0:T(8,128)(2,1)S(1)}, bf16[4,2,80,128]{3,2,1,0:T(8,128)(2,1)S(1)}, u32[]{:S(2)}, u32[]{:S(2)}) collective-permute-start(bf16[4,2,80,128]{3,2,1,0:T(8,128)(2,1)S(1)} %copy-done.28), channel_id=1, source_target_pairs={{0,8},{1,9},{2,10},{3,11},{4,12},{5,13},{6,14},{7,15},{8,0},{9,1},... | collective-permute-start | bytes 491528 | tf_op jit(solution)/shard_map/ppermute | solution.py:482
  101.0 6.9 %collective-permute-start.16 = (bf16[4,2,80,128]{3,2,1,0:T(8,128)(2,1)S(1)}, bf16[4,2,80,128]{3,2,1,0:T(8,128)(2,1)S(1)}, u32[]{:S(2)}, u32[]{:S(2)}) collective-permute-start(bf16[4,2,80,128]{3,2,1,0:T(8,128)(2,1)S(1)} %copy-done.27), channel_id=1, source_target_pairs={{0,9},{1,8},{2,11},{3,10},{4,13},{5,12},{6,15},{7,14},{8,1},{9,0},... | collective-permute-start | bytes 491528 | tf_op jit(solution)/shard_map/ppermute | solution.py:482
  102.1 17.3 %copy-start.23 = (bf16[4,2,80,128]{3,2,1,0:T(8,128)(2,1)S(1)}, bf16[4,2,80,128]{3,2,1,0:T(8,128)(2,1)}, u32[]{:S(2)}) copy-start(bf16[4,2,80,128]{3,2,1,0:T(8,128)(2,1)} %get-tuple-element.54) | copy-start | bytes 491524
  102.1 17.5 %copy-start.22 = (bf16[4,2,80,128]{3,2,1,0:T(8,128)(2,1)S(1)}, bf16[4,2,80,128]{3,2,1,0:T(8,128)(2,1)}, u32[]{:S(2)}) copy-start(bf16[4,2,80,128]{3,2,1,0:T(8,128)(2,1)} %get-tuple-element.55) | copy-start | bytes 491524
  102.1 18.4 %copy-start.21 = (bf16[4,2,80,128]{3,2,1,0:T(8,128)(2,1)S(1)}, bf16[4,2,80,128]{3,2,1,0:T(8,128)(2,1)}, u32[]{:S(2)}) copy-start(bf16[4,2,80,128]{3,2,1,0:T(8,128)(2,1)} %get-tuple-element.56) | copy-start | bytes 491524
  102.1 20.6 %copy-start.3 = (bf16[4,2,80,128]{3,2,1,0:T(8,128)(2,1)S(1)}, bf16[4,2,80,128]{3,2,1,0:T(8,128)(2,1)}, u32[]{:S(2)}) copy-start(bf16[4,2,80,128]{3,2,1,0:T(8,128)(2,1)} %get-tuple-element.69.refs_0_) | copy-start | bytes 491524
  102.1 20.6 %collective-permute-start.36 = (bf16[15,2,64,128]{3,2,1,0:T(8,128)(2,1)S(1)}, bf16[15,2,64,128]{3,2,1,0:T(8,128)(2,1)S(1)}, u32[]{:S(2)}, u32[]{:S(2)}) collective-permute-start(bf16[15,2,64,128]{3,2,1,0:T(8,128)(2,1)S(1)} %correlate.12), channel_id=1, source_target_pairs={{0,2},{1,3},{2,6},{3,7},{4,0},{5,1},{6,4},{7,5},{8,10},{9,11},{10,... | collective-permute-start | bytes 1474568 | tf_op jit(solution)/shard_map/ppermute | solution.py:482
  111.5 20.3 %copy-start.2 = (bf16[4,2,80,128]{3,2,1,0:T(8,128)(2,1)S(1)}, bf16[4,2,80,128]{3,2,1,0:T(8,128)(2,1)}, u32[]{:S(2)}) copy-start(bf16[4,2,80,128]{3,2,1,0:T(8,128)(2,1)} %get-tuple-element.53.refs_0_) | copy-start | bytes 491524
  111.5 20.3 %collective-permute-start.21 = (bf16[15,2,64,128]{3,2,1,0:T(8,128)(2,1)S(1)}, bf16[15,2,64,128]{3,2,1,0:T(8,128)(2,1)S(1)}, u32[]{:S(2)}, u32[]{:S(2)}) collective-permute-start(bf16[15,2,64,128]{3,2,1,0:T(8,128)(2,1)S(1)} %correlate.9), channel_id=1, source_target_pairs={{0,2},{1,3},{2,6},{3,7},{4,0},{5,1},{6,4},{7,5},{8,10},{9,11},{10,... | collective-permute-start | bytes 1474568 | tf_op jit(solution)/shard_map/ppermute | solution.py:482
  112.3 7.1 %collective-permute-start.26 = (bf16[4,2,80,128]{3,2,1,0:T(8,128)(2,1)S(1)}, bf16[4,2,80,128]{3,2,1,0:T(8,128)(2,1)S(1)}, u32[]{:S(2)}, u32[]{:S(2)}) collective-permute-start(bf16[4,2,80,128]{3,2,1,0:T(8,128)(2,1)S(1)} %copy-done.26), channel_id=1, source_target_pairs={{0,1},{1,0},{2,3},{3,2},{4,5},{5,4},{6,7},{7,6},{8,9},{9,8},{10,11... | collective-permute-start | bytes 491528 | tf_op jit(solution)/shard_map/ppermute | solution.py:482
  112.6 7.0 %collective-permute-start.27 = (bf16[4,2,80,128]{3,2,1,0:T(8,128)(2,1)S(1)}, bf16[4,2,80,128]{3,2,1,0:T(8,128)(2,1)S(1)}, u32[]{:S(2)}, u32[]{:S(2)}) collective-permute-start(bf16[4,2,80,128]{3,2,1,0:T(8,128)(2,1)S(1)} %copy-done.25), channel_id=1, source_target_pairs={{0,8},{1,9},{2,10},{3,11},{4,12},{5,13},{6,14},{7,15},{8,0},{9,1},... | collective-permute-start | bytes 491528 | tf_op jit(solution)/shard_map/ppermute | solution.py:482
  113.4 7.1 %collective-permute-start.28 = (bf16[4,2,80,128]{3,2,1,0:T(8,128)(2,1)S(1)}, bf16[4,2,80,128]{3,2,1,0:T(8,128)(2,1)S(1)}, u32[]{:S(2)}, u32[]{:S(2)}) collective-permute-start(bf16[4,2,80,128]{3,2,1,0:T(8,128)(2,1)S(1)} %copy-done.24), channel_id=1, source_target_pairs={{0,9},{1,8},{2,11},{3,10},{4,13},{5,12},{6,15},{7,14},{8,1},{9,0},... | collective-permute-start | bytes 491528 | tf_op jit(solution)/shard_map/ppermute | solution.py:482
  119.4 7.1 %collective-permute-start.11 = (bf16[4,2,80,128]{3,2,1,0:T(8,128)(2,1)S(1)}, bf16[4,2,80,128]{3,2,1,0:T(8,128)(2,1)S(1)}, u32[]{:S(2)}, u32[]{:S(2)}) collective-permute-start(bf16[4,2,80,128]{3,2,1,0:T(8,128)(2,1)S(1)} %copy-done.23), channel_id=1, source_target_pairs={{0,1},{1,0},{2,3},{3,2},{4,5},{5,4},{6,7},{7,6},{8,9},{9,8},{10,11... | collective-permute-start | bytes 491528 | tf_op jit(solution)/shard_map/ppermute | solution.py:482
  119.6 7.0 %collective-permute-start.12 = (bf16[4,2,80,128]{3,2,1,0:T(8,128)(2,1)S(1)}, bf16[4,2,80,128]{3,2,1,0:T(8,128)(2,1)S(1)}, u32[]{:S(2)}, u32[]{:S(2)}) collective-permute-start(bf16[4,2,80,128]{3,2,1,0:T(8,128)(2,1)S(1)} %copy-done.22), channel_id=1, source_target_pairs={{0,8},{1,9},{2,10},{3,11},{4,12},{5,13},{6,14},{7,15},{8,0},{9,1},... | collective-permute-start | bytes 491528 | tf_op jit(solution)/shard_map/ppermute | solution.py:482
  120.5 7.2 %collective-permute-start.13 = (bf16[4,2,80,128]{3,2,1,0:T(8,128)(2,1)S(1)}, bf16[4,2,80,128]{3,2,1,0:T(8,128)(2,1)S(1)}, u32[]{:S(2)}, u32[]{:S(2)}) collective-permute-start(bf16[4,2,80,128]{3,2,1,0:T(8,128)(2,1)S(1)} %copy-done.21), channel_id=1, source_target_pairs={{0,9},{1,8},{2,11},{3,10},{4,13},{5,12},{6,15},{7,14},{8,1},{9,0},... | collective-permute-start | bytes 491528 | tf_op jit(solution)/shard_map/ppermute | solution.py:482
  123.6 17.5 %copy-start.16 = (bf16[4,2,80,128]{3,2,1,0:T(8,128)(2,1)S(1)}, bf16[4,2,80,128]{3,2,1,0:T(8,128)(2,1)}, u32[]{:S(2)}) copy-start(bf16[4,2,80,128]{3,2,1,0:T(8,128)(2,1)} %get-tuple-element.51) | copy-start | bytes 491524
  123.6 18.5 %copy-start.15 = (bf16[4,2,80,128]{3,2,1,0:T(8,128)(2,1)S(1)}, bf16[4,2,80,128]{3,2,1,0:T(8,128)(2,1)}, u32[]{:S(2)}) copy-start(bf16[4,2,80,128]{3,2,1,0:T(8,128)(2,1)} %get-tuple-element.52) | copy-start | bytes 491524
  123.6 20.7 %copy-start.1 = (bf16[4,2,80,128]{3,2,1,0:T(8,128)(2,1)S(1)}, bf16[4,2,80,128]{3,2,1,0:T(8,128)(2,1)}, u32[]{:S(2)}) copy-start(bf16[4,2,80,128]{3,2,1,0:T(8,128)(2,1)} %get-tuple-element.65.refs_0_) | copy-start | bytes 491524
  123.6 20.7 %collective-permute-start.37 = (bf16[15,2,64,128]{3,2,1,0:T(8,128)(2,1)S(1)}, bf16[15,2,64,128]{3,2,1,0:T(8,128)(2,1)S(1)}, u32[]{:S(2)}, u32[]{:S(2)}) collective-permute-start(bf16[15,2,64,128]{3,2,1,0:T(8,128)(2,1)S(1)} %correlate.13), channel_id=1, source_target_pairs={{0,2},{1,3},{2,6},{3,7},{4,0},{5,1},{6,4},{7,5},{8,10},{9,11},{10,... | collective-permute-start | bytes 1474568 | tf_op jit(solution)/shard_map/ppermute | solution.py:482
  132.6 18.9 %copy-start = (bf16[4,2,80,128]{3,2,1,0:T(8,128)(2,1)S(1)}, bf16[4,2,80,128]{3,2,1,0:T(8,128)(2,1)}, u32[]{:S(2)}) copy-start(bf16[4,2,80,128]{3,2,1,0:T(8,128)(2,1)} %get-tuple-element.49.refs_0_) | copy-start | bytes 491524
  132.6 18.9 %collective-permute-start.22 = (bf16[15,2,64,128]{3,2,1,0:T(8,128)(2,1)S(1)}, bf16[15,2,64,128]{3,2,1,0:T(8,128)(2,1)S(1)}, u32[]{:S(2)}, u32[]{:S(2)}) collective-permute-start(bf16[15,2,64,128]{3,2,1,0:T(8,128)(2,1)S(1)} %correlate.10), channel_id=1, source_target_pairs={{0,2},{1,3},{2,6},{3,7},{4,0},{5,1},{6,4},{7,5},{8,10},{9,11},{10,... | collective-permute-start | bytes 1474568 | tf_op jit(solution)/shard_map/ppermute | solution.py:482
  133.3 7.1 %collective-permute-start.23 = (bf16[4,2,80,128]{3,2,1,0:T(8,128)(2,1)S(1)}, bf16[4,2,80,128]{3,2,1,0:T(8,128)(2,1)S(1)}, u32[]{:S(2)}, u32[]{:S(2)}) collective-permute-start(bf16[4,2,80,128]{3,2,1,0:T(8,128)(2,1)S(1)} %copy-done.20), channel_id=1, source_target_pairs={{0,1},{1,0},{2,3},{3,2},{4,5},{5,4},{6,7},{7,6},{8,9},{9,8},{10,11... | collective-permute-start | bytes 491528 | tf_op jit(solution)/shard_map/ppermute | solution.py:482
  134.0 7.1 %collective-permute-start.24 = (bf16[4,2,80,128]{3,2,1,0:T(8,128)(2,1)S(1)}, bf16[4,2,80,128]{3,2,1,0:T(8,128)(2,1)S(1)}, u32[]{:S(2)}, u32[]{:S(2)}) collective-permute-start(bf16[4,2,80,128]{3,2,1,0:T(8,128)(2,1)S(1)} %copy-done.19), channel_id=1, source_target_pairs={{0,8},{1,9},{2,10},{3,11},{4,12},{5,13},{6,14},{7,15},{8,0},{9,1},... | collective-permute-start | bytes 491528 | tf_op jit(solution)/shard_map/ppermute | solution.py:482
  134.5 7.6 %collective-permute-start.25 = (bf16[4,2,80,128]{3,2,1,0:T(8,128)(2,1)S(1)}, bf16[4,2,80,128]{3,2,1,0:T(8,128)(2,1)S(1)}, u32[]{:S(2)}, u32[]{:S(2)}) collective-permute-start(bf16[4,2,80,128]{3,2,1,0:T(8,128)(2,1)S(1)} %copy-done.18), channel_id=1, source_target_pairs={{0,9},{1,8},{2,11},{3,10},{4,13},{5,12},{6,15},{7,14},{8,1},{9,0},... | collective-permute-start | bytes 491528 | tf_op jit(solution)/shard_map/ppermute | solution.py:482
  140.5 6.2 %collective-permute-start.8 = (bf16[4,2,80,128]{3,2,1,0:T(8,128)(2,1)S(1)}, bf16[4,2,80,128]{3,2,1,0:T(8,128)(2,1)S(1)}, u32[]{:S(2)}, u32[]{:S(2)}) collective-permute-start(bf16[4,2,80,128]{3,2,1,0:T(8,128)(2,1)S(1)} %copy-done.17), channel_id=1, source_target_pairs={{0,1},{1,0},{2,3},{3,2},{4,5},{5,4},{6,7},{7,6},{8,9},{9,8},{10,11... | collective-permute-start | bytes 491528 | tf_op jit(solution)/shard_map/ppermute | solution.py:482
  141.0 5.6 %collective-permute-start.9 = (bf16[4,2,80,128]{3,2,1,0:T(8,128)(2,1)S(1)}, bf16[4,2,80,128]{3,2,1,0:T(8,128)(2,1)S(1)}, u32[]{:S(2)}, u32[]{:S(2)}) collective-permute-start(bf16[4,2,80,128]{3,2,1,0:T(8,128)(2,1)S(1)} %copy-done.16), channel_id=1, source_target_pairs={{0,8},{1,9},{2,10},{3,11},{4,12},{5,13},{6,14},{7,15},{8,0},{9,1},... | collective-permute-start | bytes 491528 | tf_op jit(solution)/shard_map/ppermute | solution.py:482
  142.1 6.8 %collective-permute-start.10 = (bf16[4,2,80,128]{3,2,1,0:T(8,128)(2,1)S(1)}, bf16[4,2,80,128]{3,2,1,0:T(8,128)(2,1)S(1)}, u32[]{:S(2)}, u32[]{:S(2)}) collective-permute-start(bf16[4,2,80,128]{3,2,1,0:T(8,128)(2,1)S(1)} %copy-done.15), channel_id=1, source_target_pairs={{0,9},{1,8},{2,11},{3,10},{4,13},{5,12},{6,15},{7,14},{8,1},{9,0},... | collective-permute-start | bytes 491528 | tf_op jit(solution)/shard_map/ppermute | solution.py:482
  (26 other events, 220.9 us)

commit v4 on v3

v4 whole, which is shorter than its diff:
```python
import functools
import math

import jax
import jax.numpy as jnp
import ml_dtypes
import numpy as np
from jax import lax
from jax.experimental import pallas as pl
from jax.experimental.pallas import tpu as pltpu
from jax.sharding import PartitionSpec as P

LAG = 7
HALO = 8
LANES = 128
AXES = ("depth", "freq")
VMEM_BYTES = 24 * 2**20


RADIX = 4
BLOCKS_X = 2
BLOCKS_Y = 2


def residues(length):
    found = [np.arange(residue, length, RADIX) for residue in range(RADIX)]
    found[3] = found[3][::-1]
    return found


def residue_tables(length):
    position = np.arange(length, dtype=np.int64)
    product = position[:, None] * position[None, :] % length
    angles = product.astype(np.float32) * np.float32(2.0 * math.pi / length)
    factor = np.float32(1.0 / math.sqrt(length))
    cos, sin = np.cos(angles) * factor, np.sin(angles) * factor
    tables = []
    for residue in residues(length):
        c, s = (t[residue, : length // RADIX] for t in (cos, sin))
        tables.append(np.block([[c, s], [-s, c]]).astype(ml_dtypes.bfloat16))
    return np.stack(tables)


def wavenumbers_squared(length):
    position = np.arange(length)
    signed = np.where(position < length // 2, position, position - length)
    wave = signed.astype(np.float32) * np.float32(2.0 * math.pi / length)
    squared = wave * wave
    return np.concatenate([squared[residue] for residue in residues(length)[:3]])


def mix_forward(re, im):
    sum_re, dif_re = re[0] + re[2], re[0] - re[2]
    sum_im, dif_im = im[0] + im[2], im[0] - im[2]
    odd_re, gap_re = re[1] + re[3], re[1] - re[3]
    odd_im, gap_im = im[1] + im[3], im[1] - im[3]
    return (
        (sum_re + odd_re, sum_im + odd_im),
        (dif_re + gap_im, dif_im - gap_re),
        (sum_re - odd_re, sum_im - odd_im),
        (dif_re - gap_im, dif_im + gap_re),
    )


def mix_inverse(re, im):
    found = mix_forward(re, im)
    return found[0], found[3], found[2], found[1]


Q_MAX = 14.0


def fit(function, degree):
    cheb = np.polynomial.chebyshev.Chebyshev.interpolate(
        lambda t: function((t + 1.0) * Q_MAX / 2), degree
    )
    return [float(v) for v in np.polynomial.chebyshev.cheb2poly(cheb.coef)]


COS_FIT = fit(lambda q: np.cos(np.sqrt(q)), 7)
SINC_FIT = fit(lambda q: np.sinc(np.sqrt(q) / np.pi), 7)


def horner(coefficients, t):
    total = jnp.full_like(t, coefficients[-1])
    for value in coefficients[-2::-1]:
        total = total * t + value
    return total


def cos_sin(square, root):
    t = square * (2.0 / Q_MAX) - 1.0
    return horner(COS_FIT, t), horner(SINC_FIT, t) * root


def lookup(table_row, codes):
    rows = codes.shape[0]
    parts = []
    for tile in range(codes.shape[1] // LANES):
        index = codes[:, tile * LANES : (tile + 1) * LANES]
        source = jnp.broadcast_to(table_row, (rows, LANES))
        parts.append(jnp.take_along_axis(source, index, axis=1, mode="promise_in_bounds"))
    return parts


def chain_kernel(
    place, angular_ref, *refs, top, planes, begin, lead, closing, strips, width, tiles, groups, shots
):
    refs = list(refs)

    def take(count):
        return [refs.pop(0) for _ in range(count)]

    state = take(2 if top else 1)
    codes = [take(2) for _ in range(planes)]
    levels, left_x, right_x, left_y, right_y, wave_x, wave_y = take(7)
    phases, index, mid = refs[-3:]
    if closing:
        field, padded = refs[-5:-3]
        outs = refs[:-5]
    else:
        field = refs[0]
    rows_x, rows_y = field.shape[1], field.shape[2]
    part_x, part_y = rows_x // RADIX, rows_y // RADIX
    block_x, block_y = rows_x // BLOCKS_X, rows_y // BLOCKS_Y
    group, my_core, my_parity, spot = place[0], place[1], place[2], place[3]
    angular = angular_ref[0]
    f32, bf16 = jnp.float32, jnp.bfloat16

    if top:
        field[0:2] = state[0][my_core, 0]
        field[2:4] = state[1][my_core, 0]
    else:
        field[...] = state[0][...]

    def turned(kind, a, b, cos, sin):
        if kind == 0:
            return a * cos - b * sin, a * sin + b * cos
        return a * cos + b * sin, b * cos - a * sin

    def emit(target, parity):
        for s in range(strips):
            p = lax.rem(spot + (strips - 1 - s), strips)
            strip = jnp.where(p == 0, 0, jnp.where(p <= strips // 2, 2 * p - 1, 2 * (strips - p)))
            start = pl.multiple_of((2 * strip + parity) * width, 16)
            for g, (first, last) in enumerate(groups):
                for tile in range(first, last):
                    for part in range(4):
                        outs[(target * strips + s) * len(groups) + g][part, tile - first] = padded[
                            part, tile, pl.ds(start, width + 2 * HALO)
                        ]

    def step(t, carry):
        own = my_core == lax.rem(t + begin, shots)
        for j in range(planes):
            for flag, source in ((own, codes[j][0]), (jnp.logical_not(own), codes[j][1])):

                @pl.when((t == j) & flag)
                def _(source=source):
                    index[...] = source[...].astype(f32).astype(jnp.int32)

        def forward_x(i, total):
            cols = pl.ds(pl.multiple_of(i * block_y, block_y), block_y)
            for part in range(RADIX):
                at = index[part * part_x : (part + 1) * part_x, cols]
                value = functools.reduce(jnp.add, lookup(levels[0:1, :], at))
                total = total + jnp.sum(value.reshape(part_x // 8, 8, LANES), axis=0)
            for kind in range(2):
                re, im = (
                    [field[2 * kind + j, q * part_x : (q + 1) * part_x, cols] for q in range(RADIX)]
                    for j in range(2)
                )
                for r, mixed in enumerate(mix_forward(re, im)):
                    mixed = jnp.concatenate(mixed, axis=0)
                    out = jnp.dot(left_x[r], mixed, preferred_element_type=f32).astype(bf16)
                    mid[2 * kind : 2 * kind + 2, r * part_x : (r + 1) * part_x, cols] = (
                        out.reshape(2, part_x, block_y)
                    )
            return total

        total = lax.fori_loop(0, BLOCKS_Y, forward_x, jnp.zeros((8, LANES), f32), unroll=True)
        base = jnp.sum(total) / (rows_x * rows_y)
        angle = angular * (levels[0:1, :] - base)
        screen = cos_sin(angle * angle, angle)
        reach = angular * base
        reach = reach * reach

        def phase(i, carry):
            rows = pl.ds(pl.multiple_of(i * part_x, part_x), part_x)
            q = reach - wave_x[rows, :] - wave_y[0:1, :]
            root = jnp.sqrt(jnp.abs(q))
            cos, sin = cos_sin(q, root)
            phases[0, rows] = jnp.where(q > 0.0, cos, jnp.exp(-root))
            phases[1, rows] = jnp.where(q > 0.0, sin, 0.0)
            return carry

        lax.fori_loop(0, 3, phase, 0)

        def along_y(i, carry):
            rows = slice(i * part_x, (i + 1) * part_x)
            same = slice((1 if i == 3 else i) * part_x, (1 if i == 3 else i) * part_x + part_x)
            lanes = [slice(q * part_y, (q + 1) * part_y) for q in range(RADIX)]
            re, im = (
                [
                    jnp.concatenate([mid[j, rows, at], mid[2 + j, rows, at]], axis=0)
                    for at in lanes
                ]
                for j in range(2)
            )
            back = []
            for r, mixed in enumerate(mix_forward(re, im)):
                mixed = jnp.concatenate(mixed, axis=1)
                spectrum = jnp.dot(mixed, right_y[r], preferred_element_type=f32)
                at = lanes[1 if r == 3 else r]
                phase_re, phase_im = phases[0, same, at], phases[1, same, at]
                pieces = []
                for kind in range(2):
                    part = spectrum[kind * part_x : (kind + 1) * part_x]
                    new = turned(kind, part[:, :part_y], part[:, part_y:], phase_re, phase_im)
                    pieces.append(jnp.concatenate(new, axis=1).astype(bf16))
                shifted = jnp.concatenate(pieces, axis=0)
                back.append(jnp.dot(shifted, left_y[r], preferred_element_type=f32))
            back_re = [value[:, :part_y] for value in back]
            back_im = [value[:, part_y:] for value in back]
            for at, mixed in zip(lanes, mix_inverse(back_re, back_im)):
                for j in range(2):
                    value = mixed[j].astype(bf16)
                    for kind in range(2):
                        mid[2 * kind + j, rows, at] = value[kind * part_x : (kind + 1) * part_x]
            return carry

        [along_y(i, 0) for i in range(RADIX)]

        def inverse_x(i, carry):
            cols = pl.ds(pl.multiple_of(i * block_y, block_y), block_y)
            turn = []
            for part in range(RADIX):
                at = index[part * part_x : (part + 1) * part_x, cols]
                turn.append([jnp.concatenate(lookup(table, at), axis=1) for table in screen])
            for kind in range(2):
                back = [
                    jnp.dot(
                        right_x[r],
                        mid[2 * kind : 2 * kind + 2, r * part_x : (r + 1) * part_x, cols].reshape(
                            2 * part_x, block_y
                        ),
                        preferred_element_type=f32,
                    )
                    for r in range(RADIX)
                ]
                back_re = [value[:part_x] for value in back]
                back_im = [value[part_x:] for value in back]
                done = [
                    turned(kind, a, b, *turn[part])
                    for part, (a, b) in enumerate(mix_inverse(back_re, back_im))
                ]
                for j in range(2):
                    for part in range(RADIX):
                        at = slice(part * part_x, (part + 1) * part_x)
                        field[2 * kind + j, at, cols] = done[part][j].astype(bf16)
                    if closing:
                        edge = jnp.zeros((HALO, block_y), f32)
                        whole = jnp.concatenate([edge, *(d[j] for d in done), edge], axis=0)
                        whole = whole.astype(bf16)
                        for k in range(block_y // LANES):
                            padded[2 * kind + j, i * (block_y // LANES) + k] = whole[
                                :, k * LANES : (k + 1) * LANES
                            ]
            return carry

        lax.fori_loop(0, BLOCKS_Y, inverse_x, 0, unroll=True)
        if not closing:
            return carry

        @pl.when((t >= lead) & own)
        def _():
            emit(0, my_parity)
            emit(1, 1 - my_parity)

        @pl.when((t >= lead) & jnp.logical_not(own))
        def _():
            emit(2, my_parity)
            emit(3, 1 - my_parity)

        return carry

    lax.fori_loop(jnp.where(group == 0, lead, 0), planes, step, 0)


def correlate_kernel(*refs, width, tiles, partial, scale):
    fields, refs = refs[:4], refs[4:]
    received = None
    if partial:
        received, refs = refs[0], refs[1:]
    out, wide = refs[-2], refs[-1]
    for tile in range(tiles):
        lanes = slice(tile * LANES, (tile + 1) * LANES)
        for m in range(4):
            for part in range(4):
                wide[m * 4 + part] = fields[m][part, tile].astype(jnp.float32)
        for lag in range(2 * LAG + 1):
            shift = lag - LAG
            total = None
            for m in range(4):
                for part in range(2):
                    term = (
                        wide[m * 4 + part, HALO - shift : HALO - shift + width]
                        * wide[m * 4 + 2 + part, HALO + shift : HALO + shift + width]
                    )
                    total = term if total is None else total + term
            if received is not None:
                total = total + received[lag, tile].astype(jnp.float32)
            if scale is not None:
                out[0, lag, :, lanes] = total * scale
            else:
                out[lag, tile] = total.astype(out.dtype)


def window_kernel(place, anchors, mine, other, out_mine, out_other):
    del place, anchors
    out_mine[...] = mine[0].astype(jnp.float32).astype(out_mine.dtype)
    out_other[...] = other[0].astype(jnp.float32).astype(out_other.dtype)


def pinned(x):
    return pltpu.with_memory_space_constraint(x, pltpu.VMEM)


def chain(
    place, angular, table, *, tops=None, state=None, codes, begin, lead, closing, strips, width, groups, shots
):
    rows_x, rows_y = (tops[0] if tops else state).shape[-2:]
    tiles = rows_y // LANES
    bf16, f32 = jnp.bfloat16, jnp.float32
    tables_x, tables_y = residue_tables(rows_x), residue_tables(rows_y)
    left_x, right_x = jnp.asarray(tables_x), jnp.asarray(np.swapaxes(tables_x, 1, 2))
    left_y, right_y = (left_x, right_x) if rows_x == rows_y else (
        jnp.asarray(tables_y), jnp.asarray(np.swapaxes(tables_y, 1, 2))
    )
    wave_x = wavenumbers_squared(rows_x)[:, None]
    wave_y = wavenumbers_squared(rows_y)[None]
    height = width + 2 * HALO
    vmem = pl.BlockSpec(memory_space=pltpu.VMEM)
    operands = list(tops) if tops else [state]
    in_specs = []
    for pair in codes:
        operands += list(pair)
    operands += [
        jnp.pad(table, (0, LANES - table.shape[0]))[None],
        left_x, right_x, left_y, right_y, jnp.asarray(wave_x), jnp.asarray(wave_y),
    ]
    in_specs += [vmem] * (len(operands) - len(in_specs))
    whole = (4, rows_x, rows_y)
    scratch = [
        pltpu.VMEM((2, 3 * rows_x // RADIX, 3 * rows_y // RADIX), f32),
        pltpu.VMEM((rows_x, rows_y), jnp.int32),
        pltpu.VMEM(whole, bf16),
    ]
    if closing:
        out_shape = [
            pltpu.VMEM((4, last - first, height, LANES), bf16)
            for _ in range(4 * strips)
            for first, last in groups
        ]
        scratch = [
            pltpu.VMEM(whole, bf16),
            pltpu.VMEM((4, tiles, rows_x + 2 * HALO, LANES), bf16),
        ] + scratch
    else:
        out_shape = [pltpu.VMEM(whole, bf16)]
    return pl.pallas_call(
        functools.partial(
            chain_kernel, top=bool(tops), planes=len(codes), begin=begin, lead=lead, closing=closing,
            strips=strips, width=width, tiles=tiles, groups=groups, shots=shots,
        ),
        out_shape=out_shape,
        grid_spec=pltpu.PrefetchScalarGridSpec(
            num_scalar_prefetch=2,
            grid=(1,),
            in_specs=in_specs,
            out_specs=[vmem] * len(out_shape),
            scratch_shapes=scratch,
        ),
        compiler_params=pltpu.CompilerParams(vmem_limit_bytes=VMEM_BYTES),
        cost_estimate=pl.CostEstimate(
            flops=9 * 10**9 * len(codes), bytes_accessed=10**7, transcendentals=0
        ),
        name="chain",
    )(place, angular, *(pinned(x) for x in operands))


def windows(place, anchors, slowness_codes, rows_x, rows_y):
    steps = 4
    rows = rows_x // steps

    def block(flip):
        def index(i, place, anchors):
            shot = jnp.abs(place[1] - flip)
            return (0, anchors[shot, 0] // rows + i, anchors[shot, 1] // rows_y)

        return pl.BlockSpec((1, rows, rows_y), index)

    code_spec = pl.BlockSpec((rows, rows_y), lambda i, place, anchors: (i, 0))
    return pl.pallas_call(
        window_kernel,
        out_shape=[pltpu.VMEM((rows_x, rows_y), jnp.bfloat16)] * 2,
        grid_spec=pltpu.PrefetchScalarGridSpec(
            num_scalar_prefetch=2,
            grid=(steps,),
            in_specs=[block(0), block(1)],
            out_specs=[code_spec, code_spec],
        ),
        name="windows",
    )(place, anchors, slowness_codes, slowness_codes)


def shards(source_top, receiver_top, slowness_codes, slowness_table, anchors):
    shots, _, _, rows_x, rows_y = source_top.shape
    freq_count = lax.axis_size("freq")
    depth_count = lax.axis_size("depth")
    strips = freq_count // 2
    width = rows_x // freq_count
    lags = 2 * LAG + 1
    tiles = rows_y // LANES
    groups = [(0, tiles // 2), (tiles // 2, tiles)]
    factor = 1.0 / math.sqrt(2.0 * shots * freq_count)
    depth_index = lax.axis_index("depth")
    freq_index = lax.axis_index("freq")
    my_core = depth_index % shots
    group = depth_index // shots
    bf16, f32 = jnp.bfloat16, jnp.float32

    def number(group_at, core_at, strip_at, parity_at):
        return (group_at * shots + core_at) * freq_count + strip_at * 2 + parity_at

    def pairs(move):
        found = []
        for g in range(depth_count // shots):
            for c in range(shots):
                for z in range(strips):
                    for x in range(2):
                        to = move(g, c, z, x)
                        if to is not None:
                            found.append((number(g, c, z, x), number(*to)))
        return found

    def send(value, move):
        return lax.ppermute(value, AXES, pairs(move))

    def to_core(g, c, z, x):
        return (g, 1 - c, z, x)

    def to_same(g, c, z, x):
        return (g, c, z, 1 - x)

    def to_cross(g, c, z, x):
        return (g, 1 - c, z, 1 - x)

    def up(core):
        return lambda g, c, z, x: (1, c, z, x) if g == 0 and c == core else None

    ring = [0] + list(range(1, strips, 2)) + list(range(2, strips, 2))[::-1]
    spots = {z: p for p, z in enumerate(ring)}

    def onward(g, c, z, x):
        return (g, c, ring[(spots[z] + 1) % strips], x)

    my_strip = freq_index // 2
    spot = jnp.where(
        my_strip == 0,
        0,
        jnp.where(my_strip % 2 == 1, (my_strip + 1) // 2, strips - my_strip // 2),
    )
    place = jnp.stack([group, my_core, freq_index % 2, spot]).astype(jnp.int32)

    mine, other = windows(place, anchors, slowness_codes, rows_x, rows_y)
    from_core = send(other, to_core)
    near = (mine, from_core)
    far = [(send(mine, up(0)), send(from_core, up(1)))]
    mine_later, from_core_later = lax.optimization_barrier((mine, from_core))
    far.append((send(mine_later, up(1)), send(from_core_later, up(0))))

    angular = (math.pi * (0.45 + 0.5 * (freq_index.astype(f32) + 0.5) / freq_count))[None]
    common = dict(strips=strips, width=width, groups=groups, shots=shots)
    (state,) = chain(
        place, angular, slowness_table, tops=(source_top, receiver_top), codes=far[:1], begin=0, lead=1,
        closing=False, **common,
    )
    outs = chain(
        place, angular, slowness_table, state=state, codes=far[1:] + [near] * shots, begin=1, lead=shots - 1,

        closing=True, **common,
    )
    height = width + 2 * HALO

    def correlate(fields, received, last, buffer, g):
        first, end = groups[g]
        count = end - first
        operands = [pinned(x) for x in fields]
        field_spec = image_spec = pl.BlockSpec(memory_space=pltpu.VMEM)
        in_specs = [field_spec] * 4
        if received is not None:
            in_specs.append(image_spec)
            operands.append(pinned(received))
        aliases = {}
        if last:
            out_shape = jax.ShapeDtypeStruct((1, lags, width, rows_y), f32)
            out_spec = pl.BlockSpec(
                (1, lags, width, count * LANES), lambda i: (0, 0, 0, first // count)
            )
            if buffer is not None:
                in_specs.append(pl.BlockSpec(memory_space=pl.ANY))
                aliases = {len(operands): 0}
                operands.append(buffer)
        else:
            out_shape = pltpu.VMEM((lags, count, width, LANES), bf16)
            out_spec = image_spec
        return pl.pallas_call(
            functools.partial(
                correlate_kernel,
                width=width,
                tiles=count,
                partial=received is not None,
                scale=factor if last else None,
            ),
            out_shape=out_shape,
            grid=(1,),
            in_specs=in_specs,
            out_specs=out_spec,
            scratch_shapes=[pltpu.VMEM((16, height, LANES), f32)],
            input_output_aliases=aliases,
            compiler_params=pltpu.CompilerParams(vmem_limit_bytes=16 * 2**20),
            cost_estimate=pl.CostEstimate(flops=10**9, bytes_accessed=6 * 10**6, transcendentals=0),
            name="correlate",
        )(*operands)

    def fetch(step, g):
        own, same, core, cross = (outs[(i * strips + step) * len(groups) + g] for i in range(4))
        return own, send(same, to_same), send(core, to_core), send(cross, to_cross)

    image = None
    received = [None] * len(groups)
    for step in range(strips):
        for g in range(len(groups)):
            last = step == strips - 1
            result = correlate(fetch(step, g), received[g], last, image, g)
            if last:
                image = result
            else:
                received[g] = send(result, onward)
    return image


def solution(mesh):
    return jax.shard_map(
        shards,
        mesh=mesh,
        in_specs=(
            P(None, "freq", None, None, None),
            P(None, "freq", None, None, None),
            P("depth", None, None),
            P(),
            P(),
        ),
        out_specs=P("depth", None, "freq", None),
        check_vma=False,
    )
```

time: 154 us -> 131 us (0.85)
  Pallas kernels: 67.6 us -> 37.9 us
  starting transfers between devices: 33.8 us -> 39.4 us
  waiting for transfers between devices: 45.5 us -> 48 us
    pallas_call x4 -> x3, Pallas kernels: 59.4 us -> 29.8 us  [the longest x2 26.4 us: chain(): pl.pallas_call(functools.partial(chain_kernel, top=bool(tops), planes=len...]
    ppermute x38 -> x35, starting transfers between devices: 33.8 us -> 39.4 us  [send(): return lax.ppermute(value, AXES, pairs(move))]
    ppermute x38 -> x35, waiting for transfers between devices: 45.5 us -> 48 us  [send(): return lax.ppermute(value, AXES, pairs(move))]
    unnamed x72 -> x22, local copies, waits for them, and re-layouts: 4.74 us -> 4.49 us
  transfers between devices with their start and end apart: 38 -> 35, of which waited for: 19 -> 19; matrix products, arithmetic and copies ran while one was open for 0% -> 0% of each run, Pallas kernels for 22% -> 11%
where the time goes in v4:
time: 131 us
  waiting for transfers between devices  48 us (37%)
  starting transfers between devices  39.4 us (30%)
  Pallas kernels  37.9 us (29%)
  local copies, waits for them, and re-layouts  4.49 us (3%)
    ppermute x35, waiting for transfers between devices, send(): return lax.ppermute(value, AXES, pairs(move))  48 us
    ppermute x35, starting transfers between devices, send(): return lax.ppermute(value, AXES, pairs(move))  39.4 us
    pallas_call x2, Pallas kernels, chain(): pl.pallas_call(functools.partial(chain_kernel, top=bool(tops), planes=len...  26.4 us
    pallas_call x8, Pallas kernels, correlate(): pl.pallas_call(functools.partial(correlate_kernel, width=width, tiles=cou...  8.15 us
    unnamed x22, local copies, waits for them, and re-layouts  4.49 us
    pallas_call x1, Pallas kernels, windows(): pl.pallas_call(window_kernel, out_shape=[pltpu.VMEM((rows_x, rows_y), jnp...  3.37 us
  transfers between devices with their start and end apart: 35, of which 19 were waited for; matrix products, arithmetic and copies ran while one was open for 0% of the time, Pallas kernels for 11%

profile of v4, /device:TPU:4, one launch (start us, length us, event | category | flops | bytes accessed | tf_op | source)
XLA Modules:
  0.0 130.6 jit_solution(6150832076807843308)
XLA Ops:
  0.6 3.4 %windows.1 = (bf16[512,512]{1,0:T(8,128)(2,1)S(1)}, bf16[512,512]{1,0:T(8,128)(2,1)S(1)}) custom-call(s32[4]{0:T(128)} %pad_add_fusion.place, s32[2,2]{1,0:T(2,128)} %anchors.1, s32[1,1024,1024]{2,1,0:T(8,128)} %other.1, s32[1,1024,1024]{2,1,0:T(8,128)} %other.1), custom_call_target="tpu_custom_call" | custom-call | tf_op jit(solution)/shard_map/windows/pallas_call | solution.py:404
  4.0 0.8 copy-done.3
  4.8 1.3 collective-permute-start
  6.1 0.8 collective-permute-done.1.refs_4_.refs_6_
  6.9 1.5 %collective-permute-start.2 = (bf16[512,512]{1,0:T(8,128)(2,1)S(1)}, bf16[512,512]{1,0:T(8,128)(2,1)}, u32[]{:S(2)}, u32[]{:S(2)}) collective-permute-start(bf16[512,512]{1,0:T(8,128)(2,1)S(1)} %collective-permute-done.1.refs_4_.refs_6_), channel_id=1, source_target_pairs={{8,24},{9,25},{10,26},{11,27},{12,28},{13,29},{14,30},{15,31}} | collective-permute-start | bytes 1572872 | tf_op jit(solution)/shard_map/ppermute | solution.py:448
  9.1 1.3 collective-permute-start.4
  10.4 9.9 %collective-permute-done.refs_2_ = bf16[512,512]{1,0:T(8,128)(2,1)} collective-permute-done((bf16[512,512]{1,0:T(8,128)(2,1)S(1)}, bf16[512,512]{1,0:T(8,128)(2,1)}, u32[]{:S(2)}, u32[]{:S(2)}) %collective-permute-start) | collective-permute-done | bytes 524320 | tf_op jit(solution)/shard_map/ppermute | solution.py:448
  20.3 1.6 %copy-done.2 = bf16[2,1,2,512,512]{4,3,2,1,0:T(8,128)(2,1)S(1)} copy-done((bf16[2,1,2,512,512]{4,3,2,1,0:T(8,128)(2,1)S(1)}, bf16[2,1,2,512,512]{4,3,2,1,0:T(8,128)(2,1)}, u32[]{:S(2)}) %copy-start.2) | copy-done | bytes 2097176
  21.9 1.0 copy-done.4
  22.9 1.0 copy-done.6
  24.0 7.4 %chain.2.refs_0_ = bf16[4,512,512]{2,1,0:T(8,128)(2,1)S(1)} custom-call(s32[4]{0:T(128)S(1)} %copy-done, f32[1]{0:T(128)} %bitcast.4.angular_ref, bf16[2,1,2,512,512]{4,3,2,1,0:T(8,128)(2,1)S(1)} %copy-done.1, bf16[2,1,2,512,512]{4,3,2,1,0:T(8,128)(2,1)S(1)} %copy-done.2, bf16[512,512]{1,0:T(8,128)(2,1)} %collective-permute-done.refs_2_, ...), custom_call_target="tpu_custom_call" | custom-call | flops 8999999488 | bytes 10000000 | tf_op jit(solution)/shard_map/chain/pallas_call | solution.py:371
  31.4 19.0 %chain.3 = (bf16[4,2,80,128]{3,2,1,0:T(8,128)(2,1)S(1)}, bf16[4,2,80,128]{3,2,1,0:T(8,128)(2,1)S(1)}, bf16[4,2,80,128]{3,2,1,0:T(8,128)(2,1)S(1)}, bf16[4,2,80,1...) custom-call(s32[4]{0:T(128)S(1)} %copy-done, ...), custom_call_target="tpu_custom_call" | custom-call | flops 27000000512 | bytes 10000000 | tf_op jit(solution)/shard_map/chain/pallas_call | solution.py:371
  50.4 1.6 %collective-permute-start.29 = (bf16[4,2,80,128]{3,2,1,0:T(8,128)(2,1)S(1)}, bf16[4,2,80,128]{3,2,1,0:T(8,128)(2,1)S(1)}, u32[]{:S(2)}, u32[]{:S(2)}) collective-permute-start(bf16[4,2,80,128]{3,2,1,0:T(8,128)(2,1)S(1)} %get-tuple-element.74), channel_id=1, source_target_pairs={{0,1},{1,0},{2,3},{3,2},{4,5},{5,4},{6,7},{7,6},{8,9},{9,8},{10,11... | collective-permute-start | bytes 491528 | tf_op jit(solution)/shard_map/ppermute | solution.py:448
  52.0 2.4 %collective-permute-start.30 = (bf16[4,2,80,128]{3,2,1,0:T(8,128)(2,1)S(1)}, bf16[4,2,80,128]{3,2,1,0:T(8,128)(2,1)S(1)}, u32[]{:S(2)}, u32[]{:S(2)}) collective-permute-start(bf16[4,2,80,128]{3,2,1,0:T(8,128)(2,1)S(1)} %get-tuple-element.75), channel_id=1, source_target_pairs={{0,8},{1,9},{2,10},{3,11},{4,12},{5,13},{6,14},{7,15},{8,0},{9,1},... | collective-permute-start | bytes 491528 | tf_op jit(solution)/shard_map/ppermute | solution.py:448
  54.5 1.5 %collective-permute-start.14 = (bf16[4,2,80,128]{3,2,1,0:T(8,128)(2,1)S(1)}, bf16[4,2,80,128]{3,2,1,0:T(8,128)(2,1)S(1)}, u32[]{:S(2)}, u32[]{:S(2)}) collective-permute-start(bf16[4,2,80,128]{3,2,1,0:T(8,128)(2,1)S(1)} %get-tuple-element.58), channel_id=1, source_target_pairs={{0,1},{1,0},{2,3},{3,2},{4,5},{5,4},{6,7},{7,6},{8,9},{9,8},{10,11... | collective-permute-start | bytes 491528 | tf_op jit(solution)/shard_map/ppermute | solution.py:448
  56.2 3.3 %collective-permute-start.16 = (bf16[4,2,80,128]{3,2,1,0:T(8,128)(2,1)S(1)}, bf16[4,2,80,128]{3,2,1,0:T(8,128)(2,1)S(1)}, u32[]{:S(2)}, u32[]{:S(2)}) collective-permute-start(bf16[4,2,80,128]{3,2,1,0:T(8,128)(2,1)S(1)} %get-tuple-element.60), channel_id=1, source_target_pairs={{0,9},{1,8},{2,11},{3,10},{4,13},{5,12},{6,15},{7,14},{8,1},{9,0},... | collective-permute-start | bytes 491528 | tf_op jit(solution)/shard_map/ppermute | solution.py:448
  59.6 1.5 %collective-permute-done.31.refs_3_ = bf16[4,2,80,128]{3,2,1,0:T(8,128)(2,1)S(1)} collective-permute-done((bf16[4,2,80,128]{3,2,1,0:T(8,128)(2,1)S(1)}, bf16[4,2,80,128]{3,2,1,0:T(8,128)(2,1)S(1)}, u32[]{:S(2)}, u32[]{:S(2)}) %collective-permute-start.31) | collective-permute-done | bytes 163872 | tf_op jit(solution)/shard_map/ppermute | solution.py:448
  61.8 1.6 %collective-permute-start.32 = (bf16[15,2,64,128]{3,2,1,0:T(8,128)(2,1)S(1)}, bf16[15,2,64,128]{3,2,1,0:T(8,128)(2,1)S(1)}, u32[]{:S(2)}, u32[]{:S(2)}) collective-permute-start(bf16[15,2,64,128]{3,2,1,0:T(8,128)(2,1)S(1)} %correlate.11), channel_id=1, source_target_pairs={{0,2},{1,3},{2,6},{3,7},{4,0},{5,1},{6,4},{7,5},{8,10},{9,11},{10,... | collective-permute-start | bytes 1474568 | tf_op jit(solution)/shard_map/ppermute | solution.py:448
  63.5 1.2 collective-permute-done.14.refs_1_
  64.6 3.4 %collective-permute-done.16.refs_3_ = bf16[4,2,80,128]{3,2,1,0:T(8,128)(2,1)S(1)} collective-permute-done((bf16[4,2,80,128]{3,2,1,0:T(8,128)(2,1)S(1)}, bf16[4,2,80,128]{3,2,1,0:T(8,128)(2,1)S(1)}, u32[]{:S(2)}, u32[]{:S(2)}) %collective-permute-start.16) | collective-permute-done | bytes 163872 | tf_op jit(solution)/shard_map/ppermute | solution.py:448
  68.8 1.6 %collective-permute-start.17 = (bf16[15,2,64,128]{3,2,1,0:T(8,128)(2,1)S(1)}, bf16[15,2,64,128]{3,2,1,0:T(8,128)(2,1)S(1)}, u32[]{:S(2)}, u32[]{:S(2)}) collective-permute-start(bf16[15,2,64,128]{3,2,1,0:T(8,128)(2,1)S(1)} %correlate.8), channel_id=1, source_target_pairs={{0,2},{1,3},{2,6},{3,7},{4,0},{5,1},{6,4},{7,5},{8,10},{9,11},{10,... | collective-permute-start | bytes 1474568 | tf_op jit(solution)/shard_map/ppermute | solution.py:448
  70.5 1.5 %collective-permute-start.26 = (bf16[4,2,80,128]{3,2,1,0:T(8,128)(2,1)S(1)}, bf16[4,2,80,128]{3,2,1,0:T(8,128)(2,1)S(1)}, u32[]{:S(2)}, u32[]{:S(2)}) collective-permute-start(bf16[4,2,80,128]{3,2,1,0:T(8,128)(2,1)S(1)} %get-tuple-element.70), channel_id=1, source_target_pairs={{0,1},{1,0},{2,3},{3,2},{4,5},{5,4},{6,7},{7,6},{8,9},{9,8},{10,11... | collective-permute-start | bytes 491528 | tf_op jit(solution)/shard_map/ppermute | solution.py:448
  72.6 4.9 %collective-permute-done.26.refs_1_ = bf16[4,2,80,128]{3,2,1,0:T(8,128)(2,1)S(1)} collective-permute-done((bf16[4,2,80,128]{3,2,1,0:T(8,128)(2,1)S(1)}, bf16[4,2,80,128]{3,2,1,0:T(8,128)(2,1)S(1)}, u32[]{:S(2)}, u32[]{:S(2)}) %collective-permute-start.26) | collective-permute-done | bytes 163872 | tf_op jit(solution)/shard_map/ppermute | solution.py:448
  77.6 1.5 %collective-permute-start.11 = (bf16[4,2,80,128]{3,2,1,0:T(8,128)(2,1)S(1)}, bf16[4,2,80,128]{3,2,1,0:T(8,128)(2,1)S(1)}, u32[]{:S(2)}, u32[]{:S(2)}) collective-permute-start(bf16[4,2,80,128]{3,2,1,0:T(8,128)(2,1)S(1)} %get-tuple-element.54), channel_id=1, source_target_pairs={{0,1},{1,0},{2,3},{3,2},{4,5},{5,4},{6,7},{7,6},{8,9},{9,8},{10,11... | collective-permute-start | bytes 491528 | tf_op jit(solution)/shard_map/ppermute | solution.py:448
  79.1 1.0 collective-permute-done.28.refs_3_
  80.1 2.2 %collective-permute-start.13 = (bf16[4,2,80,128]{3,2,1,0:T(8,128)(2,1)S(1)}, bf16[4,2,80,128]{3,2,1,0:T(8,128)(2,1)S(1)}, u32[]{:S(2)}, u32[]{:S(2)}) collective-permute-start(bf16[4,2,80,128]{3,2,1,0:T(8,128)(2,1)S(1)} %get-tuple-element.56), channel_id=1, source_target_pairs={{0,9},{1,8},{2,11},{3,10},{4,13},{5,12},{6,15},{7,14},{8,1},{9,0},... | collective-permute-start | bytes 491528 | tf_op jit(solution)/shard_map/ppermute | solution.py:448
  82.3 0.8 correlate.12
  83.0 2.6 %collective-permute-start.33 = (bf16[15,2,64,128]{3,2,1,0:T(8,128)(2,1)S(1)}, bf16[15,2,64,128]{3,2,1,0:T(8,128)(2,1)S(1)}, u32[]{:S(2)}, u32[]{:S(2)}) collective-permute-start(bf16[15,2,64,128]{3,2,1,0:T(8,128)(2,1)S(1)} %correlate.12), channel_id=1, source_target_pairs={{0,2},{1,3},{2,6},{3,7},{4,0},{5,1},{6,4},{7,5},{8,10},{9,11},{10,... | collective-permute-start | bytes 1474568 | tf_op jit(solution)/shard_map/ppermute | solution.py:448
  86.2 1.2 collective-permute-done.17.refs_4_
  87.4 0.8 correlate.9
  88.1 1.7 %collective-permute-start.18 = (bf16[15,2,64,128]{3,2,1,0:T(8,128)(2,1)S(1)}, bf16[15,2,64,128]{3,2,1,0:T(8,128)(2,1)S(1)}, u32[]{:S(2)}, u32[]{:S(2)}) collective-permute-start(bf16[15,2,64,128]{3,2,1,0:T(8,128)(2,1)S(1)} %correlate.9), channel_id=1, source_target_pairs={{0,2},{1,3},{2,6},{3,7},{4,0},{5,1},{6,4},{7,5},{8,10},{9,11},{10,... | collective-permute-start | bytes 1474568 | tf_op jit(solution)/shard_map/ppermute | solution.py:448
  90.2 0.9 collective-permute-start.24
  91.1 0.8 collective-permute-start.25
  91.9 4.9 %collective-permute-done.23.refs_1_ = bf16[4,2,80,128]{3,2,1,0:T(8,128)(2,1)S(1)} collective-permute-done((bf16[4,2,80,128]{3,2,1,0:T(8,128)(2,1)S(1)}, bf16[4,2,80,128]{3,2,1,0:T(8,128)(2,1)S(1)}, u32[]{:S(2)}, u32[]{:S(2)}) %collective-permute-start.23) | collective-permute-done | bytes 163872 | tf_op jit(solution)/shard_map/ppermute | solution.py:448
  97.3 2.5 %collective-permute-done.25.refs_3_ = bf16[4,2,80,128]{3,2,1,0:T(8,128)(2,1)S(1)} collective-permute-done((bf16[4,2,80,128]{3,2,1,0:T(8,128)(2,1)S(1)}, bf16[4,2,80,128]{3,2,1,0:T(8,128)(2,1)S(1)}, u32[]{:S(2)}, u32[]{:S(2)}) %collective-permute-start.25) | collective-permute-done | bytes 163872 | tf_op jit(solution)/shard_map/ppermute | solution.py:448
  101.1 2.8 %collective-permute-start.34 = (bf16[15,2,64,128]{3,2,1,0:T(8,128)(2,1)S(1)}, bf16[15,2,64,128]{3,2,1,0:T(8,128)(2,1)S(1)}, u32[]{:S(2)}, u32[]{:S(2)}) collective-permute-start(bf16[15,2,64,128]{3,2,1,0:T(8,128)(2,1)S(1)} %correlate.13), channel_id=1, source_target_pairs={{0,2},{1,3},{2,6},{3,7},{4,0},{5,1},{6,4},{7,5},{8,10},{9,11},{10,... | collective-permute-start | bytes 1474568 | tf_op jit(solution)/shard_map/ppermute | solution.py:448
  104.0 2.7 %collective-permute-done.10.refs_3_ = bf16[4,2,80,128]{3,2,1,0:T(8,128)(2,1)S(1)} collective-permute-done((bf16[4,2,80,128]{3,2,1,0:T(8,128)(2,1)S(1)}, bf16[4,2,80,128]{3,2,1,0:T(8,128)(2,1)S(1)}, u32[]{:S(2)}, u32[]{:S(2)}) %collective-permute-start.10) | collective-permute-done | bytes 163872 | tf_op jit(solution)/shard_map/ppermute | solution.py:448
  106.7 1.9 %collective-permute-done.18.refs_4_ = bf16[15,2,64,128]{3,2,1,0:T(8,128)(2,1)S(1)} collective-permute-done((bf16[15,2,64,128]{3,2,1,0:T(8,128)(2,1)S(1)}, bf16[15,2,64,128]{3,2,1,0:T(8,128)(2,1)S(1)}, u32[]{:S(2)}, u32[]{:S(2)}) %collective-permute-start.18) | collective-permute-done | bytes 491552 | tf_op jit(solution)/shard_map/ppermute | solution.py:448
  108.7 0.8 correlate.10
  109.5 1.5 %collective-permute-start.19 = (bf16[15,2,64,128]{3,2,1,0:T(8,128)(2,1)S(1)}, bf16[15,2,64,128]{3,2,1,0:T(8,128)(2,1)S(1)}, u32[]{:S(2)}, u32[]{:S(2)}) collective-permute-start(bf16[15,2,64,128]{3,2,1,0:T(8,128)(2,1)S(1)} %correlate.10), channel_id=1, source_target_pairs={{0,2},{1,3},{2,6},{3,7},{4,0},{5,1},{6,4},{7,5},{8,10},{9,11},{10,... | collective-permute-start | bytes 1474568 | tf_op jit(solution)/shard_map/ppermute | solution.py:448
  111.7 1.4 %collective-permute-start.22 = (bf16[4,2,80,128]{3,2,1,0:T(8,128)(2,1)S(1)}, bf16[4,2,80,128]{3,2,1,0:T(8,128)(2,1)S(1)}, u32[]{:S(2)}, u32[]{:S(2)}) collective-permute-start(bf16[4,2,80,128]{3,2,1,0:T(8,128)(2,1)S(1)} %get-tuple-element.64), channel_id=1, source_target_pairs={{0,9},{1,8},{2,11},{3,10},{4,13},{5,12},{6,15},{7,14},{8,1},{9,0},... | collective-permute-start | bytes 491528 | tf_op jit(solution)/shard_map/ppermute | solution.py:448
  113.1 4.7 %collective-permute-done.20.refs_1_ = bf16[4,2,80,128]{3,2,1,0:T(8,128)(2,1)S(1)} collective-permute-done((bf16[4,2,80,128]{3,2,1,0:T(8,128)(2,1)S(1)}, bf16[4,2,80,128]{3,2,1,0:T(8,128)(2,1)S(1)}, u32[]{:S(2)}, u32[]{:S(2)}) %collective-permute-start.20) | collective-permute-done | bytes 163872 | tf_op jit(solution)/shard_map/ppermute | solution.py:448
  118.2 1.0 collective-permute-done.22.refs_3_
  119.2 2.2 %collective-permute-start.7 = (bf16[4,2,80,128]{3,2,1,0:T(8,128)(2,1)S(1)}, bf16[4,2,80,128]{3,2,1,0:T(8,128)(2,1)S(1)}, u32[]{:S(2)}, u32[]{:S(2)}) collective-permute-start(bf16[4,2,80,128]{3,2,1,0:T(8,128)(2,1)S(1)} %get-tuple-element.48), channel_id=1, source_target_pairs={{0,9},{1,8},{2,11},{3,10},{4,13},{5,12},{6,15},{7,14},{8,1},{9,0},... | collective-permute-start | bytes 491528 | tf_op jit(solution)/shard_map/ppermute | solution.py:448
  121.4 1.8 %correlate.14.refs_5_ = f32[1,15,64,512]{3,2,1,0:T(8,128)} custom-call(bf16[4,2,80,128]{3,2,1,0:T(8,128)(2,1)S(1)} %get-tuple-element.61.refs_0_, bf16[4,2,80,128]{3,2,1,0:T(8,128)(2,1)S(1)} %collective-permute-done.20.refs_1_, bf16[4,2,80,128]{3,2,1,0:T(8,128)(2,1)S(1)} %collective-permute-done.21.refs_2_, ...), custom_call_target="tpu_custom_call" | custom-call | flops 1000000000 | bytes 6000000 | tf_op jit(solution)/shard_map/correlate/pallas_call | solution.py:518
  123.9 1.5 %collective-permute-done.7.refs_3_ = bf16[4,2,80,128]{3,2,1,0:T(8,128)(2,1)S(1)} collective-permute-done((bf16[4,2,80,128]{3,2,1,0:T(8,128)(2,1)S(1)}, bf16[4,2,80,128]{3,2,1,0:T(8,128)(2,1)S(1)}, u32[]{:S(2)}, u32[]{:S(2)}) %collective-permute-start.7) | collective-permute-done | bytes 163872 | tf_op jit(solution)/shard_map/ppermute | solution.py:448
  125.4 3.4 %collective-permute-done.19.refs_4_ = bf16[15,2,64,128]{3,2,1,0:T(8,128)(2,1)S(1)} collective-permute-done((bf16[15,2,64,128]{3,2,1,0:T(8,128)(2,1)S(1)}, bf16[15,2,64,128]{3,2,1,0:T(8,128)(2,1)S(1)}, u32[]{:S(2)}, u32[]{:S(2)}) %collective-permute-start.19) | collective-permute-done | bytes 491552 | tf_op jit(solution)/shard_map/ppermute | solution.py:448
  128.8 1.8 %correlate.15 = f32[1,15,64,512]{3,2,1,0:T(8,128)} custom-call(bf16[4,2,80,128]{3,2,1,0:T(8,128)(2,1)S(1)} %get-tuple-element.45.refs_0_, bf16[4,2,80,128]{3,2,1,0:T(8,128)(2,1)S(1)} %collective-permute-done.5.refs_1_, bf16[4,2,80,128]{3,2,1,0:T(8,128)(2,1)S(1)} %collective-permute-done.6.refs_2_, ...), custom_call_target="tpu_custom_call", output_to_operand_aliasing={{}: (5, {})} | custom-call | flops 1000000000 | bytes 6000000 | tf_op jit(solution)/shard_map/correlate/pallas_call | solution.py:518
  (57 shorter events, 8.4 us)
Async XLA Ops:
  0.6 7.8 %copy-start.10 = (f32[32]{0:T(128)S(1)}, f32[32]{0:T(128)}, u32[]{:S(2)}) copy-start(f32[32]{0:T(128)} %param.16) | copy-start | bytes 388
  0.6 19.7 %copy-start = (s32[4]{0:T(128)S(1)}, s32[4]{0:T(128)}, u32[]{:S(2)}) copy-start(s32[4]{0:T(128)} %pad_add_fusion.place) | copy-start | bytes 52
  0.6 19.7 %copy-start.1 = (bf16[2,1,2,512,512]{4,3,2,1,0:T(8,128)(2,1)S(1)}, bf16[2,1,2,512,512]{4,3,2,1,0:T(8,128)(2,1)}, u32[]{:S(2)}) copy-start(bf16[2,1,2,512,512]{4,3,2,1,0:T(8,128)(2,1)} %refs_0_.1) | copy-start | bytes 6291460
  0.6 19.7 %copy-start.8 = (f32[384,1]{1,0:T(8,128)S(1)}, f32[384,1]{1,0:T(8,128)}, u32[]{:S(2)}) copy-start(f32[384,1]{1,0:T(8,128)} %constant.87.clone.refs_9_.refs_12_) | copy-start | bytes 4612
  0.6 19.7 %copy-start.9 = (f32[1,384]{1,0:T(1,128)S(1)}, f32[1,384]{1,0:T(1,128)}, u32[]{:S(2)}) copy-start(f32[1,384]{1,0:T(1,128)} %constant.88.clone.refs_10_.refs_13_) | copy-start | bytes 4612
  4.0 0.8 copy-start.3
  4.8 2.1 %collective-permute-start.1 = (bf16[512,512]{1,0:T(8,128)(2,1)}, bf16[512,512]{1,0:T(8,128)(2,1)S(1)}, u32[]{:S(2)}, u32[]{:S(2)}) collective-permute-start(bf16[512,512]{1,0:T(8,128)(2,1)} %copy-done.3), channel_id=1, source_target_pairs={{0,8},{1,9},{2,10},{3,11},{4,12},{5,13},{6,14},{7,15},{8,0},{9,1},... | collective-permute-start | bytes 1572872 | tf_op jit(solution)/shard_map/ppermute | solution.py:448
  4.8 15.5 %collective-permute-start = (bf16[512,512]{1,0:T(8,128)(2,1)S(1)}, bf16[512,512]{1,0:T(8,128)(2,1)}, u32[]{:S(2)}, u32[]{:S(2)}) collective-permute-start(bf16[512,512]{1,0:T(8,128)(2,1)S(1)} %get-tuple-element.43.refs_3_.refs_5_), channel_id=1, source_target_pairs={{0,16},{1,17},{2,18},{3,19},{4,20},{5,21},{6,22},{7,23}} | collective-permute-start | bytes 1572872 | tf_op jit(solution)/shard_map/ppermute | solution.py:448
  6.9 13.3 %collective-permute-start.2 = (bf16[512,512]{1,0:T(8,128)(2,1)S(1)}, bf16[512,512]{1,0:T(8,128)(2,1)}, u32[]{:S(2)}, u32[]{:S(2)}) collective-permute-start(bf16[512,512]{1,0:T(8,128)(2,1)S(1)} %collective-permute-done.1.refs_4_.refs_6_), channel_id=1, source_target_pairs={{8,24},{9,25},{10,26},{11,27},{12,28},{13,29},{14,30},{15,31}} | collective-permute-start | bytes 1572872 | tf_op jit(solution)/shard_map/ppermute | solution.py:448
  8.4 22.9 %collective-permute-start.3 = (bf16[512,512]{1,0:T(8,128)(2,1)S(1)}, bf16[512,512]{1,0:T(8,128)(2,1)S(1)}, u32[]{:S(2)}, u32[]{:S(2)}) collective-permute-start(bf16[512,512]{1,0:T(8,128)(2,1)S(1)} %get-tuple-element.43.refs_3_.refs_5_), channel_id=1, source_target_pairs={{8,24},{9,25},{10,26},{11,27},{12,28},{13,29},{14,30},{15,31}} | collective-permute-start | bytes 1572872 | tf_op jit(solution)/shard_map/ppermute | solution.py:448
  9.1 22.3 %collective-permute-start.4 = (bf16[512,512]{1,0:T(8,128)(2,1)S(1)}, bf16[512,512]{1,0:T(8,128)(2,1)S(1)}, u32[]{:S(2)}, u32[]{:S(2)}) collective-permute-start(bf16[512,512]{1,0:T(8,128)(2,1)S(1)} %collective-permute-done.1.refs_4_.refs_6_), channel_id=1, source_target_pairs={{0,16},{1,17},{2,18},{3,19},{4,20},{5,21},{6,22},{7,23}} | collective-permute-start | bytes 1572872 | tf_op jit(solution)/shard_map/ppermute | solution.py:448
  20.3 1.6 %copy-start.2 = (bf16[2,1,2,512,512]{4,3,2,1,0:T(8,128)(2,1)S(1)}, bf16[2,1,2,512,512]{4,3,2,1,0:T(8,128)(2,1)}, u32[]{:S(2)}) copy-start(bf16[2,1,2,512,512]{4,3,2,1,0:T(8,128)(2,1)} %refs_1_.1) | copy-start | bytes 6291460
  21.9 1.0 copy-start.4
  22.9 1.0 copy-start.6
  24.0 7.4 %copy-start.5 = (bf16[4,256,256]{2,1,0:T(8,128)(2,1)S(1)}, bf16[4,256,256]{2,1,0:T(8,128)(2,1)}, u32[]{:S(2)}) copy-start(bf16[4,256,256]{2,1,0:T(8,128)(2,1)} %constant.86.clone.refs_6_.refs_8_.refs_9_.refs_11_) | copy-start | bytes 1572868
  24.0 7.4 %copy-start.7 = (bf16[4,256,256]{2,1,0:T(8,128)(2,1)S(1)}, bf16[4,256,256]{2,1,0:T(8,128)(2,1)}, u32[]{:S(2)}) copy-start(bf16[4,256,256]{2,1,0:T(8,128)(2,1)} %constant.85.clone.refs_5_.refs_7_.refs_8_.refs_10_) | copy-start | bytes 1572868
  50.4 5.8 %collective-permute-start.29 = (bf16[4,2,80,128]{3,2,1,0:T(8,128)(2,1)S(1)}, bf16[4,2,80,128]{3,2,1,0:T(8,128)(2,1)S(1)}, u32[]{:S(2)}, u32[]{:S(2)}) collective-permute-start(bf16[4,2,80,128]{3,2,1,0:T(8,128)(2,1)S(1)} %get-tuple-element.74), channel_id=1, source_target_pairs={{0,1},{1,0},{2,3},{3,2},{4,5},{5,4},{6,7},{7,6},{8,9},{9,8},{10,11... | collective-permute-start | bytes 491528 | tf_op jit(solution)/shard_map/ppermute | solution.py:448
  52.0 7.6 %collective-permute-start.30 = (bf16[4,2,80,128]{3,2,1,0:T(8,128)(2,1)S(1)}, bf16[4,2,80,128]{3,2,1,0:T(8,128)(2,1)S(1)}, u32[]{:S(2)}, u32[]{:S(2)}) collective-permute-start(bf16[4,2,80,128]{3,2,1,0:T(8,128)(2,1)S(1)} %get-tuple-element.75), channel_id=1, source_target_pairs={{0,8},{1,9},{2,10},{3,11},{4,12},{5,13},{6,14},{7,15},{8,0},{9,1},... | collective-permute-start | bytes 491528 | tf_op jit(solution)/shard_map/ppermute | solution.py:448
  54.4 6.7 %collective-permute-start.31 = (bf16[4,2,80,128]{3,2,1,0:T(8,128)(2,1)S(1)}, bf16[4,2,80,128]{3,2,1,0:T(8,128)(2,1)S(1)}, u32[]{:S(2)}, u32[]{:S(2)}) collective-permute-start(bf16[4,2,80,128]{3,2,1,0:T(8,128)(2,1)S(1)} %get-tuple-element.76), channel_id=1, source_target_pairs={{0,9},{1,8},{2,11},{3,10},{4,13},{5,12},{6,15},{7,14},{8,1},{9,0},... | collective-permute-start | bytes 491528 | tf_op jit(solution)/shard_map/ppermute | solution.py:448
  54.5 10.1 %collective-permute-start.14 = (bf16[4,2,80,128]{3,2,1,0:T(8,128)(2,1)S(1)}, bf16[4,2,80,128]{3,2,1,0:T(8,128)(2,1)S(1)}, u32[]{:S(2)}, u32[]{:S(2)}) collective-permute-start(bf16[4,2,80,128]{3,2,1,0:T(8,128)(2,1)S(1)} %get-tuple-element.58), channel_id=1, source_target_pairs={{0,1},{1,0},{2,3},{3,2},{4,5},{5,4},{6,7},{7,6},{8,9},{9,8},{10,11... | collective-permute-start | bytes 491528 | tf_op jit(solution)/shard_map/ppermute | solution.py:448
  56.0 8.6 %collective-permute-start.15 = (bf16[4,2,80,128]{3,2,1,0:T(8,128)(2,1)S(1)}, bf16[4,2,80,128]{3,2,1,0:T(8,128)(2,1)S(1)}, u32[]{:S(2)}, u32[]{:S(2)}) collective-permute-start(bf16[4,2,80,128]{3,2,1,0:T(8,128)(2,1)S(1)} %get-tuple-element.59), channel_id=1, source_target_pairs={{0,8},{1,9},{2,10},{3,11},{4,12},{5,13},{6,14},{7,15},{8,0},{9,1},... | collective-permute-start | bytes 491528 | tf_op jit(solution)/shard_map/ppermute | solution.py:448
  56.2 11.8 %collective-permute-start.16 = (bf16[4,2,80,128]{3,2,1,0:T(8,128)(2,1)S(1)}, bf16[4,2,80,128]{3,2,1,0:T(8,128)(2,1)S(1)}, u32[]{:S(2)}, u32[]{:S(2)}) collective-permute-start(bf16[4,2,80,128]{3,2,1,0:T(8,128)(2,1)S(1)} %get-tuple-element.60), channel_id=1, source_target_pairs={{0,9},{1,8},{2,11},{3,10},{4,13},{5,12},{6,15},{7,14},{8,1},{9,0},... | collective-permute-start | bytes 491528 | tf_op jit(solution)/shard_map/ppermute | solution.py:448
  61.8 20.4 %collective-permute-start.32 = (bf16[15,2,64,128]{3,2,1,0:T(8,128)(2,1)S(1)}, bf16[15,2,64,128]{3,2,1,0:T(8,128)(2,1)S(1)}, u32[]{:S(2)}, u32[]{:S(2)}) collective-permute-start(bf16[15,2,64,128]{3,2,1,0:T(8,128)(2,1)S(1)} %correlate.11), channel_id=1, source_target_pairs={{0,2},{1,3},{2,6},{3,7},{4,0},{5,1},{6,4},{7,5},{8,10},{9,11},{10,... | collective-permute-start | bytes 1474568 | tf_op jit(solution)/shard_map/ppermute | solution.py:448
  68.8 18.5 %collective-permute-start.17 = (bf16[15,2,64,128]{3,2,1,0:T(8,128)(2,1)S(1)}, bf16[15,2,64,128]{3,2,1,0:T(8,128)(2,1)S(1)}, u32[]{:S(2)}, u32[]{:S(2)}) collective-permute-start(bf16[15,2,64,128]{3,2,1,0:T(8,128)(2,1)S(1)} %correlate.8), channel_id=1, source_target_pairs={{0,2},{1,3},{2,6},{3,7},{4,0},{5,1},{6,4},{7,5},{8,10},{9,11},{10,... | collective-permute-start | bytes 1474568 | tf_op jit(solution)/shard_map/ppermute | solution.py:448
  70.5 7.1 %collective-permute-start.26 = (bf16[4,2,80,128]{3,2,1,0:T(8,128)(2,1)S(1)}, bf16[4,2,80,128]{3,2,1,0:T(8,128)(2,1)S(1)}, u32[]{:S(2)}, u32[]{:S(2)}) collective-permute-start(bf16[4,2,80,128]{3,2,1,0:T(8,128)(2,1)S(1)} %get-tuple-element.70), channel_id=1, source_target_pairs={{0,1},{1,0},{2,3},{3,2},{4,5},{5,4},{6,7},{7,6},{8,9},{9,8},{10,11... | collective-permute-start | bytes 491528 | tf_op jit(solution)/shard_map/ppermute | solution.py:448
  72.0 7.1 %collective-permute-start.27 = (bf16[4,2,80,128]{3,2,1,0:T(8,128)(2,1)S(1)}, bf16[4,2,80,128]{3,2,1,0:T(8,128)(2,1)S(1)}, u32[]{:S(2)}, u32[]{:S(2)}) collective-permute-start(bf16[4,2,80,128]{3,2,1,0:T(8,128)(2,1)S(1)} %get-tuple-element.71), channel_id=1, source_target_pairs={{0,8},{1,9},{2,10},{3,11},{4,12},{5,13},{6,14},{7,15},{8,0},{9,1},... | collective-permute-start | bytes 491528 | tf_op jit(solution)/shard_map/ppermute | solution.py:448
  72.0 8.1 %collective-permute-start.28 = (bf16[4,2,80,128]{3,2,1,0:T(8,128)(2,1)S(1)}, bf16[4,2,80,128]{3,2,1,0:T(8,128)(2,1)S(1)}, u32[]{:S(2)}, u32[]{:S(2)}) collective-permute-start(bf16[4,2,80,128]{3,2,1,0:T(8,128)(2,1)S(1)} %get-tuple-element.72), channel_id=1, source_target_pairs={{0,9},{1,8},{2,11},{3,10},{4,13},{5,12},{6,15},{7,14},{8,1},{9,0},... | collective-permute-start | bytes 491528 | tf_op jit(solution)/shard_map/ppermute | solution.py:448
  77.6 8.1 %collective-permute-start.11 = (bf16[4,2,80,128]{3,2,1,0:T(8,128)(2,1)S(1)}, bf16[4,2,80,128]{3,2,1,0:T(8,128)(2,1)S(1)}, u32[]{:S(2)}, u32[]{:S(2)}) collective-permute-start(bf16[4,2,80,128]{3,2,1,0:T(8,128)(2,1)S(1)} %get-tuple-element.54), channel_id=1, source_target_pairs={{0,1},{1,0},{2,3},{3,2},{4,5},{5,4},{6,7},{7,6},{8,9},{9,8},{10,11... | collective-permute-start | bytes 491528 | tf_op jit(solution)/shard_map/ppermute | solution.py:448
  79.1 6.6 %collective-permute-start.12 = (bf16[4,2,80,128]{3,2,1,0:T(8,128)(2,1)S(1)}, bf16[4,2,80,128]{3,2,1,0:T(8,128)(2,1)S(1)}, u32[]{:S(2)}, u32[]{:S(2)}) collective-permute-start(bf16[4,2,80,128]{3,2,1,0:T(8,128)(2,1)S(1)} %get-tuple-element.55), channel_id=1, source_target_pairs={{0,8},{1,9},{2,10},{3,11},{4,12},{5,13},{6,14},{7,15},{8,0},{9,1},... | collective-permute-start | bytes 491528 | tf_op jit(solution)/shard_map/ppermute | solution.py:448
  80.1 6.1 %collective-permute-start.13 = (bf16[4,2,80,128]{3,2,1,0:T(8,128)(2,1)S(1)}, bf16[4,2,80,128]{3,2,1,0:T(8,128)(2,1)S(1)}, u32[]{:S(2)}, u32[]{:S(2)}) collective-permute-start(bf16[4,2,80,128]{3,2,1,0:T(8,128)(2,1)S(1)} %get-tuple-element.56), channel_id=1, source_target_pairs={{0,9},{1,8},{2,11},{3,10},{4,13},{5,12},{6,15},{7,14},{8,1},{9,0},... | collective-permute-start | bytes 491528 | tf_op jit(solution)/shard_map/ppermute | solution.py:448
  83.0 17.3 %collective-permute-start.33 = (bf16[15,2,64,128]{3,2,1,0:T(8,128)(2,1)S(1)}, bf16[15,2,64,128]{3,2,1,0:T(8,128)(2,1)S(1)}, u32[]{:S(2)}, u32[]{:S(2)}) collective-permute-start(bf16[15,2,64,128]{3,2,1,0:T(8,128)(2,1)S(1)} %correlate.12), channel_id=1, source_target_pairs={{0,2},{1,3},{2,6},{3,7},{4,0},{5,1},{6,4},{7,5},{8,10},{9,11},{10,... | collective-permute-start | bytes 1474568 | tf_op jit(solution)/shard_map/ppermute | solution.py:448
  88.1 20.5 %collective-permute-start.18 = (bf16[15,2,64,128]{3,2,1,0:T(8,128)(2,1)S(1)}, bf16[15,2,64,128]{3,2,1,0:T(8,128)(2,1)S(1)}, u32[]{:S(2)}, u32[]{:S(2)}) collective-permute-start(bf16[15,2,64,128]{3,2,1,0:T(8,128)(2,1)S(1)} %correlate.9), channel_id=1, source_target_pairs={{0,2},{1,3},{2,6},{3,7},{4,0},{5,1},{6,4},{7,5},{8,10},{9,11},{10,... | collective-permute-start | bytes 1474568 | tf_op jit(solution)/shard_map/ppermute | solution.py:448
  89.8 7.1 %collective-permute-start.23 = (bf16[4,2,80,128]{3,2,1,0:T(8,128)(2,1)S(1)}, bf16[4,2,80,128]{3,2,1,0:T(8,128)(2,1)S(1)}, u32[]{:S(2)}, u32[]{:S(2)}) collective-permute-start(bf16[4,2,80,128]{3,2,1,0:T(8,128)(2,1)S(1)} %get-tuple-element.66), channel_id=1, source_target_pairs={{0,1},{1,0},{2,3},{3,2},{4,5},{5,4},{6,7},{7,6},{8,9},{9,8},{10,11... | collective-permute-start | bytes 491528 | tf_op jit(solution)/shard_map/ppermute | solution.py:448
  90.2 6.9 %collective-permute-start.24 = (bf16[4,2,80,128]{3,2,1,0:T(8,128)(2,1)S(1)}, bf16[4,2,80,128]{3,2,1,0:T(8,128)(2,1)S(1)}, u32[]{:S(2)}, u32[]{:S(2)}) collective-permute-start(bf16[4,2,80,128]{3,2,1,0:T(8,128)(2,1)S(1)} %get-tuple-element.67), channel_id=1, source_target_pairs={{0,8},{1,9},{2,10},{3,11},{4,12},{5,13},{6,14},{7,15},{8,0},{9,1},... | collective-permute-start | bytes 491528 | tf_op jit(solution)/shard_map/ppermute | solution.py:448
  91.1 8.7 %collective-permute-start.25 = (bf16[4,2,80,128]{3,2,1,0:T(8,128)(2,1)S(1)}, bf16[4,2,80,128]{3,2,1,0:T(8,128)(2,1)S(1)}, u32[]{:S(2)}, u32[]{:S(2)}) collective-permute-start(bf16[4,2,80,128]{3,2,1,0:T(8,128)(2,1)S(1)} %get-tuple-element.68), channel_id=1, source_target_pairs={{0,9},{1,8},{2,11},{3,10},{4,13},{5,12},{6,15},{7,14},{8,1},{9,0},... | collective-permute-start | bytes 491528 | tf_op jit(solution)/shard_map/ppermute | solution.py:448
  96.9 7.1 %collective-permute-start.8 = (bf16[4,2,80,128]{3,2,1,0:T(8,128)(2,1)S(1)}, bf16[4,2,80,128]{3,2,1,0:T(8,128)(2,1)S(1)}, u32[]{:S(2)}, u32[]{:S(2)}) collective-permute-start(bf16[4,2,80,128]{3,2,1,0:T(8,128)(2,1)S(1)} %get-tuple-element.50), channel_id=1, source_target_pairs={{0,1},{1,0},{2,3},{3,2},{4,5},{5,4},{6,7},{7,6},{8,9},{9,8},{10,11... | collective-permute-start | bytes 491528 | tf_op jit(solution)/shard_map/ppermute | solution.py:448
  97.1 7.0 %collective-permute-start.9 = (bf16[4,2,80,128]{3,2,1,0:T(8,128)(2,1)S(1)}, bf16[4,2,80,128]{3,2,1,0:T(8,128)(2,1)S(1)}, u32[]{:S(2)}, u32[]{:S(2)}) collective-permute-start(bf16[4,2,80,128]{3,2,1,0:T(8,128)(2,1)S(1)} %get-tuple-element.51), channel_id=1, source_target_pairs={{0,8},{1,9},{2,10},{3,11},{4,12},{5,13},{6,14},{7,15},{8,0},{9,1},... | collective-permute-start | bytes 491528 | tf_op jit(solution)/shard_map/ppermute | solution.py:448
  99.8 6.9 %collective-permute-start.10 = (bf16[4,2,80,128]{3,2,1,0:T(8,128)(2,1)S(1)}, bf16[4,2,80,128]{3,2,1,0:T(8,128)(2,1)S(1)}, u32[]{:S(2)}, u32[]{:S(2)}) collective-permute-start(bf16[4,2,80,128]{3,2,1,0:T(8,128)(2,1)S(1)} %get-tuple-element.52), channel_id=1, source_target_pairs={{0,9},{1,8},{2,11},{3,10},{4,13},{5,12},{6,15},{7,14},{8,1},{9,0},... | collective-permute-start | bytes 491528 | tf_op jit(solution)/shard_map/ppermute | solution.py:448
  101.1 20.3 %collective-permute-start.34 = (bf16[15,2,64,128]{3,2,1,0:T(8,128)(2,1)S(1)}, bf16[15,2,64,128]{3,2,1,0:T(8,128)(2,1)S(1)}, u32[]{:S(2)}, u32[]{:S(2)}) collective-permute-start(bf16[15,2,64,128]{3,2,1,0:T(8,128)(2,1)S(1)} %correlate.13), channel_id=1, source_target_pairs={{0,2},{1,3},{2,6},{3,7},{4,0},{5,1},{6,4},{7,5},{8,10},{9,11},{10,... | collective-permute-start | bytes 1474568 | tf_op jit(solution)/shard_map/ppermute | solution.py:448
  109.5 19.3 %collective-permute-start.19 = (bf16[15,2,64,128]{3,2,1,0:T(8,128)(2,1)S(1)}, bf16[15,2,64,128]{3,2,1,0:T(8,128)(2,1)S(1)}, u32[]{:S(2)}, u32[]{:S(2)}) collective-permute-start(bf16[15,2,64,128]{3,2,1,0:T(8,128)(2,1)S(1)} %correlate.10), channel_id=1, source_target_pairs={{0,2},{1,3},{2,6},{3,7},{4,0},{5,1},{6,4},{7,5},{8,10},{9,11},{10,... | collective-permute-start | bytes 1474568 | tf_op jit(solution)/shard_map/ppermute | solution.py:448
  111.0 6.9 %collective-permute-start.20 = (bf16[4,2,80,128]{3,2,1,0:T(8,128)(2,1)S(1)}, bf16[4,2,80,128]{3,2,1,0:T(8,128)(2,1)S(1)}, u32[]{:S(2)}, u32[]{:S(2)}) collective-permute-start(bf16[4,2,80,128]{3,2,1,0:T(8,128)(2,1)S(1)} %get-tuple-element.62), channel_id=1, source_target_pairs={{0,1},{1,0},{2,3},{3,2},{4,5},{5,4},{6,7},{7,6},{8,9},{9,8},{10,11... | collective-permute-start | bytes 491528 | tf_op jit(solution)/shard_map/ppermute | solution.py:448
  111.7 6.4 %collective-permute-start.21 = (bf16[4,2,80,128]{3,2,1,0:T(8,128)(2,1)S(1)}, bf16[4,2,80,128]{3,2,1,0:T(8,128)(2,1)S(1)}, u32[]{:S(2)}, u32[]{:S(2)}) collective-permute-start(bf16[4,2,80,128]{3,2,1,0:T(8,128)(2,1)S(1)} %get-tuple-element.63), channel_id=1, source_target_pairs={{0,8},{1,9},{2,10},{3,11},{4,12},{5,13},{6,14},{7,15},{8,0},{9,1},... | collective-permute-start | bytes 491528 | tf_op jit(solution)/shard_map/ppermute | solution.py:448
  111.7 7.5 %collective-permute-start.22 = (bf16[4,2,80,128]{3,2,1,0:T(8,128)(2,1)S(1)}, bf16[4,2,80,128]{3,2,1,0:T(8,128)(2,1)S(1)}, u32[]{:S(2)}, u32[]{:S(2)}) collective-permute-start(bf16[4,2,80,128]{3,2,1,0:T(8,128)(2,1)S(1)} %get-tuple-element.64), channel_id=1, source_target_pairs={{0,9},{1,8},{2,11},{3,10},{4,13},{5,12},{6,15},{7,14},{8,1},{9,0},... | collective-permute-start | bytes 491528 | tf_op jit(solution)/shard_map/ppermute | solution.py:448
  117.8 6.1 %collective-permute-start.5 = (bf16[4,2,80,128]{3,2,1,0:T(8,128)(2,1)S(1)}, bf16[4,2,80,128]{3,2,1,0:T(8,128)(2,1)S(1)}, u32[]{:S(2)}, u32[]{:S(2)}) collective-permute-start(bf16[4,2,80,128]{3,2,1,0:T(8,128)(2,1)S(1)} %get-tuple-element.46), channel_id=1, source_target_pairs={{0,1},{1,0},{2,3},{3,2},{4,5},{5,4},{6,7},{7,6},{8,9},{9,8},{10,11... | collective-permute-start | bytes 491528 | tf_op jit(solution)/shard_map/ppermute | solution.py:448
  118.2 5.7 %collective-permute-start.6 = (bf16[4,2,80,128]{3,2,1,0:T(8,128)(2,1)S(1)}, bf16[4,2,80,128]{3,2,1,0:T(8,128)(2,1)S(1)}, u32[]{:S(2)}, u32[]{:S(2)}) collective-permute-start(bf16[4,2,80,128]{3,2,1,0:T(8,128)(2,1)S(1)} %get-tuple-element.47), channel_id=1, source_target_pairs={{0,8},{1,9},{2,10},{3,11},{4,12},{5,13},{6,14},{7,15},{8,0},{9,1},... | collective-permute-start | bytes 491528 | tf_op jit(solution)/shard_map/ppermute | solution.py:448
  119.2 6.2 %collective-permute-start.7 = (bf16[4,2,80,128]{3,2,1,0:T(8,128)(2,1)S(1)}, bf16[4,2,80,128]{3,2,1,0:T(8,128)(2,1)S(1)}, u32[]{:S(2)}, u32[]{:S(2)}) collective-permute-start(bf16[4,2,80,128]{3,2,1,0:T(8,128)(2,1)S(1)} %get-tuple-element.48), channel_id=1, source_target_pairs={{0,9},{1,8},{2,11},{3,10},{4,13},{5,12},{6,15},{7,14},{8,1},{9,0},... | collective-permute-start | bytes 491528 | tf_op jit(solution)/shard_map/ppermute | solution.py:448

commit v5 on v4

v5 whole, which is shorter than its diff:
```python
import functools
import math

import jax
import jax.numpy as jnp
import ml_dtypes
import numpy as np
from jax import lax
from jax.experimental import pallas as pl
from jax.experimental.pallas import tpu as pltpu
from jax.sharding import PartitionSpec as P

LAG = 7
HALO = 8
LANES = 128
AXES = ("depth", "freq")
VMEM_BYTES = 24 * 2**20


RADIX = 4
BLOCKS_X = 2
BLOCKS_Y = 2


def residues(length):
    found = [np.arange(residue, length, RADIX) for residue in range(RADIX)]
    found[3] = found[3][::-1]
    return found


def residue_tables(length):
    position = np.arange(length, dtype=np.int64)
    product = position[:, None] * position[None, :] % length
    angles = product.astype(np.float32) * np.float32(2.0 * math.pi / length)
    factor = np.float32(1.0 / math.sqrt(length))
    cos, sin = np.cos(angles) * factor, np.sin(angles) * factor
    tables = []
    for residue in residues(length):
        c, s = (t[residue, : length // RADIX] for t in (cos, sin))
        tables.append(np.block([[c, s], [-s, c]]).astype(ml_dtypes.bfloat16))
    return np.stack(tables)


def wavenumbers_squared(length):
    position = np.arange(length)
    signed = np.where(position < length // 2, position, position - length)
    wave = signed.astype(np.float32) * np.float32(2.0 * math.pi / length)
    squared = wave * wave
    return np.concatenate([squared[residue] for residue in residues(length)[:3]])


def mix_forward(re, im):
    sum_re, dif_re = re[0] + re[2], re[0] - re[2]
    sum_im, dif_im = im[0] + im[2], im[0] - im[2]
    odd_re, gap_re = re[1] + re[3], re[1] - re[3]
    odd_im, gap_im = im[1] + im[3], im[1] - im[3]
    return (
        (sum_re + odd_re, sum_im + odd_im),
        (dif_re + gap_im, dif_im - gap_re),
        (sum_re - odd_re, sum_im - odd_im),
        (dif_re - gap_im, dif_im + gap_re),
    )


def mix_inverse(re, im):
    found = mix_forward(re, im)
    return found[0], found[3], found[2], found[1]


Q_MAX = 14.0


def fit(function, degree):
    cheb = np.polynomial.chebyshev.Chebyshev.interpolate(
        lambda t: function((t + 1.0) * Q_MAX / 2), degree
    )
    return [float(v) for v in np.polynomial.chebyshev.cheb2poly(cheb.coef)]


COS_FIT = fit(lambda q: np.cos(np.sqrt(q)), 7)
SINC_FIT = fit(lambda q: np.sinc(np.sqrt(q) / np.pi), 7)


def horner(coefficients, t):
    total = jnp.full_like(t, coefficients[-1])
    for value in coefficients[-2::-1]:
        total = total * t + value
    return total


def cos_sin(square, root):
    t = square * (2.0 / Q_MAX) - 1.0
    return horner(COS_FIT, t), horner(SINC_FIT, t) * root


def lookup(table_row, codes):
    rows = codes.shape[0]
    parts = []
    for tile in range(codes.shape[1] // LANES):
        index = codes[:, tile * LANES : (tile + 1) * LANES]
        source = jnp.broadcast_to(table_row, (rows, LANES))
        parts.append(jnp.take_along_axis(source, index, axis=1, mode="promise_in_bounds"))
    return parts


def turned(kind, a, b, cos, sin):
    if kind == 0:
        return a * cos - b * sin, a * sin + b * cos
    return a * cos + b * sin, b * cos - a * sin


def extent(ref):
    rows_x, rows_y = ref.shape[1], ref.shape[2]
    return rows_x // RADIX, rows_y // RADIX, rows_y // BLOCKS_Y


def forward_x(field, mid, left_x):
    part_x, _, block_y = extent(field)
    for i in range(BLOCKS_Y):
        cols = slice(i * block_y, (i + 1) * block_y)
        for kind in range(2):
            re, im = (
                [field[2 * kind + j, q * part_x : (q + 1) * part_x, cols] for q in range(RADIX)]
                for j in range(2)
            )
            for r, mixed in enumerate(mix_forward(re, im)):
                mixed = jnp.concatenate(mixed, axis=0)
                out = jnp.dot(left_x[r], mixed, preferred_element_type=jnp.float32)
                mid[2 * kind : 2 * kind + 2, r * part_x : (r + 1) * part_x, cols] = out.astype(
                    jnp.bfloat16
                ).reshape(2, part_x, block_y)


def fill_phases(angular, base, wave_x, wave_y, phases):
    reach = angular * base
    reach = reach * reach
    part = wave_x.shape[0] // 3

    def block(i, carry):
        rows = pl.ds(pl.multiple_of(i * part, part), part)
        q = reach - wave_x[rows, :] - wave_y[0:1, :]
        root = jnp.sqrt(jnp.abs(q))
        cos, sin = cos_sin(q, root)
        phases[0, rows] = jnp.where(q > 0.0, cos, jnp.exp(-root))
        phases[1, rows] = jnp.where(q > 0.0, sin, 0.0)
        return carry

    lax.fori_loop(0, 3, block, 0)


def along_y(mid, phases, left_y, right_y):
    part_x, part_y, _ = extent(mid)
    lanes = [slice(q * part_y, (q + 1) * part_y) for q in range(RADIX)]
    for i in range(RADIX):
        rows = slice(i * part_x, (i + 1) * part_x)
        same = slice(part_x, 2 * part_x) if i == 3 else rows
        re, im = (
            [jnp.concatenate([mid[j, rows, at], mid[2 + j, rows, at]], axis=0) for at in lanes]
            for j in range(2)
        )
        back = []
        for r, mixed in enumerate(mix_forward(re, im)):
            mixed = jnp.concatenate(mixed, axis=1)
            spectrum = jnp.dot(mixed, right_y[r], preferred_element_type=jnp.float32)
            at = lanes[1 if r == 3 else r]
            phase_re, phase_im = phases[0, same, at], phases[1, same, at]
            pieces = []
            for kind in range(2):
                part = spectrum[kind * part_x : (kind + 1) * part_x]
                new = turned(kind, part[:, :part_y], part[:, part_y:], phase_re, phase_im)
                pieces.append(jnp.concatenate(new, axis=1).astype(jnp.bfloat16))
            shifted = jnp.concatenate(pieces, axis=0)
            back.append(jnp.dot(shifted, left_y[r], preferred_element_type=jnp.float32))
        back_re = [value[:, :part_y] for value in back]
        back_im = [value[:, part_y:] for value in back]
        for at, mixed in zip(lanes, mix_inverse(back_re, back_im)):
            for j in range(2):
                value = mixed[j].astype(jnp.bfloat16)
                for kind in range(2):
                    mid[2 * kind + j, rows, at] = value[kind * part_x : (kind + 1) * part_x]


def inverse_x(mid, right_x, sink):
    part_x, _, block_y = extent(mid)
    for i in range(BLOCKS_Y):
        cols = slice(i * block_y, (i + 1) * block_y)
        for kind in range(2):
            back = [
                jnp.dot(
                    right_x[r],
                    mid[2 * kind : 2 * kind + 2, r * part_x : (r + 1) * part_x, cols].reshape(
                        2 * part_x, block_y
                    ),
                    preferred_element_type=jnp.float32,
                )
                for r in range(RADIX)
            ]
            back_re = [value[:part_x] for value in back]
            back_im = [value[part_x:] for value in back]
            sink(i, cols, kind, mix_inverse(back_re, back_im))


def screen_tables(angular, base, levels):
    angle = angular * (levels[0:1, :] - base)
    return cos_sin(angle * angle, angle)


def fill_index(index, pair, flag):
    for value, source in ((flag, pair[0]), (jnp.logical_not(flag), pair[1])):

        @pl.when(value)
        def _(source=source):
            index[...] = source[...].astype(jnp.float32).astype(jnp.int32)


def screens_of(tables, index, rows, cols):
    return [jnp.concatenate(lookup(table, index[rows, cols]), axis=1) for table in tables]


def put_screened(tables, index, field, padded=None):
    part_x, _, block_y = extent(field)
    kept = {}

    def sink(i, cols, kind, parts):
        if i not in kept:
            kept.clear()
            kept[i] = [
                screens_of(tables, index, slice(p * part_x, (p + 1) * part_x), cols)
                for p in range(RADIX)
            ]
        done = [turned(kind, a, b, *kept[i][p]) for p, (a, b) in enumerate(parts)]
        for j in range(2):
            for p in range(RADIX):
                at = slice(p * part_x, (p + 1) * part_x)
                field[2 * kind + j, at, cols] = done[p][j].astype(jnp.bfloat16)
            if padded is not None:
                edge = jnp.zeros((HALO, block_y), jnp.float32)
                whole = jnp.concatenate([edge, *(d[j] for d in done), edge], axis=0)
                whole = whole.astype(jnp.bfloat16)
                for k in range(block_y // LANES):
                    padded[2 * kind + j, i * (block_y // LANES) + k] = whole[
                        :, k * LANES : (k + 1) * LANES
                    ]

    return sink


def prepare_kernel(place, angular_ref, source, receiver, mine, from_core, levels, *refs, shots):
    count = (len(refs) - 7) // 2
    tables, refs = refs[:count], refs[count:]
    wave_x, wave_y, top, mid, means, phases = refs[:6]
    kept, index = refs[6:-1], refs[-1]
    angular, my_core = angular_ref[0], place[1]
    for table, copy in zip(tables, kept):
        copy[...] = table[...]
    top[0:2] = source[0, 0]
    top[2:4] = receiver[0, 0]
    rows_x, rows_y = index.shape
    for p in range(shots):
        fill_index(index, (mine, from_core), my_core == p)
        if p == 0:
            forward_x(top, mid, tables[0])
        value = functools.reduce(jnp.add, lookup(levels[0:1, :], index[...]))
        base = jnp.sum(jnp.sum(value.reshape(rows_x // 8, 8, LANES), axis=0)) / (rows_x * rows_y)
        means[p : p + 1, :] = jnp.full((1, LANES), base, jnp.float32)
        fill_phases(angular, base, wave_x, wave_y, phases.at[p])


def lead_kernel(
    place, angular_ref, first, far_a, far_b, means, levels, left_x, right_x, left_y, right_y,
    wave_x, wave_y, before, mid, field, index, phases,
):
    angular, my_core = angular_ref[0], place[1]

    def put_plain(i, cols, kind, parts):
        part_x = extent(field)[0]
        for p, values in enumerate(parts):
            for j in range(2):
                before[2 * kind + j, p * part_x : (p + 1) * part_x, cols] = values[j]

    @pl.when(place[0] > 0)
    def _():
        fill_phases(angular, means[0:1, 0:1], wave_x, wave_y, phases)
        mid[...] = first[...]
        along_y(mid, phases, left_y, right_y)
        fill_index(index, (far_a, far_b), my_core == 0)
        tables = screen_tables(angular, means[0:1, 0:1], levels)
        inverse_x(mid, right_x, put_screened(tables, index, field))
        forward_x(field, mid, left_x)
        fill_phases(angular, means[1:2, 0:1], wave_x, wave_y, phases)
        along_y(mid, phases, left_y, right_y)
        inverse_x(mid, right_x, put_plain)


def planes_kernel(place, angular_ref, *refs, shots, strips, width, groups, later):
    refs = list(refs)
    top, before, far_a, far_b, far_means, near_a, near_b, means, phases, levels = refs[:10]
    left_x, right_x, left_y, right_y = refs[10:14]
    outs = refs[14:-4]
    field, mid, padded, index = refs[-4:]
    angular, my_core, parity, spot = angular_ref[0], place[1], place[2], place[3]

    @pl.when(place[0] == 0)
    def _():
        field[...] = top[...]

    @pl.when(place[0] > 0)
    def _():
        fill_index(index, (far_a, far_b), my_core == 1)
        tables = screen_tables(angular, far_means[1:2, 0:1], levels)
        block = 128

        def part(i, carry):
            rows = pl.ds(pl.multiple_of(i * block, block), block)
            cos, sin = screens_of(tables, index, rows, slice(None))
            for kind in range(2):
                new = turned(kind, before[2 * kind, rows], before[2 * kind + 1, rows], cos, sin)
                for j in range(2):
                    field[2 * kind + j, rows] = new[j].astype(jnp.bfloat16)
            return carry

        lax.fori_loop(0, index.shape[0] // block, part, 0)

    def emit(target, to):
        for s in range(strips):
            p = lax.rem(spot + (strips - 1 - s), strips)
            strip = jnp.where(p == 0, 0, jnp.where(p <= strips // 2, 2 * p - 1, 2 * (strips - p)))
            start = pl.multiple_of((2 * strip + to) * width, 16)
            for n, (first, last) in enumerate(groups if s == 0 else later):
                at = n if s == 0 else len(groups) + (s - 1) * len(later) + n
                out = outs[target * (len(groups) + (strips - 1) * len(later)) + at]
                for tile in range(first, last):
                    for part in range(4):
                        out[part, tile - first] = padded[part, tile, pl.ds(start, width + 2 * HALO)]

    for plane in range(shots):
        forward_x(field, mid, left_x)
        fill_index(index, (near_a, near_b), my_core == plane)
        along_y(mid, phases.at[plane], left_y, right_y)
        tables = screen_tables(angular, means[plane : plane + 1, 0:1], levels)
        inverse_x(mid, right_x, put_screened(tables, index, field, padded))

        @pl.when(my_core == plane)
        def _():
            emit(0, parity)
            emit(1, 1 - parity)

        @pl.when(my_core != plane)
        def _():
            emit(2, parity)
            emit(3, 1 - parity)


def correlate_kernel(*refs, width, begin, tiles, partial, scale):
    fields, out, wide = refs[:4], refs[-2], refs[-1]
    for tile in range(tiles):
        lanes = slice(tile * LANES, (tile + 1) * LANES)
        for m in range(4):
            for part in range(4):
                wide[m * 4 + part] = fields[m][part, begin + tile].astype(jnp.float32)
        for lag in range(2 * LAG + 1):
            shift = lag - LAG
            total = None
            for m in range(4):
                for part in range(2):
                    term = (
                        wide[m * 4 + part, HALO - shift : HALO - shift + width]
                        * wide[m * 4 + 2 + part, HALO + shift : HALO + shift + width]
                    )
                    total = term if total is None else total + term
            if partial:
                total = total + refs[4][lag, tile].astype(jnp.float32)
            if scale is not None:
                out[0, lag, :, lanes] = total * scale
            else:
                out[lag, tile] = total.astype(out.dtype)


def window_kernel(place, anchors, mine, other, out_mine, out_other):
    del place, anchors
    out_mine[...] = mine[0].astype(jnp.float32).astype(out_mine.dtype)
    out_other[...] = other[0].astype(jnp.float32).astype(out_other.dtype)


def pinned(x):
    return pltpu.with_memory_space_constraint(x, pltpu.VMEM)


def unpinned(x):
    return pltpu.with_memory_space_constraint(x, pltpu.HBM)


VMEM_SPEC = pl.BlockSpec(memory_space=pltpu.VMEM)


def call(kernel, name, scalars, operands, outs, scratch, flops):
    return pl.pallas_call(
        kernel,
        out_shape=[pltpu.VMEM(shape, dtype) for shape, dtype in outs],
        grid_spec=pltpu.PrefetchScalarGridSpec(
            num_scalar_prefetch=len(scalars),
            grid=(1,),
            in_specs=[VMEM_SPEC] * len(operands),
            out_specs=[VMEM_SPEC] * len(outs),
            scratch_shapes=scratch,
        ),
        compiler_params=pltpu.CompilerParams(vmem_limit_bytes=VMEM_BYTES),
        cost_estimate=pl.CostEstimate(flops=flops, bytes_accessed=10**6, transcendentals=0),
        name=name,
    )(*scalars, *(pinned(x) for x in operands))


def windows(place, anchors, slowness_codes, rows_x, rows_y):
    steps = 4
    rows = rows_x // steps

    def block(flip):
        def index(i, place, anchors):
            shot = jnp.abs(place[1] - flip)
            return (0, anchors[shot, 0] // rows + i, anchors[shot, 1] // rows_y)

        return pl.BlockSpec((1, rows, rows_y), index)

    code_spec = pl.BlockSpec((rows, rows_y), lambda i, place, anchors: (i, 0))
    return pl.pallas_call(
        window_kernel,
        out_shape=[
            pltpu.VMEM((rows_x, rows_y), jnp.bfloat16),
            pltpu.HBM((rows_x, rows_y), jnp.bfloat16),
        ],
        grid_spec=pltpu.PrefetchScalarGridSpec(
            num_scalar_prefetch=2,
            grid=(steps,),
            in_specs=[block(0), block(1)],
            out_specs=[code_spec, code_spec],
        ),
        name="windows",
    )(place, anchors, slowness_codes, slowness_codes)


def shards(source_top, receiver_top, slowness_codes, slowness_table, anchors):
    shots, _, _, rows_x, rows_y = source_top.shape
    freq_count = lax.axis_size("freq")
    depth_count = lax.axis_size("depth")
    strips = freq_count // 2
    width = rows_x // freq_count
    height = width + 2 * HALO
    lags = 2 * LAG + 1
    tiles = rows_y // LANES
    groups = [(0, tiles // 2), (tiles // 2, tiles)]
    later = groups
    factor = 1.0 / math.sqrt(2.0 * shots * freq_count)
    depth_index = lax.axis_index("depth")
    freq_index = lax.axis_index("freq")
    my_core = depth_index % shots
    group = depth_index // shots
    bf16, f32 = jnp.bfloat16, jnp.float32

    def number(group_at, core_at, strip_at, parity_at):
        return (group_at * shots + core_at) * freq_count + strip_at * 2 + parity_at

    def pairs(move, core):
        found = []
        for g in range(depth_count // shots):
            for c in range(shots):
                for z in range(strips):
                    for x in range(2):
                        to = move(g, c, z, x)
                        if core in (None, c) and to is not None:
                            found.append((number(g, c, z, x), number(*to)))
        return found

    def send(value, move, core=None):
        return lax.ppermute(value, AXES, pairs(move, core))

    def to_core(g, c, z, x):
        return (g, 1 - c, z, x)

    def to_same(g, c, z, x):
        return (g, c, z, 1 - x)

    def to_cross(g, c, z, x):
        return (g, 1 - c, z, 1 - x)

    def up(g, c, z, x):
        return (1, c, z, x) if g == 0 else None

    ring = [0] + list(range(1, strips, 2)) + list(range(2, strips, 2))[::-1]
    spots = {z: p for p, z in enumerate(ring)}

    def onward(g, c, z, x):
        return (g, c, ring[(spots[z] + 1) % strips], x)

    my_strip = freq_index // 2
    spot = jnp.where(
        my_strip == 0,
        0,
        jnp.where(my_strip % 2 == 1, (my_strip + 1) // 2, strips - my_strip // 2),
    )
    place = jnp.stack([group, my_core, freq_index % 2, spot]).astype(jnp.int32)
    angular = (math.pi * (0.45 + 0.5 * (freq_index.astype(f32) + 0.5) / freq_count))[None]
    scalars = (place, angular)

    mine, other = windows(place, anchors, slowness_codes, rows_x, rows_y)
    from_core = send(other, to_core)
    near = (mine, from_core)
    far_first = (send(mine, up, 0), send(from_core, up, 1))

    levels = jnp.pad(slowness_table, (0, LANES - slowness_table.shape[0]))[None]
    tables = []
    for length in (rows_x,) if rows_x == rows_y else (rows_x, rows_y):
        left = residue_tables(length)
        tables += [jnp.asarray(left), jnp.asarray(np.swapaxes(left, 1, 2))]
    wave_x = jnp.asarray(wavenumbers_squared(rows_x)[:, None])
    wave_y = jnp.asarray(wavenumbers_squared(rows_y)[None])
    whole = (4, rows_x, rows_y)
    phase_shape = (2, wave_x.shape[0], wave_y.shape[1])
    index_scratch = pltpu.VMEM((rows_x, rows_y), jnp.int32)
    top_spec = pl.BlockSpec(
        (1, 1, 2, rows_x, rows_y), lambda i, place, angular: (place[1], 0, 0, 0, 0)
    )
    prepared = pl.pallas_call(
        functools.partial(prepare_kernel, shots=shots),
        out_shape=[
            pltpu.VMEM(whole, bf16),
            pltpu.VMEM(whole, bf16),
            pltpu.VMEM((8, LANES), f32),
            pltpu.VMEM((shots, *phase_shape), f32),
            *(pltpu.VMEM(t.shape, t.dtype) for t in tables),
        ],
        grid_spec=pltpu.PrefetchScalarGridSpec(
            num_scalar_prefetch=2,
            grid=(1,),
            in_specs=[top_spec] * 2 + [VMEM_SPEC] * (5 + len(tables)),
            out_specs=[VMEM_SPEC] * (4 + len(tables)),
            scratch_shapes=[index_scratch],
        ),
        compiler_params=pltpu.CompilerParams(vmem_limit_bytes=VMEM_BYTES),
        cost_estimate=pl.CostEstimate(flops=4 * 10**9, bytes_accessed=10**6, transcendentals=0),
        name="prepare",
    )(
        *scalars, unpinned(source_top), unpinned(receiver_top), pinned(mine), pinned(from_core),
        levels, *(unpinned(t) for t in tables), wave_x, wave_y,
    )
    top, first, means, phases, *tables = prepared
    tables = list(tables) if len(tables) == 4 else list(tables) * 2

    far_means = send(means, up)
    mine_later, from_core_later, _ = lax.optimization_barrier((mine, from_core, means))
    far_second = (send(mine_later, up, 1), send(from_core_later, up, 0))

    (before,) = call(
        lead_kernel,
        "lead",
        scalars,
        [first, *far_first, far_means, levels, *tables, wave_x, wave_y],
        [(whole, f32)],
        [pltpu.VMEM(whole, bf16), pltpu.VMEM(whole, bf16), index_scratch, pltpu.VMEM(phase_shape, f32)],
        15 * 10**9,
    )
    sizes = [end - begin for begin, end in groups]
    sizes += [end - begin for begin, end in later] * (strips - 1)
    pieces = call(
        functools.partial(
            planes_kernel, shots=shots, strips=strips, width=width, groups=groups, later=later
        ),
        "planes",
        scalars,
        [top, before, *far_second, far_means, *near, means, phases, levels, *tables],
        [((4, size, height, LANES), bf16) for _ in range(4) for size in sizes],
        [
            pltpu.VMEM(whole, bf16),
            pltpu.VMEM(whole, bf16),
            pltpu.VMEM((4, tiles, rows_x + 2 * HALO, LANES), bf16),
            index_scratch,
        ],
        15 * 10**9,
    )

    def fetch(at):
        own, same, core, cross = (pieces[i * len(sizes) + at] for i in range(4))
        return [own, send(same, to_same), send(core, to_core), send(cross, to_cross)]

    def correlate(fields, received, begin, end, offset, last, buffer):
        count = end - begin
        operands = [pinned(x) for x in fields + received]
        in_specs = [VMEM_SPEC] * len(operands)
        aliases = {}
        if last:
            out_shape = jax.ShapeDtypeStruct((1, lags, width, rows_y), f32)
            out_spec = pl.BlockSpec(
                (1, lags, width, count * LANES), lambda i: (0, 0, 0, begin // count)
            )
            if buffer is not None:
                in_specs.append(pl.BlockSpec(memory_space=pl.ANY))
                aliases = {len(operands): 0}
                operands.append(buffer)
        else:
            out_shape = pltpu.VMEM((lags, count, width, LANES), bf16)
            out_spec = VMEM_SPEC
        return pl.pallas_call(
            functools.partial(
                correlate_kernel,
                width=width,
                begin=offset,
                tiles=count,
                partial=bool(received),
                scale=factor if last else None,
            ),
            out_shape=out_shape,
            grid=(1,),
            in_specs=in_specs,
            out_specs=out_spec,
            scratch_shapes=[pltpu.VMEM((16, height, LANES), f32)],
            input_output_aliases=aliases,
            compiler_params=pltpu.CompilerParams(vmem_limit_bytes=8 * 2**20),
            cost_estimate=pl.CostEstimate(flops=10**9, bytes_accessed=10**6, transcendentals=0),
            name="correlate",
        )(*operands)

    image = None
    received = [[]] * len(groups)
    for step in range(strips):
        last = step == strips - 1
        fields = {}
        for g, (begin, end) in enumerate(groups):
            if step == 0:
                at, offset = g, 0
            else:
                n = [n for n, cut in enumerate(later) if cut[0] <= begin < cut[1]][0]
                at, offset = len(groups) + (step - 1) * len(later) + n, begin - later[n][0]
            if at not in fields:
                fields[at] = fetch(at)
            parts = fields[at]
            result = correlate(parts, received[g], begin, end, offset, last, image)
            if last:
                image = result
            else:
                received[g] = [send(result, onward)]
    return image


def solution(mesh):
    return jax.shard_map(
        shards,
        mesh=mesh,
        in_specs=(
            P(None, "freq", None, None, None),
            P(None, "freq", None, None, None),
            P("depth", None, None),
            P(),
            P(),
        ),
        out_specs=P("depth", None, "freq", None),
        check_vma=False,
    )
```

time: 131 us -> 124 us (0.947)
  starting transfers between devices: 39.4 us -> 32.5 us
  local copies, waits for them, and re-layouts: 4.49 us -> 0.02 us
  Pallas kernels: 37.9 us -> 41.5 us
    ppermute x35 -> x36, starting transfers between devices: 39.4 us -> 32.5 us  [send(): return lax.ppermute(value, AXES, pairs(move, core))]
    unnamed x22 -> x8, local copies, waits for them, and re-layouts: 4.49 us -> 0.01 us
    pallas_call x10 -> x11, Pallas kernels: 34.6 us -> 37.2 us  [the longest x2 21.8 us: call(): pl.pallas_call(kernel, out_shape=[pltpu.VMEM(shape, dtype) for shape, dty...]
    ppermute x35 -> x36, waiting for transfers between devices: 48 us -> 49.1 us  [send(): return lax.ppermute(value, AXES, pairs(move, core))]
  transfers between devices with their start and end apart: 35 -> 36, of which waited for: 19 -> 22; matrix products, arithmetic and copies ran while one was open for 0% -> 0% of each run, Pallas kernels for 11% -> 19%
where the time goes in v5:
time: 124 us
  waiting for transfers between devices  49.1 us (40%)
  Pallas kernels  41.5 us (33%)
  starting transfers between devices  32.5 us (26%)
    ppermute x36, waiting for transfers between devices, send(): return lax.ppermute(value, AXES, pairs(move, core))  49.1 us
    ppermute x36, starting transfers between devices, send(): return lax.ppermute(value, AXES, pairs(move, core))  32.5 us
    pallas_call x2, Pallas kernels, call(): pl.pallas_call(kernel, out_shape=[pltpu.VMEM(shape, dtype) for shape, dty...  21.8 us
    pallas_call x8, Pallas kernels, correlate(): pl.pallas_call(functools.partial(correlate_kernel, width=width, begin=off...  8.15 us
    pallas_call x1, Pallas kernels, shards(): pl.pallas_call(functools.partial(prepare_kernel, shots=shots), out_shape=...  7.23 us
    pallas_call x1, Pallas kernels, windows(): pl.pallas_call(window_kernel, out_shape=[pltpu.VMEM((rows_x, rows_y), jnp...  4.35 us
  transfers between devices with their start and end apart: 36, of which 22 were waited for; matrix products, arithmetic and copies ran while one was open for 0% of the time, Pallas kernels for 19%

profile of v5, /device:TPU:4, one launch (start us, length us, event | category | flops | bytes accessed | tf_op | source)
XLA Modules:
  0.0 124.0 jit_solution(5380531216788639553)
XLA Ops:
  0.7 4.3 %windows.1 = (bf16[512,512]{1,0:T(8,128)(2,1)S(1)}, bf16[512,512]{1,0:T(8,128)(2,1)}) custom-call(s32[4]{0:T(128)} %pad_add_fusion.place, s32[2,2]{1,0:T(2,128)} %anchors.1, s32[1,1024,1024]{2,1,0:T(8,128)} %other.1, s32[1,1024,1024]{2,1,0:T(8,128)} %other.1), custom_call_target="tpu_custom_call" | custom-call | tf_op jit(solution)/shard_map/windows/pallas_call | solution.py:425
  5.0 1.3 %collective-permute-start.1 = (bf16[512,512]{1,0:T(8,128)(2,1)S(1)}, bf16[512,512]{1,0:T(8,128)(2,1)S(1)}, u32[]{:S(2)}, u32[]{:S(2)}) collective-permute-start(bf16[512,512]{1,0:T(8,128)(2,1)S(1)} %get-tuple-element.54.mine.refs_5_), channel_id=1, source_target_pairs={{0,16},{1,17},{2,18},{3,19},{4,20},{5,21},{6,22},{7,23}} | collective-permute-start | bytes 1572872 | tf_op jit(solution)/shard_map/ppermute | solution.py:474
  6.3 0.8 collective-permute-done.from_core.refs_6_
  7.9 7.2 %prepare.1 = (bf16[4,512,512]{2,1,0:T(8,128)(2,1)S(1)}, bf16[4,512,512]{2,1,0:T(8,128)(2,1)S(1)}, f32[8,128]{1,0:T(8,128)S(1)}, f32[2,2,384,384]{3,2,1,0:T(8,128...) custom-call(s32[4]{0:T(128)S(1)} %copy-done, f32[1]{0:T(128)} %bitcast.4.angular_ref, ...), custom_call_target="tpu_custom_call" | custom-call | flops 4000000000 | bytes 1000000 | tf_op jit(solution)/shard_map/prepare/pallas_call | solution.py:522
  15.1 1.3 %collective-permute-start.3 = (f32[8,128]{1,0:T(8,128)S(1)}, f32[8,128]{1,0:T(8,128)S(1)}, u32[]{:S(2)}, u32[]{:S(2)}) collective-permute-start(f32[8,128]{1,0:T(8,128)S(1)} %get-tuple-element.51.refs_7_), channel_id=1, source_target_pairs={{0,16},{1,17},{2,18},{3,19},{4,20},{5,21},{6,22},{7,23},{8,24},{9,... | collective-permute-start | bytes 12296 | tf_op jit(solution)/shard_map/ppermute | solution.py:474
  17.1 1.3 %collective-permute-start.5 = (bf16[512,512]{1,0:T(8,128)(2,1)S(1)}, bf16[512,512]{1,0:T(8,128)(2,1)S(1)}, u32[]{:S(2)}, u32[]{:S(2)}) collective-permute-start(bf16[512,512]{1,0:T(8,128)(2,1)S(1)} %collective-permute-done.from_core.refs_6_), channel_id=1, source_target_pairs={{0,16},{1,17},{2,18},{3,19},{4,20},{5,21},{6,22},{7,23}} | collective-permute-start | bytes 1572872 | tf_op jit(solution)/shard_map/ppermute | solution.py:474
  18.4 1.9 %collective-permute-done.1.far_a = bf16[512,512]{1,0:T(8,128)(2,1)S(1)} collective-permute-done((bf16[512,512]{1,0:T(8,128)(2,1)S(1)}, bf16[512,512]{1,0:T(8,128)(2,1)S(1)}, u32[]{:S(2)}, u32[]{:S(2)}) %collective-permute-start.1) | collective-permute-done | bytes 524320 | tf_op jit(solution)/shard_map/ppermute | solution.py:474
  20.7 9.9 %lead.1.refs_1_ = f32[4,512,512]{2,1,0:T(8,128)S(1)} custom-call(s32[4]{0:T(128)S(1)} %copy-done, f32[1]{0:T(128)} %bitcast.4.angular_ref, bf16[4,512,512]{2,1,0:T(8,128)(2,1)S(1)} %get-tuple-element.50.first, bf16[512,512]{1,0:T(8,128)(2,1)S(1)} %collective-permute-done.1.far_a, bf16[512,512]{1,0:T(8,128)(2,1)S(1)} %collective-permute-done.2.far_b, ...), custom_call_target="tpu_custom_call" | custom-call | flops 15000000512 | bytes 1000000 | tf_op jit(solution)/shard_map/lead/pallas_call | solution.py:397
  30.7 2.3 %collective-permute-done.5.refs_3_ = bf16[512,512]{1,0:T(8,128)(2,1)S(1)} collective-permute-done((bf16[512,512]{1,0:T(8,128)(2,1)S(1)}, bf16[512,512]{1,0:T(8,128)(2,1)S(1)}, u32[]{:S(2)}, u32[]{:S(2)}) %collective-permute-start.5) | collective-permute-done | bytes 524320 | tf_op jit(solution)/shard_map/ppermute | solution.py:474
  33.0 11.9 %planes.1 = (bf16[4,2,80,128]{3,2,1,0:T(8,128)(2,1)S(1)}, bf16[4,2,80,128]{3,2,1,0:T(8,128)(2,1)S(1)}, bf16[4,2,80,128]{3,2,1,0:T(8,128)(2,1)S(1)}, bf16[4,2,80,...) custom-call(s32[4]{0:T(128)S(1)} %copy-done, ...), custom_call_target="tpu_custom_call" | custom-call | flops 15000000512 | bytes 1000000 | tf_op jit(solution)/shard_map/planes/pallas_call | solution.py:397
  44.9 1.6 %collective-permute-start.30 = (bf16[4,2,80,128]{3,2,1,0:T(8,128)(2,1)S(1)}, bf16[4,2,80,128]{3,2,1,0:T(8,128)(2,1)S(1)}, u32[]{:S(2)}, u32[]{:S(2)}) collective-permute-start(bf16[4,2,80,128]{3,2,1,0:T(8,128)(2,1)S(1)} %get-tuple-element.86), channel_id=1, source_target_pairs={{0,1},{1,0},{2,3},{3,2},{4,5},{5,4},{6,7},{7,6},{8,9},{9,8},{10,11... | collective-permute-start | bytes 491528 | tf_op jit(solution)/shard_map/ppermute | solution.py:474
  47.1 1.5 %collective-permute-start.15 = (bf16[4,2,80,128]{3,2,1,0:T(8,128)(2,1)S(1)}, bf16[4,2,80,128]{3,2,1,0:T(8,128)(2,1)S(1)}, u32[]{:S(2)}, u32[]{:S(2)}) collective-permute-start(bf16[4,2,80,128]{3,2,1,0:T(8,128)(2,1)S(1)} %get-tuple-element.70), channel_id=1, source_target_pairs={{0,1},{1,0},{2,3},{3,2},{4,5},{5,4},{6,7},{7,6},{8,9},{9,8},{10,11... | collective-permute-start | bytes 491528 | tf_op jit(solution)/shard_map/ppermute | solution.py:474
  48.6 2.6 %collective-permute-done.30.refs_1_ = bf16[4,2,80,128]{3,2,1,0:T(8,128)(2,1)S(1)} collective-permute-done((bf16[4,2,80,128]{3,2,1,0:T(8,128)(2,1)S(1)}, bf16[4,2,80,128]{3,2,1,0:T(8,128)(2,1)S(1)}, u32[]{:S(2)}, u32[]{:S(2)}) %collective-permute-start.30) | collective-permute-done | bytes 163872 | tf_op jit(solution)/shard_map/ppermute | solution.py:474
  51.2 3.4 %collective-permute-done.32.refs_3_ = bf16[4,2,80,128]{3,2,1,0:T(8,128)(2,1)S(1)} collective-permute-done((bf16[4,2,80,128]{3,2,1,0:T(8,128)(2,1)S(1)}, bf16[4,2,80,128]{3,2,1,0:T(8,128)(2,1)S(1)}, u32[]{:S(2)}, u32[]{:S(2)}) %collective-permute-start.32) | collective-permute-done | bytes 163872 | tf_op jit(solution)/shard_map/ppermute | solution.py:474
  55.4 1.8 %collective-permute-start.33 = (bf16[15,2,64,128]{3,2,1,0:T(8,128)(2,1)S(1)}, bf16[15,2,64,128]{3,2,1,0:T(8,128)(2,1)S(1)}, u32[]{:S(2)}, u32[]{:S(2)}) collective-permute-start(bf16[15,2,64,128]{3,2,1,0:T(8,128)(2,1)S(1)} %correlate.11), channel_id=1, source_target_pairs={{0,2},{1,3},{2,6},{3,7},{4,0},{5,1},{6,4},{7,5},{8,10},{9,11},{10,... | collective-permute-start | bytes 1474568 | tf_op jit(solution)/shard_map/ppermute | solution.py:474
  57.2 1.0 collective-permute-done.15.refs_1_
  58.2 1.8 %collective-permute-done.17.refs_3_ = bf16[4,2,80,128]{3,2,1,0:T(8,128)(2,1)S(1)} collective-permute-done((bf16[4,2,80,128]{3,2,1,0:T(8,128)(2,1)S(1)}, bf16[4,2,80,128]{3,2,1,0:T(8,128)(2,1)S(1)}, u32[]{:S(2)}, u32[]{:S(2)}) %collective-permute-start.17) | collective-permute-done | bytes 163872 | tf_op jit(solution)/shard_map/ppermute | solution.py:474
  60.7 1.6 %collective-permute-start.18 = (bf16[15,2,64,128]{3,2,1,0:T(8,128)(2,1)S(1)}, bf16[15,2,64,128]{3,2,1,0:T(8,128)(2,1)S(1)}, u32[]{:S(2)}, u32[]{:S(2)}) collective-permute-start(bf16[15,2,64,128]{3,2,1,0:T(8,128)(2,1)S(1)} %correlate.8), channel_id=1, source_target_pairs={{0,2},{1,3},{2,6},{3,7},{4,0},{5,1},{6,4},{7,5},{8,10},{9,11},{10,... | collective-permute-start | bytes 1474568 | tf_op jit(solution)/shard_map/ppermute | solution.py:474
  63.0 1.3 %collective-permute-start.28 = (bf16[4,2,80,128]{3,2,1,0:T(8,128)(2,1)S(1)}, bf16[4,2,80,128]{3,2,1,0:T(8,128)(2,1)S(1)}, u32[]{:S(2)}, u32[]{:S(2)}) collective-permute-start(bf16[4,2,80,128]{3,2,1,0:T(8,128)(2,1)S(1)} %get-tuple-element.83), channel_id=1, source_target_pairs={{0,8},{1,9},{2,10},{3,11},{4,12},{5,13},{6,14},{7,15},{8,0},{9,1},... | collective-permute-start | bytes 491528 | tf_op jit(solution)/shard_map/ppermute | solution.py:474
  64.5 4.9 %collective-permute-done.27.refs_1_ = bf16[4,2,80,128]{3,2,1,0:T(8,128)(2,1)S(1)} collective-permute-done((bf16[4,2,80,128]{3,2,1,0:T(8,128)(2,1)S(1)}, bf16[4,2,80,128]{3,2,1,0:T(8,128)(2,1)S(1)}, u32[]{:S(2)}, u32[]{:S(2)}) %collective-permute-start.27) | collective-permute-done | bytes 163872 | tf_op jit(solution)/shard_map/ppermute | solution.py:474
  69.5 0.9 collective-permute-start.13
  70.5 2.0 %collective-permute-done.29.refs_3_ = bf16[4,2,80,128]{3,2,1,0:T(8,128)(2,1)S(1)} collective-permute-done((bf16[4,2,80,128]{3,2,1,0:T(8,128)(2,1)S(1)}, bf16[4,2,80,128]{3,2,1,0:T(8,128)(2,1)S(1)}, u32[]{:S(2)}, u32[]{:S(2)}) %collective-permute-start.29) | collective-permute-done | bytes 163872 | tf_op jit(solution)/shard_map/ppermute | solution.py:474
  72.7 0.8 correlate.12
  73.5 2.6 %collective-permute-start.34 = (bf16[15,2,64,128]{3,2,1,0:T(8,128)(2,1)S(1)}, bf16[15,2,64,128]{3,2,1,0:T(8,128)(2,1)S(1)}, u32[]{:S(2)}, u32[]{:S(2)}) collective-permute-start(bf16[15,2,64,128]{3,2,1,0:T(8,128)(2,1)S(1)} %correlate.12), channel_id=1, source_target_pairs={{0,2},{1,3},{2,6},{3,7},{4,0},{5,1},{6,4},{7,5},{8,10},{9,11},{10,... | collective-permute-start | bytes 1474568 | tf_op jit(solution)/shard_map/ppermute | solution.py:474
  76.6 2.8 %collective-permute-done.14.refs_3_ = bf16[4,2,80,128]{3,2,1,0:T(8,128)(2,1)S(1)} collective-permute-done((bf16[4,2,80,128]{3,2,1,0:T(8,128)(2,1)S(1)}, bf16[4,2,80,128]{3,2,1,0:T(8,128)(2,1)S(1)}, u32[]{:S(2)}, u32[]{:S(2)}) %collective-permute-start.14) | collective-permute-done | bytes 163872 | tf_op jit(solution)/shard_map/ppermute | solution.py:474
  79.4 1.8 %collective-permute-done.18.refs_4_ = bf16[15,2,64,128]{3,2,1,0:T(8,128)(2,1)S(1)} collective-permute-done((bf16[15,2,64,128]{3,2,1,0:T(8,128)(2,1)S(1)}, bf16[15,2,64,128]{3,2,1,0:T(8,128)(2,1)S(1)}, u32[]{:S(2)}, u32[]{:S(2)}) %collective-permute-start.18) | collective-permute-done | bytes 491552 | tf_op jit(solution)/shard_map/ppermute | solution.py:474
  81.2 0.8 correlate.9
  82.0 0.8 collective-permute-start.19
  82.8 1.2 collective-permute-start.24
  84.0 0.9 collective-permute-start.26
  84.9 4.9 %collective-permute-done.24.refs_1_ = bf16[4,2,80,128]{3,2,1,0:T(8,128)(2,1)S(1)} collective-permute-done((bf16[4,2,80,128]{3,2,1,0:T(8,128)(2,1)S(1)}, bf16[4,2,80,128]{3,2,1,0:T(8,128)(2,1)S(1)}, u32[]{:S(2)}, u32[]{:S(2)}) %collective-permute-start.24) | collective-permute-done | bytes 163872 | tf_op jit(solution)/shard_map/ppermute | solution.py:474
  89.8 1.2 collective-permute-start.9
  91.1 1.0 collective-permute-done.26.refs_3_
  92.1 2.2 %collective-permute-start.11 = (bf16[4,2,80,128]{3,2,1,0:T(8,128)(2,1)S(1)}, bf16[4,2,80,128]{3,2,1,0:T(8,128)(2,1)S(1)}, u32[]{:S(2)}, u32[]{:S(2)}) collective-permute-start(bf16[4,2,80,128]{3,2,1,0:T(8,128)(2,1)S(1)} %get-tuple-element.64), channel_id=1, source_target_pairs={{0,9},{1,8},{2,11},{3,10},{4,13},{5,12},{6,15},{7,14},{8,1},{9,0},... | collective-permute-start | bytes 491528 | tf_op jit(solution)/shard_map/ppermute | solution.py:474
  94.3 0.8 correlate.13
  95.1 1.9 %collective-permute-start.35 = (bf16[15,2,64,128]{3,2,1,0:T(8,128)(2,1)S(1)}, bf16[15,2,64,128]{3,2,1,0:T(8,128)(2,1)S(1)}, u32[]{:S(2)}, u32[]{:S(2)}) collective-permute-start(bf16[15,2,64,128]{3,2,1,0:T(8,128)(2,1)S(1)} %correlate.13), channel_id=1, source_target_pairs={{0,2},{1,3},{2,6},{3,7},{4,0},{5,1},{6,4},{7,5},{8,10},{9,11},{10,... | collective-permute-start | bytes 1474568 | tf_op jit(solution)/shard_map/ppermute | solution.py:474
  97.0 2.1 %collective-permute-done.11.refs_3_ = bf16[4,2,80,128]{3,2,1,0:T(8,128)(2,1)S(1)} collective-permute-done((bf16[4,2,80,128]{3,2,1,0:T(8,128)(2,1)S(1)}, bf16[4,2,80,128]{3,2,1,0:T(8,128)(2,1)S(1)}, u32[]{:S(2)}, u32[]{:S(2)}) %collective-permute-start.11) | collective-permute-done | bytes 163872 | tf_op jit(solution)/shard_map/ppermute | solution.py:474
  99.1 3.2 %collective-permute-done.19.refs_4_ = bf16[15,2,64,128]{3,2,1,0:T(8,128)(2,1)S(1)} collective-permute-done((bf16[15,2,64,128]{3,2,1,0:T(8,128)(2,1)S(1)}, bf16[15,2,64,128]{3,2,1,0:T(8,128)(2,1)S(1)}, u32[]{:S(2)}, u32[]{:S(2)}) %collective-permute-start.19) | collective-permute-done | bytes 491552 | tf_op jit(solution)/shard_map/ppermute | solution.py:474
  102.3 0.8 correlate.10
  103.0 0.8 collective-permute-start.20
  105.0 1.0 collective-permute-start.23
  106.0 5.0 %collective-permute-done.21.refs_1_ = bf16[4,2,80,128]{3,2,1,0:T(8,128)(2,1)S(1)} collective-permute-done((bf16[4,2,80,128]{3,2,1,0:T(8,128)(2,1)S(1)}, bf16[4,2,80,128]{3,2,1,0:T(8,128)(2,1)S(1)}, u32[]{:S(2)}, u32[]{:S(2)}) %collective-permute-start.21) | collective-permute-done | bytes 163872 | tf_op jit(solution)/shard_map/ppermute | solution.py:474
  111.6 1.0 collective-permute-done.23.refs_3_
  112.6 2.2 %collective-permute-start.8 = (bf16[4,2,80,128]{3,2,1,0:T(8,128)(2,1)S(1)}, bf16[4,2,80,128]{3,2,1,0:T(8,128)(2,1)S(1)}, u32[]{:S(2)}, u32[]{:S(2)}) collective-permute-start(bf16[4,2,80,128]{3,2,1,0:T(8,128)(2,1)S(1)} %get-tuple-element.60), channel_id=1, source_target_pairs={{0,9},{1,8},{2,11},{3,10},{4,13},{5,12},{6,15},{7,14},{8,1},{9,0},... | collective-permute-start | bytes 491528 | tf_op jit(solution)/shard_map/ppermute | solution.py:474
  114.8 1.8 %correlate.14.refs_5_ = f32[1,15,64,512]{3,2,1,0:T(8,128)} custom-call(bf16[4,2,80,128]{3,2,1,0:T(8,128)(2,1)S(1)} %get-tuple-element.73.refs_0_, bf16[4,2,80,128]{3,2,1,0:T(8,128)(2,1)S(1)} %collective-permute-done.21.refs_1_, bf16[4,2,80,128]{3,2,1,0:T(8,128)(2,1)S(1)} %collective-permute-done.22.refs_2_, ...), custom_call_target="tpu_custom_call" | custom-call | flops 1000000000 | bytes 1000000 | tf_op jit(solution)/shard_map/correlate/pallas_call | solution.py:601
  117.2 2.2 %collective-permute-done.8.refs_3_ = bf16[4,2,80,128]{3,2,1,0:T(8,128)(2,1)S(1)} collective-permute-done((bf16[4,2,80,128]{3,2,1,0:T(8,128)(2,1)S(1)}, bf16[4,2,80,128]{3,2,1,0:T(8,128)(2,1)S(1)}, u32[]{:S(2)}, u32[]{:S(2)}) %collective-permute-start.8) | collective-permute-done | bytes 163872 | tf_op jit(solution)/shard_map/ppermute | solution.py:474
  119.4 2.8 %collective-permute-done.20.refs_4_ = bf16[15,2,64,128]{3,2,1,0:T(8,128)(2,1)S(1)} collective-permute-done((bf16[15,2,64,128]{3,2,1,0:T(8,128)(2,1)S(1)}, bf16[15,2,64,128]{3,2,1,0:T(8,128)(2,1)S(1)}, u32[]{:S(2)}, u32[]{:S(2)}) %collective-permute-start.20) | collective-permute-done | bytes 491552 | tf_op jit(solution)/shard_map/ppermute | solution.py:474
  122.2 1.8 %correlate.15 = f32[1,15,64,512]{3,2,1,0:T(8,128)} custom-call(bf16[4,2,80,128]{3,2,1,0:T(8,128)(2,1)S(1)} %get-tuple-element.57.refs_0_, bf16[4,2,80,128]{3,2,1,0:T(8,128)(2,1)S(1)} %collective-permute-done.6.refs_1_, bf16[4,2,80,128]{3,2,1,0:T(8,128)(2,1)S(1)} %collective-permute-done.7.refs_2_, ...), custom_call_target="tpu_custom_call", output_to_operand_aliasing={{}: (5, {})} | custom-call | flops 1000000000 | bytes 1000000 | tf_op jit(solution)/shard_map/correlate/pallas_call | solution.py:601
  (46 shorter events, 8.5 us)
Async XLA Ops:
  0.7 7.2 %copy-start.3 = (f32[32]{0:T(128)S(1)}, f32[32]{0:T(128)}, u32[]{:S(2)}) copy-start(f32[32]{0:T(128)} %param.12) | copy-start | bytes 388
  0.7 7.2 %copy-start = (s32[4]{0:T(128)S(1)}, s32[4]{0:T(128)}, u32[]{:S(2)}) copy-start(s32[4]{0:T(128)} %pad_add_fusion.place) | copy-start | bytes 52
  0.7 7.2 %copy-start.1 = (f32[384,1]{1,0:T(8,128)S(1)}, f32[384,1]{1,0:T(8,128)}, u32[]{:S(2)}) copy-start(f32[384,1]{1,0:T(8,128)} %constant.87.clone.refs_2_.wave_x) | copy-start | bytes 4612
  0.7 7.2 %copy-start.2 = (f32[1,384]{1,0:T(1,128)S(1)}, f32[1,384]{1,0:T(1,128)}, u32[]{:S(2)}) copy-start(f32[1,384]{1,0:T(1,128)} %constant.88.clone.refs_3_.wave_y) | copy-start | bytes 4612
  5.0 2.1 %collective-permute-start = (bf16[512,512]{1,0:T(8,128)(2,1)}, bf16[512,512]{1,0:T(8,128)(2,1)S(1)}, u32[]{:S(2)}, u32[]{:S(2)}) collective-permute-start(bf16[512,512]{1,0:T(8,128)(2,1)} %get-tuple-element.48), channel_id=1, source_target_pairs={{0,8},{1,9},{2,10},{3,11},{4,12},{5,13},{6,14},{7,15},{8,0},{9,1},... | collective-permute-start | bytes 1572872 | tf_op jit(solution)/shard_map/ppermute | solution.py:474
  5.0 15.4 %collective-permute-start.1 = (bf16[512,512]{1,0:T(8,128)(2,1)S(1)}, bf16[512,512]{1,0:T(8,128)(2,1)S(1)}, u32[]{:S(2)}, u32[]{:S(2)}) collective-permute-start(bf16[512,512]{1,0:T(8,128)(2,1)S(1)} %get-tuple-element.54.mine.refs_5_), channel_id=1, source_target_pairs={{0,16},{1,17},{2,18},{3,19},{4,20},{5,21},{6,22},{7,23}} | collective-permute-start | bytes 1572872 | tf_op jit(solution)/shard_map/ppermute | solution.py:474
  7.1 13.6 %collective-permute-start.2 = (bf16[512,512]{1,0:T(8,128)(2,1)S(1)}, bf16[512,512]{1,0:T(8,128)(2,1)S(1)}, u32[]{:S(2)}, u32[]{:S(2)}) collective-permute-start(bf16[512,512]{1,0:T(8,128)(2,1)S(1)} %collective-permute-done.from_core.refs_6_), channel_id=1, source_target_pairs={{8,24},{9,25},{10,26},{11,27},{12,28},{13,29},{14,30},{15,31}} | collective-permute-start | bytes 1572872 | tf_op jit(solution)/shard_map/ppermute | solution.py:474
  15.1 5.6 %collective-permute-start.3 = (f32[8,128]{1,0:T(8,128)S(1)}, f32[8,128]{1,0:T(8,128)S(1)}, u32[]{:S(2)}, u32[]{:S(2)}) collective-permute-start(f32[8,128]{1,0:T(8,128)S(1)} %get-tuple-element.51.refs_7_), channel_id=1, source_target_pairs={{0,16},{1,17},{2,18},{3,19},{4,20},{5,21},{6,22},{7,23},{8,24},{9,... | collective-permute-start | bytes 12296 | tf_op jit(solution)/shard_map/ppermute | solution.py:474
  16.4 14.2 %collective-permute-start.4 = (bf16[512,512]{1,0:T(8,128)(2,1)S(1)}, bf16[512,512]{1,0:T(8,128)(2,1)S(1)}, u32[]{:S(2)}, u32[]{:S(2)}) collective-permute-start(bf16[512,512]{1,0:T(8,128)(2,1)S(1)} %get-tuple-element.54.mine.refs_5_), channel_id=1, source_target_pairs={{8,24},{9,25},{10,26},{11,27},{12,28},{13,29},{14,30},{15,31}} | collective-permute-start | bytes 1572872 | tf_op jit(solution)/shard_map/ppermute | solution.py:474
  17.1 15.9 %collective-permute-start.5 = (bf16[512,512]{1,0:T(8,128)(2,1)S(1)}, bf16[512,512]{1,0:T(8,128)(2,1)S(1)}, u32[]{:S(2)}, u32[]{:S(2)}) collective-permute-start(bf16[512,512]{1,0:T(8,128)(2,1)S(1)} %collective-permute-done.from_core.refs_6_), channel_id=1, source_target_pairs={{0,16},{1,17},{2,18},{3,19},{4,20},{5,21},{6,22},{7,23}} | collective-permute-start | bytes 1572872 | tf_op jit(solution)/shard_map/ppermute | solution.py:474
  44.9 6.3 %collective-permute-start.30 = (bf16[4,2,80,128]{3,2,1,0:T(8,128)(2,1)S(1)}, bf16[4,2,80,128]{3,2,1,0:T(8,128)(2,1)S(1)}, u32[]{:S(2)}, u32[]{:S(2)}) collective-permute-start(bf16[4,2,80,128]{3,2,1,0:T(8,128)(2,1)S(1)} %get-tuple-element.86), channel_id=1, source_target_pairs={{0,1},{1,0},{2,3},{3,2},{4,5},{5,4},{6,7},{7,6},{8,9},{9,8},{10,11... | collective-permute-start | bytes 491528 | tf_op jit(solution)/shard_map/ppermute | solution.py:474
  46.5 4.7 %collective-permute-start.31 = (bf16[4,2,80,128]{3,2,1,0:T(8,128)(2,1)S(1)}, bf16[4,2,80,128]{3,2,1,0:T(8,128)(2,1)S(1)}, u32[]{:S(2)}, u32[]{:S(2)}) collective-permute-start(bf16[4,2,80,128]{3,2,1,0:T(8,128)(2,1)S(1)} %get-tuple-element.87), channel_id=1, source_target_pairs={{0,8},{1,9},{2,10},{3,11},{4,12},{5,13},{6,14},{7,15},{8,0},{9,1},... | collective-permute-start | bytes 491528 | tf_op jit(solution)/shard_map/ppermute | solution.py:474
  46.5 8.2 %collective-permute-start.32 = (bf16[4,2,80,128]{3,2,1,0:T(8,128)(2,1)S(1)}, bf16[4,2,80,128]{3,2,1,0:T(8,128)(2,1)S(1)}, u32[]{:S(2)}, u32[]{:S(2)}) collective-permute-start(bf16[4,2,80,128]{3,2,1,0:T(8,128)(2,1)S(1)} %get-tuple-element.88), channel_id=1, source_target_pairs={{0,9},{1,8},{2,11},{3,10},{4,13},{5,12},{6,15},{7,14},{8,1},{9,0},... | collective-permute-start | bytes 491528 | tf_op jit(solution)/shard_map/ppermute | solution.py:474
  47.1 11.1 %collective-permute-start.15 = (bf16[4,2,80,128]{3,2,1,0:T(8,128)(2,1)S(1)}, bf16[4,2,80,128]{3,2,1,0:T(8,128)(2,1)S(1)}, u32[]{:S(2)}, u32[]{:S(2)}) collective-permute-start(bf16[4,2,80,128]{3,2,1,0:T(8,128)(2,1)S(1)} %get-tuple-element.70), channel_id=1, source_target_pairs={{0,1},{1,0},{2,3},{3,2},{4,5},{5,4},{6,7},{7,6},{8,9},{9,8},{10,11... | collective-permute-start | bytes 491528 | tf_op jit(solution)/shard_map/ppermute | solution.py:474
  48.6 9.6 %collective-permute-start.16 = (bf16[4,2,80,128]{3,2,1,0:T(8,128)(2,1)S(1)}, bf16[4,2,80,128]{3,2,1,0:T(8,128)(2,1)S(1)}, u32[]{:S(2)}, u32[]{:S(2)}) collective-permute-start(bf16[4,2,80,128]{3,2,1,0:T(8,128)(2,1)S(1)} %get-tuple-element.71), channel_id=1, source_target_pairs={{0,8},{1,9},{2,10},{3,11},{4,12},{5,13},{6,14},{7,15},{8,0},{9,1},... | collective-permute-start | bytes 491528 | tf_op jit(solution)/shard_map/ppermute | solution.py:474
  51.2 8.8 %collective-permute-start.17 = (bf16[4,2,80,128]{3,2,1,0:T(8,128)(2,1)S(1)}, bf16[4,2,80,128]{3,2,1,0:T(8,128)(2,1)S(1)}, u32[]{:S(2)}, u32[]{:S(2)}) collective-permute-start(bf16[4,2,80,128]{3,2,1,0:T(8,128)(2,1)S(1)} %get-tuple-element.72), channel_id=1, source_target_pairs={{0,9},{1,8},{2,11},{3,10},{4,13},{5,12},{6,15},{7,14},{8,1},{9,0},... | collective-permute-start | bytes 491528 | tf_op jit(solution)/shard_map/ppermute | solution.py:474
  55.4 17.4 %collective-permute-start.33 = (bf16[15,2,64,128]{3,2,1,0:T(8,128)(2,1)S(1)}, bf16[15,2,64,128]{3,2,1,0:T(8,128)(2,1)S(1)}, u32[]{:S(2)}, u32[]{:S(2)}) collective-permute-start(bf16[15,2,64,128]{3,2,1,0:T(8,128)(2,1)S(1)} %correlate.11), channel_id=1, source_target_pairs={{0,2},{1,3},{2,6},{3,7},{4,0},{5,1},{6,4},{7,5},{8,10},{9,11},{10,... | collective-permute-start | bytes 1474568 | tf_op jit(solution)/shard_map/ppermute | solution.py:474
  60.7 20.5 %collective-permute-start.18 = (bf16[15,2,64,128]{3,2,1,0:T(8,128)(2,1)S(1)}, bf16[15,2,64,128]{3,2,1,0:T(8,128)(2,1)S(1)}, u32[]{:S(2)}, u32[]{:S(2)}) collective-permute-start(bf16[15,2,64,128]{3,2,1,0:T(8,128)(2,1)S(1)} %correlate.8), channel_id=1, source_target_pairs={{0,2},{1,3},{2,6},{3,7},{4,0},{5,1},{6,4},{7,5},{8,10},{9,11},{10,... | collective-permute-start | bytes 1474568 | tf_op jit(solution)/shard_map/ppermute | solution.py:474
  62.4 7.1 %collective-permute-start.27 = (bf16[4,2,80,128]{3,2,1,0:T(8,128)(2,1)S(1)}, bf16[4,2,80,128]{3,2,1,0:T(8,128)(2,1)S(1)}, u32[]{:S(2)}, u32[]{:S(2)}) collective-permute-start(bf16[4,2,80,128]{3,2,1,0:T(8,128)(2,1)S(1)} %get-tuple-element.82), channel_id=1, source_target_pairs={{0,1},{1,0},{2,3},{3,2},{4,5},{5,4},{6,7},{7,6},{8,9},{9,8},{10,11... | collective-permute-start | bytes 491528 | tf_op jit(solution)/shard_map/ppermute | solution.py:474
  63.0 6.5 %collective-permute-start.28 = (bf16[4,2,80,128]{3,2,1,0:T(8,128)(2,1)S(1)}, bf16[4,2,80,128]{3,2,1,0:T(8,128)(2,1)S(1)}, u32[]{:S(2)}, u32[]{:S(2)}) collective-permute-start(bf16[4,2,80,128]{3,2,1,0:T(8,128)(2,1)S(1)} %get-tuple-element.83), channel_id=1, source_target_pairs={{0,8},{1,9},{2,10},{3,11},{4,12},{5,13},{6,14},{7,15},{8,0},{9,1},... | collective-permute-start | bytes 491528 | tf_op jit(solution)/shard_map/ppermute | solution.py:474
  64.3 8.2 %collective-permute-start.29 = (bf16[4,2,80,128]{3,2,1,0:T(8,128)(2,1)S(1)}, bf16[4,2,80,128]{3,2,1,0:T(8,128)(2,1)S(1)}, u32[]{:S(2)}, u32[]{:S(2)}) collective-permute-start(bf16[4,2,80,128]{3,2,1,0:T(8,128)(2,1)S(1)} %get-tuple-element.84), channel_id=1, source_target_pairs={{0,9},{1,8},{2,11},{3,10},{4,13},{5,12},{6,15},{7,14},{8,1},{9,0},... | collective-permute-start | bytes 491528 | tf_op jit(solution)/shard_map/ppermute | solution.py:474
  69.4 7.1 %collective-permute-start.12 = (bf16[4,2,80,128]{3,2,1,0:T(8,128)(2,1)S(1)}, bf16[4,2,80,128]{3,2,1,0:T(8,128)(2,1)S(1)}, u32[]{:S(2)}, u32[]{:S(2)}) collective-permute-start(bf16[4,2,80,128]{3,2,1,0:T(8,128)(2,1)S(1)} %get-tuple-element.66), channel_id=1, source_target_pairs={{0,1},{1,0},{2,3},{3,2},{4,5},{5,4},{6,7},{7,6},{8,9},{9,8},{10,11... | collective-permute-start | bytes 491528 | tf_op jit(solution)/shard_map/ppermute | solution.py:474
  69.5 7.0 %collective-permute-start.13 = (bf16[4,2,80,128]{3,2,1,0:T(8,128)(2,1)S(1)}, bf16[4,2,80,128]{3,2,1,0:T(8,128)(2,1)S(1)}, u32[]{:S(2)}, u32[]{:S(2)}) collective-permute-start(bf16[4,2,80,128]{3,2,1,0:T(8,128)(2,1)S(1)} %get-tuple-element.67), channel_id=1, source_target_pairs={{0,8},{1,9},{2,10},{3,11},{4,12},{5,13},{6,14},{7,15},{8,0},{9,1},... | collective-permute-start | bytes 491528 | tf_op jit(solution)/shard_map/ppermute | solution.py:474
  72.5 6.9 %collective-permute-start.14 = (bf16[4,2,80,128]{3,2,1,0:T(8,128)(2,1)S(1)}, bf16[4,2,80,128]{3,2,1,0:T(8,128)(2,1)S(1)}, u32[]{:S(2)}, u32[]{:S(2)}) collective-permute-start(bf16[4,2,80,128]{3,2,1,0:T(8,128)(2,1)S(1)} %get-tuple-element.68), channel_id=1, source_target_pairs={{0,9},{1,8},{2,11},{3,10},{4,13},{5,12},{6,15},{7,14},{8,1},{9,0},... | collective-permute-start | bytes 491528 | tf_op jit(solution)/shard_map/ppermute | solution.py:474
  73.5 20.8 %collective-permute-start.34 = (bf16[15,2,64,128]{3,2,1,0:T(8,128)(2,1)S(1)}, bf16[15,2,64,128]{3,2,1,0:T(8,128)(2,1)S(1)}, u32[]{:S(2)}, u32[]{:S(2)}) collective-permute-start(bf16[15,2,64,128]{3,2,1,0:T(8,128)(2,1)S(1)} %correlate.12), channel_id=1, source_target_pairs={{0,2},{1,3},{2,6},{3,7},{4,0},{5,1},{6,4},{7,5},{8,10},{9,11},{10,... | collective-permute-start | bytes 1474568 | tf_op jit(solution)/shard_map/ppermute | solution.py:474
  82.0 20.3 %collective-permute-start.19 = (bf16[15,2,64,128]{3,2,1,0:T(8,128)(2,1)S(1)}, bf16[15,2,64,128]{3,2,1,0:T(8,128)(2,1)S(1)}, u32[]{:S(2)}, u32[]{:S(2)}) collective-permute-start(bf16[15,2,64,128]{3,2,1,0:T(8,128)(2,1)S(1)} %correlate.9), channel_id=1, source_target_pairs={{0,2},{1,3},{2,6},{3,7},{4,0},{5,1},{6,4},{7,5},{8,10},{9,11},{10,... | collective-permute-start | bytes 1474568 | tf_op jit(solution)/shard_map/ppermute | solution.py:474
  82.8 7.0 %collective-permute-start.24 = (bf16[4,2,80,128]{3,2,1,0:T(8,128)(2,1)S(1)}, bf16[4,2,80,128]{3,2,1,0:T(8,128)(2,1)S(1)}, u32[]{:S(2)}, u32[]{:S(2)}) collective-permute-start(bf16[4,2,80,128]{3,2,1,0:T(8,128)(2,1)S(1)} %get-tuple-element.78), channel_id=1, source_target_pairs={{0,1},{1,0},{2,3},{3,2},{4,5},{5,4},{6,7},{7,6},{8,9},{9,8},{10,11... | collective-permute-start | bytes 491528 | tf_op jit(solution)/shard_map/ppermute | solution.py:474
  84.0 7.0 %collective-permute-start.25 = (bf16[4,2,80,128]{3,2,1,0:T(8,128)(2,1)S(1)}, bf16[4,2,80,128]{3,2,1,0:T(8,128)(2,1)S(1)}, u32[]{:S(2)}, u32[]{:S(2)}) collective-permute-start(bf16[4,2,80,128]{3,2,1,0:T(8,128)(2,1)S(1)} %get-tuple-element.79), channel_id=1, source_target_pairs={{0,8},{1,9},{2,10},{3,11},{4,12},{5,13},{6,14},{7,15},{8,0},{9,1},... | collective-permute-start | bytes 491528 | tf_op jit(solution)/shard_map/ppermute | solution.py:474
  84.0 8.1 %collective-permute-start.26 = (bf16[4,2,80,128]{3,2,1,0:T(8,128)(2,1)S(1)}, bf16[4,2,80,128]{3,2,1,0:T(8,128)(2,1)S(1)}, u32[]{:S(2)}, u32[]{:S(2)}) collective-permute-start(bf16[4,2,80,128]{3,2,1,0:T(8,128)(2,1)S(1)} %get-tuple-element.80), channel_id=1, source_target_pairs={{0,9},{1,8},{2,11},{3,10},{4,13},{5,12},{6,15},{7,14},{8,1},{9,0},... | collective-permute-start | bytes 491528 | tf_op jit(solution)/shard_map/ppermute | solution.py:474
  89.8 7.1 %collective-permute-start.9 = (bf16[4,2,80,128]{3,2,1,0:T(8,128)(2,1)S(1)}, bf16[4,2,80,128]{3,2,1,0:T(8,128)(2,1)S(1)}, u32[]{:S(2)}, u32[]{:S(2)}) collective-permute-start(bf16[4,2,80,128]{3,2,1,0:T(8,128)(2,1)S(1)} %get-tuple-element.62), channel_id=1, source_target_pairs={{0,1},{1,0},{2,3},{3,2},{4,5},{5,4},{6,7},{7,6},{8,9},{9,8},{10,11... | collective-permute-start | bytes 491528 | tf_op jit(solution)/shard_map/ppermute | solution.py:474
  91.1 5.9 %collective-permute-start.10 = (bf16[4,2,80,128]{3,2,1,0:T(8,128)(2,1)S(1)}, bf16[4,2,80,128]{3,2,1,0:T(8,128)(2,1)S(1)}, u32[]{:S(2)}, u32[]{:S(2)}) collective-permute-start(bf16[4,2,80,128]{3,2,1,0:T(8,128)(2,1)S(1)} %get-tuple-element.63), channel_id=1, source_target_pairs={{0,8},{1,9},{2,10},{3,11},{4,12},{5,13},{6,14},{7,15},{8,0},{9,1},... | collective-permute-start | bytes 491528 | tf_op jit(solution)/shard_map/ppermute | solution.py:474
  92.1 7.0 %collective-permute-start.11 = (bf16[4,2,80,128]{3,2,1,0:T(8,128)(2,1)S(1)}, bf16[4,2,80,128]{3,2,1,0:T(8,128)(2,1)S(1)}, u32[]{:S(2)}, u32[]{:S(2)}) collective-permute-start(bf16[4,2,80,128]{3,2,1,0:T(8,128)(2,1)S(1)} %get-tuple-element.64), channel_id=1, source_target_pairs={{0,9},{1,8},{2,11},{3,10},{4,13},{5,12},{6,15},{7,14},{8,1},{9,0},... | collective-permute-start | bytes 491528 | tf_op jit(solution)/shard_map/ppermute | solution.py:474
  95.1 19.7 %collective-permute-start.35 = (bf16[15,2,64,128]{3,2,1,0:T(8,128)(2,1)S(1)}, bf16[15,2,64,128]{3,2,1,0:T(8,128)(2,1)S(1)}, u32[]{:S(2)}, u32[]{:S(2)}) collective-permute-start(bf16[15,2,64,128]{3,2,1,0:T(8,128)(2,1)S(1)} %correlate.13), channel_id=1, source_target_pairs={{0,2},{1,3},{2,6},{3,7},{4,0},{5,1},{6,4},{7,5},{8,10},{9,11},{10,... | collective-permute-start | bytes 1474568 | tf_op jit(solution)/shard_map/ppermute | solution.py:474
  103.0 19.2 %collective-permute-start.20 = (bf16[15,2,64,128]{3,2,1,0:T(8,128)(2,1)S(1)}, bf16[15,2,64,128]{3,2,1,0:T(8,128)(2,1)S(1)}, u32[]{:S(2)}, u32[]{:S(2)}) collective-permute-start(bf16[15,2,64,128]{3,2,1,0:T(8,128)(2,1)S(1)} %correlate.10), channel_id=1, source_target_pairs={{0,2},{1,3},{2,6},{3,7},{4,0},{5,1},{6,4},{7,5},{8,10},{9,11},{10,... | collective-permute-start | bytes 1474568 | tf_op jit(solution)/shard_map/ppermute | solution.py:474
  103.9 7.1 %collective-permute-start.21 = (bf16[4,2,80,128]{3,2,1,0:T(8,128)(2,1)S(1)}, bf16[4,2,80,128]{3,2,1,0:T(8,128)(2,1)S(1)}, u32[]{:S(2)}, u32[]{:S(2)}) collective-permute-start(bf16[4,2,80,128]{3,2,1,0:T(8,128)(2,1)S(1)} %get-tuple-element.74), channel_id=1, source_target_pairs={{0,1},{1,0},{2,3},{3,2},{4,5},{5,4},{6,7},{7,6},{8,9},{9,8},{10,11... | collective-permute-start | bytes 491528 | tf_op jit(solution)/shard_map/ppermute | solution.py:474
  104.5 7.1 %collective-permute-start.22 = (bf16[4,2,80,128]{3,2,1,0:T(8,128)(2,1)S(1)}, bf16[4,2,80,128]{3,2,1,0:T(8,128)(2,1)S(1)}, u32[]{:S(2)}, u32[]{:S(2)}) collective-permute-start(bf16[4,2,80,128]{3,2,1,0:T(8,128)(2,1)S(1)} %get-tuple-element.75), channel_id=1, source_target_pairs={{0,8},{1,9},{2,10},{3,11},{4,12},{5,13},{6,14},{7,15},{8,0},{9,1},... | collective-permute-start | bytes 491528 | tf_op jit(solution)/shard_map/ppermute | solution.py:474
  105.0 7.6 %collective-permute-start.23 = (bf16[4,2,80,128]{3,2,1,0:T(8,128)(2,1)S(1)}, bf16[4,2,80,128]{3,2,1,0:T(8,128)(2,1)S(1)}, u32[]{:S(2)}, u32[]{:S(2)}) collective-permute-start(bf16[4,2,80,128]{3,2,1,0:T(8,128)(2,1)S(1)} %get-tuple-element.76), channel_id=1, source_target_pairs={{0,9},{1,8},{2,11},{3,10},{4,13},{5,12},{6,15},{7,14},{8,1},{9,0},... | collective-permute-start | bytes 491528 | tf_op jit(solution)/shard_map/ppermute | solution.py:474
  111.0 6.2 %collective-permute-start.6 = (bf16[4,2,80,128]{3,2,1,0:T(8,128)(2,1)S(1)}, bf16[4,2,80,128]{3,2,1,0:T(8,128)(2,1)S(1)}, u32[]{:S(2)}, u32[]{:S(2)}) collective-permute-start(bf16[4,2,80,128]{3,2,1,0:T(8,128)(2,1)S(1)} %get-tuple-element.58), channel_id=1, source_target_pairs={{0,1},{1,0},{2,3},{3,2},{4,5},{5,4},{6,7},{7,6},{8,9},{9,8},{10,11... | collective-permute-start | bytes 491528 | tf_op jit(solution)/shard_map/ppermute | solution.py:474
  111.5 5.7 %collective-permute-start.7 = (bf16[4,2,80,128]{3,2,1,0:T(8,128)(2,1)S(1)}, bf16[4,2,80,128]{3,2,1,0:T(8,128)(2,1)S(1)}, u32[]{:S(2)}, u32[]{:S(2)}) collective-permute-start(bf16[4,2,80,128]{3,2,1,0:T(8,128)(2,1)S(1)} %get-tuple-element.59), channel_id=1, source_target_pairs={{0,8},{1,9},{2,10},{3,11},{4,12},{5,13},{6,14},{7,15},{8,0},{9,1},... | collective-permute-start | bytes 491528 | tf_op jit(solution)/shard_map/ppermute | solution.py:474
  112.6 6.9 %collective-permute-start.8 = (bf16[4,2,80,128]{3,2,1,0:T(8,128)(2,1)S(1)}, bf16[4,2,80,128]{3,2,1,0:T(8,128)(2,1)S(1)}, u32[]{:S(2)}, u32[]{:S(2)}) collective-permute-start(bf16[4,2,80,128]{3,2,1,0:T(8,128)(2,1)S(1)} %get-tuple-element.60), channel_id=1, source_target_pairs={{0,9},{1,8},{2,11},{3,10},{4,13},{5,12},{6,15},{7,14},{8,1},{9,0},... | collective-permute-start | bytes 491528 | tf_op jit(solution)/shard_map/ppermute | solution.py:474

commit v6 on v5

--- a/solution.py
+++ b/solution.py
@@ -376,10 +376,27 @@
                 out[lag, tile] = total.astype(out.dtype)
 
 
-def window_kernel(place, anchors, mine, other, out_mine, out_other):
-    del place, anchors
-    out_mine[...] = mine[0].astype(jnp.float32).astype(out_mine.dtype)
-    out_other[...] = other[0].astype(jnp.float32).astype(out_other.dtype)
+def window_kernel(place, anchors, codes, mine, other, held, arrived, *, blocks):
+    rows_x, rows_y = mine.shape
+    rows = rows_x // blocks
+    copies = []
+    for i in range(blocks):
+        for flip in range(2):
+            shot = jnp.abs(place[1] - flip)
+            at_x = pl.multiple_of(anchors[shot, 0] // rows_x * rows_x, rows_x) + i * rows
+            at_y = pl.multiple_of(anchors[shot, 1] // rows_y * rows_y, rows_y)
+            copy = pltpu.make_async_copy(
+                codes.at[0, pl.ds(at_x, rows), pl.ds(at_y, rows_y)],
+                held.at[flip, pl.ds(i * rows, rows)],
+                arrived.at[flip, i],
+            )
+            copy.start()
+            copies.append(copy)
+    for i in range(blocks):
+        for flip, out in enumerate((mine, other)):
+            copies[2 * i + flip].wait()
+            at = slice(i * rows, (i + 1) * rows)
+            out[at] = held[flip, at].astype(jnp.float32).astype(out.dtype)
 
 
 def pinned(x):
@@ -411,31 +428,26 @@
 
 
 def windows(place, anchors, slowness_codes, rows_x, rows_y):
-    steps = 4
-    rows = rows_x // steps
-
-    def block(flip):
-        def index(i, place, anchors):
-            shot = jnp.abs(place[1] - flip)
-            return (0, anchors[shot, 0] // rows + i, anchors[shot, 1] // rows_y)
-
-        return pl.BlockSpec((1, rows, rows_y), index)
-
-    code_spec = pl.BlockSpec((rows, rows_y), lambda i, place, anchors: (i, 0))
+    blocks = 4
     return pl.pallas_call(
-        window_kernel,
+        functools.partial(window_kernel, blocks=blocks),
         out_shape=[
             pltpu.VMEM((rows_x, rows_y), jnp.bfloat16),
             pltpu.HBM((rows_x, rows_y), jnp.bfloat16),
         ],
         grid_spec=pltpu.PrefetchScalarGridSpec(
             num_scalar_prefetch=2,
-            grid=(steps,),
-            in_specs=[block(0), block(1)],
-            out_specs=[code_spec, code_spec],
+            grid=(1,),
+            in_specs=[pl.BlockSpec(memory_space=pl.ANY)],
+            out_specs=[VMEM_SPEC, VMEM_SPEC],
+            scratch_shapes=[
+                pltpu.VMEM((2, rows_x, rows_y), jnp.int32),
+                pltpu.SemaphoreType.DMA((2, blocks)),
+            ],
         ),
+        compiler_params=pltpu.CompilerParams(vmem_limit_bytes=VMEM_BYTES),
         name="windows",
-    )(place, anchors, slowness_codes, slowness_codes)
+    )(place, anchors, unpinned(slowness_codes))
 
 
 def shards(source_top, receiver_top, slowness_codes, slowness_table, anchors):
@@ -581,10 +593,13 @@
         own, same, core, cross = (pieces[i * len(sizes) + at] for i in range(4))
         return [own, send(same, to_same), send(core, to_core), send(cross, to_cross)]
 
-    def correlate(fields, received, begin, end, offset, last, buffer):
+    def correlate(fields, received, begin, end, offset, last, buffer, before):
         count = end - begin
         operands = [pinned(x) for x in fields + received]
         in_specs = [VMEM_SPEC] * len(operands)
+        if before is not None and False:
+            operands.append(pinned(before))
+            in_specs.append(VMEM_SPEC)
         aliases = {}
         if last:
             out_shape = jax.ShapeDtypeStruct((1, lags, width, rows_y), f32)
@@ -619,6 +634,7 @@
         )(*operands)
 
     image = None
+    before = None
     received = [[]] * len(groups)
     for step in range(strips):
         last = step == strips - 1
@@ -632,10 +648,12 @@
             if at not in fields:
                 fields[at] = fetch(at)
             parts = fields[at]
-            result = correlate(parts, received[g], begin, end, offset, last, image)
+            result = correlate(parts, received[g], begin, end, offset, last, image, before)
             if last:
                 image = result
+                before = None
             else:
+                before = result
                 received[g] = [send(result, onward)]
     return image
 

time: 124 us -> 123 us (level)
  Pallas kernels: 41.5 us -> 40.2 us
    pallas_call x1, Pallas kernels: 4.35 us -> 2.97 us  [windows(): pl.pallas_call(functools.partial(window_kernel, blocks=blocks), out_shape...]
where the time goes in v6:
time: 123 us
  waiting for transfers between devices  49.1 us (40%)
  Pallas kernels  40.2 us (33%)
  starting transfers between devices  32.7 us (27%)
    ppermute x36, waiting for transfers between devices, send(): return lax.ppermute(value, AXES, pairs(move, core))  49.1 us
    ppermute x36, starting transfers between devices, send(): return lax.ppermute(value, AXES, pairs(move, core))  32.7 us
    pallas_call x2, Pallas kernels, call(): pl.pallas_call(kernel, out_shape=[pltpu.VMEM(shape, dtype) for shape, dty...  21.8 us
    pallas_call x8, Pallas kernels, correlate(): pl.pallas_call(functools.partial(correlate_kernel, width=width, begin=off...  8.15 us
    pallas_call x1, Pallas kernels, shards(): pl.pallas_call(functools.partial(prepare_kernel, shots=shots), out_shape=...  7.23 us
    pallas_call x1, Pallas kernels, windows(): pl.pallas_call(functools.partial(window_kernel, blocks=blocks), out_shape...  2.97 us
  transfers between devices with their start and end apart: 36, of which 22 were waited for; matrix products, arithmetic and copies ran while one was open for 0% of the time, Pallas kernels for 19%

profile of v6, /device:TPU:4, one launch (start us, length us, event | category | flops | bytes accessed | tf_op | source)
XLA Modules:
  0.0 122.9 jit_solution(9826076748366068228)
XLA Ops:
  0.8 3.0 %windows.1 = (bf16[512,512]{1,0:T(8,128)(2,1)S(1)}, bf16[512,512]{1,0:T(8,128)(2,1)}) custom-call(s32[4]{0:T(128)S(1)} %pad_add_fusion.place, s32[2,2]{1,0:T(2,128)S(1)} %copy-done, s32[1,1024,1024]{2,1,0:T(8,128)} %codes.1), custom_call_target="tpu_custom_call" | custom-call | tf_op jit(solution)/shard_map/windows/pallas_call | solution.py:432
  3.8 1.3 %collective-permute-start.1 = (bf16[512,512]{1,0:T(8,128)(2,1)S(1)}, bf16[512,512]{1,0:T(8,128)(2,1)S(1)}, u32[]{:S(2)}, u32[]{:S(2)}) collective-permute-start(bf16[512,512]{1,0:T(8,128)(2,1)S(1)} %get-tuple-element.54.mine.refs_5_), channel_id=1, source_target_pairs={{0,16},{1,17},{2,18},{3,19},{4,20},{5,21},{6,22},{7,23}} | collective-permute-start | bytes 1572872 | tf_op jit(solution)/shard_map/ppermute | solution.py:486
  5.1 0.8 collective-permute-done.from_core.refs_6_
  6.7 7.2 %prepare.1 = (bf16[4,512,512]{2,1,0:T(8,128)(2,1)S(1)}, bf16[4,512,512]{2,1,0:T(8,128)(2,1)S(1)}, f32[8,128]{1,0:T(8,128)S(1)}, f32[2,2,384,384]{3,2,1,0:T(8,128...) custom-call(s32[4]{0:T(128)S(1)} %pad_add_fusion.place, f32[1]{0:T(128)} %bitcast.4.angular_ref, ...), custom_call_target="tpu_custom_call" | custom-call | flops 4000000000 | bytes 1000000 | tf_op jit(solution)/shard_map/prepare/pallas_call | solution.py:534
  13.9 1.3 %collective-permute-start.3 = (f32[8,128]{1,0:T(8,128)S(1)}, f32[8,128]{1,0:T(8,128)S(1)}, u32[]{:S(2)}, u32[]{:S(2)}) collective-permute-start(f32[8,128]{1,0:T(8,128)S(1)} %get-tuple-element.51.refs_7_), channel_id=1, source_target_pairs={{0,16},{1,17},{2,18},{3,19},{4,20},{5,21},{6,22},{7,23},{8,24},{9,... | collective-permute-start | bytes 12296 | tf_op jit(solution)/shard_map/ppermute | solution.py:486
  15.9 1.3 %collective-permute-start.5 = (bf16[512,512]{1,0:T(8,128)(2,1)S(1)}, bf16[512,512]{1,0:T(8,128)(2,1)S(1)}, u32[]{:S(2)}, u32[]{:S(2)}) collective-permute-start(bf16[512,512]{1,0:T(8,128)(2,1)S(1)} %collective-permute-done.from_core.refs_6_), channel_id=1, source_target_pairs={{0,16},{1,17},{2,18},{3,19},{4,20},{5,21},{6,22},{7,23}} | collective-permute-start | bytes 1572872 | tf_op jit(solution)/shard_map/ppermute | solution.py:486
  17.2 2.0 %collective-permute-done.1.far_a = bf16[512,512]{1,0:T(8,128)(2,1)S(1)} collective-permute-done((bf16[512,512]{1,0:T(8,128)(2,1)S(1)}, bf16[512,512]{1,0:T(8,128)(2,1)S(1)}, u32[]{:S(2)}, u32[]{:S(2)}) %collective-permute-start.1) | collective-permute-done | bytes 524320 | tf_op jit(solution)/shard_map/ppermute | solution.py:486
  19.5 9.9 %lead.1.refs_1_ = f32[4,512,512]{2,1,0:T(8,128)S(1)} custom-call(s32[4]{0:T(128)S(1)} %pad_add_fusion.place, f32[1]{0:T(128)} %bitcast.4.angular_ref, bf16[4,512,512]{2,1,0:T(8,128)(2,1)S(1)} %get-tuple-element.50.first, bf16[512,512]{1,0:T(8,128)(2,1)S(1)} %collective-permute-done.1.far_a, bf16[512,512]{1,0:T(8,128)(2,1)S(1)} %collective-permute-done.2.far_b, ...), custom_call_target="tpu_custom_call" | custom-call | flops 15000000512 | bytes 1000000 | tf_op jit(solution)/shard_map/lead/pallas_call | solution.py:414
  29.5 2.4 %collective-permute-done.5.refs_3_ = bf16[512,512]{1,0:T(8,128)(2,1)S(1)} collective-permute-done((bf16[512,512]{1,0:T(8,128)(2,1)S(1)}, bf16[512,512]{1,0:T(8,128)(2,1)S(1)}, u32[]{:S(2)}, u32[]{:S(2)}) %collective-permute-start.5) | collective-permute-done | bytes 524320 | tf_op jit(solution)/shard_map/ppermute | solution.py:486
  31.8 11.9 %planes.1 = (bf16[4,2,80,128]{3,2,1,0:T(8,128)(2,1)S(1)}, bf16[4,2,80,128]{3,2,1,0:T(8,128)(2,1)S(1)}, bf16[4,2,80,128]{3,2,1,0:T(8,128)(2,1)S(1)}, bf16[4,2,80,...) custom-call(s32[4]{0:T(128)S(1)} %pad_add_fusion.place, ...), custom_call_target="tpu_custom_call" | custom-call | flops 15000000512 | bytes 1000000 | tf_op jit(solution)/shard_map/planes/pallas_call | solution.py:414
  43.7 1.6 %collective-permute-start.30 = (bf16[4,2,80,128]{3,2,1,0:T(8,128)(2,1)S(1)}, bf16[4,2,80,128]{3,2,1,0:T(8,128)(2,1)S(1)}, u32[]{:S(2)}, u32[]{:S(2)}) collective-permute-start(bf16[4,2,80,128]{3,2,1,0:T(8,128)(2,1)S(1)} %get-tuple-element.86), channel_id=1, source_target_pairs={{0,1},{1,0},{2,3},{3,2},{4,5},{5,4},{6,7},{7,6},{8,9},{9,8},{10,11... | collective-permute-start | bytes 491528 | tf_op jit(solution)/shard_map/ppermute | solution.py:486
  45.9 1.5 %collective-permute-start.15 = (bf16[4,2,80,128]{3,2,1,0:T(8,128)(2,1)S(1)}, bf16[4,2,80,128]{3,2,1,0:T(8,128)(2,1)S(1)}, u32[]{:S(2)}, u32[]{:S(2)}) collective-permute-start(bf16[4,2,80,128]{3,2,1,0:T(8,128)(2,1)S(1)} %get-tuple-element.70), channel_id=1, source_target_pairs={{0,1},{1,0},{2,3},{3,2},{4,5},{5,4},{6,7},{7,6},{8,9},{9,8},{10,11... | collective-permute-start | bytes 491528 | tf_op jit(solution)/shard_map/ppermute | solution.py:486
  47.4 2.6 %collective-permute-done.30.refs_1_ = bf16[4,2,80,128]{3,2,1,0:T(8,128)(2,1)S(1)} collective-permute-done((bf16[4,2,80,128]{3,2,1,0:T(8,128)(2,1)S(1)}, bf16[4,2,80,128]{3,2,1,0:T(8,128)(2,1)S(1)}, u32[]{:S(2)}, u32[]{:S(2)}) %collective-permute-start.30) | collective-permute-done | bytes 163872 | tf_op jit(solution)/shard_map/ppermute | solution.py:486
  50.1 3.4 %collective-permute-done.32.refs_3_ = bf16[4,2,80,128]{3,2,1,0:T(8,128)(2,1)S(1)} collective-permute-done((bf16[4,2,80,128]{3,2,1,0:T(8,128)(2,1)S(1)}, bf16[4,2,80,128]{3,2,1,0:T(8,128)(2,1)S(1)}, u32[]{:S(2)}, u32[]{:S(2)}) %collective-permute-start.32) | collective-permute-done | bytes 163872 | tf_op jit(solution)/shard_map/ppermute | solution.py:486
  54.2 1.8 %collective-permute-start.33 = (bf16[15,2,64,128]{3,2,1,0:T(8,128)(2,1)S(1)}, bf16[15,2,64,128]{3,2,1,0:T(8,128)(2,1)S(1)}, u32[]{:S(2)}, u32[]{:S(2)}) collective-permute-start(bf16[15,2,64,128]{3,2,1,0:T(8,128)(2,1)S(1)} %correlate.11), channel_id=1, source_target_pairs={{0,2},{1,3},{2,6},{3,7},{4,0},{5,1},{6,4},{7,5},{8,10},{9,11},{10,... | collective-permute-start | bytes 1474568 | tf_op jit(solution)/shard_map/ppermute | solution.py:486
  56.1 1.0 collective-permute-done.15.refs_1_
  57.1 1.7 %collective-permute-done.17.refs_3_ = bf16[4,2,80,128]{3,2,1,0:T(8,128)(2,1)S(1)} collective-permute-done((bf16[4,2,80,128]{3,2,1,0:T(8,128)(2,1)S(1)}, bf16[4,2,80,128]{3,2,1,0:T(8,128)(2,1)S(1)}, u32[]{:S(2)}, u32[]{:S(2)}) %collective-permute-start.17) | collective-permute-done | bytes 163872 | tf_op jit(solution)/shard_map/ppermute | solution.py:486
  59.5 1.6 %collective-permute-start.18 = (bf16[15,2,64,128]{3,2,1,0:T(8,128)(2,1)S(1)}, bf16[15,2,64,128]{3,2,1,0:T(8,128)(2,1)S(1)}, u32[]{:S(2)}, u32[]{:S(2)}) collective-permute-start(bf16[15,2,64,128]{3,2,1,0:T(8,128)(2,1)S(1)} %correlate.8), channel_id=1, source_target_pairs={{0,2},{1,3},{2,6},{3,7},{4,0},{5,1},{6,4},{7,5},{8,10},{9,11},{10,... | collective-permute-start | bytes 1474568 | tf_op jit(solution)/shard_map/ppermute | solution.py:486
  61.8 1.3 %collective-permute-start.28 = (bf16[4,2,80,128]{3,2,1,0:T(8,128)(2,1)S(1)}, bf16[4,2,80,128]{3,2,1,0:T(8,128)(2,1)S(1)}, u32[]{:S(2)}, u32[]{:S(2)}) collective-permute-start(bf16[4,2,80,128]{3,2,1,0:T(8,128)(2,1)S(1)} %get-tuple-element.83), channel_id=1, source_target_pairs={{0,8},{1,9},{2,10},{3,11},{4,12},{5,13},{6,14},{7,15},{8,0},{9,1},... | collective-permute-start | bytes 491528 | tf_op jit(solution)/shard_map/ppermute | solution.py:486
  63.3 4.9 %collective-permute-done.27.refs_1_ = bf16[4,2,80,128]{3,2,1,0:T(8,128)(2,1)S(1)} collective-permute-done((bf16[4,2,80,128]{3,2,1,0:T(8,128)(2,1)S(1)}, bf16[4,2,80,128]{3,2,1,0:T(8,128)(2,1)S(1)}, u32[]{:S(2)}, u32[]{:S(2)}) %collective-permute-start.27) | collective-permute-done | bytes 163872 | tf_op jit(solution)/shard_map/ppermute | solution.py:486
  68.3 1.0 collective-permute-start.13
  69.3 2.0 %collective-permute-done.29.refs_3_ = bf16[4,2,80,128]{3,2,1,0:T(8,128)(2,1)S(1)} collective-permute-done((bf16[4,2,80,128]{3,2,1,0:T(8,128)(2,1)S(1)}, bf16[4,2,80,128]{3,2,1,0:T(8,128)(2,1)S(1)}, u32[]{:S(2)}, u32[]{:S(2)}) %collective-permute-start.29) | collective-permute-done | bytes 163872 | tf_op jit(solution)/shard_map/ppermute | solution.py:486
  71.6 0.8 correlate.12
  72.4 2.6 %collective-permute-start.34 = (bf16[15,2,64,128]{3,2,1,0:T(8,128)(2,1)S(1)}, bf16[15,2,64,128]{3,2,1,0:T(8,128)(2,1)S(1)}, u32[]{:S(2)}, u32[]{:S(2)}) collective-permute-start(bf16[15,2,64,128]{3,2,1,0:T(8,128)(2,1)S(1)} %correlate.12), channel_id=1, source_target_pairs={{0,2},{1,3},{2,6},{3,7},{4,0},{5,1},{6,4},{7,5},{8,10},{9,11},{10,... | collective-permute-start | bytes 1474568 | tf_op jit(solution)/shard_map/ppermute | solution.py:486
  75.4 2.8 %collective-permute-done.14.refs_3_ = bf16[4,2,80,128]{3,2,1,0:T(8,128)(2,1)S(1)} collective-permute-done((bf16[4,2,80,128]{3,2,1,0:T(8,128)(2,1)S(1)}, bf16[4,2,80,128]{3,2,1,0:T(8,128)(2,1)S(1)}, u32[]{:S(2)}, u32[]{:S(2)}) %collective-permute-start.14) | collective-permute-done | bytes 163872 | tf_op jit(solution)/shard_map/ppermute | solution.py:486
  78.2 1.8 %collective-permute-done.18.refs_4_ = bf16[15,2,64,128]{3,2,1,0:T(8,128)(2,1)S(1)} collective-permute-done((bf16[15,2,64,128]{3,2,1,0:T(8,128)(2,1)S(1)}, bf16[15,2,64,128]{3,2,1,0:T(8,128)(2,1)S(1)}, u32[]{:S(2)}, u32[]{:S(2)}) %collective-permute-start.18) | collective-permute-done | bytes 491552 | tf_op jit(solution)/shard_map/ppermute | solution.py:486
  80.0 0.8 correlate.9
  80.8 0.9 collective-permute-start.19
  81.7 1.2 collective-permute-start.24
  82.9 0.9 collective-permute-start.26
  83.8 4.9 %collective-permute-done.24.refs_1_ = bf16[4,2,80,128]{3,2,1,0:T(8,128)(2,1)S(1)} collective-permute-done((bf16[4,2,80,128]{3,2,1,0:T(8,128)(2,1)S(1)}, bf16[4,2,80,128]{3,2,1,0:T(8,128)(2,1)S(1)}, u32[]{:S(2)}, u32[]{:S(2)}) %collective-permute-start.24) | collective-permute-done | bytes 163872 | tf_op jit(solution)/shard_map/ppermute | solution.py:486
  88.7 1.2 collective-permute-start.9
  89.9 1.0 collective-permute-done.26.refs_3_
  91.0 2.2 %collective-permute-start.11 = (bf16[4,2,80,128]{3,2,1,0:T(8,128)(2,1)S(1)}, bf16[4,2,80,128]{3,2,1,0:T(8,128)(2,1)S(1)}, u32[]{:S(2)}, u32[]{:S(2)}) collective-permute-start(bf16[4,2,80,128]{3,2,1,0:T(8,128)(2,1)S(1)} %get-tuple-element.64), channel_id=1, source_target_pairs={{0,9},{1,8},{2,11},{3,10},{4,13},{5,12},{6,15},{7,14},{8,1},{9,0},... | collective-permute-start | bytes 491528 | tf_op jit(solution)/shard_map/ppermute | solution.py:486
  93.2 0.8 correlate.13
  93.9 1.9 %collective-permute-start.35 = (bf16[15,2,64,128]{3,2,1,0:T(8,128)(2,1)S(1)}, bf16[15,2,64,128]{3,2,1,0:T(8,128)(2,1)S(1)}, u32[]{:S(2)}, u32[]{:S(2)}) collective-permute-start(bf16[15,2,64,128]{3,2,1,0:T(8,128)(2,1)S(1)} %correlate.13), channel_id=1, source_target_pairs={{0,2},{1,3},{2,6},{3,7},{4,0},{5,1},{6,4},{7,5},{8,10},{9,11},{10,... | collective-permute-start | bytes 1474568 | tf_op jit(solution)/shard_map/ppermute | solution.py:486
  95.9 2.0 %collective-permute-done.11.refs_3_ = bf16[4,2,80,128]{3,2,1,0:T(8,128)(2,1)S(1)} collective-permute-done((bf16[4,2,80,128]{3,2,1,0:T(8,128)(2,1)S(1)}, bf16[4,2,80,128]{3,2,1,0:T(8,128)(2,1)S(1)}, u32[]{:S(2)}, u32[]{:S(2)}) %collective-permute-start.11) | collective-permute-done | bytes 163872 | tf_op jit(solution)/shard_map/ppermute | solution.py:486
  97.9 3.2 %collective-permute-done.19.refs_4_ = bf16[15,2,64,128]{3,2,1,0:T(8,128)(2,1)S(1)} collective-permute-done((bf16[15,2,64,128]{3,2,1,0:T(8,128)(2,1)S(1)}, bf16[15,2,64,128]{3,2,1,0:T(8,128)(2,1)S(1)}, u32[]{:S(2)}, u32[]{:S(2)}) %collective-permute-start.19) | collective-permute-done | bytes 491552 | tf_op jit(solution)/shard_map/ppermute | solution.py:486
  101.1 0.8 correlate.10
  101.9 0.8 collective-permute-start.20
  103.6 1.2 collective-permute-start.23
  104.8 5.0 %collective-permute-done.21.refs_1_ = bf16[4,2,80,128]{3,2,1,0:T(8,128)(2,1)S(1)} collective-permute-done((bf16[4,2,80,128]{3,2,1,0:T(8,128)(2,1)S(1)}, bf16[4,2,80,128]{3,2,1,0:T(8,128)(2,1)S(1)}, u32[]{:S(2)}, u32[]{:S(2)}) %collective-permute-start.21) | collective-permute-done | bytes 163872 | tf_op jit(solution)/shard_map/ppermute | solution.py:486
  110.3 1.0 collective-permute-done.23.refs_3_
  111.4 2.2 %collective-permute-start.8 = (bf16[4,2,80,128]{3,2,1,0:T(8,128)(2,1)S(1)}, bf16[4,2,80,128]{3,2,1,0:T(8,128)(2,1)S(1)}, u32[]{:S(2)}, u32[]{:S(2)}) collective-permute-start(bf16[4,2,80,128]{3,2,1,0:T(8,128)(2,1)S(1)} %get-tuple-element.60), channel_id=1, source_target_pairs={{0,9},{1,8},{2,11},{3,10},{4,13},{5,12},{6,15},{7,14},{8,1},{9,0},... | collective-permute-start | bytes 491528 | tf_op jit(solution)/shard_map/ppermute | solution.py:486
  113.6 1.8 %correlate.14.refs_5_ = f32[1,15,64,512]{3,2,1,0:T(8,128)} custom-call(bf16[4,2,80,128]{3,2,1,0:T(8,128)(2,1)S(1)} %get-tuple-element.73.refs_0_, bf16[4,2,80,128]{3,2,1,0:T(8,128)(2,1)S(1)} %collective-permute-done.21.refs_1_, bf16[4,2,80,128]{3,2,1,0:T(8,128)(2,1)S(1)} %collective-permute-done.22.refs_2_, ...), custom_call_target="tpu_custom_call" | custom-call | flops 1000000000 | bytes 1000000 | tf_op jit(solution)/shard_map/correlate/pallas_call | solution.py:616
  115.8 2.3 %collective-permute-done.8.refs_3_ = bf16[4,2,80,128]{3,2,1,0:T(8,128)(2,1)S(1)} collective-permute-done((bf16[4,2,80,128]{3,2,1,0:T(8,128)(2,1)S(1)}, bf16[4,2,80,128]{3,2,1,0:T(8,128)(2,1)S(1)}, u32[]{:S(2)}, u32[]{:S(2)}) %collective-permute-start.8) | collective-permute-done | bytes 163872 | tf_op jit(solution)/shard_map/ppermute | solution.py:486
  118.1 3.0 %collective-permute-done.20.refs_4_ = bf16[15,2,64,128]{3,2,1,0:T(8,128)(2,1)S(1)} collective-permute-done((bf16[15,2,64,128]{3,2,1,0:T(8,128)(2,1)S(1)}, bf16[15,2,64,128]{3,2,1,0:T(8,128)(2,1)S(1)}, u32[]{:S(2)}, u32[]{:S(2)}) %collective-permute-start.20) | collective-permute-done | bytes 491552 | tf_op jit(solution)/shard_map/ppermute | solution.py:486
  121.1 1.8 %correlate.15 = f32[1,15,64,512]{3,2,1,0:T(8,128)} custom-call(bf16[4,2,80,128]{3,2,1,0:T(8,128)(2,1)S(1)} %get-tuple-element.57.refs_0_, bf16[4,2,80,128]{3,2,1,0:T(8,128)(2,1)S(1)} %collective-permute-done.6.refs_1_, bf16[4,2,80,128]{3,2,1,0:T(8,128)(2,1)S(1)} %collective-permute-done.7.refs_2_, ...), custom_call_target="tpu_custom_call", output_to_operand_aliasing={{}: (5, {})} | custom-call | flops 1000000000 | bytes 1000000 | tf_op jit(solution)/shard_map/correlate/pallas_call | solution.py:616
  (46 shorter events, 8.1 us)
Async XLA Ops:
  0.1 0.7 copy-start
  0.8 5.9 %copy-start.3 = (f32[32]{0:T(128)S(1)}, f32[32]{0:T(128)}, u32[]{:S(2)}) copy-start(f32[32]{0:T(128)} %param.12) | copy-start | bytes 388
  0.8 5.9 %copy-start.1 = (f32[384,1]{1,0:T(8,128)S(1)}, f32[384,1]{1,0:T(8,128)}, u32[]{:S(2)}) copy-start(f32[384,1]{1,0:T(8,128)} %constant.87.clone.refs_2_.wave_x) | copy-start | bytes 4612
  0.8 5.9 %copy-start.2 = (f32[1,384]{1,0:T(1,128)S(1)}, f32[1,384]{1,0:T(1,128)}, u32[]{:S(2)}) copy-start(f32[1,384]{1,0:T(1,128)} %constant.88.clone.refs_3_.wave_y) | copy-start | bytes 4612
  3.7 2.2 %collective-permute-start = (bf16[512,512]{1,0:T(8,128)(2,1)}, bf16[512,512]{1,0:T(8,128)(2,1)S(1)}, u32[]{:S(2)}, u32[]{:S(2)}) collective-permute-start(bf16[512,512]{1,0:T(8,128)(2,1)} %get-tuple-element.48), channel_id=1, source_target_pairs={{0,8},{1,9},{2,10},{3,11},{4,12},{5,13},{6,14},{7,15},{8,0},{9,1},... | collective-permute-start | bytes 1572872 | tf_op jit(solution)/shard_map/ppermute | solution.py:486
  3.8 15.4 %collective-permute-start.1 = (bf16[512,512]{1,0:T(8,128)(2,1)S(1)}, bf16[512,512]{1,0:T(8,128)(2,1)S(1)}, u32[]{:S(2)}, u32[]{:S(2)}) collective-permute-start(bf16[512,512]{1,0:T(8,128)(2,1)S(1)} %get-tuple-element.54.mine.refs_5_), channel_id=1, source_target_pairs={{0,16},{1,17},{2,18},{3,19},{4,20},{5,21},{6,22},{7,23}} | collective-permute-start | bytes 1572872 | tf_op jit(solution)/shard_map/ppermute | solution.py:486
  5.9 13.6 %collective-permute-start.2 = (bf16[512,512]{1,0:T(8,128)(2,1)S(1)}, bf16[512,512]{1,0:T(8,128)(2,1)S(1)}, u32[]{:S(2)}, u32[]{:S(2)}) collective-permute-start(bf16[512,512]{1,0:T(8,128)(2,1)S(1)} %collective-permute-done.from_core.refs_6_), channel_id=1, source_target_pairs={{8,24},{9,25},{10,26},{11,27},{12,28},{13,29},{14,30},{15,31}} | collective-permute-start | bytes 1572872 | tf_op jit(solution)/shard_map/ppermute | solution.py:486
  13.9 5.6 %collective-permute-start.3 = (f32[8,128]{1,0:T(8,128)S(1)}, f32[8,128]{1,0:T(8,128)S(1)}, u32[]{:S(2)}, u32[]{:S(2)}) collective-permute-start(f32[8,128]{1,0:T(8,128)S(1)} %get-tuple-element.51.refs_7_), channel_id=1, source_target_pairs={{0,16},{1,17},{2,18},{3,19},{4,20},{5,21},{6,22},{7,23},{8,24},{9,... | collective-permute-start | bytes 12296 | tf_op jit(solution)/shard_map/ppermute | solution.py:486
  15.2 14.2 %collective-permute-start.4 = (bf16[512,512]{1,0:T(8,128)(2,1)S(1)}, bf16[512,512]{1,0:T(8,128)(2,1)S(1)}, u32[]{:S(2)}, u32[]{:S(2)}) collective-permute-start(bf16[512,512]{1,0:T(8,128)(2,1)S(1)} %get-tuple-element.54.mine.refs_5_), channel_id=1, source_target_pairs={{8,24},{9,25},{10,26},{11,27},{12,28},{13,29},{14,30},{15,31}} | collective-permute-start | bytes 1572872 | tf_op jit(solution)/shard_map/ppermute | solution.py:486
  15.9 15.9 %collective-permute-start.5 = (bf16[512,512]{1,0:T(8,128)(2,1)S(1)}, bf16[512,512]{1,0:T(8,128)(2,1)S(1)}, u32[]{:S(2)}, u32[]{:S(2)}) collective-permute-start(bf16[512,512]{1,0:T(8,128)(2,1)S(1)} %collective-permute-done.from_core.refs_6_), channel_id=1, source_target_pairs={{0,16},{1,17},{2,18},{3,19},{4,20},{5,21},{6,22},{7,23}} | collective-permute-start | bytes 1572872 | tf_op jit(solution)/shard_map/ppermute | solution.py:486
  43.7 6.4 %collective-permute-start.30 = (bf16[4,2,80,128]{3,2,1,0:T(8,128)(2,1)S(1)}, bf16[4,2,80,128]{3,2,1,0:T(8,128)(2,1)S(1)}, u32[]{:S(2)}, u32[]{:S(2)}) collective-permute-start(bf16[4,2,80,128]{3,2,1,0:T(8,128)(2,1)S(1)} %get-tuple-element.86), channel_id=1, source_target_pairs={{0,1},{1,0},{2,3},{3,2},{4,5},{5,4},{6,7},{7,6},{8,9},{9,8},{10,11... | collective-permute-start | bytes 491528 | tf_op jit(solution)/shard_map/ppermute | solution.py:486
  45.3 4.8 %collective-permute-start.31 = (bf16[4,2,80,128]{3,2,1,0:T(8,128)(2,1)S(1)}, bf16[4,2,80,128]{3,2,1,0:T(8,128)(2,1)S(1)}, u32[]{:S(2)}, u32[]{:S(2)}) collective-permute-start(bf16[4,2,80,128]{3,2,1,0:T(8,128)(2,1)S(1)} %get-tuple-element.87), channel_id=1, source_target_pairs={{0,8},{1,9},{2,10},{3,11},{4,12},{5,13},{6,14},{7,15},{8,0},{9,1},... | collective-permute-start | bytes 491528 | tf_op jit(solution)/shard_map/ppermute | solution.py:486
  45.3 8.2 %collective-permute-start.32 = (bf16[4,2,80,128]{3,2,1,0:T(8,128)(2,1)S(1)}, bf16[4,2,80,128]{3,2,1,0:T(8,128)(2,1)S(1)}, u32[]{:S(2)}, u32[]{:S(2)}) collective-permute-start(bf16[4,2,80,128]{3,2,1,0:T(8,128)(2,1)S(1)} %get-tuple-element.88), channel_id=1, source_target_pairs={{0,9},{1,8},{2,11},{3,10},{4,13},{5,12},{6,15},{7,14},{8,1},{9,0},... | collective-permute-start | bytes 491528 | tf_op jit(solution)/shard_map/ppermute | solution.py:486
  45.9 11.2 %collective-permute-start.15 = (bf16[4,2,80,128]{3,2,1,0:T(8,128)(2,1)S(1)}, bf16[4,2,80,128]{3,2,1,0:T(8,128)(2,1)S(1)}, u32[]{:S(2)}, u32[]{:S(2)}) collective-permute-start(bf16[4,2,80,128]{3,2,1,0:T(8,128)(2,1)S(1)} %get-tuple-element.70), channel_id=1, source_target_pairs={{0,1},{1,0},{2,3},{3,2},{4,5},{5,4},{6,7},{7,6},{8,9},{9,8},{10,11... | collective-permute-start | bytes 491528 | tf_op jit(solution)/shard_map/ppermute | solution.py:486
  47.4 9.7 %collective-permute-start.16 = (bf16[4,2,80,128]{3,2,1,0:T(8,128)(2,1)S(1)}, bf16[4,2,80,128]{3,2,1,0:T(8,128)(2,1)S(1)}, u32[]{:S(2)}, u32[]{:S(2)}) collective-permute-start(bf16[4,2,80,128]{3,2,1,0:T(8,128)(2,1)S(1)} %get-tuple-element.71), channel_id=1, source_target_pairs={{0,8},{1,9},{2,10},{3,11},{4,12},{5,13},{6,14},{7,15},{8,0},{9,1},... | collective-permute-start | bytes 491528 | tf_op jit(solution)/shard_map/ppermute | solution.py:486
  50.1 8.7 %collective-permute-start.17 = (bf16[4,2,80,128]{3,2,1,0:T(8,128)(2,1)S(1)}, bf16[4,2,80,128]{3,2,1,0:T(8,128)(2,1)S(1)}, u32[]{:S(2)}, u32[]{:S(2)}) collective-permute-start(bf16[4,2,80,128]{3,2,1,0:T(8,128)(2,1)S(1)} %get-tuple-element.72), channel_id=1, source_target_pairs={{0,9},{1,8},{2,11},{3,10},{4,13},{5,12},{6,15},{7,14},{8,1},{9,0},... | collective-permute-start | bytes 491528 | tf_op jit(solution)/shard_map/ppermute | solution.py:486
  54.2 17.4 %collective-permute-start.33 = (bf16[15,2,64,128]{3,2,1,0:T(8,128)(2,1)S(1)}, bf16[15,2,64,128]{3,2,1,0:T(8,128)(2,1)S(1)}, u32[]{:S(2)}, u32[]{:S(2)}) collective-permute-start(bf16[15,2,64,128]{3,2,1,0:T(8,128)(2,1)S(1)} %correlate.11), channel_id=1, source_target_pairs={{0,2},{1,3},{2,6},{3,7},{4,0},{5,1},{6,4},{7,5},{8,10},{9,11},{10,... | collective-permute-start | bytes 1474568 | tf_op jit(solution)/shard_map/ppermute | solution.py:486
  59.5 20.5 %collective-permute-start.18 = (bf16[15,2,64,128]{3,2,1,0:T(8,128)(2,1)S(1)}, bf16[15,2,64,128]{3,2,1,0:T(8,128)(2,1)S(1)}, u32[]{:S(2)}, u32[]{:S(2)}) collective-permute-start(bf16[15,2,64,128]{3,2,1,0:T(8,128)(2,1)S(1)} %correlate.8), channel_id=1, source_target_pairs={{0,2},{1,3},{2,6},{3,7},{4,0},{5,1},{6,4},{7,5},{8,10},{9,11},{10,... | collective-permute-start | bytes 1474568 | tf_op jit(solution)/shard_map/ppermute | solution.py:486
  61.2 7.1 %collective-permute-start.27 = (bf16[4,2,80,128]{3,2,1,0:T(8,128)(2,1)S(1)}, bf16[4,2,80,128]{3,2,1,0:T(8,128)(2,1)S(1)}, u32[]{:S(2)}, u32[]{:S(2)}) collective-permute-start(bf16[4,2,80,128]{3,2,1,0:T(8,128)(2,1)S(1)} %get-tuple-element.82), channel_id=1, source_target_pairs={{0,1},{1,0},{2,3},{3,2},{4,5},{5,4},{6,7},{7,6},{8,9},{9,8},{10,11... | collective-permute-start | bytes 491528 | tf_op jit(solution)/shard_map/ppermute | solution.py:486
  61.8 6.5 %collective-permute-start.28 = (bf16[4,2,80,128]{3,2,1,0:T(8,128)(2,1)S(1)}, bf16[4,2,80,128]{3,2,1,0:T(8,128)(2,1)S(1)}, u32[]{:S(2)}, u32[]{:S(2)}) collective-permute-start(bf16[4,2,80,128]{3,2,1,0:T(8,128)(2,1)S(1)} %get-tuple-element.83), channel_id=1, source_target_pairs={{0,8},{1,9},{2,10},{3,11},{4,12},{5,13},{6,14},{7,15},{8,0},{9,1},... | collective-permute-start | bytes 491528 | tf_op jit(solution)/shard_map/ppermute | solution.py:486
  63.1 8.2 %collective-permute-start.29 = (bf16[4,2,80,128]{3,2,1,0:T(8,128)(2,1)S(1)}, bf16[4,2,80,128]{3,2,1,0:T(8,128)(2,1)S(1)}, u32[]{:S(2)}, u32[]{:S(2)}) collective-permute-start(bf16[4,2,80,128]{3,2,1,0:T(8,128)(2,1)S(1)} %get-tuple-element.84), channel_id=1, source_target_pairs={{0,9},{1,8},{2,11},{3,10},{4,13},{5,12},{6,15},{7,14},{8,1},{9,0},... | collective-permute-start | bytes 491528 | tf_op jit(solution)/shard_map/ppermute | solution.py:486
  68.3 7.1 %collective-permute-start.12 = (bf16[4,2,80,128]{3,2,1,0:T(8,128)(2,1)S(1)}, bf16[4,2,80,128]{3,2,1,0:T(8,128)(2,1)S(1)}, u32[]{:S(2)}, u32[]{:S(2)}) collective-permute-start(bf16[4,2,80,128]{3,2,1,0:T(8,128)(2,1)S(1)} %get-tuple-element.66), channel_id=1, source_target_pairs={{0,1},{1,0},{2,3},{3,2},{4,5},{5,4},{6,7},{7,6},{8,9},{9,8},{10,11... | collective-permute-start | bytes 491528 | tf_op jit(solution)/shard_map/ppermute | solution.py:486
  68.3 7.0 %collective-permute-start.13 = (bf16[4,2,80,128]{3,2,1,0:T(8,128)(2,1)S(1)}, bf16[4,2,80,128]{3,2,1,0:T(8,128)(2,1)S(1)}, u32[]{:S(2)}, u32[]{:S(2)}) collective-permute-start(bf16[4,2,80,128]{3,2,1,0:T(8,128)(2,1)S(1)} %get-tuple-element.67), channel_id=1, source_target_pairs={{0,8},{1,9},{2,10},{3,11},{4,12},{5,13},{6,14},{7,15},{8,0},{9,1},... | collective-permute-start | bytes 491528 | tf_op jit(solution)/shard_map/ppermute | solution.py:486
  71.3 6.9 %collective-permute-start.14 = (bf16[4,2,80,128]{3,2,1,0:T(8,128)(2,1)S(1)}, bf16[4,2,80,128]{3,2,1,0:T(8,128)(2,1)S(1)}, u32[]{:S(2)}, u32[]{:S(2)}) collective-permute-start(bf16[4,2,80,128]{3,2,1,0:T(8,128)(2,1)S(1)} %get-tuple-element.68), channel_id=1, source_target_pairs={{0,9},{1,8},{2,11},{3,10},{4,13},{5,12},{6,15},{7,14},{8,1},{9,0},... | collective-permute-start | bytes 491528 | tf_op jit(solution)/shard_map/ppermute | solution.py:486
  72.4 20.8 %collective-permute-start.34 = (bf16[15,2,64,128]{3,2,1,0:T(8,128)(2,1)S(1)}, bf16[15,2,64,128]{3,2,1,0:T(8,128)(2,1)S(1)}, u32[]{:S(2)}, u32[]{:S(2)}) collective-permute-start(bf16[15,2,64,128]{3,2,1,0:T(8,128)(2,1)S(1)} %correlate.12), channel_id=1, source_target_pairs={{0,2},{1,3},{2,6},{3,7},{4,0},{5,1},{6,4},{7,5},{8,10},{9,11},{10,... | collective-permute-start | bytes 1474568 | tf_op jit(solution)/shard_map/ppermute | solution.py:486
  80.8 20.3 %collective-permute-start.19 = (bf16[15,2,64,128]{3,2,1,0:T(8,128)(2,1)S(1)}, bf16[15,2,64,128]{3,2,1,0:T(8,128)(2,1)S(1)}, u32[]{:S(2)}, u32[]{:S(2)}) collective-permute-start(bf16[15,2,64,128]{3,2,1,0:T(8,128)(2,1)S(1)} %correlate.9), channel_id=1, source_target_pairs={{0,2},{1,3},{2,6},{3,7},{4,0},{5,1},{6,4},{7,5},{8,10},{9,11},{10,... | collective-permute-start | bytes 1474568 | tf_op jit(solution)/shard_map/ppermute | solution.py:486
  81.7 7.0 %collective-permute-start.24 = (bf16[4,2,80,128]{3,2,1,0:T(8,128)(2,1)S(1)}, bf16[4,2,80,128]{3,2,1,0:T(8,128)(2,1)S(1)}, u32[]{:S(2)}, u32[]{:S(2)}) collective-permute-start(bf16[4,2,80,128]{3,2,1,0:T(8,128)(2,1)S(1)} %get-tuple-element.78), channel_id=1, source_target_pairs={{0,1},{1,0},{2,3},{3,2},{4,5},{5,4},{6,7},{7,6},{8,9},{9,8},{10,11... | collective-permute-start | bytes 491528 | tf_op jit(solution)/shard_map/ppermute | solution.py:486
  82.9 7.1 %collective-permute-start.25 = (bf16[4,2,80,128]{3,2,1,0:T(8,128)(2,1)S(1)}, bf16[4,2,80,128]{3,2,1,0:T(8,128)(2,1)S(1)}, u32[]{:S(2)}, u32[]{:S(2)}) collective-permute-start(bf16[4,2,80,128]{3,2,1,0:T(8,128)(2,1)S(1)} %get-tuple-element.79), channel_id=1, source_target_pairs={{0,8},{1,9},{2,10},{3,11},{4,12},{5,13},{6,14},{7,15},{8,0},{9,1},... | collective-permute-start | bytes 491528 | tf_op jit(solution)/shard_map/ppermute | solution.py:486
  82.9 8.1 %collective-permute-start.26 = (bf16[4,2,80,128]{3,2,1,0:T(8,128)(2,1)S(1)}, bf16[4,2,80,128]{3,2,1,0:T(8,128)(2,1)S(1)}, u32[]{:S(2)}, u32[]{:S(2)}) collective-permute-start(bf16[4,2,80,128]{3,2,1,0:T(8,128)(2,1)S(1)} %get-tuple-element.80), channel_id=1, source_target_pairs={{0,9},{1,8},{2,11},{3,10},{4,13},{5,12},{6,15},{7,14},{8,1},{9,0},... | collective-permute-start | bytes 491528 | tf_op jit(solution)/shard_map/ppermute | solution.py:486
  88.7 7.2 %collective-permute-start.9 = (bf16[4,2,80,128]{3,2,1,0:T(8,128)(2,1)S(1)}, bf16[4,2,80,128]{3,2,1,0:T(8,128)(2,1)S(1)}, u32[]{:S(2)}, u32[]{:S(2)}) collective-permute-start(bf16[4,2,80,128]{3,2,1,0:T(8,128)(2,1)S(1)} %get-tuple-element.62), channel_id=1, source_target_pairs={{0,1},{1,0},{2,3},{3,2},{4,5},{5,4},{6,7},{7,6},{8,9},{9,8},{10,11... | collective-permute-start | bytes 491528 | tf_op jit(solution)/shard_map/ppermute | solution.py:486
  89.9 5.9 %collective-permute-start.10 = (bf16[4,2,80,128]{3,2,1,0:T(8,128)(2,1)S(1)}, bf16[4,2,80,128]{3,2,1,0:T(8,128)(2,1)S(1)}, u32[]{:S(2)}, u32[]{:S(2)}) collective-permute-start(bf16[4,2,80,128]{3,2,1,0:T(8,128)(2,1)S(1)} %get-tuple-element.63), channel_id=1, source_target_pairs={{0,8},{1,9},{2,10},{3,11},{4,12},{5,13},{6,14},{7,15},{8,0},{9,1},... | collective-permute-start | bytes 491528 | tf_op jit(solution)/shard_map/ppermute | solution.py:486
  91.0 6.9 %collective-permute-start.11 = (bf16[4,2,80,128]{3,2,1,0:T(8,128)(2,1)S(1)}, bf16[4,2,80,128]{3,2,1,0:T(8,128)(2,1)S(1)}, u32[]{:S(2)}, u32[]{:S(2)}) collective-permute-start(bf16[4,2,80,128]{3,2,1,0:T(8,128)(2,1)S(1)} %get-tuple-element.64), channel_id=1, source_target_pairs={{0,9},{1,8},{2,11},{3,10},{4,13},{5,12},{6,15},{7,14},{8,1},{9,0},... | collective-permute-start | bytes 491528 | tf_op jit(solution)/shard_map/ppermute | solution.py:486
  93.9 19.6 %collective-permute-start.35 = (bf16[15,2,64,128]{3,2,1,0:T(8,128)(2,1)S(1)}, bf16[15,2,64,128]{3,2,1,0:T(8,128)(2,1)S(1)}, u32[]{:S(2)}, u32[]{:S(2)}) collective-permute-start(bf16[15,2,64,128]{3,2,1,0:T(8,128)(2,1)S(1)} %correlate.13), channel_id=1, source_target_pairs={{0,2},{1,3},{2,6},{3,7},{4,0},{5,1},{6,4},{7,5},{8,10},{9,11},{10,... | collective-permute-start | bytes 1474568 | tf_op jit(solution)/shard_map/ppermute | solution.py:486
  101.9 19.3 %collective-permute-start.20 = (bf16[15,2,64,128]{3,2,1,0:T(8,128)(2,1)S(1)}, bf16[15,2,64,128]{3,2,1,0:T(8,128)(2,1)S(1)}, u32[]{:S(2)}, u32[]{:S(2)}) collective-permute-start(bf16[15,2,64,128]{3,2,1,0:T(8,128)(2,1)S(1)} %correlate.10), channel_id=1, source_target_pairs={{0,2},{1,3},{2,6},{3,7},{4,0},{5,1},{6,4},{7,5},{8,10},{9,11},{10,... | collective-permute-start | bytes 1474568 | tf_op jit(solution)/shard_map/ppermute | solution.py:486
  102.7 7.1 %collective-permute-start.21 = (bf16[4,2,80,128]{3,2,1,0:T(8,128)(2,1)S(1)}, bf16[4,2,80,128]{3,2,1,0:T(8,128)(2,1)S(1)}, u32[]{:S(2)}, u32[]{:S(2)}) collective-permute-start(bf16[4,2,80,128]{3,2,1,0:T(8,128)(2,1)S(1)} %get-tuple-element.74), channel_id=1, source_target_pairs={{0,1},{1,0},{2,3},{3,2},{4,5},{5,4},{6,7},{7,6},{8,9},{9,8},{10,11... | collective-permute-start | bytes 491528 | tf_op jit(solution)/shard_map/ppermute | solution.py:486
  103.3 7.1 %collective-permute-start.22 = (bf16[4,2,80,128]{3,2,1,0:T(8,128)(2,1)S(1)}, bf16[4,2,80,128]{3,2,1,0:T(8,128)(2,1)S(1)}, u32[]{:S(2)}, u32[]{:S(2)}) collective-permute-start(bf16[4,2,80,128]{3,2,1,0:T(8,128)(2,1)S(1)} %get-tuple-element.75), channel_id=1, source_target_pairs={{0,8},{1,9},{2,10},{3,11},{4,12},{5,13},{6,14},{7,15},{8,0},{9,1},... | collective-permute-start | bytes 491528 | tf_op jit(solution)/shard_map/ppermute | solution.py:486
  103.6 7.7 %collective-permute-start.23 = (bf16[4,2,80,128]{3,2,1,0:T(8,128)(2,1)S(1)}, bf16[4,2,80,128]{3,2,1,0:T(8,128)(2,1)S(1)}, u32[]{:S(2)}, u32[]{:S(2)}) collective-permute-start(bf16[4,2,80,128]{3,2,1,0:T(8,128)(2,1)S(1)} %get-tuple-element.76), channel_id=1, source_target_pairs={{0,9},{1,8},{2,11},{3,10},{4,13},{5,12},{6,15},{7,14},{8,1},{9,0},... | collective-permute-start | bytes 491528 | tf_op jit(solution)/shard_map/ppermute | solution.py:486
  109.8 5.9 %collective-permute-start.6 = (bf16[4,2,80,128]{3,2,1,0:T(8,128)(2,1)S(1)}, bf16[4,2,80,128]{3,2,1,0:T(8,128)(2,1)S(1)}, u32[]{:S(2)}, u32[]{:S(2)}) collective-permute-start(bf16[4,2,80,128]{3,2,1,0:T(8,128)(2,1)S(1)} %get-tuple-element.58), channel_id=1, source_target_pairs={{0,1},{1,0},{2,3},{3,2},{4,5},{5,4},{6,7},{7,6},{8,9},{9,8},{10,11... | collective-permute-start | bytes 491528 | tf_op jit(solution)/shard_map/ppermute | solution.py:486
  110.3 5.4 %collective-permute-start.7 = (bf16[4,2,80,128]{3,2,1,0:T(8,128)(2,1)S(1)}, bf16[4,2,80,128]{3,2,1,0:T(8,128)(2,1)S(1)}, u32[]{:S(2)}, u32[]{:S(2)}) collective-permute-start(bf16[4,2,80,128]{3,2,1,0:T(8,128)(2,1)S(1)} %get-tuple-element.59), channel_id=1, source_target_pairs={{0,8},{1,9},{2,10},{3,11},{4,12},{5,13},{6,14},{7,15},{8,0},{9,1},... | collective-permute-start | bytes 491528 | tf_op jit(solution)/shard_map/ppermute | solution.py:486
  111.4 6.7 %collective-permute-start.8 = (bf16[4,2,80,128]{3,2,1,0:T(8,128)(2,1)S(1)}, bf16[4,2,80,128]{3,2,1,0:T(8,128)(2,1)S(1)}, u32[]{:S(2)}, u32[]{:S(2)}) collective-permute-start(bf16[4,2,80,128]{3,2,1,0:T(8,128)(2,1)S(1)} %get-tuple-element.60), channel_id=1, source_target_pairs={{0,9},{1,8},{2,11},{3,10},{4,13},{5,12},{6,15},{7,14},{8,1},{9,0},... | collective-permute-start | bytes 491528 | tf_op jit(solution)/shard_map/ppermute | solution.py:486

commit v7 on v6

--- a/solution.py
+++ b/solution.py
@@ -114,21 +114,43 @@
     return rows_x // RADIX, rows_y // RADIX, rows_y // BLOCKS_Y
 
 
-def forward_x(field, mid, left_x):
-    part_x, _, block_y = extent(field)
+def forward_x(load, mid, left_x):
+    part_x, _, block_y = extent(mid)
     for i in range(BLOCKS_Y):
         cols = slice(i * block_y, (i + 1) * block_y)
         for kind in range(2):
-            re, im = (
-                [field[2 * kind + j, q * part_x : (q + 1) * part_x, cols] for q in range(RADIX)]
-                for j in range(2)
-            )
+            re, im = load(cols, kind)
             for r, mixed in enumerate(mix_forward(re, im)):
                 mixed = jnp.concatenate(mixed, axis=0)
                 out = jnp.dot(left_x[r], mixed, preferred_element_type=jnp.float32)
                 mid[2 * kind : 2 * kind + 2, r * part_x : (r + 1) * part_x, cols] = out.astype(
                     jnp.bfloat16
                 ).reshape(2, part_x, block_y)
+
+
+def rows_of(ref):
+    part_x = extent(ref)[0]
+    return [slice(q * part_x, (q + 1) * part_x) for q in range(RADIX)]
+
+
+def plainly(field):
+    return lambda cols, kind: [[field[2 * kind + j, q, cols] for q in rows_of(field)] for j in range(2)]
+
+
+def screening(before, tables, index):
+    kept = {}
+
+    def load(cols, kind):
+        if cols.start not in kept:
+            kept.clear()
+            kept[cols.start] = [screens_of(tables, index, q, cols) for q in rows_of(before)]
+        done = [
+            turned(kind, before[2 * kind, q, cols], before[2 * kind + 1, q, cols], *screen)
+            for q, screen in zip(rows_of(before), kept[cols.start])
+        ]
+        return [[value[j].astype(jnp.bfloat16) for value in done] for j in range(2)]
+
+    return load
 
 
 def fill_phases(angular, base, wave_x, wave_y, phases):
@@ -259,7 +281,7 @@
     for p in range(shots):
         fill_index(index, (mine, from_core), my_core == p)
         if p == 0:
-            forward_x(top, mid, tables[0])
+            forward_x(plainly(top), mid, tables[0])
         value = functools.reduce(jnp.add, lookup(levels[0:1, :], index[...]))
         base = jnp.sum(jnp.sum(value.reshape(rows_x // 8, 8, LANES), axis=0)) / (rows_x * rows_y)
         means[p : p + 1, :] = jnp.full((1, LANES), base, jnp.float32)
@@ -286,78 +308,76 @@
         fill_index(index, (far_a, far_b), my_core == 0)
         tables = screen_tables(angular, means[0:1, 0:1], levels)
         inverse_x(mid, right_x, put_screened(tables, index, field))
-        forward_x(field, mid, left_x)
+        forward_x(plainly(field), mid, left_x)
         fill_phases(angular, means[1:2, 0:1], wave_x, wave_y, phases)
         along_y(mid, phases, left_y, right_y)
         inverse_x(mid, right_x, put_plain)
 
 
-def planes_kernel(place, angular_ref, *refs, shots, strips, width, groups, later):
+def planes_kernel(place, angular_ref, *refs, shots, strips, width, groups):
     refs = list(refs)
     top, before, far_a, far_b, far_means, near_a, near_b, means, phases, levels = refs[:10]
     left_x, right_x, left_y, right_y = refs[10:14]
-    outs = refs[14:-4]
-    field, mid, padded, index = refs[-4:]
+    padded_planes, outs = refs[14 : 14 + shots], refs[14 + shots : -3]
+    field, mid, index = refs[-3:]
     angular, my_core, parity, spot = angular_ref[0], place[1], place[2], place[3]
 
     @pl.when(place[0] == 0)
     def _():
-        field[...] = top[...]
+        forward_x(plainly(top), mid, left_x)
 
     @pl.when(place[0] > 0)
     def _():
         fill_index(index, (far_a, far_b), my_core == 1)
         tables = screen_tables(angular, far_means[1:2, 0:1], levels)
-        block = 128
-
-        def part(i, carry):
-            rows = pl.ds(pl.multiple_of(i * block, block), block)
-            cos, sin = screens_of(tables, index, rows, slice(None))
-            for kind in range(2):
-                new = turned(kind, before[2 * kind, rows], before[2 * kind + 1, rows], cos, sin)
-                for j in range(2):
-                    field[2 * kind + j, rows] = new[j].astype(jnp.bfloat16)
-            return carry
-
-        lax.fori_loop(0, index.shape[0] // block, part, 0)
-
-    def emit(target, to):
-        for s in range(strips):
-            p = lax.rem(spot + (strips - 1 - s), strips)
-            strip = jnp.where(p == 0, 0, jnp.where(p <= strips // 2, 2 * p - 1, 2 * (strips - p)))
-            start = pl.multiple_of((2 * strip + to) * width, 16)
-            for n, (first, last) in enumerate(groups if s == 0 else later):
-                at = n if s == 0 else len(groups) + (s - 1) * len(later) + n
-                out = outs[target * (len(groups) + (strips - 1) * len(later)) + at]
-                for tile in range(first, last):
-                    for part in range(4):
-                        out[part, tile - first] = padded[part, tile, pl.ds(start, width + 2 * HALO)]
+        forward_x(screening(before, tables, index), mid, left_x)
 
     for plane in range(shots):
-        forward_x(field, mid, left_x)
+        if plane > 0:
+            forward_x(plainly(field), mid, left_x)
         fill_index(index, (near_a, near_b), my_core == plane)
         along_y(mid, phases.at[plane], left_y, right_y)
         tables = screen_tables(angular, means[plane : plane + 1, 0:1], levels)
-        inverse_x(mid, right_x, put_screened(tables, index, field, padded))
-
-        @pl.when(my_core == plane)
-        def _():
-            emit(0, parity)
-            emit(1, 1 - parity)
-
-        @pl.when(my_core != plane)
-        def _():
-            emit(2, parity)
-            emit(3, 1 - parity)
-
-
-def correlate_kernel(*refs, width, begin, tiles, partial, scale):
+        inverse_x(mid, right_x, put_screened(tables, index, field, padded_planes[plane]))
+    hand_out(place, padded_planes, outs, 0, 1, strips, width, groups)
+
+
+def strip_start(spot, step, strips, width, parity):
+    p = lax.rem(spot + (strips - 1 - step), strips)
+    strip = jnp.where(p == 0, 0, jnp.where(p <= strips // 2, 2 * p - 1, 2 * (strips - p)))
+    return pl.multiple_of((2 * strip + parity) * width, 16)
+
+
+def hand_out(place, padded_planes, outs, begin, end, strips, width, groups):
+    my_core, parity, spot = place[1], place[2], place[3]
+    for core in range(2):
+
+        @pl.when(my_core == core)
+        def _(core=core):
+            for target in range(4):
+                padded = padded_planes[core if target < 2 else 1 - core]
+                to = parity if target % 2 == 0 else 1 - parity
+                for step in range(begin, end):
+                    start = strip_start(spot, step, strips, width, to)
+                    for g, (first, last) in enumerate(groups):
+                        out = outs[(target * (end - begin) + step - begin) * len(groups) + g]
+                        for tile in range(first, last):
+                            for part in range(4):
+                                out[part, tile - first] = padded[
+                                    part, tile, pl.ds(start, width + 2 * HALO)
+                                ]
+
+
+def strips_kernel(place, *refs, shots, strips, width, groups):
+    hand_out(place, refs[:shots], refs[shots:], 1, strips, strips, width, groups)
+
+
+def correlate_kernel(*refs, width, tiles, partial):
     fields, out, wide = refs[:4], refs[-2], refs[-1]
     for tile in range(tiles):
-        lanes = slice(tile * LANES, (tile + 1) * LANES)
         for m in range(4):
             for part in range(4):
-                wide[m * 4 + part] = fields[m][part, begin + tile].astype(jnp.float32)
+                wide[m * 4 + part] = fields[m][part, tile].astype(jnp.float32)
         for lag in range(2 * LAG + 1):
             shift = lag - LAG
             total = None
@@ -370,10 +390,16 @@
                     total = term if total is None else total + term
             if partial:
                 total = total + refs[4][lag, tile].astype(jnp.float32)
-            if scale is not None:
-                out[0, lag, :, lanes] = total * scale
-            else:
-                out[lag, tile] = total.astype(out.dtype)
+            out[lag, tile] = total.astype(out.dtype)
+
+
+def finish_kernel(mine, received, *refs, scale):
+    out = refs[-1]
+    for tile in range(mine.shape[1]):
+        lanes = slice(tile * LANES, (tile + 1) * LANES)
+        for lag in range(mine.shape[0]):
+            total = mine[lag, tile] + received[lag, tile].astype(jnp.float32)
+            out[0, lag, :, lanes] = total * scale
 
 
 def window_kernel(place, anchors, codes, mine, other, held, arrived, *, blocks):
@@ -460,7 +486,6 @@
     lags = 2 * LAG + 1
     tiles = rows_y // LANES
     groups = [(0, tiles // 2), (tiles // 2, tiles)]
-    later = groups
     factor = 1.0 / math.sqrt(2.0 * shots * freq_count)
     depth_index = lax.axis_index("depth")
     freq_index = lax.axis_index("freq")
@@ -570,91 +595,92 @@
         [pltpu.VMEM(whole, bf16), pltpu.VMEM(whole, bf16), index_scratch, pltpu.VMEM(phase_shape, f32)],
         15 * 10**9,
     )
-    sizes = [end - begin for begin, end in groups]
-    sizes += [end - begin for begin, end in later] * (strips - 1)
-    pieces = call(
-        functools.partial(
-            planes_kernel, shots=shots, strips=strips, width=width, groups=groups, later=later
-        ),
+    def strip_shapes(steps):
+        return [
+            ((4, end - begin, height, LANES), bf16)
+            for _ in range(4 * steps)
+            for begin, end in groups
+        ]
+
+    made = call(
+        functools.partial(planes_kernel, shots=shots, strips=strips, width=width, groups=groups),
         "planes",
         scalars,
         [top, before, *far_second, far_means, *near, means, phases, levels, *tables],
-        [((4, size, height, LANES), bf16) for _ in range(4) for size in sizes],
-        [
-            pltpu.VMEM(whole, bf16),
-            pltpu.VMEM(whole, bf16),
-            pltpu.VMEM((4, tiles, rows_x + 2 * HALO, LANES), bf16),
-            index_scratch,
-        ],
+        [((4, tiles, rows_x + 2 * HALO, LANES), bf16)] * shots + strip_shapes(1),
+        [pltpu.VMEM(whole, bf16), pltpu.VMEM(whole, bf16), index_scratch],
         15 * 10**9,
     )
-
-    def fetch(at):
-        own, same, core, cross = (pieces[i * len(sizes) + at] for i in range(4))
+    padded_planes, first_strips = made[:shots], made[shots:]
+    later_strips = call(
+        functools.partial(strips_kernel, shots=shots, strips=strips, width=width, groups=groups),
+        "strips",
+        (place,),
+        padded_planes,
+        strip_shapes(strips - 1),
+        [],
+        10**9,
+    )
+
+    def fetch(step, g, after=None):
+        if step == 0:
+            own, same, core, cross = (first_strips[i * len(groups) + g] for i in range(4))
+        else:
+            own, same, core, cross = (
+                later_strips[(i * (strips - 1) + step - 1) * len(groups) + g] for i in range(4)
+            )
+        if after is not None:
+            own, same, core, cross, _ = lax.optimization_barrier((own, same, core, cross, after))
         return [own, send(same, to_same), send(core, to_core), send(cross, to_cross)]
 
-    def correlate(fields, received, begin, end, offset, last, buffer, before):
-        count = end - begin
-        operands = [pinned(x) for x in fields + received]
-        in_specs = [VMEM_SPEC] * len(operands)
-        if before is not None and False:
-            operands.append(pinned(before))
-            in_specs.append(VMEM_SPEC)
-        aliases = {}
-        if last:
-            out_shape = jax.ShapeDtypeStruct((1, lags, width, rows_y), f32)
-            out_spec = pl.BlockSpec(
-                (1, lags, width, count * LANES), lambda i: (0, 0, 0, begin // count)
-            )
-            if buffer is not None:
-                in_specs.append(pl.BlockSpec(memory_space=pl.ANY))
-                aliases = {len(operands): 0}
-                operands.append(buffer)
-        else:
-            out_shape = pltpu.VMEM((lags, count, width, LANES), bf16)
-            out_spec = VMEM_SPEC
+    def correlate(fields, received, count, dtype):
+        operands = fields + received
         return pl.pallas_call(
             functools.partial(
-                correlate_kernel,
-                width=width,
-                begin=offset,
-                tiles=count,
-                partial=bool(received),
-                scale=factor if last else None,
+                correlate_kernel, width=width, tiles=count, partial=bool(received)
             ),
-            out_shape=out_shape,
+            out_shape=pltpu.VMEM((lags, count, width, LANES), dtype),
+            grid=(1,),
+            in_specs=[VMEM_SPEC] * len(operands),
+            out_specs=VMEM_SPEC,
+            scratch_shapes=[pltpu.VMEM((16, height, LANES), f32)],
+            compiler_params=pltpu.CompilerParams(vmem_limit_bytes=8 * 2**20),
+            cost_estimate=pl.CostEstimate(flops=10**9, bytes_accessed=10**6, transcendentals=0),
+            name="correlate",
+        )(*(pinned(x) for x in operands))
+
+    def finish(own, received, begin, end, image):
+        count = end - begin
+        operands = [pinned(own), pinned(received)]
+        in_specs = [VMEM_SPEC] * 2
+        aliases = {}
+        if image is not None:
+            operands.append(image)
+            in_specs.append(pl.BlockSpec(memory_space=pl.ANY))
+            aliases = {2: 0}
+        return pl.pallas_call(
+            functools.partial(finish_kernel, scale=factor),
+            out_shape=jax.ShapeDtypeStruct((1, lags, width, rows_y), f32),
             grid=(1,),
             in_specs=in_specs,
-            out_specs=out_spec,
-            scratch_shapes=[pltpu.VMEM((16, height, LANES), f32)],
+            out_specs=pl.BlockSpec(
+                (1, lags, width, count * LANES), lambda i: (0, 0, 0, begin // count)
+            ),
             input_output_aliases=aliases,
             compiler_params=pltpu.CompilerParams(vmem_limit_bytes=8 * 2**20),
             cost_estimate=pl.CostEstimate(flops=10**9, bytes_accessed=10**6, transcendentals=0),
-            name="correlate",
+            name="finish",
         )(*operands)
 
     image = None
-    before = None
-    received = [[]] * len(groups)
-    for step in range(strips):
-        last = step == strips - 1
-        fields = {}
+    received = [[] for _ in groups]
+    for step in range(strips - 1):
         for g, (begin, end) in enumerate(groups):
-            if step == 0:
-                at, offset = g, 0
-            else:
-                n = [n for n, cut in enumerate(later) if cut[0] <= begin < cut[1]][0]
-                at, offset = len(groups) + (step - 1) * len(later) + n, begin - later[n][0]
-            if at not in fields:
-                fields[at] = fetch(at)
-            parts = fields[at]
-            result = correlate(parts, received[g], begin, end, offset, last, image, before)
-            if last:
-                image = result
-                before = None
-            else:
-                before = result
-                received[g] = [send(result, onward)]
+            result = correlate(fetch(step, g), received[g], end - begin, bf16)
+            received[g] = [send(result, onward)]
+    for g, (begin, end) in enumerate(groups):
+        own = correlate(fetch(strips - 1, g, result), [], end - begin, f32)
+        image = finish(own, received[g][0], begin, end, image)
     return image
 
 

time: 123 us -> 121 us (0.984)
  waiting for transfers between devices: 49.1 us -> 47.1 us
    ppermute x36, waiting for transfers between devices: 49.1 us -> 47.1 us  [send(): return lax.ppermute(value, AXES, pairs(move, core))]
    pallas_call x2 -> x3, Pallas kernels: 21.8 us -> 21.4 us  [call(): pl.pallas_call(kernel, out_shape=[pltpu.VMEM(shape, dtype) for shape, dty...]
    pallas_call x8 -> x10, Pallas kernels: 8.15 us -> 8.26 us  [the longest x8 6.17 us: correlate(): pl.pallas_call(functools.partial(correlate_kernel, width=width, tiles=cou...]
  transfers between devices with their start and end apart: 36 -> 36, of which waited for: 22 -> 23; matrix products, arithmetic and copies ran while one was open for 0% -> 0% of each run, Pallas kernels for 19% -> 21%
where the time goes in v7:
time: 121 us
  waiting for transfers between devices  47.1 us (39%)
  Pallas kernels  39.8 us (33%)
  starting transfers between devices  33 us (27%)
    ppermute x36, waiting for transfers between devices, send(): return lax.ppermute(value, AXES, pairs(move, core))  47.1 us
    ppermute x36, starting transfers between devices, send(): return lax.ppermute(value, AXES, pairs(move, core))  33 us
    pallas_call x3, Pallas kernels, call(): pl.pallas_call(kernel, out_shape=[pltpu.VMEM(shape, dtype) for shape, dty...  21.4 us
    pallas_call x1, Pallas kernels, shards(): pl.pallas_call(functools.partial(prepare_kernel, shots=shots), out_shape=...  7.23 us
    pallas_call x8, Pallas kernels, correlate(): pl.pallas_call(functools.partial(correlate_kernel, width=width, tiles=cou...  6.17 us
    pallas_call x1, Pallas kernels, windows(): pl.pallas_call(functools.partial(window_kernel, blocks=blocks), out_shape...  2.97 us
  transfers between devices with their start and end apart: 36, of which 23 were waited for; matrix products, arithmetic and copies ran while one was open for 0% of the time, Pallas kernels for 21%

profile of v7, /device:TPU:4, one launch (start us, length us, event | category | flops | bytes accessed | tf_op | source)
XLA Modules:
  0.0 120.9 jit_solution(12697945816786359898)
XLA Ops:
  0.8 3.0 %windows.1 = (bf16[512,512]{1,0:T(8,128)(2,1)S(1)}, bf16[512,512]{1,0:T(8,128)(2,1)}) custom-call(s32[4]{0:T(128)S(1)} %pad_add_fusion.place, s32[2,2]{1,0:T(2,128)S(1)} %copy-done, s32[1,1024,1024]{2,1,0:T(8,128)} %codes.1), custom_call_target="tpu_custom_call" | custom-call | tf_op jit(solution)/shard_map/windows/pallas_call | solution.py:458
  3.8 1.3 %collective-permute-start.1 = (bf16[512,512]{1,0:T(8,128)(2,1)S(1)}, bf16[512,512]{1,0:T(8,128)(2,1)S(1)}, u32[]{:S(2)}, u32[]{:S(2)}) collective-permute-start(bf16[512,512]{1,0:T(8,128)(2,1)S(1)} %get-tuple-element.64.mine.refs_5_), channel_id=1, source_target_pairs={{0,16},{1,17},{2,18},{3,19},{4,20},{5,21},{6,22},{7,23}} | collective-permute-start | bytes 1572872 | tf_op jit(solution)/shard_map/ppermute | solution.py:511
  5.1 0.8 collective-permute-done.from_core.refs_6_
  6.7 7.2 %prepare.1 = (bf16[4,512,512]{2,1,0:T(8,128)(2,1)S(1)}, bf16[4,512,512]{2,1,0:T(8,128)(2,1)S(1)}, f32[8,128]{1,0:T(8,128)S(1)}, f32[2,2,384,384]{3,2,1,0:T(8,128...) custom-call(s32[4]{0:T(128)S(1)} %pad_add_fusion.place, f32[1]{0:T(128)} %bitcast.4.angular_ref, ...), custom_call_target="tpu_custom_call" | custom-call | flops 4000000000 | bytes 1000000 | tf_op jit(solution)/shard_map/prepare/pallas_call | solution.py:559
  13.9 1.3 %collective-permute-start.3 = (f32[8,128]{1,0:T(8,128)S(1)}, f32[8,128]{1,0:T(8,128)S(1)}, u32[]{:S(2)}, u32[]{:S(2)}) collective-permute-start(f32[8,128]{1,0:T(8,128)S(1)} %get-tuple-element.61.refs_7_), channel_id=1, source_target_pairs={{0,16},{1,17},{2,18},{3,19},{4,20},{5,21},{6,22},{7,23},{8,24},{9,... | collective-permute-start | bytes 12296 | tf_op jit(solution)/shard_map/ppermute | solution.py:511
  15.9 1.3 %collective-permute-start.5 = (bf16[512,512]{1,0:T(8,128)(2,1)S(1)}, bf16[512,512]{1,0:T(8,128)(2,1)S(1)}, u32[]{:S(2)}, u32[]{:S(2)}) collective-permute-start(bf16[512,512]{1,0:T(8,128)(2,1)S(1)} %collective-permute-done.from_core.refs_6_), channel_id=1, source_target_pairs={{0,16},{1,17},{2,18},{3,19},{4,20},{5,21},{6,22},{7,23}} | collective-permute-start | bytes 1572872 | tf_op jit(solution)/shard_map/ppermute | solution.py:511
  17.2 2.0 %collective-permute-done.1.far_a = bf16[512,512]{1,0:T(8,128)(2,1)S(1)} collective-permute-done((bf16[512,512]{1,0:T(8,128)(2,1)S(1)}, bf16[512,512]{1,0:T(8,128)(2,1)S(1)}, u32[]{:S(2)}, u32[]{:S(2)}) %collective-permute-start.1) | collective-permute-done | bytes 524320 | tf_op jit(solution)/shard_map/ppermute | solution.py:511
  19.5 9.9 %lead.1.refs_1_ = f32[4,512,512]{2,1,0:T(8,128)S(1)} custom-call(s32[4]{0:T(128)S(1)} %pad_add_fusion.place, f32[1]{0:T(128)} %bitcast.4.angular_ref, bf16[4,512,512]{2,1,0:T(8,128)(2,1)S(1)} %get-tuple-element.60.first, bf16[512,512]{1,0:T(8,128)(2,1)S(1)} %collective-permute-done.1.far_a, bf16[512,512]{1,0:T(8,128)(2,1)S(1)} %collective-permute-done.2.far_b, ...), custom_call_target="tpu_custom_call" | custom-call | flops 15000000512 | bytes 1000000 | tf_op jit(solution)/shard_map/lead/pallas_call | solution.py:440
  29.5 2.4 %collective-permute-done.5.refs_3_ = bf16[512,512]{1,0:T(8,128)(2,1)S(1)} collective-permute-done((bf16[512,512]{1,0:T(8,128)(2,1)S(1)}, bf16[512,512]{1,0:T(8,128)(2,1)S(1)}, u32[]{:S(2)}, u32[]{:S(2)}) %collective-permute-start.5) | collective-permute-done | bytes 524320 | tf_op jit(solution)/shard_map/ppermute | solution.py:511
  31.8 10.6 %planes.1 = (bf16[4,4,528,128]{3,2,1,0:T(8,128)(2,1)S(1)}, bf16[4,4,528,128]{3,2,1,0:T(8,128)(2,1)S(1)}, bf16[4,2,80,128]{3,2,1,0:T(8,128)(2,1)S(1)}, bf16[4,2,8...) custom-call(s32[4]{0:T(128)S(1)} %pad_add_fusion.place, ...), custom_call_target="tpu_custom_call" | custom-call | flops 15000000512 | bytes 1000000 | tf_op jit(solution)/shard_map/planes/pallas_call | solution.py:440
  42.5 1.6 %collective-permute-start.30 = (bf16[4,2,80,128]{3,2,1,0:T(8,128)(2,1)S(1)}, bf16[4,2,80,128]{3,2,1,0:T(8,128)(2,1)S(1)}, u32[]{:S(2)}, u32[]{:S(2)}) collective-permute-start(bf16[4,2,80,128]{3,2,1,0:T(8,128)(2,1)S(1)} %get-tuple-element.106), channel_id=1, source_target_pairs={{0,1},{1,0},{2,3},{3,2},{4,5},{5,4},{6,7},{7,6},{8,9},{9,8},{10,11... | collective-permute-start | bytes 491528 | tf_op jit(solution)/shard_map/ppermute | solution.py:511
  44.7 1.5 %collective-permute-start.12 = (bf16[4,2,80,128]{3,2,1,0:T(8,128)(2,1)S(1)}, bf16[4,2,80,128]{3,2,1,0:T(8,128)(2,1)S(1)}, u32[]{:S(2)}, u32[]{:S(2)}) collective-permute-start(bf16[4,2,80,128]{3,2,1,0:T(8,128)(2,1)S(1)} %get-tuple-element.82), channel_id=1, source_target_pairs={{0,1},{1,0},{2,3},{3,2},{4,5},{5,4},{6,7},{7,6},{8,9},{9,8},{10,11... | collective-permute-start | bytes 491528 | tf_op jit(solution)/shard_map/ppermute | solution.py:511
  46.1 2.7 %collective-permute-done.30.refs_1_ = bf16[4,2,80,128]{3,2,1,0:T(8,128)(2,1)S(1)} collective-permute-done((bf16[4,2,80,128]{3,2,1,0:T(8,128)(2,1)S(1)}, bf16[4,2,80,128]{3,2,1,0:T(8,128)(2,1)S(1)}, u32[]{:S(2)}, u32[]{:S(2)}) %collective-permute-start.30) | collective-permute-done | bytes 163872 | tf_op jit(solution)/shard_map/ppermute | solution.py:511
  48.8 3.4 %collective-permute-done.32.refs_3_ = bf16[4,2,80,128]{3,2,1,0:T(8,128)(2,1)S(1)} collective-permute-done((bf16[4,2,80,128]{3,2,1,0:T(8,128)(2,1)S(1)}, bf16[4,2,80,128]{3,2,1,0:T(8,128)(2,1)S(1)}, u32[]{:S(2)}, u32[]{:S(2)}) %collective-permute-start.32) | collective-permute-done | bytes 163872 | tf_op jit(solution)/shard_map/ppermute | solution.py:511
  52.9 1.9 %collective-permute-start.33 = (bf16[15,2,64,128]{3,2,1,0:T(8,128)(2,1)S(1)}, bf16[15,2,64,128]{3,2,1,0:T(8,128)(2,1)S(1)}, u32[]{:S(2)}, u32[]{:S(2)}) collective-permute-start(bf16[15,2,64,128]{3,2,1,0:T(8,128)(2,1)S(1)} %correlate.13), channel_id=1, source_target_pairs={{0,2},{1,3},{2,6},{3,7},{4,0},{5,1},{6,4},{7,5},{8,10},{9,11},{10,... | collective-permute-start | bytes 1474568 | tf_op jit(solution)/shard_map/ppermute | solution.py:511
  54.8 1.0 collective-permute-done.12.refs_1_
  55.8 1.7 %collective-permute-done.14.refs_3_ = bf16[4,2,80,128]{3,2,1,0:T(8,128)(2,1)S(1)} collective-permute-done((bf16[4,2,80,128]{3,2,1,0:T(8,128)(2,1)S(1)}, bf16[4,2,80,128]{3,2,1,0:T(8,128)(2,1)S(1)}, u32[]{:S(2)}, u32[]{:S(2)}) %collective-permute-start.14) | collective-permute-done | bytes 163872 | tf_op jit(solution)/shard_map/ppermute | solution.py:511
  58.3 1.6 %collective-permute-start.15 = (bf16[15,2,64,128]{3,2,1,0:T(8,128)(2,1)S(1)}, bf16[15,2,64,128]{3,2,1,0:T(8,128)(2,1)S(1)}, u32[]{:S(2)}, u32[]{:S(2)}) collective-permute-start(bf16[15,2,64,128]{3,2,1,0:T(8,128)(2,1)S(1)} %correlate.8), channel_id=1, source_target_pairs={{0,2},{1,3},{2,6},{3,7},{4,0},{5,1},{6,4},{7,5},{8,10},{9,11},{10,... | collective-permute-start | bytes 1474568 | tf_op jit(solution)/shard_map/ppermute | solution.py:511
  59.9 0.8 strips.1
  61.4 1.3 %collective-permute-start.28 = (bf16[4,2,80,128]{3,2,1,0:T(8,128)(2,1)S(1)}, bf16[4,2,80,128]{3,2,1,0:T(8,128)(2,1)S(1)}, u32[]{:S(2)}, u32[]{:S(2)}) collective-permute-start(bf16[4,2,80,128]{3,2,1,0:T(8,128)(2,1)S(1)} %get-tuple-element.103), channel_id=1, source_target_pairs={{0,8},{1,9},{2,10},{3,11},{4,12},{5,13},{6,14},{7,15},{8,0},{9,1},... | collective-permute-start | bytes 491528 | tf_op jit(solution)/shard_map/ppermute | solution.py:511
  62.9 4.9 %collective-permute-done.27.refs_1_ = bf16[4,2,80,128]{3,2,1,0:T(8,128)(2,1)S(1)} collective-permute-done((bf16[4,2,80,128]{3,2,1,0:T(8,128)(2,1)S(1)}, bf16[4,2,80,128]{3,2,1,0:T(8,128)(2,1)S(1)}, u32[]{:S(2)}, u32[]{:S(2)}) %collective-permute-start.27) | collective-permute-done | bytes 163872 | tf_op jit(solution)/shard_map/ppermute | solution.py:511
  68.0 1.0 collective-permute-start.10
  68.9 2.0 %collective-permute-done.29.refs_3_ = bf16[4,2,80,128]{3,2,1,0:T(8,128)(2,1)S(1)} collective-permute-done((bf16[4,2,80,128]{3,2,1,0:T(8,128)(2,1)S(1)}, bf16[4,2,80,128]{3,2,1,0:T(8,128)(2,1)S(1)}, u32[]{:S(2)}, u32[]{:S(2)}) %collective-permute-start.29) | collective-permute-done | bytes 163872 | tf_op jit(solution)/shard_map/ppermute | solution.py:511
  71.2 0.8 correlate.14
  72.0 2.6 %collective-permute-start.34 = (bf16[15,2,64,128]{3,2,1,0:T(8,128)(2,1)S(1)}, bf16[15,2,64,128]{3,2,1,0:T(8,128)(2,1)S(1)}, u32[]{:S(2)}, u32[]{:S(2)}) collective-permute-start(bf16[15,2,64,128]{3,2,1,0:T(8,128)(2,1)S(1)} %correlate.14), channel_id=1, source_target_pairs={{0,2},{1,3},{2,6},{3,7},{4,0},{5,1},{6,4},{7,5},{8,10},{9,11},{10,... | collective-permute-start | bytes 1474568 | tf_op jit(solution)/shard_map/ppermute | solution.py:511
  75.0 2.8 %collective-permute-done.11.refs_3_ = bf16[4,2,80,128]{3,2,1,0:T(8,128)(2,1)S(1)} collective-permute-done((bf16[4,2,80,128]{3,2,1,0:T(8,128)(2,1)S(1)}, bf16[4,2,80,128]{3,2,1,0:T(8,128)(2,1)S(1)}, u32[]{:S(2)}, u32[]{:S(2)}) %collective-permute-start.11) | collective-permute-done | bytes 163872 | tf_op jit(solution)/shard_map/ppermute | solution.py:511
  78.4 0.8 correlate.9
  79.2 2.0 %collective-permute-start.16 = (bf16[15,2,64,128]{3,2,1,0:T(8,128)(2,1)S(1)}, bf16[15,2,64,128]{3,2,1,0:T(8,128)(2,1)S(1)}, u32[]{:S(2)}, u32[]{:S(2)}) collective-permute-start(bf16[15,2,64,128]{3,2,1,0:T(8,128)(2,1)S(1)} %correlate.9), channel_id=1, source_target_pairs={{0,2},{1,3},{2,6},{3,7},{4,0},{5,1},{6,4},{7,5},{8,10},{9,11},{10,... | collective-permute-start | bytes 1474568 | tf_op jit(solution)/shard_map/ppermute | solution.py:511
  81.3 1.2 %collective-permute-start.24 = (bf16[4,2,80,128]{3,2,1,0:T(8,128)(2,1)S(1)}, bf16[4,2,80,128]{3,2,1,0:T(8,128)(2,1)S(1)}, u32[]{:S(2)}, u32[]{:S(2)}) collective-permute-start(bf16[4,2,80,128]{3,2,1,0:T(8,128)(2,1)S(1)} %get-tuple-element.98), channel_id=1, source_target_pairs={{0,1},{1,0},{2,3},{3,2},{4,5},{5,4},{6,7},{7,6},{8,9},{9,8},{10,11... | collective-permute-start | bytes 491528 | tf_op jit(solution)/shard_map/ppermute | solution.py:511
  82.5 0.9 collective-permute-start.26
  83.4 4.9 %collective-permute-done.24.refs_1_ = bf16[4,2,80,128]{3,2,1,0:T(8,128)(2,1)S(1)} collective-permute-done((bf16[4,2,80,128]{3,2,1,0:T(8,128)(2,1)S(1)}, bf16[4,2,80,128]{3,2,1,0:T(8,128)(2,1)S(1)}, u32[]{:S(2)}, u32[]{:S(2)}) %collective-permute-start.24) | collective-permute-done | bytes 163872 | tf_op jit(solution)/shard_map/ppermute | solution.py:511
  88.3 1.3 %collective-permute-start.6 = (bf16[4,2,80,128]{3,2,1,0:T(8,128)(2,1)S(1)}, bf16[4,2,80,128]{3,2,1,0:T(8,128)(2,1)S(1)}, u32[]{:S(2)}, u32[]{:S(2)}) collective-permute-start(bf16[4,2,80,128]{3,2,1,0:T(8,128)(2,1)S(1)} %get-tuple-element.74), channel_id=1, source_target_pairs={{0,1},{1,0},{2,3},{3,2},{4,5},{5,4},{6,7},{7,6},{8,9},{9,8},{10,11... | collective-permute-start | bytes 491528 | tf_op jit(solution)/shard_map/ppermute | solution.py:511
  89.6 1.0 collective-permute-done.26.refs_3_
  90.7 2.2 %collective-permute-start.8 = (bf16[4,2,80,128]{3,2,1,0:T(8,128)(2,1)S(1)}, bf16[4,2,80,128]{3,2,1,0:T(8,128)(2,1)S(1)}, u32[]{:S(2)}, u32[]{:S(2)}) collective-permute-start(bf16[4,2,80,128]{3,2,1,0:T(8,128)(2,1)S(1)} %get-tuple-element.76), channel_id=1, source_target_pairs={{0,9},{1,8},{2,11},{3,10},{4,13},{5,12},{6,15},{7,14},{8,1},{9,0},... | collective-permute-start | bytes 491528 | tf_op jit(solution)/shard_map/ppermute | solution.py:511
  92.9 0.8 correlate.15
  93.6 1.2 collective-permute-start.35
  95.0 2.6 %collective-permute-done.8.refs_3_ = bf16[4,2,80,128]{3,2,1,0:T(8,128)(2,1)S(1)} collective-permute-done((bf16[4,2,80,128]{3,2,1,0:T(8,128)(2,1)S(1)}, bf16[4,2,80,128]{3,2,1,0:T(8,128)(2,1)S(1)}, u32[]{:S(2)}, u32[]{:S(2)}) %collective-permute-start.8) | collective-permute-done | bytes 163872 | tf_op jit(solution)/shard_map/ppermute | solution.py:511
  97.6 1.9 %collective-permute-done.16.refs_4_ = bf16[15,2,64,128]{3,2,1,0:T(8,128)(2,1)S(1)} collective-permute-done((bf16[15,2,64,128]{3,2,1,0:T(8,128)(2,1)S(1)}, bf16[15,2,64,128]{3,2,1,0:T(8,128)(2,1)S(1)}, u32[]{:S(2)}, u32[]{:S(2)}) %collective-permute-start.16) | collective-permute-done | bytes 491552 | tf_op jit(solution)/shard_map/ppermute | solution.py:511
  100.4 2.0 %collective-permute-start.23 = (bf16[4,2,80,128]{3,2,1,0:T(8,128)(2,1)S(1)}, bf16[4,2,80,128]{3,2,1,0:T(8,128)(2,1)S(1)}, u32[]{:S(2)}, u32[]{:S(2)}) collective-permute-start(bf16[4,2,80,128]{3,2,1,0:T(8,128)(2,1)S(1)} %get-tuple-element.96), channel_id=1, source_target_pairs={{0,9},{1,8},{2,11},{3,10},{4,13},{5,12},{6,15},{7,14},{8,1},{9,0},... | collective-permute-start | bytes 491528 | tf_op jit(solution)/shard_map/ppermute | solution.py:511
  102.5 1.1 collective-permute-start.20
  103.6 3.9 %collective-permute-done.21.refs_1_ = bf16[4,2,80,128]{3,2,1,0:T(8,128)(2,1)S(1)} collective-permute-done((bf16[4,2,80,128]{3,2,1,0:T(8,128)(2,1)S(1)}, bf16[4,2,80,128]{3,2,1,0:T(8,128)(2,1)S(1)}, u32[]{:S(2)}, u32[]{:S(2)}) %collective-permute-start.21) | collective-permute-done | bytes 163872 | tf_op jit(solution)/shard_map/ppermute | solution.py:511
  107.5 1.0 collective-permute-done.23.refs_3_
  108.5 2.2 %collective-permute-start.19 = (bf16[4,2,80,128]{3,2,1,0:T(8,128)(2,1)S(1)}, bf16[4,2,80,128]{3,2,1,0:T(8,128)(2,1)S(1)}, u32[]{:S(2)}, u32[]{:S(2)}) collective-permute-start(bf16[4,2,80,128]{3,2,1,0:T(8,128)(2,1)S(1)} %get-tuple-element.88), channel_id=1, source_target_pairs={{0,9},{1,8},{2,11},{3,10},{4,13},{5,12},{6,15},{7,14},{8,1},{9,0},... | collective-permute-start | bytes 491528 | tf_op jit(solution)/shard_map/ppermute | solution.py:511
  111.5 2.1 %collective-permute-done.17.refs_1_ = bf16[4,2,80,128]{3,2,1,0:T(8,128)(2,1)S(1)} collective-permute-done((bf16[4,2,80,128]{3,2,1,0:T(8,128)(2,1)S(1)}, bf16[4,2,80,128]{3,2,1,0:T(8,128)(2,1)S(1)}, u32[]{:S(2)}, u32[]{:S(2)}) %collective-permute-start.17) | collective-permute-done | bytes 163872 | tf_op jit(solution)/shard_map/ppermute | solution.py:511
  113.5 1.3 %collective-permute-done.19.refs_3_ = bf16[4,2,80,128]{3,2,1,0:T(8,128)(2,1)S(1)} collective-permute-done((bf16[4,2,80,128]{3,2,1,0:T(8,128)(2,1)S(1)}, bf16[4,2,80,128]{3,2,1,0:T(8,128)(2,1)S(1)}, u32[]{:S(2)}, u32[]{:S(2)}) %collective-permute-start.19) | collective-permute-done | bytes 163872 | tf_op jit(solution)/shard_map/ppermute | solution.py:511
  115.7 1.0 finish.2.refs_0_
  116.7 3.1 %collective-permute-done.20.received = bf16[15,2,64,128]{3,2,1,0:T(8,128)(2,1)S(1)} collective-permute-done((bf16[15,2,64,128]{3,2,1,0:T(8,128)(2,1)S(1)}, bf16[15,2,64,128]{3,2,1,0:T(8,128)(2,1)S(1)}, u32[]{:S(2)}, u32[]{:S(2)}) %collective-permute-start.20) | collective-permute-done | bytes 491552 | tf_op jit(solution)/shard_map/ppermute | solution.py:511
  119.9 1.0 finish.3
  (49 shorter events, 9.6 us)
Async XLA Ops:
  0.1 0.7 copy-start
  0.8 5.9 %copy-start.3 = (f32[32]{0:T(128)S(1)}, f32[32]{0:T(128)}, u32[]{:S(2)}) copy-start(f32[32]{0:T(128)} %param.12) | copy-start | bytes 388
  0.8 5.9 %copy-start.1 = (f32[384,1]{1,0:T(8,128)S(1)}, f32[384,1]{1,0:T(8,128)}, u32[]{:S(2)}) copy-start(f32[384,1]{1,0:T(8,128)} %constant.87.clone.refs_2_.wave_x) | copy-start | bytes 4612
  0.8 5.9 %copy-start.2 = (f32[1,384]{1,0:T(1,128)S(1)}, f32[1,384]{1,0:T(1,128)}, u32[]{:S(2)}) copy-start(f32[1,384]{1,0:T(1,128)} %constant.88.clone.refs_3_.wave_y) | copy-start | bytes 4612
  3.7 2.2 %collective-permute-start = (bf16[512,512]{1,0:T(8,128)(2,1)}, bf16[512,512]{1,0:T(8,128)(2,1)S(1)}, u32[]{:S(2)}, u32[]{:S(2)}) collective-permute-start(bf16[512,512]{1,0:T(8,128)(2,1)} %get-tuple-element.58), channel_id=1, source_target_pairs={{0,8},{1,9},{2,10},{3,11},{4,12},{5,13},{6,14},{7,15},{8,0},{9,1},... | collective-permute-start | bytes 1572872 | tf_op jit(solution)/shard_map/ppermute | solution.py:511
  3.8 15.4 %collective-permute-start.1 = (bf16[512,512]{1,0:T(8,128)(2,1)S(1)}, bf16[512,512]{1,0:T(8,128)(2,1)S(1)}, u32[]{:S(2)}, u32[]{:S(2)}) collective-permute-start(bf16[512,512]{1,0:T(8,128)(2,1)S(1)} %get-tuple-element.64.mine.refs_5_), channel_id=1, source_target_pairs={{0,16},{1,17},{2,18},{3,19},{4,20},{5,21},{6,22},{7,23}} | collective-permute-start | bytes 1572872 | tf_op jit(solution)/shard_map/ppermute | solution.py:511
  5.9 13.6 %collective-permute-start.2 = (bf16[512,512]{1,0:T(8,128)(2,1)S(1)}, bf16[512,512]{1,0:T(8,128)(2,1)S(1)}, u32[]{:S(2)}, u32[]{:S(2)}) collective-permute-start(bf16[512,512]{1,0:T(8,128)(2,1)S(1)} %collective-permute-done.from_core.refs_6_), channel_id=1, source_target_pairs={{8,24},{9,25},{10,26},{11,27},{12,28},{13,29},{14,30},{15,31}} | collective-permute-start | bytes 1572872 | tf_op jit(solution)/shard_map/ppermute | solution.py:511
  13.9 5.6 %collective-permute-start.3 = (f32[8,128]{1,0:T(8,128)S(1)}, f32[8,128]{1,0:T(8,128)S(1)}, u32[]{:S(2)}, u32[]{:S(2)}) collective-permute-start(f32[8,128]{1,0:T(8,128)S(1)} %get-tuple-element.61.refs_7_), channel_id=1, source_target_pairs={{0,16},{1,17},{2,18},{3,19},{4,20},{5,21},{6,22},{7,23},{8,24},{9,... | collective-permute-start | bytes 12296 | tf_op jit(solution)/shard_map/ppermute | solution.py:511
  15.2 14.2 %collective-permute-start.4 = (bf16[512,512]{1,0:T(8,128)(2,1)S(1)}, bf16[512,512]{1,0:T(8,128)(2,1)S(1)}, u32[]{:S(2)}, u32[]{:S(2)}) collective-permute-start(bf16[512,512]{1,0:T(8,128)(2,1)S(1)} %get-tuple-element.64.mine.refs_5_), channel_id=1, source_target_pairs={{8,24},{9,25},{10,26},{11,27},{12,28},{13,29},{14,30},{15,31}} | collective-permute-start | bytes 1572872 | tf_op jit(solution)/shard_map/ppermute | solution.py:511
  15.9 15.9 %collective-permute-start.5 = (bf16[512,512]{1,0:T(8,128)(2,1)S(1)}, bf16[512,512]{1,0:T(8,128)(2,1)S(1)}, u32[]{:S(2)}, u32[]{:S(2)}) collective-permute-start(bf16[512,512]{1,0:T(8,128)(2,1)S(1)} %collective-permute-done.from_core.refs_6_), channel_id=1, source_target_pairs={{0,16},{1,17},{2,18},{3,19},{4,20},{5,21},{6,22},{7,23}} | collective-permute-start | bytes 1572872 | tf_op jit(solution)/shard_map/ppermute | solution.py:511
  42.5 6.4 %collective-permute-start.30 = (bf16[4,2,80,128]{3,2,1,0:T(8,128)(2,1)S(1)}, bf16[4,2,80,128]{3,2,1,0:T(8,128)(2,1)S(1)}, u32[]{:S(2)}, u32[]{:S(2)}) collective-permute-start(bf16[4,2,80,128]{3,2,1,0:T(8,128)(2,1)S(1)} %get-tuple-element.106), channel_id=1, source_target_pairs={{0,1},{1,0},{2,3},{3,2},{4,5},{5,4},{6,7},{7,6},{8,9},{9,8},{10,11... | collective-permute-start | bytes 491528 | tf_op jit(solution)/shard_map/ppermute | solution.py:511
  44.0 4.8 %collective-permute-start.31 = (bf16[4,2,80,128]{3,2,1,0:T(8,128)(2,1)S(1)}, bf16[4,2,80,128]{3,2,1,0:T(8,128)(2,1)S(1)}, u32[]{:S(2)}, u32[]{:S(2)}) collective-permute-start(bf16[4,2,80,128]{3,2,1,0:T(8,128)(2,1)S(1)} %get-tuple-element.107), channel_id=1, source_target_pairs={{0,8},{1,9},{2,10},{3,11},{4,12},{5,13},{6,14},{7,15},{8,0},{9,1},... | collective-permute-start | bytes 491528 | tf_op jit(solution)/shard_map/ppermute | solution.py:511
  44.0 8.2 %collective-permute-start.32 = (bf16[4,2,80,128]{3,2,1,0:T(8,128)(2,1)S(1)}, bf16[4,2,80,128]{3,2,1,0:T(8,128)(2,1)S(1)}, u32[]{:S(2)}, u32[]{:S(2)}) collective-permute-start(bf16[4,2,80,128]{3,2,1,0:T(8,128)(2,1)S(1)} %get-tuple-element.108), channel_id=1, source_target_pairs={{0,9},{1,8},{2,11},{3,10},{4,13},{5,12},{6,15},{7,14},{8,1},{9,0},... | collective-permute-start | bytes 491528 | tf_op jit(solution)/shard_map/ppermute | solution.py:511
  44.7 11.2 %collective-permute-start.12 = (bf16[4,2,80,128]{3,2,1,0:T(8,128)(2,1)S(1)}, bf16[4,2,80,128]{3,2,1,0:T(8,128)(2,1)S(1)}, u32[]{:S(2)}, u32[]{:S(2)}) collective-permute-start(bf16[4,2,80,128]{3,2,1,0:T(8,128)(2,1)S(1)} %get-tuple-element.82), channel_id=1, source_target_pairs={{0,1},{1,0},{2,3},{3,2},{4,5},{5,4},{6,7},{7,6},{8,9},{9,8},{10,11... | collective-permute-start | bytes 491528 | tf_op jit(solution)/shard_map/ppermute | solution.py:511
  46.1 9.7 %collective-permute-start.13 = (bf16[4,2,80,128]{3,2,1,0:T(8,128)(2,1)S(1)}, bf16[4,2,80,128]{3,2,1,0:T(8,128)(2,1)S(1)}, u32[]{:S(2)}, u32[]{:S(2)}) collective-permute-start(bf16[4,2,80,128]{3,2,1,0:T(8,128)(2,1)S(1)} %get-tuple-element.83), channel_id=1, source_target_pairs={{0,8},{1,9},{2,10},{3,11},{4,12},{5,13},{6,14},{7,15},{8,0},{9,1},... | collective-permute-start | bytes 491528 | tf_op jit(solution)/shard_map/ppermute | solution.py:511
  48.8 8.7 %collective-permute-start.14 = (bf16[4,2,80,128]{3,2,1,0:T(8,128)(2,1)S(1)}, bf16[4,2,80,128]{3,2,1,0:T(8,128)(2,1)S(1)}, u32[]{:S(2)}, u32[]{:S(2)}) collective-permute-start(bf16[4,2,80,128]{3,2,1,0:T(8,128)(2,1)S(1)} %get-tuple-element.84), channel_id=1, source_target_pairs={{0,9},{1,8},{2,11},{3,10},{4,13},{5,12},{6,15},{7,14},{8,1},{9,0},... | collective-permute-start | bytes 491528 | tf_op jit(solution)/shard_map/ppermute | solution.py:511
  52.9 18.3 %collective-permute-start.33 = (bf16[15,2,64,128]{3,2,1,0:T(8,128)(2,1)S(1)}, bf16[15,2,64,128]{3,2,1,0:T(8,128)(2,1)S(1)}, u32[]{:S(2)}, u32[]{:S(2)}) collective-permute-start(bf16[15,2,64,128]{3,2,1,0:T(8,128)(2,1)S(1)} %correlate.13), channel_id=1, source_target_pairs={{0,2},{1,3},{2,6},{3,7},{4,0},{5,1},{6,4},{7,5},{8,10},{9,11},{10,... | collective-permute-start | bytes 1474568 | tf_op jit(solution)/shard_map/ppermute | solution.py:511
  58.3 20.2 %collective-permute-start.15 = (bf16[15,2,64,128]{3,2,1,0:T(8,128)(2,1)S(1)}, bf16[15,2,64,128]{3,2,1,0:T(8,128)(2,1)S(1)}, u32[]{:S(2)}, u32[]{:S(2)}) collective-permute-start(bf16[15,2,64,128]{3,2,1,0:T(8,128)(2,1)S(1)} %correlate.8), channel_id=1, source_target_pairs={{0,2},{1,3},{2,6},{3,7},{4,0},{5,1},{6,4},{7,5},{8,10},{9,11},{10,... | collective-permute-start | bytes 1474568 | tf_op jit(solution)/shard_map/ppermute | solution.py:511
  60.7 7.1 %collective-permute-start.27 = (bf16[4,2,80,128]{3,2,1,0:T(8,128)(2,1)S(1)}, bf16[4,2,80,128]{3,2,1,0:T(8,128)(2,1)S(1)}, u32[]{:S(2)}, u32[]{:S(2)}) collective-permute-start(bf16[4,2,80,128]{3,2,1,0:T(8,128)(2,1)S(1)} %get-tuple-element.102), channel_id=1, source_target_pairs={{0,1},{1,0},{2,3},{3,2},{4,5},{5,4},{6,7},{7,6},{8,9},{9,8},{10,11... | collective-permute-start | bytes 491528 | tf_op jit(solution)/shard_map/ppermute | solution.py:511
  61.4 6.5 %collective-permute-start.28 = (bf16[4,2,80,128]{3,2,1,0:T(8,128)(2,1)S(1)}, bf16[4,2,80,128]{3,2,1,0:T(8,128)(2,1)S(1)}, u32[]{:S(2)}, u32[]{:S(2)}) collective-permute-start(bf16[4,2,80,128]{3,2,1,0:T(8,128)(2,1)S(1)} %get-tuple-element.103), channel_id=1, source_target_pairs={{0,8},{1,9},{2,10},{3,11},{4,12},{5,13},{6,14},{7,15},{8,0},{9,1},... | collective-permute-start | bytes 491528 | tf_op jit(solution)/shard_map/ppermute | solution.py:511
  62.7 8.2 %collective-permute-start.29 = (bf16[4,2,80,128]{3,2,1,0:T(8,128)(2,1)S(1)}, bf16[4,2,80,128]{3,2,1,0:T(8,128)(2,1)S(1)}, u32[]{:S(2)}, u32[]{:S(2)}) collective-permute-start(bf16[4,2,80,128]{3,2,1,0:T(8,128)(2,1)S(1)} %get-tuple-element.104), channel_id=1, source_target_pairs={{0,9},{1,8},{2,11},{3,10},{4,13},{5,12},{6,15},{7,14},{8,1},{9,0},... | collective-permute-start | bytes 491528 | tf_op jit(solution)/shard_map/ppermute | solution.py:511
  67.9 7.1 %collective-permute-start.9 = (bf16[4,2,80,128]{3,2,1,0:T(8,128)(2,1)S(1)}, bf16[4,2,80,128]{3,2,1,0:T(8,128)(2,1)S(1)}, u32[]{:S(2)}, u32[]{:S(2)}) collective-permute-start(bf16[4,2,80,128]{3,2,1,0:T(8,128)(2,1)S(1)} %get-tuple-element.78), channel_id=1, source_target_pairs={{0,1},{1,0},{2,3},{3,2},{4,5},{5,4},{6,7},{7,6},{8,9},{9,8},{10,11... | collective-permute-start | bytes 491528 | tf_op jit(solution)/shard_map/ppermute | solution.py:511
  68.0 7.0 %collective-permute-start.10 = (bf16[4,2,80,128]{3,2,1,0:T(8,128)(2,1)S(1)}, bf16[4,2,80,128]{3,2,1,0:T(8,128)(2,1)S(1)}, u32[]{:S(2)}, u32[]{:S(2)}) collective-permute-start(bf16[4,2,80,128]{3,2,1,0:T(8,128)(2,1)S(1)} %get-tuple-element.79), channel_id=1, source_target_pairs={{0,8},{1,9},{2,10},{3,11},{4,12},{5,13},{6,14},{7,15},{8,0},{9,1},... | collective-permute-start | bytes 491528 | tf_op jit(solution)/shard_map/ppermute | solution.py:511
  70.9 6.9 %collective-permute-start.11 = (bf16[4,2,80,128]{3,2,1,0:T(8,128)(2,1)S(1)}, bf16[4,2,80,128]{3,2,1,0:T(8,128)(2,1)S(1)}, u32[]{:S(2)}, u32[]{:S(2)}) collective-permute-start(bf16[4,2,80,128]{3,2,1,0:T(8,128)(2,1)S(1)} %get-tuple-element.80), channel_id=1, source_target_pairs={{0,9},{1,8},{2,11},{3,10},{4,13},{5,12},{6,15},{7,14},{8,1},{9,0},... | collective-permute-start | bytes 491528 | tf_op jit(solution)/shard_map/ppermute | solution.py:511
  72.0 20.9 %collective-permute-start.34 = (bf16[15,2,64,128]{3,2,1,0:T(8,128)(2,1)S(1)}, bf16[15,2,64,128]{3,2,1,0:T(8,128)(2,1)S(1)}, u32[]{:S(2)}, u32[]{:S(2)}) collective-permute-start(bf16[15,2,64,128]{3,2,1,0:T(8,128)(2,1)S(1)} %correlate.14), channel_id=1, source_target_pairs={{0,2},{1,3},{2,6},{3,7},{4,0},{5,1},{6,4},{7,5},{8,10},{9,11},{10,... | collective-permute-start | bytes 1474568 | tf_op jit(solution)/shard_map/ppermute | solution.py:511
  79.2 20.3 %collective-permute-start.16 = (bf16[15,2,64,128]{3,2,1,0:T(8,128)(2,1)S(1)}, bf16[15,2,64,128]{3,2,1,0:T(8,128)(2,1)S(1)}, u32[]{:S(2)}, u32[]{:S(2)}) collective-permute-start(bf16[15,2,64,128]{3,2,1,0:T(8,128)(2,1)S(1)} %correlate.9), channel_id=1, source_target_pairs={{0,2},{1,3},{2,6},{3,7},{4,0},{5,1},{6,4},{7,5},{8,10},{9,11},{10,... | collective-permute-start | bytes 1474568 | tf_op jit(solution)/shard_map/ppermute | solution.py:511
  81.3 7.0 %collective-permute-start.24 = (bf16[4,2,80,128]{3,2,1,0:T(8,128)(2,1)S(1)}, bf16[4,2,80,128]{3,2,1,0:T(8,128)(2,1)S(1)}, u32[]{:S(2)}, u32[]{:S(2)}) collective-permute-start(bf16[4,2,80,128]{3,2,1,0:T(8,128)(2,1)S(1)} %get-tuple-element.98), channel_id=1, source_target_pairs={{0,1},{1,0},{2,3},{3,2},{4,5},{5,4},{6,7},{7,6},{8,9},{9,8},{10,11... | collective-permute-start | bytes 491528 | tf_op jit(solution)/shard_map/ppermute | solution.py:511
  82.5 7.1 %collective-permute-start.25 = (bf16[4,2,80,128]{3,2,1,0:T(8,128)(2,1)S(1)}, bf16[4,2,80,128]{3,2,1,0:T(8,128)(2,1)S(1)}, u32[]{:S(2)}, u32[]{:S(2)}) collective-permute-start(bf16[4,2,80,128]{3,2,1,0:T(8,128)(2,1)S(1)} %get-tuple-element.99), channel_id=1, source_target_pairs={{0,8},{1,9},{2,10},{3,11},{4,12},{5,13},{6,14},{7,15},{8,0},{9,1},... | collective-permute-start | bytes 491528 | tf_op jit(solution)/shard_map/ppermute | solution.py:511
  82.5 8.2 %collective-permute-start.26 = (bf16[4,2,80,128]{3,2,1,0:T(8,128)(2,1)S(1)}, bf16[4,2,80,128]{3,2,1,0:T(8,128)(2,1)S(1)}, u32[]{:S(2)}, u32[]{:S(2)}) collective-permute-start(bf16[4,2,80,128]{3,2,1,0:T(8,128)(2,1)S(1)} %get-tuple-element.100), channel_id=1, source_target_pairs={{0,9},{1,8},{2,11},{3,10},{4,13},{5,12},{6,15},{7,14},{8,1},{9,0},... | collective-permute-start | bytes 491528 | tf_op jit(solution)/shard_map/ppermute | solution.py:511
  88.3 6.7 %collective-permute-start.6 = (bf16[4,2,80,128]{3,2,1,0:T(8,128)(2,1)S(1)}, bf16[4,2,80,128]{3,2,1,0:T(8,128)(2,1)S(1)}, u32[]{:S(2)}, u32[]{:S(2)}) collective-permute-start(bf16[4,2,80,128]{3,2,1,0:T(8,128)(2,1)S(1)} %get-tuple-element.74), channel_id=1, source_target_pairs={{0,1},{1,0},{2,3},{3,2},{4,5},{5,4},{6,7},{7,6},{8,9},{9,8},{10,11... | collective-permute-start | bytes 491528 | tf_op jit(solution)/shard_map/ppermute | solution.py:511
  89.6 5.3 %collective-permute-start.7 = (bf16[4,2,80,128]{3,2,1,0:T(8,128)(2,1)S(1)}, bf16[4,2,80,128]{3,2,1,0:T(8,128)(2,1)S(1)}, u32[]{:S(2)}, u32[]{:S(2)}) collective-permute-start(bf16[4,2,80,128]{3,2,1,0:T(8,128)(2,1)S(1)} %get-tuple-element.75), channel_id=1, source_target_pairs={{0,8},{1,9},{2,10},{3,11},{4,12},{5,13},{6,14},{7,15},{8,0},{9,1},... | collective-permute-start | bytes 491528 | tf_op jit(solution)/shard_map/ppermute | solution.py:511
  90.7 6.9 %collective-permute-start.8 = (bf16[4,2,80,128]{3,2,1,0:T(8,128)(2,1)S(1)}, bf16[4,2,80,128]{3,2,1,0:T(8,128)(2,1)S(1)}, u32[]{:S(2)}, u32[]{:S(2)}) collective-permute-start(bf16[4,2,80,128]{3,2,1,0:T(8,128)(2,1)S(1)} %get-tuple-element.76), channel_id=1, source_target_pairs={{0,9},{1,8},{2,11},{3,10},{4,13},{5,12},{6,15},{7,14},{8,1},{9,0},... | collective-permute-start | bytes 491528 | tf_op jit(solution)/shard_map/ppermute | solution.py:511
  93.6 22.0 %collective-permute-start.35 = (bf16[15,2,64,128]{3,2,1,0:T(8,128)(2,1)S(1)}, bf16[15,2,64,128]{3,2,1,0:T(8,128)(2,1)S(1)}, u32[]{:S(2)}, u32[]{:S(2)}) collective-permute-start(bf16[15,2,64,128]{3,2,1,0:T(8,128)(2,1)S(1)} %correlate.15), channel_id=1, source_target_pairs={{0,2},{1,3},{2,6},{3,7},{4,0},{5,1},{6,4},{7,5},{8,10},{9,11},{10,... | collective-permute-start | bytes 1474568 | tf_op jit(solution)/shard_map/ppermute | solution.py:511
  100.3 7.1 %collective-permute-start.21 = (bf16[4,2,80,128]{3,2,1,0:T(8,128)(2,1)S(1)}, bf16[4,2,80,128]{3,2,1,0:T(8,128)(2,1)S(1)}, u32[]{:S(2)}, u32[]{:S(2)}) collective-permute-start(bf16[4,2,80,128]{3,2,1,0:T(8,128)(2,1)S(1)} %get-tuple-element.94), channel_id=1, source_target_pairs={{0,1},{1,0},{2,3},{3,2},{4,5},{5,4},{6,7},{7,6},{8,9},{9,8},{10,11... | collective-permute-start | bytes 491528 | tf_op jit(solution)/shard_map/ppermute | solution.py:511
  100.4 7.1 %collective-permute-start.22 = (bf16[4,2,80,128]{3,2,1,0:T(8,128)(2,1)S(1)}, bf16[4,2,80,128]{3,2,1,0:T(8,128)(2,1)S(1)}, u32[]{:S(2)}, u32[]{:S(2)}) collective-permute-start(bf16[4,2,80,128]{3,2,1,0:T(8,128)(2,1)S(1)} %get-tuple-element.95), channel_id=1, source_target_pairs={{0,8},{1,9},{2,10},{3,11},{4,12},{5,13},{6,14},{7,15},{8,0},{9,1},... | collective-permute-start | bytes 491528 | tf_op jit(solution)/shard_map/ppermute | solution.py:511
  100.4 8.1 %collective-permute-start.23 = (bf16[4,2,80,128]{3,2,1,0:T(8,128)(2,1)S(1)}, bf16[4,2,80,128]{3,2,1,0:T(8,128)(2,1)S(1)}, u32[]{:S(2)}, u32[]{:S(2)}) collective-permute-start(bf16[4,2,80,128]{3,2,1,0:T(8,128)(2,1)S(1)} %get-tuple-element.96), channel_id=1, source_target_pairs={{0,9},{1,8},{2,11},{3,10},{4,13},{5,12},{6,15},{7,14},{8,1},{9,0},... | collective-permute-start | bytes 491528 | tf_op jit(solution)/shard_map/ppermute | solution.py:511
  102.5 17.4 %collective-permute-start.20 = (bf16[15,2,64,128]{3,2,1,0:T(8,128)(2,1)S(1)}, bf16[15,2,64,128]{3,2,1,0:T(8,128)(2,1)S(1)}, u32[]{:S(2)}, u32[]{:S(2)}) collective-permute-start(bf16[15,2,64,128]{3,2,1,0:T(8,128)(2,1)S(1)} %correlate.10), channel_id=1, source_target_pairs={{0,2},{1,3},{2,6},{3,7},{4,0},{5,1},{6,4},{7,5},{8,10},{9,11},{10,... | collective-permute-start | bytes 1474568 | tf_op jit(solution)/shard_map/ppermute | solution.py:511
  107.4 6.1 %collective-permute-start.17 = (bf16[4,2,80,128]{3,2,1,0:T(8,128)(2,1)S(1)}, bf16[4,2,80,128]{3,2,1,0:T(8,128)(2,1)S(1)}, u32[]{:S(2)}, u32[]{:S(2)}) collective-permute-start(bf16[4,2,80,128]{3,2,1,0:T(8,128)(2,1)S(1)} %get-tuple-element.86), channel_id=1, source_target_pairs={{0,1},{1,0},{2,3},{3,2},{4,5},{5,4},{6,7},{7,6},{8,9},{9,8},{10,11... | collective-permute-start | bytes 491528 | tf_op jit(solution)/shard_map/ppermute | solution.py:511
  107.5 6.1 %collective-permute-start.18 = (bf16[4,2,80,128]{3,2,1,0:T(8,128)(2,1)S(1)}, bf16[4,2,80,128]{3,2,1,0:T(8,128)(2,1)S(1)}, u32[]{:S(2)}, u32[]{:S(2)}) collective-permute-start(bf16[4,2,80,128]{3,2,1,0:T(8,128)(2,1)S(1)} %get-tuple-element.87), channel_id=1, source_target_pairs={{0,8},{1,9},{2,10},{3,11},{4,12},{5,13},{6,14},{7,15},{8,0},{9,1},... | collective-permute-start | bytes 491528 | tf_op jit(solution)/shard_map/ppermute | solution.py:511
  108.5 6.4 %collective-permute-start.19 = (bf16[4,2,80,128]{3,2,1,0:T(8,128)(2,1)S(1)}, bf16[4,2,80,128]{3,2,1,0:T(8,128)(2,1)S(1)}, u32[]{:S(2)}, u32[]{:S(2)}) collective-permute-start(bf16[4,2,80,128]{3,2,1,0:T(8,128)(2,1)S(1)} %get-tuple-element.88), channel_id=1, source_target_pairs={{0,9},{1,8},{2,11},{3,10},{4,13},{5,12},{6,15},{7,14},{8,1},{9,0},... | collective-permute-start | bytes 491528 | tf_op jit(solution)/shard_map/ppermute | solution.py:511

commit v8 on v7

--- a/solution.py
+++ b/solution.py
@@ -277,12 +277,12 @@
         copy[...] = table[...]
     top[0:2] = source[0, 0]
     top[2:4] = receiver[0, 0]
-    rows_x, rows_y = index.shape
+    rows_x, rows_y = index.shape[1:]
     for p in range(shots):
-        fill_index(index, (mine, from_core), my_core == p)
+        fill_index(index.at[p], (mine, from_core), my_core == p)
         if p == 0:
             forward_x(plainly(top), mid, tables[0])
-        value = functools.reduce(jnp.add, lookup(levels[0:1, :], index[...]))
+        value = functools.reduce(jnp.add, lookup(levels[0:1, :], index[p]))
         base = jnp.sum(jnp.sum(value.reshape(rows_x // 8, 8, LANES), axis=0)) / (rows_x * rows_y)
         means[p : p + 1, :] = jnp.full((1, LANES), base, jnp.float32)
         fill_phases(angular, base, wave_x, wave_y, phases.at[p])
@@ -316,9 +316,9 @@
 
 def planes_kernel(place, angular_ref, *refs, shots, strips, width, groups):
     refs = list(refs)
-    top, before, far_a, far_b, far_means, near_a, near_b, means, phases, levels = refs[:10]
-    left_x, right_x, left_y, right_y = refs[10:14]
-    padded_planes, outs = refs[14 : 14 + shots], refs[14 + shots : -3]
+    top, before, far_a, far_b, far_means, indices, means, phases, levels = refs[:9]
+    left_x, right_x, left_y, right_y = refs[9:13]
+    padded_planes, outs = refs[13 : 13 + shots], refs[13 + shots : -3]
     field, mid, index = refs[-3:]
     angular, my_core, parity, spot = angular_ref[0], place[1], place[2], place[3]
 
@@ -335,10 +335,10 @@
     for plane in range(shots):
         if plane > 0:
             forward_x(plainly(field), mid, left_x)
-        fill_index(index, (near_a, near_b), my_core == plane)
         along_y(mid, phases.at[plane], left_y, right_y)
         tables = screen_tables(angular, means[plane : plane + 1, 0:1], levels)
-        inverse_x(mid, right_x, put_screened(tables, index, field, padded_planes[plane]))
+        screened = put_screened(tables, indices.at[plane], field, padded_planes[plane])
+        inverse_x(mid, right_x, screened)
     hand_out(place, padded_planes, outs, 0, 1, strips, width, groups)
 
 
@@ -564,13 +564,13 @@
             pltpu.VMEM((8, LANES), f32),
             pltpu.VMEM((shots, *phase_shape), f32),
             *(pltpu.VMEM(t.shape, t.dtype) for t in tables),
+            pltpu.VMEM((shots, rows_x, rows_y), jnp.int32),
         ],
         grid_spec=pltpu.PrefetchScalarGridSpec(
             num_scalar_prefetch=2,
             grid=(1,),
             in_specs=[top_spec] * 2 + [VMEM_SPEC] * (5 + len(tables)),
-            out_specs=[VMEM_SPEC] * (4 + len(tables)),
-            scratch_shapes=[index_scratch],
+            out_specs=[VMEM_SPEC] * (5 + len(tables)),
         ),
         compiler_params=pltpu.CompilerParams(vmem_limit_bytes=VMEM_BYTES),
         cost_estimate=pl.CostEstimate(flops=4 * 10**9, bytes_accessed=10**6, transcendentals=0),
@@ -579,7 +579,7 @@
         *scalars, unpinned(source_top), unpinned(receiver_top), pinned(mine), pinned(from_core),
         levels, *(unpinned(t) for t in tables), wave_x, wave_y,
     )
-    top, first, means, phases, *tables = prepared
+    top, first, means, phases, *tables, indices = prepared
     tables = list(tables) if len(tables) == 4 else list(tables) * 2
 
     far_means = send(means, up)
@@ -606,7 +606,7 @@
         functools.partial(planes_kernel, shots=shots, strips=strips, width=width, groups=groups),
         "planes",
         scalars,
-        [top, before, *far_second, far_means, *near, means, phases, levels, *tables],
+        [top, before, *far_second, far_means, indices, means, phases, levels, *tables],
         [((4, tiles, rows_x + 2 * HALO, LANES), bf16)] * shots + strip_shapes(1),
         [pltpu.VMEM(whole, bf16), pltpu.VMEM(whole, bf16), index_scratch],
         15 * 10**9,

time: 121 us -> 121 us (level)
  transfers between devices with their start and end apart: 36 -> 36, of which waited for: 23 -> 22; matrix products, arithmetic and copies ran while one was open for 0% -> 0% of each run, Pallas kernels for 21% -> 21%
where the time goes in v8:
time: 121 us; the launch traced here: 120 us
  waiting for transfers between devices  45.9 us (38%)
  Pallas kernels  39.5 us (33%)
  starting transfers between devices  34 us (28%)
    ppermute x36, waiting for transfers between devices, send(): return lax.ppermute(value, AXES, pairs(move, core))  45.9 us
    ppermute x36, starting transfers between devices, send(): return lax.ppermute(value, AXES, pairs(move, core))  34 us
    pallas_call x3, Pallas kernels, call(): pl.pallas_call(kernel, out_shape=[pltpu.VMEM(shape, dtype) for shape, dty...  21 us
    pallas_call x1, Pallas kernels, shards(): pl.pallas_call(functools.partial(prepare_kernel, shots=shots), out_shape=...  7.24 us
    pallas_call x8, Pallas kernels, correlate(): pl.pallas_call(functools.partial(correlate_kernel, width=width, tiles=cou...  6.14 us
    pallas_call x1, Pallas kernels, windows(): pl.pallas_call(functools.partial(window_kernel, blocks=blocks), out_shape...  2.97 us
  transfers between devices with their start and end apart: 36, of which 22 were waited for; matrix products, arithmetic and copies ran while one was open for 0% of the time, Pallas kernels for 21%

profile of v8, /device:TPU:4, one launch (start us, length us, event | category | flops | bytes accessed | tf_op | source)
XLA Modules:
  0.0 120.3 jit_solution(4635131083656790745)
XLA Ops:
  0.8 3.0 %windows.1 = (bf16[512,512]{1,0:T(8,128)(2,1)S(1)}, bf16[512,512]{1,0:T(8,128)(2,1)}) custom-call(s32[4]{0:T(128)S(1)} %pad_add_fusion.place, s32[2,2]{1,0:T(2,128)S(1)} %copy-done, s32[1,1024,1024]{2,1,0:T(8,128)} %codes.1), custom_call_target="tpu_custom_call" | custom-call | tf_op jit(solution)/shard_map/windows/pallas_call | solution.py:458
  3.8 1.3 %collective-permute-start.1 = (bf16[512,512]{1,0:T(8,128)(2,1)S(1)}, bf16[512,512]{1,0:T(8,128)(2,1)S(1)}, u32[]{:S(2)}, u32[]{:S(2)}) collective-permute-start(bf16[512,512]{1,0:T(8,128)(2,1)S(1)} %get-tuple-element.65.mine), channel_id=1, source_target_pairs={{0,16},{1,17},{2,18},{3,19},{4,20},{5,21},{6,22},{7,23}} | collective-permute-start | bytes 1572872 | tf_op jit(solution)/shard_map/ppermute | solution.py:511
  5.1 0.8 collective-permute-done.from_core
  6.7 7.2 %prepare.1 = (bf16[4,512,512]{2,1,0:T(8,128)(2,1)S(1)}, bf16[4,512,512]{2,1,0:T(8,128)(2,1)S(1)}, f32[8,128]{1,0:T(8,128)S(1)}, f32[2,2,384,384]{3,2,1,0:T(8,128...) custom-call(s32[4]{0:T(128)S(1)} %pad_add_fusion.place, ...), custom_call_target="tpu_custom_call" | custom-call | flops 4000000000 | bytes 1000000 | tf_op jit(solution)/shard_map/prepare/pallas_call | solution.py:559
  13.9 1.3 %collective-permute-start.3 = (f32[8,128]{1,0:T(8,128)S(1)}, f32[8,128]{1,0:T(8,128)S(1)}, u32[]{:S(2)}, u32[]{:S(2)}) collective-permute-start(f32[8,128]{1,0:T(8,128)S(1)} %get-tuple-element.62.refs_6_), channel_id=1, source_target_pairs={{0,16},{1,17},{2,18},{3,19},{4,20},{5,21},{6,22},{7,23},{8,24},{9,... | collective-permute-start | bytes 12296 | tf_op jit(solution)/shard_map/ppermute | solution.py:511
  15.9 1.3 %collective-permute-start.5 = (bf16[512,512]{1,0:T(8,128)(2,1)S(1)}, bf16[512,512]{1,0:T(8,128)(2,1)S(1)}, u32[]{:S(2)}, u32[]{:S(2)}) collective-permute-start(bf16[512,512]{1,0:T(8,128)(2,1)S(1)} %collective-permute-done.from_core), channel_id=1, source_target_pairs={{0,16},{1,17},{2,18},{3,19},{4,20},{5,21},{6,22},{7,23}} | collective-permute-start | bytes 1572872 | tf_op jit(solution)/shard_map/ppermute | solution.py:511
  17.2 2.0 %collective-permute-done.1.far_a = bf16[512,512]{1,0:T(8,128)(2,1)S(1)} collective-permute-done((bf16[512,512]{1,0:T(8,128)(2,1)S(1)}, bf16[512,512]{1,0:T(8,128)(2,1)S(1)}, u32[]{:S(2)}, u32[]{:S(2)}) %collective-permute-start.1) | collective-permute-done | bytes 524320 | tf_op jit(solution)/shard_map/ppermute | solution.py:511
  19.5 9.9 %lead.1.refs_1_ = f32[4,512,512]{2,1,0:T(8,128)S(1)} custom-call(s32[4]{0:T(128)S(1)} %pad_add_fusion.place, f32[1]{0:T(128)} %bitcast.4.angular_ref, bf16[4,512,512]{2,1,0:T(8,128)(2,1)S(1)} %get-tuple-element.61.first, bf16[512,512]{1,0:T(8,128)(2,1)S(1)} %collective-permute-done.1.far_a, bf16[512,512]{1,0:T(8,128)(2,1)S(1)} %collective-permute-done.2.far_b, ...), custom_call_target="tpu_custom_call" | custom-call | flops 15000000512 | bytes 1000000 | tf_op jit(solution)/shard_map/lead/pallas_call | solution.py:440
  29.5 2.4 %collective-permute-done.5.refs_3_ = bf16[512,512]{1,0:T(8,128)(2,1)S(1)} collective-permute-done((bf16[512,512]{1,0:T(8,128)(2,1)S(1)}, bf16[512,512]{1,0:T(8,128)(2,1)S(1)}, u32[]{:S(2)}, u32[]{:S(2)}) %collective-permute-start.5) | collective-permute-done | bytes 524320 | tf_op jit(solution)/shard_map/ppermute | solution.py:511
  31.8 10.3 %planes.1 = (bf16[4,4,528,128]{3,2,1,0:T(8,128)(2,1)S(1)}, bf16[4,4,528,128]{3,2,1,0:T(8,128)(2,1)S(1)}, bf16[4,2,80,128]{3,2,1,0:T(8,128)(2,1)S(1)}, bf16[4,2,8...) custom-call(s32[4]{0:T(128)S(1)} %pad_add_fusion.place, ...), custom_call_target="tpu_custom_call" | custom-call | flops 15000000512 | bytes 1000000 | tf_op jit(solution)/shard_map/planes/pallas_call | solution.py:440
  42.1 1.6 %collective-permute-start.30 = (bf16[4,2,80,128]{3,2,1,0:T(8,128)(2,1)S(1)}, bf16[4,2,80,128]{3,2,1,0:T(8,128)(2,1)S(1)}, u32[]{:S(2)}, u32[]{:S(2)}) collective-permute-start(bf16[4,2,80,128]{3,2,1,0:T(8,128)(2,1)S(1)} %get-tuple-element.108), channel_id=1, source_target_pairs={{0,1},{1,0},{2,3},{3,2},{4,5},{5,4},{6,7},{7,6},{8,9},{9,8},{10,11... | collective-permute-start | bytes 491528 | tf_op jit(solution)/shard_map/ppermute | solution.py:511
  44.3 1.5 %collective-permute-start.12 = (bf16[4,2,80,128]{3,2,1,0:T(8,128)(2,1)S(1)}, bf16[4,2,80,128]{3,2,1,0:T(8,128)(2,1)S(1)}, u32[]{:S(2)}, u32[]{:S(2)}) collective-permute-start(bf16[4,2,80,128]{3,2,1,0:T(8,128)(2,1)S(1)} %get-tuple-element.84), channel_id=1, source_target_pairs={{0,1},{1,0},{2,3},{3,2},{4,5},{5,4},{6,7},{7,6},{8,9},{9,8},{10,11... | collective-permute-start | bytes 491528 | tf_op jit(solution)/shard_map/ppermute | solution.py:511
  45.8 2.6 %collective-permute-done.30.refs_1_ = bf16[4,2,80,128]{3,2,1,0:T(8,128)(2,1)S(1)} collective-permute-done((bf16[4,2,80,128]{3,2,1,0:T(8,128)(2,1)S(1)}, bf16[4,2,80,128]{3,2,1,0:T(8,128)(2,1)S(1)}, u32[]{:S(2)}, u32[]{:S(2)}) %collective-permute-start.30) | collective-permute-done | bytes 163872 | tf_op jit(solution)/shard_map/ppermute | solution.py:511
  48.5 3.4 %collective-permute-done.32.refs_3_ = bf16[4,2,80,128]{3,2,1,0:T(8,128)(2,1)S(1)} collective-permute-done((bf16[4,2,80,128]{3,2,1,0:T(8,128)(2,1)S(1)}, bf16[4,2,80,128]{3,2,1,0:T(8,128)(2,1)S(1)}, u32[]{:S(2)}, u32[]{:S(2)}) %collective-permute-start.32) | collective-permute-done | bytes 163872 | tf_op jit(solution)/shard_map/ppermute | solution.py:511
  52.6 1.6 %collective-permute-start.33 = (bf16[15,2,64,128]{3,2,1,0:T(8,128)(2,1)S(1)}, bf16[15,2,64,128]{3,2,1,0:T(8,128)(2,1)S(1)}, u32[]{:S(2)}, u32[]{:S(2)}) collective-permute-start(bf16[15,2,64,128]{3,2,1,0:T(8,128)(2,1)S(1)} %correlate.13), channel_id=1, source_target_pairs={{0,2},{1,3},{2,6},{3,7},{4,0},{5,1},{6,4},{7,5},{8,10},{9,11},{10,... | collective-permute-start | bytes 1474568 | tf_op jit(solution)/shard_map/ppermute | solution.py:511
  54.2 1.3 %collective-permute-done.12.refs_1_ = bf16[4,2,80,128]{3,2,1,0:T(8,128)(2,1)S(1)} collective-permute-done((bf16[4,2,80,128]{3,2,1,0:T(8,128)(2,1)S(1)}, bf16[4,2,80,128]{3,2,1,0:T(8,128)(2,1)S(1)}, u32[]{:S(2)}, u32[]{:S(2)}) %collective-permute-start.12) | collective-permute-done | bytes 163872 | tf_op jit(solution)/shard_map/ppermute | solution.py:511
  55.5 1.7 %collective-permute-done.14.refs_3_ = bf16[4,2,80,128]{3,2,1,0:T(8,128)(2,1)S(1)} collective-permute-done((bf16[4,2,80,128]{3,2,1,0:T(8,128)(2,1)S(1)}, bf16[4,2,80,128]{3,2,1,0:T(8,128)(2,1)S(1)}, u32[]{:S(2)}, u32[]{:S(2)}) %collective-permute-start.14) | collective-permute-done | bytes 163872 | tf_op jit(solution)/shard_map/ppermute | solution.py:511
  57.9 1.8 %collective-permute-start.15 = (bf16[15,2,64,128]{3,2,1,0:T(8,128)(2,1)S(1)}, bf16[15,2,64,128]{3,2,1,0:T(8,128)(2,1)S(1)}, u32[]{:S(2)}, u32[]{:S(2)}) collective-permute-start(bf16[15,2,64,128]{3,2,1,0:T(8,128)(2,1)S(1)} %correlate.8), channel_id=1, source_target_pairs={{0,2},{1,3},{2,6},{3,7},{4,0},{5,1},{6,4},{7,5},{8,10},{9,11},{10,... | collective-permute-start | bytes 1474568 | tf_op jit(solution)/shard_map/ppermute | solution.py:511
  59.8 0.8 strips.1
  61.3 1.3 %collective-permute-start.28 = (bf16[4,2,80,128]{3,2,1,0:T(8,128)(2,1)S(1)}, bf16[4,2,80,128]{3,2,1,0:T(8,128)(2,1)S(1)}, u32[]{:S(2)}, u32[]{:S(2)}) collective-permute-start(bf16[4,2,80,128]{3,2,1,0:T(8,128)(2,1)S(1)} %get-tuple-element.105), channel_id=1, source_target_pairs={{0,8},{1,9},{2,10},{3,11},{4,12},{5,13},{6,14},{7,15},{8,0},{9,1},... | collective-permute-start | bytes 491528 | tf_op jit(solution)/shard_map/ppermute | solution.py:511
  62.8 4.9 %collective-permute-done.27.refs_1_ = bf16[4,2,80,128]{3,2,1,0:T(8,128)(2,1)S(1)} collective-permute-done((bf16[4,2,80,128]{3,2,1,0:T(8,128)(2,1)S(1)}, bf16[4,2,80,128]{3,2,1,0:T(8,128)(2,1)S(1)}, u32[]{:S(2)}, u32[]{:S(2)}) %collective-permute-start.27) | collective-permute-done | bytes 163872 | tf_op jit(solution)/shard_map/ppermute | solution.py:511
  67.8 1.0 collective-permute-start.10
  68.8 2.0 %collective-permute-done.29.refs_3_ = bf16[4,2,80,128]{3,2,1,0:T(8,128)(2,1)S(1)} collective-permute-done((bf16[4,2,80,128]{3,2,1,0:T(8,128)(2,1)S(1)}, bf16[4,2,80,128]{3,2,1,0:T(8,128)(2,1)S(1)}, u32[]{:S(2)}, u32[]{:S(2)}) %collective-permute-start.29) | collective-permute-done | bytes 163872 | tf_op jit(solution)/shard_map/ppermute | solution.py:511
  71.8 2.6 %collective-permute-start.34 = (bf16[15,2,64,128]{3,2,1,0:T(8,128)(2,1)S(1)}, bf16[15,2,64,128]{3,2,1,0:T(8,128)(2,1)S(1)}, u32[]{:S(2)}, u32[]{:S(2)}) collective-permute-start(bf16[15,2,64,128]{3,2,1,0:T(8,128)(2,1)S(1)} %correlate.14), channel_id=1, source_target_pairs={{0,2},{1,3},{2,6},{3,7},{4,0},{5,1},{6,4},{7,5},{8,10},{9,11},{10,... | collective-permute-start | bytes 1474568 | tf_op jit(solution)/shard_map/ppermute | solution.py:511
  74.9 2.8 %collective-permute-done.11.refs_3_ = bf16[4,2,80,128]{3,2,1,0:T(8,128)(2,1)S(1)} collective-permute-done((bf16[4,2,80,128]{3,2,1,0:T(8,128)(2,1)S(1)}, bf16[4,2,80,128]{3,2,1,0:T(8,128)(2,1)S(1)}, u32[]{:S(2)}, u32[]{:S(2)}) %collective-permute-start.11) | collective-permute-done | bytes 163872 | tf_op jit(solution)/shard_map/ppermute | solution.py:511
  77.7 0.8 correlate.9
  78.5 2.7 %collective-permute-start.16 = (bf16[15,2,64,128]{3,2,1,0:T(8,128)(2,1)S(1)}, bf16[15,2,64,128]{3,2,1,0:T(8,128)(2,1)S(1)}, u32[]{:S(2)}, u32[]{:S(2)}) collective-permute-start(bf16[15,2,64,128]{3,2,1,0:T(8,128)(2,1)S(1)} %correlate.9), channel_id=1, source_target_pairs={{0,2},{1,3},{2,6},{3,7},{4,0},{5,1},{6,4},{7,5},{8,10},{9,11},{10,... | collective-permute-start | bytes 1474568 | tf_op jit(solution)/shard_map/ppermute | solution.py:511
  81.2 1.2 collective-permute-start.24
  82.4 0.9 collective-permute-start.26
  83.3 4.9 %collective-permute-done.24.refs_1_ = bf16[4,2,80,128]{3,2,1,0:T(8,128)(2,1)S(1)} collective-permute-done((bf16[4,2,80,128]{3,2,1,0:T(8,128)(2,1)S(1)}, bf16[4,2,80,128]{3,2,1,0:T(8,128)(2,1)S(1)}, u32[]{:S(2)}, u32[]{:S(2)}) %collective-permute-start.24) | collective-permute-done | bytes 163872 | tf_op jit(solution)/shard_map/ppermute | solution.py:511
  88.2 1.3 %collective-permute-start.6 = (bf16[4,2,80,128]{3,2,1,0:T(8,128)(2,1)S(1)}, bf16[4,2,80,128]{3,2,1,0:T(8,128)(2,1)S(1)}, u32[]{:S(2)}, u32[]{:S(2)}) collective-permute-start(bf16[4,2,80,128]{3,2,1,0:T(8,128)(2,1)S(1)} %get-tuple-element.76), channel_id=1, source_target_pairs={{0,1},{1,0},{2,3},{3,2},{4,5},{5,4},{6,7},{7,6},{8,9},{9,8},{10,11... | collective-permute-start | bytes 491528 | tf_op jit(solution)/shard_map/ppermute | solution.py:511
  89.5 1.0 collective-permute-done.26.refs_3_
  90.5 2.2 %collective-permute-start.8 = (bf16[4,2,80,128]{3,2,1,0:T(8,128)(2,1)S(1)}, bf16[4,2,80,128]{3,2,1,0:T(8,128)(2,1)S(1)}, u32[]{:S(2)}, u32[]{:S(2)}) collective-permute-start(bf16[4,2,80,128]{3,2,1,0:T(8,128)(2,1)S(1)} %get-tuple-element.78), channel_id=1, source_target_pairs={{0,9},{1,8},{2,11},{3,10},{4,13},{5,12},{6,15},{7,14},{8,1},{9,0},... | collective-permute-start | bytes 491528 | tf_op jit(solution)/shard_map/ppermute | solution.py:511
  92.7 0.8 correlate.15
  94.9 2.5 %collective-permute-done.8.refs_3_ = bf16[4,2,80,128]{3,2,1,0:T(8,128)(2,1)S(1)} collective-permute-done((bf16[4,2,80,128]{3,2,1,0:T(8,128)(2,1)S(1)}, bf16[4,2,80,128]{3,2,1,0:T(8,128)(2,1)S(1)}, u32[]{:S(2)}, u32[]{:S(2)}) %collective-permute-start.8) | collective-permute-done | bytes 163872 | tf_op jit(solution)/shard_map/ppermute | solution.py:511
  97.4 1.1 collective-permute-done.16.refs_4_
  98.5 0.8 correlate.10
  99.3 1.0 collective-permute-start.21
  100.3 1.2 %collective-permute-start.23 = (bf16[4,2,80,128]{3,2,1,0:T(8,128)(2,1)S(1)}, bf16[4,2,80,128]{3,2,1,0:T(8,128)(2,1)S(1)}, u32[]{:S(2)}, u32[]{:S(2)}) collective-permute-start(bf16[4,2,80,128]{3,2,1,0:T(8,128)(2,1)S(1)} %get-tuple-element.98), channel_id=1, source_target_pairs={{0,9},{1,8},{2,11},{3,10},{4,13},{5,12},{6,15},{7,14},{8,1},{9,0},... | collective-permute-start | bytes 491528 | tf_op jit(solution)/shard_map/ppermute | solution.py:511
  101.5 1.5 %collective-permute-start.20 = (bf16[15,2,64,128]{3,2,1,0:T(8,128)(2,1)S(1)}, bf16[15,2,64,128]{3,2,1,0:T(8,128)(2,1)S(1)}, u32[]{:S(2)}, u32[]{:S(2)}) collective-permute-start(bf16[15,2,64,128]{3,2,1,0:T(8,128)(2,1)S(1)} %correlate.10), channel_id=1, source_target_pairs={{0,2},{1,3},{2,6},{3,7},{4,0},{5,1},{6,4},{7,5},{8,10},{9,11},{10,... | collective-permute-start | bytes 1474568 | tf_op jit(solution)/shard_map/ppermute | solution.py:511
  103.0 3.5 %collective-permute-done.21.refs_1_ = bf16[4,2,80,128]{3,2,1,0:T(8,128)(2,1)S(1)} collective-permute-done((bf16[4,2,80,128]{3,2,1,0:T(8,128)(2,1)S(1)}, bf16[4,2,80,128]{3,2,1,0:T(8,128)(2,1)S(1)}, u32[]{:S(2)}, u32[]{:S(2)}) %collective-permute-start.21) | collective-permute-done | bytes 163872 | tf_op jit(solution)/shard_map/ppermute | solution.py:511
  106.9 1.0 collective-permute-done.23.refs_3_
  107.9 2.2 %collective-permute-start.19 = (bf16[4,2,80,128]{3,2,1,0:T(8,128)(2,1)S(1)}, bf16[4,2,80,128]{3,2,1,0:T(8,128)(2,1)S(1)}, u32[]{:S(2)}, u32[]{:S(2)}) collective-permute-start(bf16[4,2,80,128]{3,2,1,0:T(8,128)(2,1)S(1)} %get-tuple-element.90), channel_id=1, source_target_pairs={{0,9},{1,8},{2,11},{3,10},{4,13},{5,12},{6,15},{7,14},{8,1},{9,0},... | collective-permute-start | bytes 491528 | tf_op jit(solution)/shard_map/ppermute | solution.py:511
  110.9 1.9 %collective-permute-done.17.refs_1_ = bf16[4,2,80,128]{3,2,1,0:T(8,128)(2,1)S(1)} collective-permute-done((bf16[4,2,80,128]{3,2,1,0:T(8,128)(2,1)S(1)}, bf16[4,2,80,128]{3,2,1,0:T(8,128)(2,1)S(1)}, u32[]{:S(2)}, u32[]{:S(2)}) %collective-permute-start.17) | collective-permute-done | bytes 163872 | tf_op jit(solution)/shard_map/ppermute | solution.py:511
  112.7 1.5 %collective-permute-done.19.refs_3_ = bf16[4,2,80,128]{3,2,1,0:T(8,128)(2,1)S(1)} collective-permute-done((bf16[4,2,80,128]{3,2,1,0:T(8,128)(2,1)S(1)}, bf16[4,2,80,128]{3,2,1,0:T(8,128)(2,1)S(1)}, u32[]{:S(2)}, u32[]{:S(2)}) %collective-permute-start.19) | collective-permute-done | bytes 163872 | tf_op jit(solution)/shard_map/ppermute | solution.py:511
  115.1 1.0 finish.2.refs_0_
  116.1 3.2 %collective-permute-done.20.received = bf16[15,2,64,128]{3,2,1,0:T(8,128)(2,1)S(1)} collective-permute-done((bf16[15,2,64,128]{3,2,1,0:T(8,128)(2,1)S(1)}, bf16[15,2,64,128]{3,2,1,0:T(8,128)(2,1)S(1)}, u32[]{:S(2)}, u32[]{:S(2)}) %collective-permute-start.20) | collective-permute-done | bytes 491552 | tf_op jit(solution)/shard_map/ppermute | solution.py:511
  119.3 1.0 finish.3
  (49 shorter events, 10.4 us)
Async XLA Ops:
  0.1 0.7 copy-start
  0.8 5.9 %copy-start.3 = (f32[32]{0:T(128)S(1)}, f32[32]{0:T(128)}, u32[]{:S(2)}) copy-start(f32[32]{0:T(128)} %param.12) | copy-start | bytes 388
  0.8 5.9 %copy-start.1 = (f32[384,1]{1,0:T(8,128)S(1)}, f32[384,1]{1,0:T(8,128)}, u32[]{:S(2)}) copy-start(f32[384,1]{1,0:T(8,128)} %constant.87.clone.refs_2_.wave_x) | copy-start | bytes 4612
  0.8 5.9 %copy-start.2 = (f32[1,384]{1,0:T(1,128)S(1)}, f32[1,384]{1,0:T(1,128)}, u32[]{:S(2)}) copy-start(f32[1,384]{1,0:T(1,128)} %constant.88.clone.refs_3_.wave_y) | copy-start | bytes 4612
  3.7 2.2 %collective-permute-start = (bf16[512,512]{1,0:T(8,128)(2,1)}, bf16[512,512]{1,0:T(8,128)(2,1)S(1)}, u32[]{:S(2)}, u32[]{:S(2)}) collective-permute-start(bf16[512,512]{1,0:T(8,128)(2,1)} %get-tuple-element.59), channel_id=1, source_target_pairs={{0,8},{1,9},{2,10},{3,11},{4,12},{5,13},{6,14},{7,15},{8,0},{9,1},... | collective-permute-start | bytes 1572872 | tf_op jit(solution)/shard_map/ppermute | solution.py:511
  3.8 15.4 %collective-permute-start.1 = (bf16[512,512]{1,0:T(8,128)(2,1)S(1)}, bf16[512,512]{1,0:T(8,128)(2,1)S(1)}, u32[]{:S(2)}, u32[]{:S(2)}) collective-permute-start(bf16[512,512]{1,0:T(8,128)(2,1)S(1)} %get-tuple-element.65.mine), channel_id=1, source_target_pairs={{0,16},{1,17},{2,18},{3,19},{4,20},{5,21},{6,22},{7,23}} | collective-permute-start | bytes 1572872 | tf_op jit(solution)/shard_map/ppermute | solution.py:511
  5.9 13.6 %collective-permute-start.2 = (bf16[512,512]{1,0:T(8,128)(2,1)S(1)}, bf16[512,512]{1,0:T(8,128)(2,1)S(1)}, u32[]{:S(2)}, u32[]{:S(2)}) collective-permute-start(bf16[512,512]{1,0:T(8,128)(2,1)S(1)} %collective-permute-done.from_core), channel_id=1, source_target_pairs={{8,24},{9,25},{10,26},{11,27},{12,28},{13,29},{14,30},{15,31}} | collective-permute-start | bytes 1572872 | tf_op jit(solution)/shard_map/ppermute | solution.py:511
  13.9 5.6 %collective-permute-start.3 = (f32[8,128]{1,0:T(8,128)S(1)}, f32[8,128]{1,0:T(8,128)S(1)}, u32[]{:S(2)}, u32[]{:S(2)}) collective-permute-start(f32[8,128]{1,0:T(8,128)S(1)} %get-tuple-element.62.refs_6_), channel_id=1, source_target_pairs={{0,16},{1,17},{2,18},{3,19},{4,20},{5,21},{6,22},{7,23},{8,24},{9,... | collective-permute-start | bytes 12296 | tf_op jit(solution)/shard_map/ppermute | solution.py:511
  15.2 14.3 %collective-permute-start.4 = (bf16[512,512]{1,0:T(8,128)(2,1)S(1)}, bf16[512,512]{1,0:T(8,128)(2,1)S(1)}, u32[]{:S(2)}, u32[]{:S(2)}) collective-permute-start(bf16[512,512]{1,0:T(8,128)(2,1)S(1)} %get-tuple-element.65.mine), channel_id=1, source_target_pairs={{8,24},{9,25},{10,26},{11,27},{12,28},{13,29},{14,30},{15,31}} | collective-permute-start | bytes 1572872 | tf_op jit(solution)/shard_map/ppermute | solution.py:511
  15.9 15.9 %collective-permute-start.5 = (bf16[512,512]{1,0:T(8,128)(2,1)S(1)}, bf16[512,512]{1,0:T(8,128)(2,1)S(1)}, u32[]{:S(2)}, u32[]{:S(2)}) collective-permute-start(bf16[512,512]{1,0:T(8,128)(2,1)S(1)} %collective-permute-done.from_core), channel_id=1, source_target_pairs={{0,16},{1,17},{2,18},{3,19},{4,20},{5,21},{6,22},{7,23}} | collective-permute-start | bytes 1572872 | tf_op jit(solution)/shard_map/ppermute | solution.py:511
  42.1 6.3 %collective-permute-start.30 = (bf16[4,2,80,128]{3,2,1,0:T(8,128)(2,1)S(1)}, bf16[4,2,80,128]{3,2,1,0:T(8,128)(2,1)S(1)}, u32[]{:S(2)}, u32[]{:S(2)}) collective-permute-start(bf16[4,2,80,128]{3,2,1,0:T(8,128)(2,1)S(1)} %get-tuple-element.108), channel_id=1, source_target_pairs={{0,1},{1,0},{2,3},{3,2},{4,5},{5,4},{6,7},{7,6},{8,9},{9,8},{10,11... | collective-permute-start | bytes 491528 | tf_op jit(solution)/shard_map/ppermute | solution.py:511
  43.7 4.8 %collective-permute-start.31 = (bf16[4,2,80,128]{3,2,1,0:T(8,128)(2,1)S(1)}, bf16[4,2,80,128]{3,2,1,0:T(8,128)(2,1)S(1)}, u32[]{:S(2)}, u32[]{:S(2)}) collective-permute-start(bf16[4,2,80,128]{3,2,1,0:T(8,128)(2,1)S(1)} %get-tuple-element.109), channel_id=1, source_target_pairs={{0,8},{1,9},{2,10},{3,11},{4,12},{5,13},{6,14},{7,15},{8,0},{9,1},... | collective-permute-start | bytes 491528 | tf_op jit(solution)/shard_map/ppermute | solution.py:511
  43.7 8.2 %collective-permute-start.32 = (bf16[4,2,80,128]{3,2,1,0:T(8,128)(2,1)S(1)}, bf16[4,2,80,128]{3,2,1,0:T(8,128)(2,1)S(1)}, u32[]{:S(2)}, u32[]{:S(2)}) collective-permute-start(bf16[4,2,80,128]{3,2,1,0:T(8,128)(2,1)S(1)} %get-tuple-element.110), channel_id=1, source_target_pairs={{0,9},{1,8},{2,11},{3,10},{4,13},{5,12},{6,15},{7,14},{8,1},{9,0},... | collective-permute-start | bytes 491528 | tf_op jit(solution)/shard_map/ppermute | solution.py:511
  44.3 11.2 %collective-permute-start.12 = (bf16[4,2,80,128]{3,2,1,0:T(8,128)(2,1)S(1)}, bf16[4,2,80,128]{3,2,1,0:T(8,128)(2,1)S(1)}, u32[]{:S(2)}, u32[]{:S(2)}) collective-permute-start(bf16[4,2,80,128]{3,2,1,0:T(8,128)(2,1)S(1)} %get-tuple-element.84), channel_id=1, source_target_pairs={{0,1},{1,0},{2,3},{3,2},{4,5},{5,4},{6,7},{7,6},{8,9},{9,8},{10,11... | collective-permute-start | bytes 491528 | tf_op jit(solution)/shard_map/ppermute | solution.py:511
  45.8 9.7 %collective-permute-start.13 = (bf16[4,2,80,128]{3,2,1,0:T(8,128)(2,1)S(1)}, bf16[4,2,80,128]{3,2,1,0:T(8,128)(2,1)S(1)}, u32[]{:S(2)}, u32[]{:S(2)}) collective-permute-start(bf16[4,2,80,128]{3,2,1,0:T(8,128)(2,1)S(1)} %get-tuple-element.85), channel_id=1, source_target_pairs={{0,8},{1,9},{2,10},{3,11},{4,12},{5,13},{6,14},{7,15},{8,0},{9,1},... | collective-permute-start | bytes 491528 | tf_op jit(solution)/shard_map/ppermute | solution.py:511
  48.5 8.7 %collective-permute-start.14 = (bf16[4,2,80,128]{3,2,1,0:T(8,128)(2,1)S(1)}, bf16[4,2,80,128]{3,2,1,0:T(8,128)(2,1)S(1)}, u32[]{:S(2)}, u32[]{:S(2)}) collective-permute-start(bf16[4,2,80,128]{3,2,1,0:T(8,128)(2,1)S(1)} %get-tuple-element.86), channel_id=1, source_target_pairs={{0,9},{1,8},{2,11},{3,10},{4,13},{5,12},{6,15},{7,14},{8,1},{9,0},... | collective-permute-start | bytes 491528 | tf_op jit(solution)/shard_map/ppermute | solution.py:511
  52.6 18.5 %collective-permute-start.33 = (bf16[15,2,64,128]{3,2,1,0:T(8,128)(2,1)S(1)}, bf16[15,2,64,128]{3,2,1,0:T(8,128)(2,1)S(1)}, u32[]{:S(2)}, u32[]{:S(2)}) collective-permute-start(bf16[15,2,64,128]{3,2,1,0:T(8,128)(2,1)S(1)} %correlate.13), channel_id=1, source_target_pairs={{0,2},{1,3},{2,6},{3,7},{4,0},{5,1},{6,4},{7,5},{8,10},{9,11},{10,... | collective-permute-start | bytes 1474568 | tf_op jit(solution)/shard_map/ppermute | solution.py:511
  57.9 19.8 %collective-permute-start.15 = (bf16[15,2,64,128]{3,2,1,0:T(8,128)(2,1)S(1)}, bf16[15,2,64,128]{3,2,1,0:T(8,128)(2,1)S(1)}, u32[]{:S(2)}, u32[]{:S(2)}) collective-permute-start(bf16[15,2,64,128]{3,2,1,0:T(8,128)(2,1)S(1)} %correlate.8), channel_id=1, source_target_pairs={{0,2},{1,3},{2,6},{3,7},{4,0},{5,1},{6,4},{7,5},{8,10},{9,11},{10,... | collective-permute-start | bytes 1474568 | tf_op jit(solution)/shard_map/ppermute | solution.py:511
  60.6 7.1 %collective-permute-start.27 = (bf16[4,2,80,128]{3,2,1,0:T(8,128)(2,1)S(1)}, bf16[4,2,80,128]{3,2,1,0:T(8,128)(2,1)S(1)}, u32[]{:S(2)}, u32[]{:S(2)}) collective-permute-start(bf16[4,2,80,128]{3,2,1,0:T(8,128)(2,1)S(1)} %get-tuple-element.104), channel_id=1, source_target_pairs={{0,1},{1,0},{2,3},{3,2},{4,5},{5,4},{6,7},{7,6},{8,9},{9,8},{10,11... | collective-permute-start | bytes 491528 | tf_op jit(solution)/shard_map/ppermute | solution.py:511
  61.3 6.5 %collective-permute-start.28 = (bf16[4,2,80,128]{3,2,1,0:T(8,128)(2,1)S(1)}, bf16[4,2,80,128]{3,2,1,0:T(8,128)(2,1)S(1)}, u32[]{:S(2)}, u32[]{:S(2)}) collective-permute-start(bf16[4,2,80,128]{3,2,1,0:T(8,128)(2,1)S(1)} %get-tuple-element.105), channel_id=1, source_target_pairs={{0,8},{1,9},{2,10},{3,11},{4,12},{5,13},{6,14},{7,15},{8,0},{9,1},... | collective-permute-start | bytes 491528 | tf_op jit(solution)/shard_map/ppermute | solution.py:511
  62.6 8.2 %collective-permute-start.29 = (bf16[4,2,80,128]{3,2,1,0:T(8,128)(2,1)S(1)}, bf16[4,2,80,128]{3,2,1,0:T(8,128)(2,1)S(1)}, u32[]{:S(2)}, u32[]{:S(2)}) collective-permute-start(bf16[4,2,80,128]{3,2,1,0:T(8,128)(2,1)S(1)} %get-tuple-element.106), channel_id=1, source_target_pairs={{0,9},{1,8},{2,11},{3,10},{4,13},{5,12},{6,15},{7,14},{8,1},{9,0},... | collective-permute-start | bytes 491528 | tf_op jit(solution)/shard_map/ppermute | solution.py:511
  67.7 7.1 %collective-permute-start.9 = (bf16[4,2,80,128]{3,2,1,0:T(8,128)(2,1)S(1)}, bf16[4,2,80,128]{3,2,1,0:T(8,128)(2,1)S(1)}, u32[]{:S(2)}, u32[]{:S(2)}) collective-permute-start(bf16[4,2,80,128]{3,2,1,0:T(8,128)(2,1)S(1)} %get-tuple-element.80), channel_id=1, source_target_pairs={{0,1},{1,0},{2,3},{3,2},{4,5},{5,4},{6,7},{7,6},{8,9},{9,8},{10,11... | collective-permute-start | bytes 491528 | tf_op jit(solution)/shard_map/ppermute | solution.py:511
  67.8 7.0 %collective-permute-start.10 = (bf16[4,2,80,128]{3,2,1,0:T(8,128)(2,1)S(1)}, bf16[4,2,80,128]{3,2,1,0:T(8,128)(2,1)S(1)}, u32[]{:S(2)}, u32[]{:S(2)}) collective-permute-start(bf16[4,2,80,128]{3,2,1,0:T(8,128)(2,1)S(1)} %get-tuple-element.81), channel_id=1, source_target_pairs={{0,8},{1,9},{2,10},{3,11},{4,12},{5,13},{6,14},{7,15},{8,0},{9,1},... | collective-permute-start | bytes 491528 | tf_op jit(solution)/shard_map/ppermute | solution.py:511
  70.8 6.9 %collective-permute-start.11 = (bf16[4,2,80,128]{3,2,1,0:T(8,128)(2,1)S(1)}, bf16[4,2,80,128]{3,2,1,0:T(8,128)(2,1)S(1)}, u32[]{:S(2)}, u32[]{:S(2)}) collective-permute-start(bf16[4,2,80,128]{3,2,1,0:T(8,128)(2,1)S(1)} %get-tuple-element.82), channel_id=1, source_target_pairs={{0,9},{1,8},{2,11},{3,10},{4,13},{5,12},{6,15},{7,14},{8,1},{9,0},... | collective-permute-start | bytes 491528 | tf_op jit(solution)/shard_map/ppermute | solution.py:511
  71.8 20.9 %collective-permute-start.34 = (bf16[15,2,64,128]{3,2,1,0:T(8,128)(2,1)S(1)}, bf16[15,2,64,128]{3,2,1,0:T(8,128)(2,1)S(1)}, u32[]{:S(2)}, u32[]{:S(2)}) collective-permute-start(bf16[15,2,64,128]{3,2,1,0:T(8,128)(2,1)S(1)} %correlate.14), channel_id=1, source_target_pairs={{0,2},{1,3},{2,6},{3,7},{4,0},{5,1},{6,4},{7,5},{8,10},{9,11},{10,... | collective-permute-start | bytes 1474568 | tf_op jit(solution)/shard_map/ppermute | solution.py:511
  78.5 20.0 %collective-permute-start.16 = (bf16[15,2,64,128]{3,2,1,0:T(8,128)(2,1)S(1)}, bf16[15,2,64,128]{3,2,1,0:T(8,128)(2,1)S(1)}, u32[]{:S(2)}, u32[]{:S(2)}) collective-permute-start(bf16[15,2,64,128]{3,2,1,0:T(8,128)(2,1)S(1)} %correlate.9), channel_id=1, source_target_pairs={{0,2},{1,3},{2,6},{3,7},{4,0},{5,1},{6,4},{7,5},{8,10},{9,11},{10,... | collective-permute-start | bytes 1474568 | tf_op jit(solution)/shard_map/ppermute | solution.py:511
  81.2 7.0 %collective-permute-start.24 = (bf16[4,2,80,128]{3,2,1,0:T(8,128)(2,1)S(1)}, bf16[4,2,80,128]{3,2,1,0:T(8,128)(2,1)S(1)}, u32[]{:S(2)}, u32[]{:S(2)}) collective-permute-start(bf16[4,2,80,128]{3,2,1,0:T(8,128)(2,1)S(1)} %get-tuple-element.100), channel_id=1, source_target_pairs={{0,1},{1,0},{2,3},{3,2},{4,5},{5,4},{6,7},{7,6},{8,9},{9,8},{10,11... | collective-permute-start | bytes 491528 | tf_op jit(solution)/shard_map/ppermute | solution.py:511
  82.4 7.1 %collective-permute-start.25 = (bf16[4,2,80,128]{3,2,1,0:T(8,128)(2,1)S(1)}, bf16[4,2,80,128]{3,2,1,0:T(8,128)(2,1)S(1)}, u32[]{:S(2)}, u32[]{:S(2)}) collective-permute-start(bf16[4,2,80,128]{3,2,1,0:T(8,128)(2,1)S(1)} %get-tuple-element.101), channel_id=1, source_target_pairs={{0,8},{1,9},{2,10},{3,11},{4,12},{5,13},{6,14},{7,15},{8,0},{9,1},... | collective-permute-start | bytes 491528 | tf_op jit(solution)/shard_map/ppermute | solution.py:511
  82.4 8.2 %collective-permute-start.26 = (bf16[4,2,80,128]{3,2,1,0:T(8,128)(2,1)S(1)}, bf16[4,2,80,128]{3,2,1,0:T(8,128)(2,1)S(1)}, u32[]{:S(2)}, u32[]{:S(2)}) collective-permute-start(bf16[4,2,80,128]{3,2,1,0:T(8,128)(2,1)S(1)} %get-tuple-element.102), channel_id=1, source_target_pairs={{0,9},{1,8},{2,11},{3,10},{4,13},{5,12},{6,15},{7,14},{8,1},{9,0},... | collective-permute-start | bytes 491528 | tf_op jit(solution)/shard_map/ppermute | solution.py:511
  88.2 6.7 %collective-permute-start.6 = (bf16[4,2,80,128]{3,2,1,0:T(8,128)(2,1)S(1)}, bf16[4,2,80,128]{3,2,1,0:T(8,128)(2,1)S(1)}, u32[]{:S(2)}, u32[]{:S(2)}) collective-permute-start(bf16[4,2,80,128]{3,2,1,0:T(8,128)(2,1)S(1)} %get-tuple-element.76), channel_id=1, source_target_pairs={{0,1},{1,0},{2,3},{3,2},{4,5},{5,4},{6,7},{7,6},{8,9},{9,8},{10,11... | collective-permute-start | bytes 491528 | tf_op jit(solution)/shard_map/ppermute | solution.py:511
  89.5 5.4 %collective-permute-start.7 = (bf16[4,2,80,128]{3,2,1,0:T(8,128)(2,1)S(1)}, bf16[4,2,80,128]{3,2,1,0:T(8,128)(2,1)S(1)}, u32[]{:S(2)}, u32[]{:S(2)}) collective-permute-start(bf16[4,2,80,128]{3,2,1,0:T(8,128)(2,1)S(1)} %get-tuple-element.77), channel_id=1, source_target_pairs={{0,8},{1,9},{2,10},{3,11},{4,12},{5,13},{6,14},{7,15},{8,0},{9,1},... | collective-permute-start | bytes 491528 | tf_op jit(solution)/shard_map/ppermute | solution.py:511
  90.5 6.9 %collective-permute-start.8 = (bf16[4,2,80,128]{3,2,1,0:T(8,128)(2,1)S(1)}, bf16[4,2,80,128]{3,2,1,0:T(8,128)(2,1)S(1)}, u32[]{:S(2)}, u32[]{:S(2)}) collective-permute-start(bf16[4,2,80,128]{3,2,1,0:T(8,128)(2,1)S(1)} %get-tuple-element.78), channel_id=1, source_target_pairs={{0,9},{1,8},{2,11},{3,10},{4,13},{5,12},{6,15},{7,14},{8,1},{9,0},... | collective-permute-start | bytes 491528 | tf_op jit(solution)/shard_map/ppermute | solution.py:511
  93.5 21.5 %collective-permute-start.35 = (bf16[15,2,64,128]{3,2,1,0:T(8,128)(2,1)S(1)}, bf16[15,2,64,128]{3,2,1,0:T(8,128)(2,1)S(1)}, u32[]{:S(2)}, u32[]{:S(2)}) collective-permute-start(bf16[15,2,64,128]{3,2,1,0:T(8,128)(2,1)S(1)} %correlate.15), channel_id=1, source_target_pairs={{0,2},{1,3},{2,6},{3,7},{4,0},{5,1},{6,4},{7,5},{8,10},{9,11},{10,... | collective-permute-start | bytes 1474568 | tf_op jit(solution)/shard_map/ppermute | solution.py:511
  99.3 7.2 %collective-permute-start.21 = (bf16[4,2,80,128]{3,2,1,0:T(8,128)(2,1)S(1)}, bf16[4,2,80,128]{3,2,1,0:T(8,128)(2,1)S(1)}, u32[]{:S(2)}, u32[]{:S(2)}) collective-permute-start(bf16[4,2,80,128]{3,2,1,0:T(8,128)(2,1)S(1)} %get-tuple-element.96), channel_id=1, source_target_pairs={{0,1},{1,0},{2,3},{3,2},{4,5},{5,4},{6,7},{7,6},{8,9},{9,8},{10,11... | collective-permute-start | bytes 491528 | tf_op jit(solution)/shard_map/ppermute | solution.py:511
  100.3 6.6 %collective-permute-start.22 = (bf16[4,2,80,128]{3,2,1,0:T(8,128)(2,1)S(1)}, bf16[4,2,80,128]{3,2,1,0:T(8,128)(2,1)S(1)}, u32[]{:S(2)}, u32[]{:S(2)}) collective-permute-start(bf16[4,2,80,128]{3,2,1,0:T(8,128)(2,1)S(1)} %get-tuple-element.97), channel_id=1, source_target_pairs={{0,8},{1,9},{2,10},{3,11},{4,12},{5,13},{6,14},{7,15},{8,0},{9,1},... | collective-permute-start | bytes 491528 | tf_op jit(solution)/shard_map/ppermute | solution.py:511
  100.3 7.6 %collective-permute-start.23 = (bf16[4,2,80,128]{3,2,1,0:T(8,128)(2,1)S(1)}, bf16[4,2,80,128]{3,2,1,0:T(8,128)(2,1)S(1)}, u32[]{:S(2)}, u32[]{:S(2)}) collective-permute-start(bf16[4,2,80,128]{3,2,1,0:T(8,128)(2,1)S(1)} %get-tuple-element.98), channel_id=1, source_target_pairs={{0,9},{1,8},{2,11},{3,10},{4,13},{5,12},{6,15},{7,14},{8,1},{9,0},... | collective-permute-start | bytes 491528 | tf_op jit(solution)/shard_map/ppermute | solution.py:511
  101.5 17.8 %collective-permute-start.20 = (bf16[15,2,64,128]{3,2,1,0:T(8,128)(2,1)S(1)}, bf16[15,2,64,128]{3,2,1,0:T(8,128)(2,1)S(1)}, u32[]{:S(2)}, u32[]{:S(2)}) collective-permute-start(bf16[15,2,64,128]{3,2,1,0:T(8,128)(2,1)S(1)} %correlate.10), channel_id=1, source_target_pairs={{0,2},{1,3},{2,6},{3,7},{4,0},{5,1},{6,4},{7,5},{8,10},{9,11},{10,... | collective-permute-start | bytes 1474568 | tf_op jit(solution)/shard_map/ppermute | solution.py:511
  106.5 6.2 %collective-permute-start.17 = (bf16[4,2,80,128]{3,2,1,0:T(8,128)(2,1)S(1)}, bf16[4,2,80,128]{3,2,1,0:T(8,128)(2,1)S(1)}, u32[]{:S(2)}, u32[]{:S(2)}) collective-permute-start(bf16[4,2,80,128]{3,2,1,0:T(8,128)(2,1)S(1)} %get-tuple-element.88), channel_id=1, source_target_pairs={{0,1},{1,0},{2,3},{3,2},{4,5},{5,4},{6,7},{7,6},{8,9},{9,8},{10,11... | collective-permute-start | bytes 491528 | tf_op jit(solution)/shard_map/ppermute | solution.py:511
  106.9 5.9 %collective-permute-start.18 = (bf16[4,2,80,128]{3,2,1,0:T(8,128)(2,1)S(1)}, bf16[4,2,80,128]{3,2,1,0:T(8,128)(2,1)S(1)}, u32[]{:S(2)}, u32[]{:S(2)}) collective-permute-start(bf16[4,2,80,128]{3,2,1,0:T(8,128)(2,1)S(1)} %get-tuple-element.89), channel_id=1, source_target_pairs={{0,8},{1,9},{2,10},{3,11},{4,12},{5,13},{6,14},{7,15},{8,0},{9,1},... | collective-permute-start | bytes 491528 | tf_op jit(solution)/shard_map/ppermute | solution.py:511
  107.9 6.4 %collective-permute-start.19 = (bf16[4,2,80,128]{3,2,1,0:T(8,128)(2,1)S(1)}, bf16[4,2,80,128]{3,2,1,0:T(8,128)(2,1)S(1)}, u32[]{:S(2)}, u32[]{:S(2)}) collective-permute-start(bf16[4,2,80,128]{3,2,1,0:T(8,128)(2,1)S(1)} %get-tuple-element.90), channel_id=1, source_target_pairs={{0,9},{1,8},{2,11},{3,10},{4,13},{5,12},{6,15},{7,14},{8,1},{9,0},... | collective-permute-start | bytes 491528 | tf_op jit(solution)/shard_map/ppermute | solution.py:511
